TPU v7x, 256 devices: a whole 4x4x8 slice. The times are simulated.
256 devices in a mesh: ctx: 32 (over x, z_hi, y), tp: 8 (over z_lo, core).
Axes of the slice: x: 4, y: 4, z: 8 (z_hi: 2, z_lo: 4; z = z_hi * 4 + z_lo), core: 2. Of those that a mesh axis runs over, the one named last changes fastest.
Arguments:
- query_states: bfloat16 [8192, 8192], P('ctx', 'tp'), may hold values from -6 to 6
- key_states: bfloat16 [8192, 1024], P('ctx', 'tp'), may hold values from -6 to 6
- value_states: bfloat16 [8192, 1024], P('ctx', 'tp'), may hold values from -6 to 6
- head_kind: int32 [8], replicated, may hold values from 0 to 1, as said below
- page_owner: int32 [512], P('ctx'), may hold values from 0 to 31, as said below
Outputs:
- attn_out: bfloat16 [8192, 8192], P('ctx', 'tp')
- decode_cache: bfloat16 [2048, 16, 2048], P('ctx', None, 'tp')
Inputs may be any that keep to these rules, and one draw needn't show every extreme that they name: `head_kind`: in every pair of KV heads 2 j and 2 j + 1 exactly one is a retrieval head. `page_owner`: the 16 pages of one token range send at most 2 pages to one owner, so an owner receives at most 64 pages; in every draw some owner receives 2 pages from every token range.
All inputs are finite; a program needn't handle non-finite values.
Results may differ from a plain program's by a relative error of at most 0.012.
Values may be sent and summed in bfloat16 or wider, within the bound.
No kernel may reach another device: no remote copies, remote signals or barrier semaphores. Data moves between devices by JAX's collectives and lax.ppermute only.
A program may use at most 64 MiB of HBM per device.

v0:
```python
import math

import jax
import jax.numpy as jnp
from jax import lax
from jax.sharding import PartitionSpec as P

GROUP = 8
HD = 128
SINK = 64
RECENT = 1024
PAGE = 16


neg_large = -1e30


def start_state(head_count, group_count, row_count, head_depth):
    return (
        jnp.full((head_count, group_count, row_count), neg_large, jnp.float32),
        jnp.zeros((head_count, group_count, row_count), jnp.float32),
        jnp.zeros((head_count, group_count, row_count, head_depth), jnp.float32),
    )


def online_update(running, queries, key_block, value_block, allowed):
    running_max, running_sum, running_acc = running
    score_scale = 1.0 / math.sqrt(queries.shape[-1])
    scores = (
        jnp.einsum("thgd,shd->hgts", queries, key_block, preferred_element_type=jnp.float32)
        * score_scale
    )
    scores = jnp.where(allowed, scores, neg_large)
    block_max = jnp.maximum(running_max, jnp.max(scores, axis=-1))
    weights = jnp.where(allowed, jnp.exp(scores - block_max[..., None]), 0.0)
    rescale = jnp.exp(running_max - block_max)
    rounded = weights.astype(jnp.bfloat16)
    update = jnp.einsum("hgts,shd->hgtd", rounded, value_block, preferred_element_type=jnp.float32)
    return (
        block_max,
        running_sum * rescale + jnp.sum(weights, axis=-1),
        running_acc * rescale[..., None] + update,
    )


def finish_heads(running):
    running_max, running_sum, running_acc = running
    mixture = (running_acc / running_sum[..., None]).astype(jnp.bfloat16)
    return mixture.transpose(2, 0, 1, 3)


def fold_keys(queries, query_first, retrieval_flags, any_retrieval, part_rows, role):
    row_count = queries.shape[0]
    head_count = queries.shape[1]
    query_last = query_first + row_count - 1
    query_pos = query_first + lax.iota(jnp.int32, row_count)

    def position_of(gathered_index):
        return (
            gathered_index // part_rows * row_count + role * part_rows + gathered_index % part_rows
        )

    def one_block(running, key_block, value_block, block_start):
        length = key_block.shape[0]
        key_pos = position_of(block_start + lax.iota(jnp.int32, length))
        first_pos = position_of(block_start)
        last_pos = position_of(block_start + length - 1)
        causal = key_pos[None, :] <= query_pos[:, None]
        inside = (key_pos[None, :] < SINK) | (query_pos[:, None] - key_pos[None, :] < RECENT)
        allowed = causal[None, None] & (retrieval_flags[:, None, None, None] | inside[None, None])
        needed = (first_pos <= query_last) & (
            any_retrieval | (first_pos < SINK) | (last_pos > query_first - RECENT)
        )
        return lax.cond(
            needed,
            lambda current: online_update(current, queries, key_block, value_block, allowed),
            lambda current: current,
            running,
        )

    def add_piece(running, pieces, start):
        key_piece, value_piece = pieces
        piece_rows = key_piece.shape[0]
        key_piece = key_piece.reshape(piece_rows, head_count, -1)
        value_piece = value_piece.reshape(piece_rows, head_count, -1)

        def loop_body(block_index, current):
            offset = block_index * 512
            return one_block(
                current,
                lax.dynamic_slice_in_dim(key_piece, offset, 512, 0),
                lax.dynamic_slice_in_dim(value_piece, offset, 512, 0),
                offset,
            )

        return lax.fori_loop(0, piece_rows // 512, loop_body, running)

    return add_piece


def move_pages(key_states, value_states, local_kinds, page_owner, kv_local):
    tok_rows = key_states.shape[0]
    page_count = tok_rows // PAGE
    ctx_count = lax.axis_size("ctx")
    most_pages = max(2, 2 * page_count // ctx_count)
    slot_count = ctx_count * most_pages
    kind_scale = local_kinds.astype(jnp.bfloat16)
    key_flag = key_states.reshape(tok_rows, kv_local, HD) * kind_scale[None, :, None]
    value_flag = value_states.reshape(tok_rows, kv_local, HD) * kind_scale[None, :, None]
    paired = jnp.stack([key_flag, value_flag], axis=2).reshape(page_count, PAGE * kv_local * 2 * HD)
    same_owner = page_owner[:, None] == page_owner[None, :]
    earlier = lax.iota(jnp.int32, page_count)[None, :] < lax.iota(jnp.int32, page_count)[:, None]
    page_rank = jnp.sum((same_owner & earlier).astype(jnp.int32), axis=1)
    slot_index = page_owner * most_pages + page_rank
    selector = (lax.iota(jnp.int32, slot_count)[:, None] == slot_index[None, :]).astype(
        jnp.bfloat16
    )
    packed = jnp.dot(selector, paired, preferred_element_type=jnp.float32).astype(jnp.bfloat16)
    packed = packed.reshape(slot_count, PAGE, kv_local * 2 * HD)
    return lax.all_to_all(packed, "ctx", split_axis=0, concat_axis=0, tiled=True)


def shards(query_states, key_states, value_states, head_kind, page_owner):
    tok_rows = query_states.shape[0]
    kv_local = key_states.shape[1] // HD
    query_first = lax.axis_index("ctx") * tok_rows
    tp_rank = lax.axis_index("tp")
    local_kinds = lax.dynamic_slice_in_dim(head_kind, tp_rank * kv_local, kv_local, 0)
    queries = query_states.reshape(tok_rows, kv_local, GROUP, HD)
    head_flags = local_kinds == 1
    add_piece = fold_keys(queries, query_first, head_flags, jnp.any(head_flags), tok_rows, 0)
    initial = start_state(kv_local, GROUP, tok_rows, HD)
    result = add_piece(
        initial,
        (
            lax.all_gather(key_states, "ctx", axis=0, tiled=True),
            lax.all_gather(value_states, "ctx", axis=0, tiled=True),
        ),
        jnp.int32(0),
    )
    attn_out = finish_heads(result).reshape(tok_rows, kv_local * GROUP * HD)
    decode_cache = move_pages(key_states, value_states, local_kinds, page_owner, kv_local)
    return (attn_out, decode_cache)


def solution(mesh):
    return jax.shard_map(
        shards,
        mesh=mesh,
        in_specs=(P("ctx", "tp"), P("ctx", "tp"), P("ctx", "tp"), P(), P("ctx")),
        out_specs=(P("ctx", "tp"), P("ctx", None, "tp")),
        check_vma=False,
    )
```

profile of v0, /device:TPU:246, one launch (start us, length us, event | category | flops | bytes accessed | tf_op | source)
XLA Modules:
  0.0 288.4 jit_solution(14860806965818076429)
XLA Ops:
  15.3 12.2 %all-to-all-start = ((bf16[64,16,256]{2,1,0:T(8,128)(2,1)}), bf16[64,16,256]{2,1,0:T(8,128)(2,1)S(1)}, u32[]{:S(2)}, u32[]{:S(2)}) async-start(bf16[64,16,256]{2,1,0:T(8,128)(2,1)} %bitcast.41), calls=%async_computation | async-start | bytes 1048576 | tf_op jit(solution)/shard_map/all_to_all | solution.py:120
  28.8 7.8 %all-to-all-done = bf16[64,16,256]{2,1,0:T(8,128)(2,1)S(1)} async-done(((bf16[64,16,256]{2,1,0:T(8,128)(2,1)}), bf16[64,16,256]{2,1,0:T(8,128)(2,1)S(1)}, u32[]{:S(2)}, u32[]{:S(2)}) %all-to-all-start) | async-done | bytes 524320 | tf_op jit(solution)/shard_map/all_to_all | solution.py:120
  36.6 61.1 %all-gather.3.cloned.1.call-done = bf16[8192,128]{1,0:T(8,128)(2,1)} async-done(((bf16[256,128]{1,0:T(8,128)(2,1)}), bf16[8192,128]{1,0:T(8,128)(2,1)}) %all-gather.3.cloned.1.call-update) | async-done | bytes 2097168 | tf_op jit(solution)/shard_map/all_gather | solution.py:136
  97.7 89.2 %all-gather.5.cloned.1.call-done = bf16[8192,128]{1,0:T(8,128)(2,1)} async-done(((bf16[256,128]{1,0:T(8,128)(2,1)}), bf16[8192,128]{1,0:T(8,128)(2,1)}) %all-gather.5.cloned.1.call-update) | async-done | bytes 2097168 | tf_op jit(solution)/shard_map/all_gather | solution.py:137
  187.0 92.2 %while.23 = (s32[]{:T(128)}, f32[1,8,256]{2,1,0:T(8,128)S(1)}, f32[1,8,256]{2,1,0:T(8,128)S(1)}, f32[1,8,256,128]{3,2,1,0:T(8,128)S(1)}, s32[]{:T(128)}, /*index...) while((s32[]{:T(128)}, f32[1,8,256]{2,1,0:T(8,128)S(1)}, ...), condition=%wide.region_5.6_spmd.clone, body=%wide.region_0.5_spmd.clone.sunk | while | flops 551842624 | bytes 16148394 | solution.py:96
  187.1 5.6 %conditional.3 = ((f32[1,8,256]{2,1,0:T(8,128)S(1)}, f32[1,8,256]{2,1,0:T(8,128)S(1)}, f32[1,8,256,128]{3,2,1,0:T(8,128)S(1)})) conditional(s32[]{:T(128)} %convert_element_type.56, (f32[1,8,256]{2,1,0:T(8,128)S(1)}, f32[1,8,256]{2,1,0:T(8,128)S(1)}, f32[1,8,256,128]{3,2,1,0:T(8,128)S(1)}) %tuple.129, (s32[512]{0:T(512)S(1)}, ...), branch_computations={%region_1.1_spmd, %region_2.4_spmd.clone.clone} | conditional | flops 551841536 | bytes 16142414 | solution.py:74
  189.2 2.5 fusion.12
  192.9 5.6 %conditional.3 = ((f32[1,8,256]{2,1,0:T(8,128)S(1)}, f32[1,8,256]{2,1,0:T(8,128)S(1)}, f32[1,8,256,128]{3,2,1,0:T(8,128)S(1)})) conditional(s32[]{:T(128)} %convert_element_type.56, (f32[1,8,256]{2,1,0:T(8,128)S(1)}, f32[1,8,256]{2,1,0:T(8,128)S(1)}, f32[1,8,256,128]{3,2,1,0:T(8,128)S(1)}) %tuple.129, (s32[512]{0:T(512)S(1)}, ...), branch_computations={%region_1.1_spmd, %region_2.4_spmd.clone.clone} | conditional | flops 551841536 | bytes 16142414 | solution.py:74
  194.9 2.5 fusion.12
  198.6 5.6 %conditional.3 = ((f32[1,8,256]{2,1,0:T(8,128)S(1)}, f32[1,8,256]{2,1,0:T(8,128)S(1)}, f32[1,8,256,128]{3,2,1,0:T(8,128)S(1)})) conditional(s32[]{:T(128)} %convert_element_type.56, (f32[1,8,256]{2,1,0:T(8,128)S(1)}, f32[1,8,256]{2,1,0:T(8,128)S(1)}, f32[1,8,256,128]{3,2,1,0:T(8,128)S(1)}) %tuple.129, (s32[512]{0:T(512)S(1)}, ...), branch_computations={%region_1.1_spmd, %region_2.4_spmd.clone.clone} | conditional | flops 551841536 | bytes 16142414 | solution.py:74
  200.7 2.5 fusion.12
  204.4 5.6 %conditional.3 = ((f32[1,8,256]{2,1,0:T(8,128)S(1)}, f32[1,8,256]{2,1,0:T(8,128)S(1)}, f32[1,8,256,128]{3,2,1,0:T(8,128)S(1)})) conditional(s32[]{:T(128)} %convert_element_type.56, (f32[1,8,256]{2,1,0:T(8,128)S(1)}, f32[1,8,256]{2,1,0:T(8,128)S(1)}, f32[1,8,256,128]{3,2,1,0:T(8,128)S(1)}) %tuple.129, (s32[512]{0:T(512)S(1)}, ...), branch_computations={%region_1.1_spmd, %region_2.4_spmd.clone.clone} | conditional | flops 551841536 | bytes 16142414 | solution.py:74
  206.4 2.5 fusion.12
  210.1 5.6 %conditional.3 = ((f32[1,8,256]{2,1,0:T(8,128)S(1)}, f32[1,8,256]{2,1,0:T(8,128)S(1)}, f32[1,8,256,128]{3,2,1,0:T(8,128)S(1)})) conditional(s32[]{:T(128)} %convert_element_type.56, (f32[1,8,256]{2,1,0:T(8,128)S(1)}, f32[1,8,256]{2,1,0:T(8,128)S(1)}, f32[1,8,256,128]{3,2,1,0:T(8,128)S(1)}) %tuple.129, (s32[512]{0:T(512)S(1)}, ...), branch_computations={%region_1.1_spmd, %region_2.4_spmd.clone.clone} | conditional | flops 551841536 | bytes 16142414 | solution.py:74
  212.2 2.5 fusion.12
  215.9 5.6 %conditional.3 = ((f32[1,8,256]{2,1,0:T(8,128)S(1)}, f32[1,8,256]{2,1,0:T(8,128)S(1)}, f32[1,8,256,128]{3,2,1,0:T(8,128)S(1)})) conditional(s32[]{:T(128)} %convert_element_type.56, (f32[1,8,256]{2,1,0:T(8,128)S(1)}, f32[1,8,256]{2,1,0:T(8,128)S(1)}, f32[1,8,256,128]{3,2,1,0:T(8,128)S(1)}) %tuple.129, (s32[512]{0:T(512)S(1)}, ...), branch_computations={%region_1.1_spmd, %region_2.4_spmd.clone.clone} | conditional | flops 551841536 | bytes 16142414 | solution.py:74
  218.0 2.5 fusion.12
  221.7 5.6 %conditional.3 = ((f32[1,8,256]{2,1,0:T(8,128)S(1)}, f32[1,8,256]{2,1,0:T(8,128)S(1)}, f32[1,8,256,128]{3,2,1,0:T(8,128)S(1)})) conditional(s32[]{:T(128)} %convert_element_type.56, (f32[1,8,256]{2,1,0:T(8,128)S(1)}, f32[1,8,256]{2,1,0:T(8,128)S(1)}, f32[1,8,256,128]{3,2,1,0:T(8,128)S(1)}) %tuple.129, (s32[512]{0:T(512)S(1)}, ...), branch_computations={%region_1.1_spmd, %region_2.4_spmd.clone.clone} | conditional | flops 551841536 | bytes 16142414 | solution.py:74
  223.7 2.5 fusion.12
  227.4 5.6 %conditional.3 = ((f32[1,8,256]{2,1,0:T(8,128)S(1)}, f32[1,8,256]{2,1,0:T(8,128)S(1)}, f32[1,8,256,128]{3,2,1,0:T(8,128)S(1)})) conditional(s32[]{:T(128)} %convert_element_type.56, (f32[1,8,256]{2,1,0:T(8,128)S(1)}, f32[1,8,256]{2,1,0:T(8,128)S(1)}, f32[1,8,256,128]{3,2,1,0:T(8,128)S(1)}) %tuple.129, (s32[512]{0:T(512)S(1)}, ...), branch_computations={%region_1.1_spmd, %region_2.4_spmd.clone.clone} | conditional | flops 551841536 | bytes 16142414 | solution.py:74
  229.5 2.5 fusion.12
  233.2 5.6 %conditional.3 = ((f32[1,8,256]{2,1,0:T(8,128)S(1)}, f32[1,8,256]{2,1,0:T(8,128)S(1)}, f32[1,8,256,128]{3,2,1,0:T(8,128)S(1)})) conditional(s32[]{:T(128)} %convert_element_type.56, (f32[1,8,256]{2,1,0:T(8,128)S(1)}, f32[1,8,256]{2,1,0:T(8,128)S(1)}, f32[1,8,256,128]{3,2,1,0:T(8,128)S(1)}) %tuple.129, (s32[512]{0:T(512)S(1)}, ...), branch_computations={%region_1.1_spmd, %region_2.4_spmd.clone.clone} | conditional | flops 551841536 | bytes 16142414 | solution.py:74
  235.2 2.5 fusion.12
  238.9 5.6 %conditional.3 = ((f32[1,8,256]{2,1,0:T(8,128)S(1)}, f32[1,8,256]{2,1,0:T(8,128)S(1)}, f32[1,8,256,128]{3,2,1,0:T(8,128)S(1)})) conditional(s32[]{:T(128)} %convert_element_type.56, (f32[1,8,256]{2,1,0:T(8,128)S(1)}, f32[1,8,256]{2,1,0:T(8,128)S(1)}, f32[1,8,256,128]{3,2,1,0:T(8,128)S(1)}) %tuple.129, (s32[512]{0:T(512)S(1)}, ...), branch_computations={%region_1.1_spmd, %region_2.4_spmd.clone.clone} | conditional | flops 551841536 | bytes 16142414 | solution.py:74
  241.0 2.5 fusion.12
  244.7 5.6 %conditional.3 = ((f32[1,8,256]{2,1,0:T(8,128)S(1)}, f32[1,8,256]{2,1,0:T(8,128)S(1)}, f32[1,8,256,128]{3,2,1,0:T(8,128)S(1)})) conditional(s32[]{:T(128)} %convert_element_type.56, (f32[1,8,256]{2,1,0:T(8,128)S(1)}, f32[1,8,256]{2,1,0:T(8,128)S(1)}, f32[1,8,256,128]{3,2,1,0:T(8,128)S(1)}) %tuple.129, (s32[512]{0:T(512)S(1)}, ...), branch_computations={%region_1.1_spmd, %region_2.4_spmd.clone.clone} | conditional | flops 551841536 | bytes 16142414 | solution.py:74
  246.8 2.5 fusion.12
  250.5 5.6 %conditional.3 = ((f32[1,8,256]{2,1,0:T(8,128)S(1)}, f32[1,8,256]{2,1,0:T(8,128)S(1)}, f32[1,8,256,128]{3,2,1,0:T(8,128)S(1)})) conditional(s32[]{:T(128)} %convert_element_type.56, (f32[1,8,256]{2,1,0:T(8,128)S(1)}, f32[1,8,256]{2,1,0:T(8,128)S(1)}, f32[1,8,256,128]{3,2,1,0:T(8,128)S(1)}) %tuple.129, (s32[512]{0:T(512)S(1)}, ...), branch_computations={%region_1.1_spmd, %region_2.4_spmd.clone.clone} | conditional | flops 551841536 | bytes 16142414 | solution.py:74
  256.2 5.6 %conditional.3 = ((f32[1,8,256]{2,1,0:T(8,128)S(1)}, f32[1,8,256]{2,1,0:T(8,128)S(1)}, f32[1,8,256,128]{3,2,1,0:T(8,128)S(1)})) conditional(s32[]{:T(128)} %convert_element_type.56, (f32[1,8,256]{2,1,0:T(8,128)S(1)}, f32[1,8,256]{2,1,0:T(8,128)S(1)}, f32[1,8,256,128]{3,2,1,0:T(8,128)S(1)}) %tuple.129, (s32[512]{0:T(512)S(1)}, ...), branch_computations={%region_1.1_spmd, %region_2.4_spmd.clone.clone} | conditional | flops 551841536 | bytes 16142414 | solution.py:74
  262.0 5.6 %conditional.3 = ((f32[1,8,256]{2,1,0:T(8,128)S(1)}, f32[1,8,256]{2,1,0:T(8,128)S(1)}, f32[1,8,256,128]{3,2,1,0:T(8,128)S(1)})) conditional(s32[]{:T(128)} %convert_element_type.56, (f32[1,8,256]{2,1,0:T(8,128)S(1)}, f32[1,8,256]{2,1,0:T(8,128)S(1)}, f32[1,8,256,128]{3,2,1,0:T(8,128)S(1)}) %tuple.129, (s32[512]{0:T(512)S(1)}, ...), branch_computations={%region_1.1_spmd, %region_2.4_spmd.clone.clone} | conditional | flops 551841536 | bytes 16142414 | solution.py:74
  267.7 5.6 %conditional.3 = ((f32[1,8,256]{2,1,0:T(8,128)S(1)}, f32[1,8,256]{2,1,0:T(8,128)S(1)}, f32[1,8,256,128]{3,2,1,0:T(8,128)S(1)})) conditional(s32[]{:T(128)} %convert_element_type.56, (f32[1,8,256]{2,1,0:T(8,128)S(1)}, f32[1,8,256]{2,1,0:T(8,128)S(1)}, f32[1,8,256,128]{3,2,1,0:T(8,128)S(1)}) %tuple.129, (s32[512]{0:T(512)S(1)}, ...), branch_computations={%region_1.1_spmd, %region_2.4_spmd.clone.clone} | conditional | flops 551841536 | bytes 16142414 | solution.py:74
  273.5 5.6 %conditional.3 = ((f32[1,8,256]{2,1,0:T(8,128)S(1)}, f32[1,8,256]{2,1,0:T(8,128)S(1)}, f32[1,8,256,128]{3,2,1,0:T(8,128)S(1)})) conditional(s32[]{:T(128)} %convert_element_type.56, (f32[1,8,256]{2,1,0:T(8,128)S(1)}, f32[1,8,256]{2,1,0:T(8,128)S(1)}, f32[1,8,256,128]{3,2,1,0:T(8,128)S(1)}) %tuple.129, (s32[512]{0:T(512)S(1)}, ...), branch_computations={%region_1.1_spmd, %region_2.4_spmd.clone.clone} | conditional | flops 551841536 | bytes 16142414 | solution.py:74
  (222 shorter events, 71.4 us)
Async XLA Ops:
  7.2 21.1 %copy-start = (bf16[256,1024]{1,0:T(8,128)(2,1)S(1)}, bf16[256,1024]{1,0:T(8,128)(2,1)}, u32[]{:S(2)}) copy-start(bf16[256,1024]{1,0:T(8,128)(2,1)} %param.9) | copy-start | bytes 1572868
  7.2 90.5 %all-gather.3.cloned.1.call-start = ((), (), s32[]{:S(2)}) async-start(), calls=%async_computation.1 | async-start | bytes 2162688 | tf_op jit(solution)/shard_map/all_gather | solution.py:136
  7.9 179.0 %all-gather.5.cloned.1.call-start = ((), (), s32[]{:S(2)}) async-start(), calls=%async_computation.2 | async-start | bytes 2162688 | tf_op jit(solution)/shard_map/all_gather | solution.py:137
  15.3 21.3 %all-to-all-start = ((bf16[64,16,256]{2,1,0:T(8,128)(2,1)}), bf16[64,16,256]{2,1,0:T(8,128)(2,1)S(1)}, u32[]{:S(2)}, u32[]{:S(2)}) async-start(bf16[64,16,256]{2,1,0:T(8,128)(2,1)} %bitcast.41), calls=%async_computation | async-start | bytes 1048576 | tf_op jit(solution)/shard_map/all_to_all | solution.py:120
Sparse Core Ops, SparseCore 0:
  11.5 86.1 all-gather.2
  101.2 85.6 all-gather.4
where the time goes:
time: 291 us; the launch traced here: 288 us
  waiting for transfers between devices  159 us (55%)
  matrix products  67.5 us (23%)
  other arithmetic  25 us (9%)
  between operations  15.5 us (5%)
  starting transfers between devices  12.3 us (4%)
  local copies, waits for them, and re-layouts  5.09 us (2%)
  loops' own time  3.45 us (1%)
    all_gather x1, waiting for transfers between devices, shards(): lax.all_gather(value_states, 'ctx', axis=0, tiled=True)  89.2 us
    all_gather x1, waiting for transfers between devices, shards(): lax.all_gather(key_states, 'ctx', axis=0, tiled=True)  61.1 us
    dot_general x16, matrix products, online_update(): jnp.einsum('hgts,shd->hgtd', rounded, value_block, preferred_element_type...  40.3 us
    dot_general x16, matrix products, online_update(): jnp.einsum('thgd,shd->hgts', queries, key_block, preferred_element_type=j...  26.9 us
    reduce_sum x16, other arithmetic, online_update(): jnp.sum(weights, axis=-1)  16.1 us
    all_to_all x1, starting transfers between devices, move_pages(): lax.all_to_all(packed, 'ctx', split_axis=0, concat_axis=0, tiled=True)  12.2 us
    all_to_all x1, waiting for transfers between devices, move_pages(): lax.all_to_all(packed, 'ctx', split_axis=0, concat_axis=0, tiled=True)  7.85 us
  transfers between devices with their start and end apart: 3, of which 3 were waited for; matrix products, arithmetic and copies ran while one was open for 2% of the time, Pallas kernels for 0%

commit v1 on v0

v1 whole, which is shorter than its diff:
```python
import functools
import math

import jax
import jax.numpy as jnp
from jax import lax
from jax.experimental import pallas as pl
from jax.experimental.pallas import tpu as pltpu
from jax.sharding import PartitionSpec as P

GROUP = 8
HD = 128
SINK = 64
RECENT = 1024
PAGE = 16
ROWS = 256
HALF = 128
QUART = 64
SINK_HALF = 32
NEG = -1e30
SCALE = math.log2(math.e) / math.sqrt(HD)
F32 = jnp.float32
BF16 = jnp.bfloat16


def ctx_of(x, z, y):
    return (x % 4) * 8 + (z % 2) * 4 + (y % 4)


CHIPS = [(x, z, y) for x in range(4) for z in range(2) for y in range(4)]
CORE_SWAP = [(i, i ^ 1) for i in range(8)]
Z_SWAP = [(ctx_of(x, z, y), ctx_of(x, z + 1, y)) for x, z, y in CHIPS]
X_SHIFT = {s: [(ctx_of(x, z, y), ctx_of(x + s, z, y)) for x, z, y in CHIPS] for s in (1, 2, 3)}
Y_SHIFT = {s: [(ctx_of(x, z, y), ctx_of(x, z, y + s)) for x, z, y in CHIPS] for s in (1, 2, 3)}


def half_row_pos(j, core):
    return ((j >> 3) << 4) + (core << 3) + (j & 7)


def nt_dot(a, b):
    return lax.dot_general(a, b, (((1,), (1,)), ((), ())), preferred_element_type=F32)


def fold_chunk(q, k, v_ext, m_old, acc_old, allowed):
    s = nt_dot(q, k)
    if allowed is not None:
        s = jnp.where(allowed, s, NEG)
    m_new = jnp.maximum(m_old, jnp.max(s, axis=1, keepdims=True))
    p = jnp.exp2((s - m_new) * SCALE)
    if allowed is not None:
        p = jnp.where(allowed, p, 0.0)
    update = jnp.dot(p.astype(BF16), v_ext, preferred_element_type=F32)
    return m_new, acc_old * jnp.exp2((m_old - m_new) * SCALE) + update


def finish_head(m, acc):
    total = acc[:, HD:HD + 1]
    out = acc[:, :HD] / jnp.maximum(acc[:, HD:], 1e-37)
    lse = jnp.where(total > 0.0, m * SCALE + jnp.log2(jnp.maximum(total, 1e-37)), NEG)
    return out.astype(BF16), lse


def pass_kernel(sc, q_own, q_other, own, p1, p2, p3, far, o_ref, lse_ref, k_s, v_s):
    y, core, c, is_r = sc[1], sc[3], sc[4], sc[5]
    v_s[:, HD:] = jnp.ones((6 * HALF, HD), BF16)
    pieces = (own, p1, p2, p3, far)
    for n, ref in enumerate(pieces):
        k_s[pl.ds(n * HALF, HALF), :] = ref[0:HALF, :]
        v_s[pl.ds(n * HALF, HALF), 0:HD] = ref[HALF:2 * HALF, :]
    base = 5 * HALF
    k_s[pl.ds(base, HALF), :] = jnp.zeros((HALF, HD), BF16)
    v_s[pl.ds(base, HALF), 0:HD] = jnp.zeros((HALF, HD), BF16)

    for n, (ref, off) in enumerate(((far, 256), (p1, 256), (p2, 256), (p3, 256))):
        @pl.when(y == n)
        def _(ref=ref, off=off):
            k_s[pl.ds(base, SINK_HALF), :] = ref[off:off + SINK_HALF, :]
            v_s[pl.ds(base, SINK_HALF), 0:HD] = ref[off + SINK_HALF:off + 2 * SINK_HALF, :]

    n = lax.broadcasted_iota(jnp.int32, (1, 6 * HALF), 1)
    slot = n >> 7
    j = n & (HALF - 1)
    is_sink = slot == 5
    rel = half_row_pos(j, core)
    pos = jnp.where(is_sink, rel, rel + (c - slot) * ROWS)
    qpos = c * ROWS + lax.broadcasted_iota(jnp.int32, (ROWS, 1), 0)
    gap = qpos - pos
    window = (gap >= 0) & (gap < RECENT) & (pos >= 0) & (slot < 5)
    sink = is_sink & (j < SINK_HALF) & (gap >= RECENT)
    allowed = window | sink
    bias = jnp.where(allowed, 0.0, NEG)
    lane = lax.broadcasted_iota(jnp.int32, (ROWS, HD), 1)
    lse_ref[...] = jnp.zeros((ROWS, HD), F32)

    def head(a, carry):
        col = pl.ds(pl.multiple_of(a * HD, HD), HD)
        q = jnp.where(is_r == 1, q_other[:, col], q_own[:, col])
        m0 = jnp.full((ROWS, 1), NEG, F32)
        m, acc = fold_chunk(q, k_s[...], v_s[...], m0, jnp.zeros((ROWS, 2 * HD), F32), bias == 0.0)
        out, lse = finish_head(m, acc)
        o_ref[:, col] = out
        lse_ref[...] = jnp.where(lane == a, lse, lse_ref[...])
        return carry

    lax.fori_loop(0, GROUP, head, 0)


def full_kernel(sc, q_own, q_other, a0, a1, a2, a3, b0, b1, b2, b3, op_ref, lsep_ref,
                keep_ref, keep_lse, send_ref, send_lse, k_s, v_s, m_s, acc_s):
    x, y, z, core, c, is_r = sc[0], sc[1], sc[2], sc[3], sc[4], sc[5]
    first = (a0, a1, a2, a3)
    second = (b0, b1, b2, b3)
    v_s[:, HD:] = jnp.ones((16 * QUART, HD), BF16)
    qpos = c * ROWS + lax.broadcasted_iota(jnp.int32, (ROWS, 1), 0)
    n = lax.broadcasted_iota(jnp.int32, (1, 16 * QUART), 1)
    dy = (n >> 7) & 3
    colour = (n >> 6) & 1
    j = (n & (QUART - 1)) + ((n >> 9) << 6)
    zz = jnp.where(colour == 0, z, 1 - z)
    yy = (y - dy) & 3
    pos = (x * 8 + zz * 4 + yy) * ROWS + half_row_pos(j, core)
    lane = lax.broadcasted_iota(jnp.int32, (ROWS, HD), 1)

    def run(dx):
        for d in range(4):
            for col in range(2):
                at = (d * 2 + col) * QUART
                k_s[pl.ds(at, QUART), :] = first[dx][d, col, 0:QUART, :]
                v_s[pl.ds(at, QUART), 0:HD] = first[dx][d, col, QUART:2 * QUART, :]
                at += 8 * QUART
                k_s[pl.ds(at, QUART), :] = second[d][dx, col, 0:QUART, :]
                v_s[pl.ds(at, QUART), 0:HD] = second[d][dx, col, QUART:2 * QUART, :]

        def head(a, carry):
            cols = pl.ds(pl.multiple_of(a * HD, HD), HD)
            q = jnp.where(is_r == 1, q_own[:, cols], q_other[:, cols])
            if dx == 0:
                m0 = jnp.full((ROWS, 1), NEG, F32)
                m, acc = fold_chunk(q, k_s[...], v_s[...], m0, jnp.zeros((ROWS, 2 * HD), F32), pos <= qpos)
            else:
                m, acc = fold_chunk(q, k_s[...], v_s[...], m_s[a][:, 0:1], acc_s[a], None)
            m_s[a] = jnp.broadcast_to(m, (ROWS, HD))
            acc_s[a] = acc
            return carry

        lax.fori_loop(0, GROUP, head, 0)

    run(0)
    for dx in (1, 2, 3):
        pl.when(x >= dx)(functools.partial(run, dx))

    keep_lse[...] = lsep_ref[...]
    send_lse[...] = lsep_ref[...]

    def finish(mine, mine_lse, other):
        mine_lse[...] = jnp.zeros((ROWS, HD), F32)

        def head(a, carry):
            cols = pl.ds(pl.multiple_of(a * HD, HD), HD)
            out, lse = finish_head(m_s[a][:, 0:1], acc_s[a])
            mine[:, cols] = out
            other[:, cols] = op_ref[:, cols]
            mine_lse[...] = jnp.where(lane == a, lse, mine_lse[...])
            return carry

        lax.fori_loop(0, GROUP, head, 0)

    @pl.when(is_r == 1)
    def _():
        finish(keep_ref, keep_lse, send_ref)

    @pl.when(is_r == 0)
    def _():
        finish(send_ref, send_lse, keep_ref)


def merge_kernel(o0, lse0, o1, lse1, out_ref):
    for a in range(GROUP):
        cols = slice(a * HD, (a + 1) * HD)
        l0, l1 = lse0[:, a:a + 1], lse1[:, a:a + 1]
        top = jnp.maximum(l0, l1)
        w0, w1 = jnp.exp2(l0 - top), jnp.exp2(l1 - top)
        scale = 1.0 / (w0 + w1)
        out = o0[:, cols].astype(F32) * (w0 * scale) + o1[:, cols].astype(F32) * (w1 * scale)
        out_ref[:, cols] = out.astype(BF16)


def pages_kernel(sc, a0, a1, a2, a3, b0, b1, b2, b3, out_ref):
    x, y, z, c = sc[0], sc[1], sc[2], sc[4]
    first = (a0, a1, a2, a3)
    second = (b0, b1, b2, b3)
    row = lax.broadcasted_iota(jnp.int32, (PAGE, HD), 0)
    lane = lax.broadcasted_iota(jnp.int32, (PAGE, HD), 1)
    same_row = (lane & 7) == (row & 7)
    want = (2 * c + (row >> 3)).astype(F32)
    for dx in range(4):
        for d in range(4):
            for col in range(2):
                f, s = first[dx], second[d]
                code = f[d, col, 2 * QUART:2 * QUART + 16, :].astype(F32)
                select = jnp.where(same_row & (code == want), 1.0, 0.0).astype(BF16)
                xx = (x - dx) & 3
                yy = (y - d) & 3
                zz = z if col == 0 else 1 - z
                block = xx * 8 + zz * 4 + yy
                for part in range(2):
                    rows = slice(part * QUART, (part + 1) * QUART)
                    pages = jnp.dot(select[:, :QUART], f[d, col, rows, :], preferred_element_type=F32)
                    pages += jnp.dot(select[:, QUART:], s[dx, col, rows, :], preferred_element_type=F32)
                    out_ref[block, :, part * HD:(part + 1) * HD] = pages.astype(BF16)


VMEM_SPEC = pl.BlockSpec(memory_space=pltpu.VMEM)
SMEM_SPEC = pl.BlockSpec(memory_space=pltpu.SMEM)


def call(kernel, out_shape, scratch, flops, sc, *args):
    many = isinstance(out_shape, tuple)
    specs = ([SMEM_SPEC] if sc is not None else []) + [VMEM_SPEC] * len(args)
    operands = ([sc] if sc is not None else []) + list(args)
    return pl.pallas_call(
        kernel,
        out_shape=out_shape,
        in_specs=specs,
        out_specs=(VMEM_SPEC,) * len(out_shape) if many else VMEM_SPEC,
        scratch_shapes=scratch,
        compiler_params=pltpu.CompilerParams(vmem_limit_bytes=40 * 1024 * 1024),
        cost_estimate=pl.CostEstimate(flops=flops, bytes_accessed=4 << 20, transcendentals=flops // 512),
    )(*operands)


def shards(q, k, v, head_kind, page_owner):
    c = lax.axis_index("ctx")
    tp = lax.axis_index("tp")
    x, z, y = c // 8, (c // 4) % 2, c % 4
    core = tp % 2
    is_r = lax.dynamic_index_in_dim(head_kind, tp, 0, keepdims=False) == 1
    sc = jnp.stack([x, y, z, core, c, is_r.astype(jnp.int32), tp, tp]).astype(jnp.int32)

    earlier = lax.iota(jnp.int32, 16)[None, :] < lax.iota(jnp.int32, 16)[:, None]
    rank = jnp.sum(((page_owner[:, None] == page_owner[None, :]) & earlier).astype(jnp.int32), axis=1)
    code = jnp.repeat((page_owner * 2 + rank).astype(BF16), 8)
    meta = jnp.broadcast_to(code[None, :], (16, HD))

    kv = jnp.stack([k, v]).reshape(2, 16, 2, 8, HD)
    stay = lax.dynamic_index_in_dim(kv, core, 2, keepdims=False).reshape(2, HALF, HD)
    leave = lax.dynamic_index_in_dim(kv, 1 - core, 2, keepdims=False).reshape(2, HALF, HD)
    came = lax.ppermute(leave, "tp", CORE_SWAP)
    q_other = lax.ppermute(q, "tp", CORE_SWAP)
    ret = jnp.where(is_r, stay, came)
    pas = jnp.where(is_r, came, stay)

    r1 = jnp.concatenate([ret[0, :QUART], ret[1, :QUART], meta])
    r2 = jnp.concatenate([ret[0, QUART:], ret[1, QUART:]])
    pas = pas.reshape(2 * HALF, HD)
    mine = jnp.concatenate([r1, r2, pas])
    theirs = lax.ppermute(mine, "ctx", Z_SWAP)
    n1, n2 = r1.shape[0], r1.shape[0] + r2.shape[0]
    r1 = jnp.stack([r1, theirs[:n1]])
    r2 = jnp.stack([r2, theirs[n1:n2]])
    pas_z = theirs[n2:]
    low = jnp.where(z == 0, pas, pas_z)
    sink = jnp.concatenate([low[:SINK_HALF], low[HALF:HALF + SINK_HALF]])

    pas_x = lax.ppermute(pas_z, "ctx", [(ctx_of(i, 0, j), ctx_of(i + 1, 0, j)) for i in range(3) for j in range(4)])
    h1 = jnp.stack([r1] + [lax.ppermute(r1, "ctx", Y_SHIFT[s]) for s in (1, 2, 3)])
    m2 = jnp.concatenate([r2.reshape(2 * HALF, HD), sink])
    got = [lax.ppermute(m2, "ctx", X_SHIFT[s]) for s in (1, 2, 3)]
    h2 = jnp.stack([r2] + [g[:2 * HALF].reshape(2, HALF, HD) for g in got])
    for s in (1, 2, 3):
        sink = jnp.where(x == s, got[s - 1][2 * HALF:], sink)

    far = jnp.where(z == 1, pas_z, pas_x)
    near_pas = {s: jnp.concatenate([jnp.where(y + s < 4, pas, far), sink]) for s in (1, 2, 3)}
    p = [lax.ppermute(near_pas[s], "ctx", Y_SHIFT[s]) for s in (1, 2, 3)]
    far = jnp.concatenate([far, sink])

    a = [h1] + [lax.ppermute(h1, "ctx", X_SHIFT[s]) for s in (1, 2, 3)]
    b = [h2] + [lax.ppermute(h2, "ctx", Y_SHIFT[s]) for s in (1, 2, 3)]

    o_shape = jax.ShapeDtypeStruct((ROWS, GROUP * HD), BF16)
    lse_shape = jax.ShapeDtypeStruct((ROWS, HD), F32)
    o_pas, lse_pas = call(
        pass_kernel, (o_shape, lse_shape),
        [pltpu.VMEM((6 * HALF, HD), BF16), pltpu.VMEM((6 * HALF, 2 * HD), BF16)],
        2 * 2048 * 768 * 384, sc, q, q_other, pas, *p, far)
    keep, keep_lse, send, send_lse = call(
        full_kernel, (o_shape, lse_shape, o_shape, lse_shape),
        [pltpu.VMEM((16 * QUART, HD), BF16), pltpu.VMEM((16 * QUART, 2 * HD), BF16),
         pltpu.VMEM((GROUP, ROWS, HD), F32), pltpu.VMEM((GROUP, ROWS, 2 * HD), F32)],
        2 * 2048 * 4096 * 384, sc, q, q_other, *a, *b, o_pas, lse_pas)
    pages = call(pages_kernel, jax.ShapeDtypeStruct((32, PAGE, 2 * HD), BF16), [], 1 << 26, sc, *a, *b)

    got_o = lax.ppermute(send, "tp", CORE_SWAP)
    got_lse = lax.ppermute(send_lse, "tp", CORE_SWAP)
    got_pages = lax.ppermute(pages, "tp", CORE_SWAP)
    attn_out = call(merge_kernel, o_shape, [], 1 << 24, None, keep, keep_lse, got_o, got_lse)
    here = pages.reshape(SINK, 1, 8, 2 * HD)
    there = got_pages.reshape(SINK, 1, 8, 2 * HD)
    both = jnp.where(core == 0, jnp.concatenate([here, there], 1), jnp.concatenate([there, here], 1))
    decode_cache = jnp.where(is_r, both.reshape(SINK, PAGE, 2 * HD), jnp.zeros((), BF16))
    return attn_out, decode_cache


def solution(mesh):
    return jax.shard_map(
        shards,
        mesh=mesh,
        in_specs=(P("ctx", "tp"), P("ctx", "tp"), P("ctx", "tp"), P(), P("ctx")),
        out_specs=(P("ctx", "tp"), P("ctx", None, "tp")),
        check_vma=False,
    )
```

time: 291 us -> 109 us (0.37)
  the two profiles are of different devices: /device:TPU:246 before, /device:TPU:47 now
where the time goes in v1:
time: 109 us; the launch traced here: 108 us
  Pallas kernels  43.6 us (40%)
  starting transfers between devices  38.7 us (36%)
  waiting for transfers between devices  15.9 us (15%)
  local copies, waits for them, and re-layouts  6.05 us (6%)
  other arithmetic  2.28 us (2%)
  between operations  1.66 us (2%)
    pallas_call x4, Pallas kernels, call(): pl.pallas_call(kernel, out_shape=out_shape, in_specs=specs, out_specs=(VM...  43.6 us
    ppermute x1, starting transfers between devices, shards(): got_o = lax.ppermute(send, 'tp', CORE_SWAP)  11.1 us
    ppermute x1, waiting for transfers between devices, shards(): theirs = lax.ppermute(mine, 'ctx', Z_SWAP)  6.42 us
    ppermute x1, starting transfers between devices, shards(): theirs = lax.ppermute(mine, 'ctx', Z_SWAP)  6.1 us
    unnamed x31, local copies, waits for them, and re-layouts  5.16 us
    ppermute x3, starting transfers between devices, shards(): b = [h2] + [lax.ppermute(h2, 'ctx', Y_SHIFT[s]) for s in (1, 2, 3)]  4.49 us
    ppermute x3, starting transfers between devices, shards(): lax.ppermute(r1, 'ctx', Y_SHIFT[s])  4.16 us
    ppermute x3, starting transfers between devices, shards(): a = [h1] + [lax.ppermute(h1, 'ctx', X_SHIFT[s]) for s in (1, 2, 3)]  3.73 us
  transfers between devices with their start and end apart: 22, of which 8 were waited for; matrix products, arithmetic and copies ran while one was open for 3% of the time, Pallas kernels for 8%

profile of v1, /device:TPU:47, one launch (start us, length us, event | category | flops | bytes accessed | tf_op | source)
XLA Modules:
  0.0 108.3 jit_solution(8261967434437854522)
XLA Ops:
  0.6 0.8 collective-permute-start
  1.4 0.8 fusion.2
  4.5 6.1 %collective-permute-start.2 = (bf16[528,128]{1,0:T(8,128)(2,1)S(1)}, bf16[528,128]{1,0:T(8,128)(2,1)S(1)}, u32[]{:S(2)}, u32[]{:S(2)}) collective-permute-start(bf16[528,128]{1,0:T(8,128)(2,1)S(1)} %constant_dynamic-update-slice_fusion), channel_id=1, source_target_pairs={{0,32},{8,40},{16,48},{24,56},{32,0},{40,8},{48,16},{56,24},{64,96... | collective-permute-start | bytes 405512 | tf_op jit(solution)/shard_map/ppermute | solution.py:258
  10.6 6.4 %collective-permute-done.2 = bf16[528,128]{1,0:T(8,128)(2,1)S(1)} collective-permute-done((bf16[528,128]{1,0:T(8,128)(2,1)S(1)}, bf16[528,128]{1,0:T(8,128)(2,1)S(1)}, u32[]{:S(2)}, u32[]{:S(2)}) %collective-permute-start.2) | collective-permute-done | bytes 135200 | tf_op jit(solution)/shard_map/ppermute | solution.py:258
  17.3 2.3 %collective-permute-start.4 = (bf16[2,144,128]{2,1,0:T(8,128)(2,1)S(1)}, bf16[2,144,128]{2,1,0:T(8,128)(2,1)S(1)}, u32[]{:S(2)}, u32[]{:S(2)}) collective-permute-start(bf16[2,144,128]{2,1,0:T(8,128)(2,1)S(1)} %get-tuple-element.22), channel_id=1, source_target_pairs={{0,16},{8,24},{16,0},{24,8},{32,48},{40,56},{48,32},{56,40},{64,80... | collective-permute-start | bytes 221192 | tf_op jit(solution)/shard_map/ppermute | solution.py:267
  19.6 1.6 %collective-permute-start.3 = (bf16[2,144,128]{2,1,0:T(8,128)(2,1)S(1)}, bf16[2,144,128]{2,1,0:T(8,128)(2,1)S(1)}, u32[]{:S(2)}, u32[]{:S(2)}) collective-permute-start(bf16[2,144,128]{2,1,0:T(8,128)(2,1)S(1)} %get-tuple-element.22), channel_id=1, source_target_pairs={{0,8},{8,16},{16,24},{24,0},{32,40},{40,48},{48,56},{56,32},{64,72... | collective-permute-start | bytes 221192 | tf_op jit(solution)/shard_map/ppermute | solution.py:267
  21.3 1.3 %collective-permute-start.15 = (bf16[256,128]{1,0:T(8,128)(2,1)S(1)}, bf16[256,128]{1,0:T(8,128)(2,1)S(1)}, u32[]{:S(2)}, u32[]{:S(2)}) collective-permute-start(bf16[256,128]{1,0:T(8,128)(2,1)S(1)} %slice.66), channel_id=1, source_target_pairs={{0,64},{8,72},{16,80},{24,88},{64,128},{72,136},{80,144},{88,152},... | collective-permute-start | bytes 196616 | tf_op jit(solution)/shard_map/ppermute | solution.py:266
  22.6 3.7 %collective-permute-done.15 = bf16[256,128]{1,0:T(8,128)(2,1)S(1)} collective-permute-done((bf16[256,128]{1,0:T(8,128)(2,1)S(1)}, bf16[256,128]{1,0:T(8,128)(2,1)S(1)}, u32[]{:S(2)}, u32[]{:S(2)}) %collective-permute-start.15) | collective-permute-done | bytes 65568 | tf_op jit(solution)/shard_map/ppermute | solution.py:266
  27.0 0.7 collective-permute-start.10
  27.7 2.0 %collective-permute-start.9 = (bf16[320,128]{1,0:T(8,128)(2,1)S(1)}, bf16[320,128]{1,0:T(8,128)(2,1)S(1)}, u32[]{:S(2)}, u32[]{:S(2)}) collective-permute-start(bf16[320,128]{1,0:T(8,128)(2,1)S(1)} %pad_maximum_fusion.6), channel_id=1, source_target_pairs={{0,64},{8,72},{16,80},{24,88},{32,96},{40,104},{48,112},{56,120},{... | collective-permute-start | bytes 245768 | tf_op jit(solution)/shard_map/ppermute | solution.py:269
  29.8 0.7 collective-permute-start.6
  30.9 1.2 %collective-permute-done.10 = bf16[320,128]{1,0:T(8,128)(2,1)S(1)} collective-permute-done((bf16[320,128]{1,0:T(8,128)(2,1)S(1)}, bf16[320,128]{1,0:T(8,128)(2,1)S(1)}, u32[]{:S(2)}, u32[]{:S(2)}) %collective-permute-start.10) | collective-permute-done | bytes 81952 | tf_op jit(solution)/shard_map/ppermute | solution.py:269
  33.0 1.5 %collective-permute-start.17 = (bf16[320,128]{1,0:T(8,128)(2,1)S(1)}, bf16[320,128]{1,0:T(8,128)(2,1)S(1)}, u32[]{:S(2)}, u32[]{:S(2)}) collective-permute-start(bf16[320,128]{1,0:T(8,128)(2,1)S(1)} %get-tuple-element.32), channel_id=1, source_target_pairs={{0,16},{8,24},{16,0},{24,8},{32,48},{40,56},{48,32},{56,40},{64,80... | collective-permute-start | bytes 245768 | tf_op jit(solution)/shard_map/ppermute | solution.py:276
  34.5 1.4 %collective-permute-start.7 = (bf16[4,2,144,128]{3,2,1,0:T(8,128)(2,1)S(1)}, bf16[4,2,144,128]{3,2,1,0:T(8,128)(2,1)S(1)}, u32[]{:S(2)}, u32[]{:S(2)}) collective-permute-start(bf16[4,2,144,128]{3,2,1,0:T(8,128)(2,1)S(1)} %pad_maximum_fusion.a0), channel_id=1, source_target_pairs={{0,128},{8,136},{16,144},{24,152},{32,160},{40,168},{48,176},{56,1... | collective-permute-start | bytes 884744 | tf_op jit(solution)/shard_map/ppermute | solution.py:279
  36.0 1.6 %collective-permute-start.8 = (bf16[4,2,144,128]{3,2,1,0:T(8,128)(2,1)S(1)}, bf16[4,2,144,128]{3,2,1,0:T(8,128)(2,1)S(1)}, u32[]{:S(2)}, u32[]{:S(2)}) collective-permute-start(bf16[4,2,144,128]{3,2,1,0:T(8,128)(2,1)S(1)} %pad_maximum_fusion.a0), channel_id=1, source_target_pairs={{0,192},{8,200},{16,208},{24,216},{32,224},{40,232},{48,240},{56,2... | collective-permute-start | bytes 884744 | tf_op jit(solution)/shard_map/ppermute | solution.py:279
  37.8 0.6 copy-done.5
  38.5 1.0 collective-permute-start.18
  39.5 2.5 %collective-permute-done.18.p3 = bf16[320,128]{1,0:T(8,128)(2,1)S(1)} collective-permute-done((bf16[320,128]{1,0:T(8,128)(2,1)S(1)}, bf16[320,128]{1,0:T(8,128)(2,1)S(1)}, u32[]{:S(2)}, u32[]{:S(2)}) %collective-permute-start.18) | collective-permute-done | bytes 81952 | tf_op jit(solution)/shard_map/ppermute | solution.py:276
  42.7 0.7 collective-permute-start.12
  43.4 2.1 %collective-permute-start.13 = (bf16[4,2,128,128]{3,2,1,0:T(8,128)(2,1)S(1)}, bf16[4,2,128,128]{3,2,1,0:T(8,128)(2,1)S(1)}, u32[]{:S(2)}, u32[]{:S(2)}) collective-permute-start(bf16[4,2,128,128]{3,2,1,0:T(8,128)(2,1)S(1)} %pad_maximum_fusion.1.b0), channel_id=1, source_target_pairs={{0,16},{8,24},{16,0},{24,8},{32,48},{40,56},{48,32},{56,40},{64,80... | collective-permute-start | bytes 786440 | tf_op jit(solution)/shard_map/ppermute | solution.py:280
  45.5 1.7 %collective-permute-start.14 = (bf16[4,2,128,128]{3,2,1,0:T(8,128)(2,1)S(1)}, bf16[4,2,128,128]{3,2,1,0:T(8,128)(2,1)S(1)}, u32[]{:S(2)}, u32[]{:S(2)}) collective-permute-start(bf16[4,2,128,128]{3,2,1,0:T(8,128)(2,1)S(1)} %pad_maximum_fusion.1.b0), channel_id=1, source_target_pairs={{0,24},{8,0},{16,8},{24,16},{32,56},{40,32},{48,40},{56,48},{64,88... | collective-permute-start | bytes 786440 | tf_op jit(solution)/shard_map/ppermute | solution.py:280
  47.3 0.9 copy-done.6
  48.2 0.9 copy-done.8
  49.1 7.6 %shard_map.68 = (bf16[256,1024]{1,0:T(8,128)(2,1)S(1)}, f32[256,128]{1,0:T(8,128)S(1)}) custom-call(s32[8]{0:T(128)S(1)} %stack.81.sc, bf16[256,1024]{1,0:T(8,128)(2,1)S(1)} %copy-done.2, bf16[256,1024]{1,0:T(8,128)(2,1)S(1)} %collective-permute-done.q_other, bf16[256,128]{1,0:T(8,128)(2,1)S(1)} %bitcast.66, ...), custom_call_target="tpu_custom_call" | custom-call | flops 1207959552 | bytes 4194304 | tf_op jit(solution)/shard_map/pallas_call | solution.py:222
  56.7 1.0 copy-done.4
  57.8 33.2 %shard_map.69 = (bf16[256,1024]{1,0:T(8,128)(2,1)S(1)}, f32[256,128]{1,0:T(8,128)S(1)}, bf16[256,1024]{1,0:T(8,128)(2,1)}, f32[256,128]{1,0:T(8,128)}) custom-call(s32[8]{0:T(128)S(1)} %stack.81.sc, bf16[256,1024]{1,0:T(8,128)(2,1)S(1)} %copy-done.2, bf16[256,1024]{1,0:T(8,128)(2,1)S(1)} %copy-done.4, bf16[4,2,144,128]{3,2,1,0:T(8,128)(2,1)S(1)} %pad_maximum_fusion.a0, ...), custom_call_target="tpu_custom_call" | custom-call | flops 6442450944 | bytes 4194304 | tf_op jit(solution)/shard_map/pallas_call | solution.py:222
  91.0 0.6 copy-done
  91.7 11.1 %collective-permute-start.19 = (bf16[256,1024]{1,0:T(8,128)(2,1)}, bf16[256,1024]{1,0:T(8,128)(2,1)S(1)}, u32[]{:S(2)}, u32[]{:S(2)}) collective-permute-start(bf16[256,1024]{1,0:T(8,128)(2,1)} %get-tuple-element.12), channel_id=1, source_target_pairs={{0,1},{1,0},{2,3},{3,2},{4,5},{5,4},{6,7},{7,6},{8,9},{9,8},{10,11... | collective-permute-start | bytes 1572872 | tf_op jit(solution)/shard_map/ppermute | solution.py:295
  102.8 1.3 %shard_map.71 = bf16[32,16,256]{2,1,0:T(8,128)(2,1)S(1)} custom-call(s32[8]{0:T(128)S(1)} %stack.81.sc, bf16[4,2,144,128]{3,2,1,0:T(8,128)(2,1)S(1)} %pad_maximum_fusion.a0, bf16[4,2,144,128]{3,2,1,0:T(8,128)(2,1)S(1)} %collective-permute-done.6.a1, bf16[4,2,144,128]{3,2,1,0:T(8,128)(2,1)S(1)} %collective-permute-done.7.a2, ...), custom_call_target="tpu_custom_call" | custom-call | flops 67108864 | bytes 4194304 | tf_op jit(solution)/shard_map/pallas_call | solution.py:222
  104.6 1.0 collective-permute-done.21
  105.7 1.1 copy_bitcast_fusion
  106.7 1.5 %shard_map.70 = bf16[256,1024]{1,0:T(8,128)(2,1)} custom-call(bf16[256,1024]{1,0:T(8,128)(2,1)S(1)} %get-tuple-element.10.o0, f32[256,128]{1,0:T(8,128)S(1)} %copy-done.1, bf16[256,1024]{1,0:T(8,128)(2,1)S(1)} %collective-permute-done.19.o1, f32[256,128]{1,0:T(8,128)S(1)} %collective-permute-done.20.lse1), custom_call_target="tpu_custom_call" | custom-call | flops 16777216 | bytes 4194304 | tf_op jit(solution)/shard_map/pallas_call | solution.py:222
  (77 shorter events, 5.5 us)
Async XLA Ops:
  0.6 42.7 %collective-permute-start = (bf16[256,1024]{1,0:T(8,128)(2,1)}, bf16[256,1024]{1,0:T(8,128)(2,1)S(1)}, u32[]{:S(2)}, u32[]{:S(2)}) collective-permute-start(bf16[256,1024]{1,0:T(8,128)(2,1)} %q_own.3), channel_id=1, source_target_pairs={{0,1},{1,0},{2,3},{3,2},{4,5},{5,4},{6,7},{7,6},{8,9},{9,8},{10,11... | collective-permute-start | bytes 1572872 | tf_op jit(solution)/shard_map/ppermute | solution.py:250
  1.4 0.9 copy-start.11
  2.2 2.2 %collective-permute-start.1 = (bf16[2,128,128]{2,1,0:T(8,128)(2,1)S(1)}, bf16[2,128,128]{2,1,0:T(8,128)(2,1)S(1)}, u32[]{:S(2)}, u32[]{:S(2)}) collective-permute-start(bf16[2,128,128]{2,1,0:T(8,128)(2,1)S(1)} %fusion.2), channel_id=1, source_target_pairs={{0,1},{1,0},{2,3},{3,2},{4,5},{5,4},{6,7},{7,6},{8,9},{9,8},{10,11... | collective-permute-start | bytes 196616 | tf_op jit(solution)/shard_map/ppermute | solution.py:249
  2.5 0.7 copy-start.12
  2.5 1.9 %copy-start.10 = (bf16[256,128]{1,0:T(8,128)(2,1)S(1)}, bf16[256,128]{1,0:T(8,128)(2,1)}, u32[]{:S(2)}) copy-start(bf16[256,128]{1,0:T(8,128)(2,1)} %param.7) | copy-start | bytes 196612
  2.5 1.9 %copy-start.9 = (bf16[256,128]{1,0:T(8,128)(2,1)S(1)}, bf16[256,128]{1,0:T(8,128)(2,1)}, u32[]{:S(2)}) copy-start(bf16[256,128]{1,0:T(8,128)(2,1)} %param.6) | copy-start | bytes 196612
  4.5 12.5 %collective-permute-start.2 = (bf16[528,128]{1,0:T(8,128)(2,1)S(1)}, bf16[528,128]{1,0:T(8,128)(2,1)S(1)}, u32[]{:S(2)}, u32[]{:S(2)}) collective-permute-start(bf16[528,128]{1,0:T(8,128)(2,1)S(1)} %constant_dynamic-update-slice_fusion), channel_id=1, source_target_pairs={{0,32},{8,40},{16,48},{24,56},{32,0},{40,8},{48,16},{56,24},{64,96... | collective-permute-start | bytes 405512 | tf_op jit(solution)/shard_map/ppermute | solution.py:258
  17.1 9.9 %collective-permute-start.5 = (bf16[2,144,128]{2,1,0:T(8,128)(2,1)S(1)}, bf16[2,144,128]{2,1,0:T(8,128)(2,1)S(1)}, u32[]{:S(2)}, u32[]{:S(2)}) collective-permute-start(bf16[2,144,128]{2,1,0:T(8,128)(2,1)S(1)} %get-tuple-element.22), channel_id=1, source_target_pairs={{0,24},{8,0},{16,8},{24,16},{32,56},{40,32},{48,40},{56,48},{64,88... | collective-permute-start | bytes 221192 | tf_op jit(solution)/shard_map/ppermute | solution.py:267
  17.3 10.3 %collective-permute-start.4 = (bf16[2,144,128]{2,1,0:T(8,128)(2,1)S(1)}, bf16[2,144,128]{2,1,0:T(8,128)(2,1)S(1)}, u32[]{:S(2)}, u32[]{:S(2)}) collective-permute-start(bf16[2,144,128]{2,1,0:T(8,128)(2,1)S(1)} %get-tuple-element.22), channel_id=1, source_target_pairs={{0,16},{8,24},{16,0},{24,8},{32,48},{40,56},{48,32},{56,40},{64,80... | collective-permute-start | bytes 221192 | tf_op jit(solution)/shard_map/ppermute | solution.py:267
  19.6 10.1 %collective-permute-start.3 = (bf16[2,144,128]{2,1,0:T(8,128)(2,1)S(1)}, bf16[2,144,128]{2,1,0:T(8,128)(2,1)S(1)}, u32[]{:S(2)}, u32[]{:S(2)}) collective-permute-start(bf16[2,144,128]{2,1,0:T(8,128)(2,1)S(1)} %get-tuple-element.22), channel_id=1, source_target_pairs={{0,8},{8,16},{16,24},{24,0},{32,40},{40,48},{48,56},{56,32},{64,72... | collective-permute-start | bytes 221192 | tf_op jit(solution)/shard_map/ppermute | solution.py:267
  21.3 5.0 %collective-permute-start.15 = (bf16[256,128]{1,0:T(8,128)(2,1)S(1)}, bf16[256,128]{1,0:T(8,128)(2,1)S(1)}, u32[]{:S(2)}, u32[]{:S(2)}) collective-permute-start(bf16[256,128]{1,0:T(8,128)(2,1)S(1)} %slice.66), channel_id=1, source_target_pairs={{0,64},{8,72},{16,80},{24,88},{64,128},{72,136},{80,144},{88,152},... | collective-permute-start | bytes 196616 | tf_op jit(solution)/shard_map/ppermute | solution.py:266
  26.3 4.6 %collective-permute-start.11 = (bf16[320,128]{1,0:T(8,128)(2,1)S(1)}, bf16[320,128]{1,0:T(8,128)(2,1)S(1)}, u32[]{:S(2)}, u32[]{:S(2)}) collective-permute-start(bf16[320,128]{1,0:T(8,128)(2,1)S(1)} %pad_maximum_fusion.6), channel_id=1, source_target_pairs={{0,192},{8,200},{16,208},{24,216},{32,224},{40,232},{48,240},{56,2... | collective-permute-start | bytes 245768 | tf_op jit(solution)/shard_map/ppermute | solution.py:269
  27.0 5.1 %collective-permute-start.10 = (bf16[320,128]{1,0:T(8,128)(2,1)S(1)}, bf16[320,128]{1,0:T(8,128)(2,1)S(1)}, u32[]{:S(2)}, u32[]{:S(2)}) collective-permute-start(bf16[320,128]{1,0:T(8,128)(2,1)S(1)} %pad_maximum_fusion.6), channel_id=1, source_target_pairs={{0,128},{8,136},{16,144},{24,152},{32,160},{40,168},{48,176},{56,1... | collective-permute-start | bytes 245768 | tf_op jit(solution)/shard_map/ppermute | solution.py:269
  27.7 4.8 %collective-permute-start.9 = (bf16[320,128]{1,0:T(8,128)(2,1)S(1)}, bf16[320,128]{1,0:T(8,128)(2,1)S(1)}, u32[]{:S(2)}, u32[]{:S(2)}) collective-permute-start(bf16[320,128]{1,0:T(8,128)(2,1)S(1)} %pad_maximum_fusion.6), channel_id=1, source_target_pairs={{0,64},{8,72},{16,80},{24,88},{32,96},{40,104},{48,112},{56,120},{... | collective-permute-start | bytes 245768 | tf_op jit(solution)/shard_map/ppermute | solution.py:269
  29.8 15.8 %collective-permute-start.6 = (bf16[4,2,144,128]{3,2,1,0:T(8,128)(2,1)S(1)}, bf16[4,2,144,128]{3,2,1,0:T(8,128)(2,1)S(1)}, u32[]{:S(2)}, u32[]{:S(2)}) collective-permute-start(bf16[4,2,144,128]{3,2,1,0:T(8,128)(2,1)S(1)} %pad_maximum_fusion.a0), channel_id=1, source_target_pairs={{0,64},{8,72},{16,80},{24,88},{32,96},{40,104},{48,112},{56,120},{... | collective-permute-start | bytes 884744 | tf_op jit(solution)/shard_map/ppermute | solution.py:279
  32.5 14.8 %copy-start.2 = (bf16[256,1024]{1,0:T(8,128)(2,1)S(1)}, bf16[256,1024]{1,0:T(8,128)(2,1)}, u32[]{:S(2)}) copy-start(bf16[256,1024]{1,0:T(8,128)(2,1)} %q_own.3) | copy-start | bytes 1572868
  32.5 3.5 %collective-permute-start.16 = (bf16[320,128]{1,0:T(8,128)(2,1)S(1)}, bf16[320,128]{1,0:T(8,128)(2,1)S(1)}, u32[]{:S(2)}, u32[]{:S(2)}) collective-permute-start(bf16[320,128]{1,0:T(8,128)(2,1)S(1)} %get-tuple-element.34), channel_id=1, source_target_pairs={{0,8},{8,16},{16,24},{24,0},{32,40},{40,48},{48,56},{56,32},{64,72... | collective-permute-start | bytes 245768 | tf_op jit(solution)/shard_map/ppermute | solution.py:276
  33.0 4.8 %collective-permute-start.17 = (bf16[320,128]{1,0:T(8,128)(2,1)S(1)}, bf16[320,128]{1,0:T(8,128)(2,1)S(1)}, u32[]{:S(2)}, u32[]{:S(2)}) collective-permute-start(bf16[320,128]{1,0:T(8,128)(2,1)S(1)} %get-tuple-element.32), channel_id=1, source_target_pairs={{0,16},{8,24},{16,0},{24,8},{32,48},{40,56},{48,32},{56,40},{64,80... | collective-permute-start | bytes 245768 | tf_op jit(solution)/shard_map/ppermute | solution.py:276
  34.5 22.1 %collective-permute-start.7 = (bf16[4,2,144,128]{3,2,1,0:T(8,128)(2,1)S(1)}, bf16[4,2,144,128]{3,2,1,0:T(8,128)(2,1)S(1)}, u32[]{:S(2)}, u32[]{:S(2)}) collective-permute-start(bf16[4,2,144,128]{3,2,1,0:T(8,128)(2,1)S(1)} %pad_maximum_fusion.a0), channel_id=1, source_target_pairs={{0,128},{8,136},{16,144},{24,152},{32,160},{40,168},{48,176},{56,1... | collective-permute-start | bytes 884744 | tf_op jit(solution)/shard_map/ppermute | solution.py:279
  36.0 20.7 %collective-permute-start.8 = (bf16[4,2,144,128]{3,2,1,0:T(8,128)(2,1)S(1)}, bf16[4,2,144,128]{3,2,1,0:T(8,128)(2,1)S(1)}, u32[]{:S(2)}, u32[]{:S(2)}) collective-permute-start(bf16[4,2,144,128]{3,2,1,0:T(8,128)(2,1)S(1)} %pad_maximum_fusion.a0), channel_id=1, source_target_pairs={{0,192},{8,200},{16,208},{24,216},{32,224},{40,232},{48,240},{56,2... | collective-permute-start | bytes 884744 | tf_op jit(solution)/shard_map/ppermute | solution.py:279
  38.5 3.6 %collective-permute-start.18 = (bf16[320,128]{1,0:T(8,128)(2,1)S(1)}, bf16[320,128]{1,0:T(8,128)(2,1)S(1)}, u32[]{:S(2)}, u32[]{:S(2)}) collective-permute-start(bf16[320,128]{1,0:T(8,128)(2,1)S(1)} %get-tuple-element.33), channel_id=1, source_target_pairs={{0,24},{8,0},{16,8},{24,16},{32,56},{40,32},{48,40},{56,48},{64,88... | collective-permute-start | bytes 245768 | tf_op jit(solution)/shard_map/ppermute | solution.py:276
  42.7 14.0 %collective-permute-start.12 = (bf16[4,2,128,128]{3,2,1,0:T(8,128)(2,1)S(1)}, bf16[4,2,128,128]{3,2,1,0:T(8,128)(2,1)S(1)}, u32[]{:S(2)}, u32[]{:S(2)}) collective-permute-start(bf16[4,2,128,128]{3,2,1,0:T(8,128)(2,1)S(1)} %pad_maximum_fusion.1.b0), channel_id=1, source_target_pairs={{0,8},{8,16},{16,24},{24,0},{32,40},{40,48},{48,56},{56,32},{64,72... | collective-permute-start | bytes 786440 | tf_op jit(solution)/shard_map/ppermute | solution.py:280
  43.4 13.3 %copy-start.3 = (bf16[256,1024]{1,0:T(8,128)(2,1)}, bf16[256,1024]{1,0:T(8,128)(2,1)S(1)}, u32[]{:S(2)}) copy-start(bf16[256,1024]{1,0:T(8,128)(2,1)S(1)} %collective-permute-done.q_other) | copy-start | bytes 1572868
  43.4 13.3 %collective-permute-start.13 = (bf16[4,2,128,128]{3,2,1,0:T(8,128)(2,1)S(1)}, bf16[4,2,128,128]{3,2,1,0:T(8,128)(2,1)S(1)}, u32[]{:S(2)}, u32[]{:S(2)}) collective-permute-start(bf16[4,2,128,128]{3,2,1,0:T(8,128)(2,1)S(1)} %pad_maximum_fusion.1.b0), channel_id=1, source_target_pairs={{0,16},{8,24},{16,0},{24,8},{32,48},{40,56},{48,32},{56,40},{64,80... | collective-permute-start | bytes 786440 | tf_op jit(solution)/shard_map/ppermute | solution.py:280
  45.5 11.2 %collective-permute-start.14 = (bf16[4,2,128,128]{3,2,1,0:T(8,128)(2,1)S(1)}, bf16[4,2,128,128]{3,2,1,0:T(8,128)(2,1)S(1)}, u32[]{:S(2)}, u32[]{:S(2)}) collective-permute-start(bf16[4,2,128,128]{3,2,1,0:T(8,128)(2,1)S(1)} %pad_maximum_fusion.1.b0), channel_id=1, source_target_pairs={{0,24},{8,0},{16,8},{24,16},{32,56},{40,32},{48,40},{56,48},{64,88... | collective-permute-start | bytes 786440 | tf_op jit(solution)/shard_map/ppermute | solution.py:280
  47.3 0.9 copy-start.6
  48.2 0.9 copy-start.8
  56.7 1.0 copy-start.4
  91.7 15.1 %collective-permute-start.19 = (bf16[256,1024]{1,0:T(8,128)(2,1)}, bf16[256,1024]{1,0:T(8,128)(2,1)S(1)}, u32[]{:S(2)}, u32[]{:S(2)}) collective-permute-start(bf16[256,1024]{1,0:T(8,128)(2,1)} %get-tuple-element.12), channel_id=1, source_target_pairs={{0,1},{1,0},{2,3},{3,2},{4,5},{5,4},{6,7},{7,6},{8,9},{9,8},{10,11... | collective-permute-start | bytes 1572872 | tf_op jit(solution)/shard_map/ppermute | solution.py:295
  104.1 1.6 %collective-permute-start.21 = (bf16[32,16,256]{2,1,0:T(8,128)(2,1)S(1)}, bf16[32,16,256]{2,1,0:T(8,128)(2,1)S(1)}, u32[]{:S(2)}, u32[]{:S(2)}) collective-permute-start(bf16[32,16,256]{2,1,0:T(8,128)(2,1)S(1)} %shard_map.71), channel_id=1, source_target_pairs={{0,1},{1,0},{2,3},{3,2},{4,5},{5,4},{6,7},{7,6},{8,9},{9,8},{10,11... | collective-permute-start | bytes 786440 | tf_op jit(solution)/shard_map/ppermute | solution.py:297
  104.1 2.6 %collective-permute-start.20 = (f32[256,128]{1,0:T(8,128)}, f32[256,128]{1,0:T(8,128)S(1)}, u32[]{:S(2)}, u32[]{:S(2)}) collective-permute-start(f32[256,128]{1,0:T(8,128)} %get-tuple-element.13), channel_id=1, source_target_pairs={{0,1},{1,0},{2,3},{3,2},{4,5},{5,4},{6,7},{7,6},{8,9},{9,8},{10,11... | collective-permute-start | bytes 393224 | tf_op jit(solution)/shard_map/ppermute | solution.py:296
  105.7 1.1 copy-start.1
  (3 other events, 1.9 us)

commit v2 on v0

v2 whole, which is shorter than its diff:
```python
import math

import jax
import jax.numpy as jnp
from jax import lax
from jax.experimental import pallas as pl
from jax.experimental.pallas import tpu as pltpu
from jax.sharding import PartitionSpec as P

GROUP = 8
HD = 128
SINK = 64
RECENT = 1024
PAGE = 16
ROWS = 256
HALF = 128
QUART = 64
META = 16
FIRST = 2 * QUART + META
CHUNK = 512
NEG = -1e30
SCALE = math.log2(math.e) / math.sqrt(HD)
F32 = jnp.float32
BF16 = jnp.bfloat16


def ctx_of(x, z, y):
    return (x % 4) * 8 + (z % 2) * 4 + (y % 4)


CHIPS = [(x, z, y) for x in range(4) for z in range(2) for y in range(4)]
CORE_SWAP = [(i, i ^ 1) for i in range(8)]
Z_SWAP = [(ctx_of(x, z, y), ctx_of(x, z + 1, y)) for x, z, y in CHIPS]
FOUR_ON = [(i, i + 4) for i in range(28)]
X_SHIFT = {s: [(ctx_of(x, z, y), ctx_of(x + s, z, y)) for x, z, y in CHIPS] for s in (1, 2, 3)}
Y_SHIFT = {s: [(ctx_of(x, z, y), ctx_of(x, z, y + s)) for x, z, y in CHIPS] for s in (1, 2, 3)}


def nt_dot(a, b):
    return lax.dot_general(a, b, (((1,), (1,)), ((), ())), preferred_element_type=F32)


def iota(shape, axis):
    return lax.broadcasted_iota(jnp.int32, shape, axis)


def fold(state, q, k, v, left=None, right=None):
    m, l, o = state
    s = nt_dot(q, k)
    if left is not None:
        s = jnp.concatenate([s[:, :HD] + left, s[:, HD:]], axis=1) if s.shape[1] > HD else s + left
    if right is not None:
        s = jnp.concatenate([s[:, :-HD], s[:, -HD:] + right], axis=1)
    top = jnp.maximum(m, jnp.max(s, axis=1, keepdims=True))
    p = jnp.exp2((s - top) * SCALE).astype(BF16)
    up = jnp.dot(p, v, preferred_element_type=F32)
    keep = jnp.exp2((m - top) * SCALE)
    return top, l * keep + up[:, HD:HD + 1], o * keep + up[:, :HD]


def start():
    return jnp.full((ROWS, 1), NEG, F32), jnp.zeros((ROWS, 1), F32), jnp.zeros((ROWS, HD), F32)


def put_keys(k_s, v_s, at, ref, first, rows, gap):
    k_s[pl.ds(at, rows), 0:HD] = ref[first:first + rows, :]
    v_s[pl.ds(at, rows), 0:HD] = ref[first + gap:first + gap + rows, :]


def put_first(k_s, v_s, at, ref):
    for n in range(8):
        put_keys(k_s, v_s, at + n * QUART, ref, n * FIRST, QUART, QUART)


def put_second(k_s, v_s, at, ref):
    for n in range(8):
        put_keys(k_s, v_s, at + n * QUART, ref, n * 2 * QUART, QUART, QUART)


def put_bias(k_s, v_s, bias):
    lane = iota(bias.shape, 1)
    k_s[:, HD:] = jnp.where(lane == 0, bias, 0.0).astype(BF16)
    v_s[:, HD:] = jnp.ones(bias.shape, BF16)


def range_bias(sc, shape, chunks):
    x, y, z, c = sc[0], sc[1], sc[2], sc[4]
    n = iota(shape, 0)
    outer, far = (n >> 7) & 3, (n >> 6) & 1
    which = n >> 9
    dx, dy = outer, outer
    for i, (fixed_x, fixed_y) in enumerate(chunks):
        if fixed_x is not None:
            dx = jnp.where(which == i, fixed_x, dx)
        else:
            dy = jnp.where(which == i, fixed_y, dy)
    zz = jnp.where(far == 0, z, 1 - z)
    block = ((x - dx) & 3) * 8 + zz * 4 + ((y - dy) & 3)
    return jnp.where(block <= c, 0.0, NEG)


def load_head(q_a, q_b, flag, a):
    cols = pl.ds(pl.multiple_of(a * HD, HD), HD)
    q = jnp.where(flag == 1, q_a[:, cols], q_b[:, cols])
    one = jnp.where(iota((ROWS, HD), 1) == 0, 1.0, 0.0).astype(BF16)
    return jnp.concatenate([q, one], axis=1)


def load_state(acc, lm, a):
    lane = iota((ROWS, HD), 1)
    block = lm[...]
    m = jnp.max(jnp.where(lane == a, block, -jnp.inf), axis=1, keepdims=True)
    l = jnp.max(jnp.where(lane == a + GROUP, block, -jnp.inf), axis=1, keepdims=True)
    return m, l, acc[a]


def store_state(acc, lm, a, state):
    lane = iota((ROWS, HD), 1)
    m, l, o = state
    acc[a] = o
    lm[...] = jnp.where(lane == a, m, jnp.where(lane == a + GROUP, l, lm[...]))


def near_kernel(sc, q_own, q_other, pas, y1, y2, y3, far, h1, h2, acc_p, lm_p, acc_r, lm_r, kp, vp, kr, vr):
    core, c, is_r = sc[3], sc[4], sc[5]
    put_keys(kp, vp, 0, pas, 0, HALF, HALF)
    for n, ref in enumerate((y1, y2, y3)):
        put_keys(kp, vp, (n + 1) * HALF, ref, 2 * FIRST, HALF, HALF)
    put_keys(kp, vp, 4 * HALF, far, 0, HALF, HALF)
    put_bias(kp, vp, jnp.where((iota((5 * HALF, HD), 0) >> 7) <= c, 0.0, NEG))
    put_first(kr, vr, 0, h1)
    put_second(kr, vr, CHUNK, h2)
    put_bias(kr, vr, range_bias(sc, (2 * CHUNK, HD), ((0, None), (None, 0))))

    row = iota((ROWS, HD), 0)
    lane = iota((ROWS, HD), 1)
    key = core * HALF + lane
    own = jnp.where(key > row, NEG, 0.0)
    edge = jnp.where(key <= row, NEG, 0.0)
    first = jnp.where((lane < QUART) & (key > row), NEG, 0.0)
    second = jnp.where((lane < QUART) & (key + QUART > row), NEG, 0.0)
    lm_p[...] = jnp.zeros((ROWS, HD), F32)
    lm_r[...] = jnp.zeros((ROWS, HD), F32)

    def heads(i, carry):
        at = [2 * i, 2 * i + 1]
        qp = [load_head(q_other, q_own, is_r, a) for a in at]
        qr = [load_head(q_own, q_other, is_r, a) for a in at]
        sr = [start(), start()]
        sp = [start(), start()]
        for u in range(2):
            sr[u] = fold(sr[u], qr[u], kr[0:CHUNK, :], vr[0:CHUNK, :], left=first)
        for u in range(2):
            sp[u] = fold(sp[u], qp[u], kp[0:3 * HALF, :], vp[0:3 * HALF, :], left=own)
        for u in range(2):
            sr[u] = fold(sr[u], qr[u], kr[CHUNK:, :], vr[CHUNK:, :], left=second)
        for u in range(2):
            sp[u] = fold(sp[u], qp[u], kp[3 * HALF:, :], vp[3 * HALF:, :], right=edge)
        for u in range(2):
            store_state(acc_p, lm_p, at[u], sp[u])
            store_state(acc_r, lm_r, at[u], sr[u])
        return carry

    lax.fori_loop(0, GROUP // 2, heads, 0)


def middle_kernel(sc, q_own, q_other, x1, x3, y1, y3, acc_in, lm_in, acc_r, lm_r, kr, vr):
    is_r = sc[5]
    put_first(kr, vr, 0, x1)
    put_first(kr, vr, CHUNK, x3)
    put_second(kr, vr, 2 * CHUNK, y1)
    put_second(kr, vr, 3 * CHUNK, y3)
    put_bias(kr, vr, range_bias(sc, (4 * CHUNK, HD), ((1, None), (3, None), (None, 1), (None, 3))))
    lm_r[...] = jnp.zeros((ROWS, HD), F32)

    def heads(i, carry):
        at = [2 * i, 2 * i + 1]
        q = [load_head(q_own, q_other, is_r, a) for a in at]
        state = [load_state(acc_in, lm_in, a) for a in at]
        for n in range(4):
            rows = slice(n * CHUNK, (n + 1) * CHUNK)
            for u in range(2):
                state[u] = fold(state[u], q[u], kr[rows, :], vr[rows, :])
        for u in range(2):
            store_state(acc_r, lm_r, at[u], state[u])
        return carry

    lax.fori_loop(0, GROUP // 2, heads, 0)


def finish(state):
    m, l, o = state
    total = jnp.maximum(l, 1e-37)
    return o / total, m * SCALE + jnp.log2(total)


def last_kernel(sc, q_own, q_other, x2, y2, sink, acc_r, lm_r, acc_p, lm_p, keep, keep_lse, send, kr, vr, ks, vs):
    core, c, is_r = sc[3], sc[4], sc[5]
    put_first(kr, vr, 0, x2)
    put_second(kr, vr, CHUNK, y2)
    put_bias(kr, vr, range_bias(sc, (2 * CHUNK, HD), ((2, None), (None, 2))))
    ks[...] = jnp.zeros((HALF, 2 * HD), BF16)
    vs[...] = jnp.where(iota((HALF, 2 * HD), 1) >= HD, 1.0, 0.0).astype(BF16)
    put_keys(ks, vs, 0, sink, 0, SINK, SINK)
    row = iota((ROWS, HD), 0)
    lane = iota((ROWS, HD), 1)
    seen = (core == 0) & (lane < SINK) & (c * ROWS + row - lane >= RECENT)
    sink_bias = jnp.where(seen, 0.0, NEG)
    keep_lse[...] = jnp.zeros((ROWS, HD), F32)
    send[:, GROUP * HD:] = jnp.zeros((ROWS, HD), BF16)

    def heads(i, carry):
        at = [2 * i, 2 * i + 1]
        qp = [load_head(q_other, q_own, is_r, a) for a in at]
        qr = [load_head(q_own, q_other, is_r, a) for a in at]
        sr = [load_state(acc_r, lm_r, a) for a in at]
        sp = [load_state(acc_p, lm_p, a) for a in at]
        for n in range(2):
            rows = slice(n * CHUNK, (n + 1) * CHUNK)
            for u in range(2):
                sr[u] = fold(sr[u], qr[u], kr[rows, :], vr[rows, :])
        for u in range(2):
            sp[u] = fold(sp[u], qp[u], ks[...], vs[...], left=sink_bias)
        for u in range(2):
            cols = pl.ds(pl.multiple_of(at[u] * HD, HD), HD)
            out_r, lse_r = finish(sr[u])
            out_p, lse_p = finish(sp[u])
            keep[:, cols] = jnp.where(is_r == 1, out_r, out_p).astype(BF16)
            send[:, cols] = jnp.where(is_r == 1, out_p, out_r).astype(BF16)
            mine = jnp.where(is_r == 1, lse_r, lse_p)
            theirs = jnp.where(is_r == 1, lse_p, lse_r)
            keep_lse[...] = jnp.where(lane == at[u], mine, keep_lse[...])
            high = theirs.astype(BF16)
            rest = theirs - high.astype(F32)
            mid = rest.astype(BF16)
            low = (rest - mid.astype(F32)).astype(BF16)
            ext = send[:, GROUP * HD:].astype(F32)
            for n, part in enumerate((high, mid, low)):
                ext = jnp.where(lane == at[u] + n * GROUP, part.astype(F32), ext)
            send[:, GROUP * HD:] = ext.astype(BF16)
        return carry

    lax.fori_loop(0, GROUP // 2, heads, 0)


def merge_kernel(keep, keep_lse, got, out_ref):
    ext = got[:, GROUP * HD:].astype(F32)
    for a in range(GROUP):
        cols = slice(a * HD, (a + 1) * HD)
        l0 = keep_lse[:, a:a + 1]
        l1 = ext[:, a:a + 1] + ext[:, a + GROUP:a + GROUP + 1] + ext[:, a + 2 * GROUP:a + 2 * GROUP + 1]
        top = jnp.maximum(l0, l1)
        w0, w1 = jnp.exp2(l0 - top), jnp.exp2(l1 - top)
        scale = 1.0 / (w0 + w1)
        out = keep[:, cols].astype(F32) * (w0 * scale) + got[:, cols].astype(F32) * (w1 * scale)
        out_ref[:, cols] = out.astype(BF16)


def pages_kernel(sc, a0, a1, a2, a3, b0, b1, b2, b3, out_ref):
    x, y, z, c = sc[0], sc[1], sc[2], sc[4]
    first = (a0, a1, a2, a3)
    second = (b0, b1, b2, b3)
    row = iota((2 * PAGE, HD), 0)
    lane = iota((2 * PAGE, HD), 1)
    same_row = (lane & (PAGE - 1)) == (row & (PAGE - 1))
    want = (2 * c + (row >> 4)).astype(F32)
    for dx in range(4):
        for d in range(4):
            for col in range(2):
                f, at = first[dx], (d * 2 + col) * FIRST
                s, on = second[d], (dx * 2 + col) * 2 * QUART
                code = jnp.concatenate([f[at + 2 * QUART:at + FIRST, :]] * 2, axis=0).astype(F32)
                select = jnp.where(same_row & (code == want), 1.0, 0.0).astype(BF16)
                zz = z if col == 0 else 1 - z
                block = ((x - dx) & 3) * 8 + zz * 4 + ((y - d) & 3)
                for part in range(2):
                    k1 = f[at + part * QUART:at + (part + 1) * QUART, :]
                    k2 = s[on + part * QUART:on + (part + 1) * QUART, :]
                    pages = jnp.dot(select, jnp.concatenate([k1, k2], axis=0), preferred_element_type=F32)
                    out_ref[block, :, part * HD:(part + 1) * HD] = pages.astype(BF16)


VMEM_SPEC = pl.BlockSpec(memory_space=pltpu.VMEM)
SMEM_SPEC = pl.BlockSpec(memory_space=pltpu.SMEM)


def call(kernel, out_shape, scratch, flops, sc, *args):
    many = isinstance(out_shape, tuple)
    specs = ([SMEM_SPEC] if sc is not None else []) + [VMEM_SPEC] * len(args)
    operands = ([sc] if sc is not None else []) + list(args)
    return pl.pallas_call(
        kernel,
        out_shape=out_shape,
        in_specs=specs,
        out_specs=(VMEM_SPEC,) * len(out_shape) if many else VMEM_SPEC,
        scratch_shapes=scratch,
        compiler_params=pltpu.CompilerParams(vmem_limit_bytes=24 * 1024 * 1024),
        cost_estimate=pl.CostEstimate(flops=flops, bytes_accessed=4 << 20, transcendentals=flops // 512),
    )(*operands)


def keys(rows):
    return [pltpu.VMEM((rows, 2 * HD), BF16), pltpu.VMEM((rows, 2 * HD), BF16)]


def shards(q, k, v, head_kind, page_owner):
    c = lax.axis_index("ctx")
    tp = lax.axis_index("tp")
    x, z, y = c // 8, (c // 4) % 2, c % 4
    core = tp % 2
    is_r = lax.dynamic_index_in_dim(head_kind, tp, 0, keepdims=False) == 1
    sc = jnp.stack([x, y, z, core, c, is_r.astype(jnp.int32), tp, tp]).astype(jnp.int32)

    def half(which):
        return jnp.concatenate([lax.dynamic_slice_in_dim(t, which * HALF, HALF, 0) for t in (k, v)])

    stay = half(core)
    came = lax.ppermute(half(1 - core), "tp", CORE_SWAP)
    q_other = lax.ppermute(q, "tp", CORE_SWAP)
    ret = jnp.where(is_r, stay, came)
    pas = jnp.where(is_r, came, stay)

    earlier = lax.iota(jnp.int32, 16)[None, :] < lax.iota(jnp.int32, 16)[:, None]
    rank = jnp.sum(((page_owner[:, None] == page_owner[None, :]) & earlier).astype(jnp.int32), axis=1)
    code = lax.dynamic_slice_in_dim(page_owner * 2 + rank, core * 8, 8, 0).astype(BF16)
    meta = jnp.broadcast_to(jnp.repeat(code, PAGE)[None, :], (META, HD))

    r1 = jnp.concatenate([ret[:QUART], ret[HALF:HALF + QUART], meta])
    r2 = jnp.concatenate([ret[QUART:HALF], ret[HALF + QUART:]])
    theirs = lax.ppermute(jnp.concatenate([r1, r2]), "ctx", Z_SWAP)
    far = lax.ppermute(pas, "ctx", FOUR_ON)
    r1 = jnp.concatenate([r1, theirs[:FIRST]])
    r2 = jnp.concatenate([r2, theirs[FIRST:]])
    low = jnp.where(z == 0, pas, far)
    sink = jnp.concatenate([low[:SINK], low[HALF:HALF + SINK]])

    ys = {s: lax.ppermute(jnp.concatenate([r1, jnp.where(y + s < 4, pas, far)]), "ctx", Y_SHIFT[s]) for s in (1, 3, 2)}
    along_x = jnp.concatenate([r2, sink])
    xs = {s: lax.ppermute(along_x, "ctx", X_SHIFT[s]) for s in (1, 3, 2)}
    h1 = jnp.concatenate([r1] + [ys[s][:2 * FIRST] for s in (1, 2, 3)])
    for s in (1, 2, 3):
        sink = jnp.where(x == s, xs[s][2 * HALF:], sink)
    h2 = jnp.concatenate([r2] + [xs[s][:2 * HALF] for s in (1, 2, 3)] + [sink])

    a = {0: h1} | {s: lax.ppermute(h1, "ctx", X_SHIFT[s]) for s in (1, 3, 2)}
    b = {0: h2} | {s: lax.ppermute(h2, "ctx", Y_SHIFT[s]) for s in (1, 3, 2)}

    acc_shape = jax.ShapeDtypeStruct((GROUP, ROWS, HD), F32)
    lm_shape = jax.ShapeDtypeStruct((ROWS, HD), F32)
    unit = 2 * 2048 * 256 * 512
    acc_p, lm_p, acc_r, lm_r = call(
        near_kernel, (acc_shape, lm_shape, acc_shape, lm_shape), keys(5 * HALF) + keys(2 * CHUNK),
        7 * unit, sc, q, q_other, pas, ys[1], ys[2], ys[3], far, h1, h2)
    acc_r, lm_r = call(
        middle_kernel, (acc_shape, lm_shape), keys(4 * CHUNK),
        8 * unit, sc, q, q_other, a[1], a[3], b[1], b[3], acc_r, lm_r)
    for s in (1, 2, 3):
        sink = jnp.where(y == s, b[s][8 * HALF:], sink)
    keep, keep_lse, send = call(
        last_kernel,
        (jax.ShapeDtypeStruct((ROWS, GROUP * HD), BF16), lm_shape, jax.ShapeDtypeStruct((ROWS, (GROUP + 1) * HD), BF16)),
        keys(2 * CHUNK) + keys(HALF), 4 * unit, sc, q, q_other, a[2], b[2], sink, acc_r, lm_r, acc_p, lm_p)

    got = lax.ppermute(send, "tp", CORE_SWAP)
    pages = call(pages_kernel, jax.ShapeDtypeStruct((32, 2 * PAGE, 2 * HD), BF16), [], unit, sc, *[a[s] for s in range(4)], *[b[s] for s in range(4)])
    got_pages = lax.ppermute(pages, "tp", CORE_SWAP)
    attn_out = call(merge_kernel, jax.ShapeDtypeStruct((ROWS, GROUP * HD), BF16), [], unit, None, keep, keep_lse, got)
    decode_cache = jnp.where(is_r, pages + got_pages, jnp.zeros((), BF16)).reshape(64, PAGE, 2 * HD)
    return attn_out, decode_cache


def solution(mesh):
    return jax.shard_map(
        shards,
        mesh=mesh,
        in_specs=(P("ctx", "tp"), P("ctx", "tp"), P("ctx", "tp"), P(), P("ctx")),
        out_specs=(P("ctx", "tp"), P("ctx", None, "tp")),
        check_vma=False,
    )
```

time: 291 us -> 81.1 us (0.28)
  the two profiles are of different devices: /device:TPU:246 before, /device:TPU:21 now
where the time goes in v2:
time: 81.1 us; the launch traced here: 80.9 us
  starting transfers between devices  33.2 us (41%)
  Pallas kernels  27.5 us (34%)
  waiting for transfers between devices  14.1 us (17%)
  local copies, waits for them, and re-layouts  3.27 us (4%)
  between operations  1.58 us (2%)
  other arithmetic  1.33 us (2%)
    pallas_call x5, Pallas kernels, call(): pl.pallas_call(kernel, out_shape=out_shape, in_specs=specs, out_specs=(VM...  27.5 us
    ppermute x1, starting transfers between devices, shards(): got_pages = lax.ppermute(pages, 'tp', CORE_SWAP)  9.82 us
    ppermute x1, starting transfers between devices, shards(): far = lax.ppermute(pas, 'ctx', FOUR_ON)  8.82 us
    ppermute x1, waiting for transfers between devices, shards(): theirs = lax.ppermute(jnp.concatenate([r1, r2]), 'ctx', Z_SWAP)  7.07 us
    ppermute x3, starting transfers between devices, shards(): b = {0: h2} | {s: lax.ppermute(h2, 'ctx', Y_SHIFT[s]) for s in (1, 3, 2)}  4.89 us
    ppermute x3, starting transfers between devices, shards(): a = {0: h1} | {s: lax.ppermute(h1, 'ctx', X_SHIFT[s]) for s in (1, 3, 2)}  4.11 us
    ppermute x3, waiting for transfers between devices, shards(): xs = {s: lax.ppermute(along_x, 'ctx', X_SHIFT[s]) for s in (1, 3, 2)}  3.63 us
    ppermute x3, starting transfers between devices, shards(): xs = {s: lax.ppermute(along_x, 'ctx', X_SHIFT[s]) for s in (1, 3, 2)}  2.78 us
  transfers between devices with their start and end apart: 18, of which 5 were waited for; matrix products, arithmetic and copies ran while one was open for 3% of the time, Pallas kernels for 31%

profile of v2, /device:TPU:21, one launch (start us, length us, event | category | flops | bytes accessed | tf_op | source)
XLA Modules:
  0.0 80.9 jit_solution(7458242345519861646)
XLA Ops:
  0.7 0.8 %constant_dynamic-slice_fusion.2 = (bf16[128,128]{1,0:T(8,128)(2,1)S(1)}, bf16[128,128]{1,0:T(8,128)(2,1)S(1)}, bf16[128,128]{1,0:T(8,128)(2,1)S(1)}, bf16[128,128]{1,0:T(8,128)(2,1)S(1)}) fusion(bf16[256,128]{1,0:T(8,128)(2,1)} %param.7, s32[]{:T(128)S(6)} %select_n.126, s32[]{:T(128)S(6)} %select_n.127, bf16[256,128]{1,0:T(8,128)(2,1)} %param.6), kind=kLoop, calls=%fused_computation.56 | loop fusion | bytes 262152 | tf_op jit(solution)/shard_map/dynamic_slice | solution.py:315
  1.5 0.8 collective-permute-start.1
  2.3 0.1 collective-permute-start
  2.4 0.7 copy-done.1
  3.0 0.6 dynamic_slice.19
  4.4 0.6 copy-done.2
  5.0 0.2 convert_reduce_fusion
  5.6 8.8 %collective-permute-start.3 = (bf16[256,128]{1,0:T(8,128)(2,1)S(1)}, bf16[256,128]{1,0:T(8,128)(2,1)S(1)}, u32[]{:S(2)}, u32[]{:S(2)}) collective-permute-start(bf16[256,128]{1,0:T(8,128)(2,1)S(1)} %get-tuple-element.24.pas), channel_id=1, source_target_pairs={{0,32},{8,40},{16,48},{24,56},{32,64},{40,72},{48,80},{56,88},{64,... | collective-permute-start | bytes 196616 | tf_op jit(solution)/shard_map/ppermute | solution.py:331
  14.6 7.1 %collective-permute-done.2 = bf16[272,128]{1,0:T(8,128)(2,1)S(1)} collective-permute-done((bf16[272,128]{1,0:T(8,128)(2,1)S(1)}, bf16[272,128]{1,0:T(8,128)(2,1)S(1)}, u32[]{:S(2)}, u32[]{:S(2)}) %collective-permute-start.2) | collective-permute-done | bytes 69664 | tf_op jit(solution)/shard_map/ppermute | solution.py:330
  21.8 0.3 collective-permute-start.10
  22.2 2.5 %collective-permute-start.9 = (bf16[384,128]{1,0:T(8,128)(2,1)S(1)}, bf16[384,128]{1,0:T(8,128)(2,1)S(1)}, u32[]{:S(2)}, u32[]{:S(2)}) collective-permute-start(bf16[384,128]{1,0:T(8,128)(2,1)S(1)} %constant_dynamic-update-slice_fusion.27), channel_id=1, source_target_pairs={{0,128},{8,136},{16,144},{24,152},{32,160},{40,168},{48,176},{56,1... | collective-permute-start | bytes 294920 | tf_op jit(solution)/shard_map/ppermute | solution.py:339
  24.7 0.1 collective-permute-start.5
  24.9 3.6 %collective-permute-done.8 = bf16[384,128]{1,0:T(8,128)(2,1)S(1)} collective-permute-done((bf16[384,128]{1,0:T(8,128)(2,1)S(1)}, bf16[384,128]{1,0:T(8,128)(2,1)S(1)}, u32[]{:S(2)}, u32[]{:S(2)}) %collective-permute-start.8) | collective-permute-done | bytes 98336 | tf_op jit(solution)/shard_map/ppermute | solution.py:339
  28.5 1.0 %collective-permute-start.4 = (bf16[544,128]{1,0:T(8,128)(2,1)S(1)}, bf16[544,128]{1,0:T(8,128)(2,1)S(1)}, u32[]{:S(2)}, u32[]{:S(2)}) collective-permute-start(bf16[544,128]{1,0:T(8,128)(2,1)S(1)} %constant_dynamic-update-slice_fusion.5), channel_id=1, source_target_pairs={{0,8},{8,16},{16,24},{24,0},{32,40},{40,48},{48,56},{56,32},{64,72... | collective-permute-start | bytes 417800 | tf_op jit(solution)/shard_map/ppermute | solution.py:337
  29.5 0.5 collective-permute-start.6
  30.1 1.1 %collective-permute-start.13 = (bf16[1152,128]{1,0:T(8,128)(2,1)S(1)}, bf16[1152,128]{1,0:T(8,128)(2,1)S(1)}, u32[]{:S(2)}, u32[]{:S(2)}) collective-permute-start(bf16[1152,128]{1,0:T(8,128)(2,1)S(1)} %get-tuple-element.20.h2.b0), channel_id=1, source_target_pairs={{0,8},{8,16},{16,24},{24,0},{32,40},{40,48},{48,56},{56,32},{64,72... | collective-permute-start | bytes 884744 | tf_op jit(solution)/shard_map/ppermute | solution.py:346
  31.2 1.2 %collective-permute-done.4.y1 = bf16[544,128]{1,0:T(8,128)(2,1)S(1)} collective-permute-done((bf16[544,128]{1,0:T(8,128)(2,1)S(1)}, bf16[544,128]{1,0:T(8,128)(2,1)S(1)}, u32[]{:S(2)}, u32[]{:S(2)}) %collective-permute-start.4) | collective-permute-done | bytes 139296 | tf_op jit(solution)/shard_map/ppermute | solution.py:337
  32.4 0.2 collective-permute-start.12
  32.6 3.6 %collective-permute-start.11 = (bf16[1152,128]{1,0:T(8,128)(2,1)S(1)}, bf16[1152,128]{1,0:T(8,128)(2,1)S(1)}, u32[]{:S(2)}, u32[]{:S(2)}) collective-permute-start(bf16[1152,128]{1,0:T(8,128)(2,1)S(1)} %get-tuple-element.20.h2.b0), channel_id=1, source_target_pairs={{0,16},{8,24},{16,0},{24,8},{32,48},{40,56},{48,32},{56,40},{64,80... | collective-permute-start | bytes 884744 | tf_op jit(solution)/shard_map/ppermute | solution.py:346
  36.3 0.8 %collective-permute-start.15 = (bf16[1152,128]{1,0:T(8,128)(2,1)S(1)}, bf16[1152,128]{1,0:T(8,128)(2,1)S(1)}, u32[]{:S(2)}, u32[]{:S(2)}) collective-permute-start(bf16[1152,128]{1,0:T(8,128)(2,1)S(1)} %constant_dynamic-update-slice_fusion.20.h1.a0), channel_id=1, source_target_pairs={{0,192},{8,200},{16,208},{24,216},{32,224},{40,232},{48,240},{56,2... | collective-permute-start | bytes 884744 | tf_op jit(solution)/shard_map/ppermute | solution.py:345
  37.1 1.1 %collective-permute-start.14 = (bf16[1152,128]{1,0:T(8,128)(2,1)S(1)}, bf16[1152,128]{1,0:T(8,128)(2,1)S(1)}, u32[]{:S(2)}, u32[]{:S(2)}) collective-permute-start(bf16[1152,128]{1,0:T(8,128)(2,1)S(1)} %constant_dynamic-update-slice_fusion.20.h1.a0), channel_id=1, source_target_pairs={{0,64},{8,72},{16,80},{24,88},{32,96},{40,104},{48,112},{56,120},{... | collective-permute-start | bytes 884744 | tf_op jit(solution)/shard_map/ppermute | solution.py:345
  38.2 1.0 %collective-permute-done.13.y1.b1 = bf16[1152,128]{1,0:T(8,128)(2,1)S(1)} collective-permute-done((bf16[1152,128]{1,0:T(8,128)(2,1)S(1)}, bf16[1152,128]{1,0:T(8,128)(2,1)S(1)}, u32[]{:S(2)}, u32[]{:S(2)}) %collective-permute-start.13) | collective-permute-done | bytes 294944 | tf_op jit(solution)/shard_map/ppermute | solution.py:346
  39.2 2.2 %collective-permute-start.7 = (bf16[1152,128]{1,0:T(8,128)(2,1)S(1)}, bf16[1152,128]{1,0:T(8,128)(2,1)S(1)}, u32[]{:S(2)}, u32[]{:S(2)}) collective-permute-start(bf16[1152,128]{1,0:T(8,128)(2,1)S(1)} %constant_dynamic-update-slice_fusion.20.h1.a0), channel_id=1, source_target_pairs={{0,128},{8,136},{16,144},{24,152},{32,160},{40,168},{48,176},{56,1... | collective-permute-start | bytes 884744 | tf_op jit(solution)/shard_map/ppermute | solution.py:345
  41.4 7.9 %shard_map.68 = (f32[8,256,128]{2,1,0:T(8,128)S(1)}, f32[256,128]{1,0:T(8,128)S(1)}, f32[8,256,128]{2,1,0:T(8,128)S(1)}, f32[256,128]{1,0:T(8,128)S(1)}) custom-call(s32[8]{0:T(128)S(1)} %stack.33.sc, bf16[256,1024]{1,0:T(8,128)(2,1)S(1)} %copy-done, bf16[256,1024]{1,0:T(8,128)(2,1)S(1)} %collective-permute-done.q_other, ...), custom_call_target="tpu_custom_call" | custom-call | flops 3758096384 | bytes 4194304 | tf_op jit(solution)/shard_map/pallas_call | solution.py:291
  49.3 1.2 %shard_map.72 = bf16[32,32,256]{2,1,0:T(8,128)(2,1)S(1)} custom-call(s32[8]{0:T(128)S(1)} %stack.33.sc, bf16[1152,128]{1,0:T(8,128)(2,1)S(1)} %constant_dynamic-update-slice_fusion.20.h1.a0, bf16[1152,128]{1,0:T(8,128)(2,1)S(1)} %collective-permute-done.14.x1.a1, bf16[1152,128]{1,0:T(8,128)(2,1)S(1)} %collective-permute-done.7.x2.a2, ...), custom_call_target="tpu_custom_call" | custom-call | flops 536870912 | bytes 4194304 | tf_op jit(solution)/shard_map/pallas_call | solution.py:291
  50.6 9.8 %collective-permute-start.17 = (bf16[32,32,256]{2,1,0:T(8,128)(2,1)S(1)}, bf16[32,32,256]{2,1,0:T(8,128)(2,1)S(1)}, u32[]{:S(2)}, u32[]{:S(2)}) collective-permute-start(bf16[32,32,256]{2,1,0:T(8,128)(2,1)S(1)} %shard_map.72), channel_id=1, source_target_pairs={{0,1},{1,0},{2,3},{3,2},{4,5},{5,4},{6,7},{7,6},{8,9},{9,8},{10,11... | collective-permute-start | bytes 1572872 | tf_op jit(solution)/shard_map/ppermute | solution.py:366
  60.4 8.8 %shard_map.69 = (f32[8,256,128]{2,1,0:T(8,128)S(1)}, f32[256,128]{1,0:T(8,128)S(1)}) custom-call(s32[8]{0:T(128)S(1)} %stack.33.sc, bf16[256,1024]{1,0:T(8,128)(2,1)S(1)} %copy-done, bf16[256,1024]{1,0:T(8,128)(2,1)S(1)} %collective-permute-done.q_other, bf16[1152,128]{1,0:T(8,128)(2,1)S(1)} %collective-permute-done.14.x1.a1, ...), custom_call_target="tpu_custom_call" | custom-call | flops 4294967296 | bytes 4194304 | tf_op jit(solution)/shard_map/pallas_call | solution.py:291
  69.2 8.0 %shard_map.70 = (bf16[256,1024]{1,0:T(8,128)(2,1)S(1)}, f32[256,128]{1,0:T(8,128)S(1)}, bf16[256,1152]{1,0:T(8,128)(2,1)S(1)}) custom-call(s32[8]{0:T(128)S(1)} %stack.33.sc, bf16[256,1024]{1,0:T(8,128)(2,1)S(1)} %copy-done, bf16[256,1024]{1,0:T(8,128)(2,1)S(1)} %collective-permute-done.q_other, bf16[1152,128]{1,0:T(8,128)(2,1)S(1)} %collective-permute-done.7.x2.a2, ...), custom_call_target="tpu_custom_call" | custom-call | flops 2147483648 | bytes 4194304 | tf_op jit(solution)/shard_map/pallas_call | solution.py:291
  77.2 0.1 collective-permute-start.16
  77.3 0.9 %add_select_fusion = bf16[32,32,256]{2,1,0:T(8,128)(2,1)} fusion(bf16[32,32,256]{2,1,0:T(8,128)(2,1)S(1)} %shard_map.72, bf16[32,32,256]{2,1,0:T(8,128)(2,1)S(1)} %collective-permute-done.17, pred[]{:T(512)} %bitcast.6), kind=kLoop, calls=%fused_computation | loop fusion | flops 524288 | bytes 1572865 | tf_op jit(solution)/shard_map/jit(_where)/select_n | solution.py:368
  78.2 1.1 %collective-permute-done.16.got = bf16[256,1152]{1,0:T(8,128)(2,1)S(1)} collective-permute-done((bf16[256,1152]{1,0:T(8,128)(2,1)S(1)}, bf16[256,1152]{1,0:T(8,128)(2,1)S(1)}, u32[]{:S(2)}, u32[]{:S(2)}) %collective-permute-start.16) | collective-permute-done | bytes 589856 | tf_op jit(solution)/shard_map/ppermute | solution.py:364
  79.3 1.6 %shard_map.71 = bf16[256,1024]{1,0:T(8,128)(2,1)} custom-call(bf16[256,1024]{1,0:T(8,128)(2,1)S(1)} %get-tuple-element.17.keep, f32[256,128]{1,0:T(8,128)S(1)} %get-tuple-element.18.keep_lse, bf16[256,1152]{1,0:T(8,128)(2,1)S(1)} %collective-permute-done.16.got), custom_call_target="tpu_custom_call" | custom-call | flops 536870912 | bytes 4194304 | tf_op jit(solution)/shard_map/pallas_call | solution.py:291
  (50 shorter events, 0.9 us)
Async XLA Ops:
  1.5 4.0 %collective-permute-start.1 = (bf16[256,128]{1,0:T(8,128)(2,1)S(1)}, bf16[256,128]{1,0:T(8,128)(2,1)S(1)}, u32[]{:S(2)}, u32[]{:S(2)}) collective-permute-start(bf16[256,128]{1,0:T(8,128)(2,1)S(1)} %pad_maximum_fusion.1), channel_id=1, source_target_pairs={{0,1},{1,0},{2,3},{3,2},{4,5},{5,4},{6,7},{7,6},{8,9},{9,8},{10,11... | collective-permute-start | bytes 196616 | tf_op jit(solution)/shard_map/ppermute | solution.py:318
  2.3 34.8 %collective-permute-start = (bf16[256,1024]{1,0:T(8,128)(2,1)}, bf16[256,1024]{1,0:T(8,128)(2,1)S(1)}, u32[]{:S(2)}, u32[]{:S(2)}) collective-permute-start(bf16[256,1024]{1,0:T(8,128)(2,1)} %q_own.5), channel_id=1, source_target_pairs={{0,1},{1,0},{2,3},{3,2},{4,5},{5,4},{6,7},{7,6},{8,9},{9,8},{10,11... | collective-permute-start | bytes 1572872 | tf_op jit(solution)/shard_map/ppermute | solution.py:319
  2.4 0.7 copy-start.1
  4.3 0.7 copy-start.2
  5.6 16.1 %collective-permute-start.3 = (bf16[256,128]{1,0:T(8,128)(2,1)S(1)}, bf16[256,128]{1,0:T(8,128)(2,1)S(1)}, u32[]{:S(2)}, u32[]{:S(2)}) collective-permute-start(bf16[256,128]{1,0:T(8,128)(2,1)S(1)} %get-tuple-element.24.pas), channel_id=1, source_target_pairs={{0,32},{8,40},{16,48},{24,56},{32,64},{40,72},{48,80},{56,88},{64,... | collective-permute-start | bytes 196616 | tf_op jit(solution)/shard_map/ppermute | solution.py:331
  14.5 7.2 %collective-permute-start.2 = (bf16[272,128]{1,0:T(8,128)(2,1)S(1)}, bf16[272,128]{1,0:T(8,128)(2,1)S(1)}, u32[]{:S(2)}, u32[]{:S(2)}) collective-permute-start(bf16[272,128]{1,0:T(8,128)(2,1)S(1)} %get-tuple-element.37), channel_id=1, source_target_pairs={{0,32},{8,40},{16,48},{24,56},{32,0},{40,8},{48,16},{56,24},{64,96... | collective-permute-start | bytes 208904 | tf_op jit(solution)/shard_map/ppermute | solution.py:330
  21.8 8.2 %collective-permute-start.10 = (bf16[384,128]{1,0:T(8,128)(2,1)S(1)}, bf16[384,128]{1,0:T(8,128)(2,1)S(1)}, u32[]{:S(2)}, u32[]{:S(2)}) collective-permute-start(bf16[384,128]{1,0:T(8,128)(2,1)S(1)} %constant_dynamic-update-slice_fusion.27), channel_id=1, source_target_pairs={{0,192},{8,200},{16,208},{24,216},{32,224},{40,232},{48,240},{56,2... | collective-permute-start | bytes 294920 | tf_op jit(solution)/shard_map/ppermute | solution.py:339
  22.2 7.3 %collective-permute-start.9 = (bf16[384,128]{1,0:T(8,128)(2,1)S(1)}, bf16[384,128]{1,0:T(8,128)(2,1)S(1)}, u32[]{:S(2)}, u32[]{:S(2)}) collective-permute-start(bf16[384,128]{1,0:T(8,128)(2,1)S(1)} %constant_dynamic-update-slice_fusion.27), channel_id=1, source_target_pairs={{0,128},{8,136},{16,144},{24,152},{32,160},{40,168},{48,176},{56,1... | collective-permute-start | bytes 294920 | tf_op jit(solution)/shard_map/ppermute | solution.py:339
  24.6 3.9 %collective-permute-start.8 = (bf16[384,128]{1,0:T(8,128)(2,1)S(1)}, bf16[384,128]{1,0:T(8,128)(2,1)S(1)}, u32[]{:S(2)}, u32[]{:S(2)}) collective-permute-start(bf16[384,128]{1,0:T(8,128)(2,1)S(1)} %constant_dynamic-update-slice_fusion.27), channel_id=1, source_target_pairs={{0,64},{8,72},{16,80},{24,88},{32,96},{40,104},{48,112},{56,120},{... | collective-permute-start | bytes 294920 | tf_op jit(solution)/shard_map/ppermute | solution.py:339
  24.7 7.9 %collective-permute-start.5 = (bf16[544,128]{1,0:T(8,128)(2,1)S(1)}, bf16[544,128]{1,0:T(8,128)(2,1)S(1)}, u32[]{:S(2)}, u32[]{:S(2)}) collective-permute-start(bf16[544,128]{1,0:T(8,128)(2,1)S(1)} %constant_dynamic-update-slice_fusion.10), channel_id=1, source_target_pairs={{0,16},{8,24},{16,0},{24,8},{32,48},{40,56},{48,32},{56,40},{64,80... | collective-permute-start | bytes 417800 | tf_op jit(solution)/shard_map/ppermute | solution.py:337
  24.8 16.6 %copy-start = (bf16[256,1024]{1,0:T(8,128)(2,1)S(1)}, bf16[256,1024]{1,0:T(8,128)(2,1)}, u32[]{:S(2)}) copy-start(bf16[256,1024]{1,0:T(8,128)(2,1)} %q_own.5) | copy-start | bytes 1572868
  28.5 3.9 %collective-permute-start.4 = (bf16[544,128]{1,0:T(8,128)(2,1)S(1)}, bf16[544,128]{1,0:T(8,128)(2,1)S(1)}, u32[]{:S(2)}, u32[]{:S(2)}) collective-permute-start(bf16[544,128]{1,0:T(8,128)(2,1)S(1)} %constant_dynamic-update-slice_fusion.5), channel_id=1, source_target_pairs={{0,8},{8,16},{16,24},{24,0},{32,40},{40,48},{48,56},{56,32},{64,72... | collective-permute-start | bytes 417800 | tf_op jit(solution)/shard_map/ppermute | solution.py:337
  29.5 6.7 %collective-permute-start.6 = (bf16[544,128]{1,0:T(8,128)(2,1)S(1)}, bf16[544,128]{1,0:T(8,128)(2,1)S(1)}, u32[]{:S(2)}, u32[]{:S(2)}) collective-permute-start(bf16[544,128]{1,0:T(8,128)(2,1)S(1)} %get-tuple-element.23), channel_id=1, source_target_pairs={{0,24},{8,0},{16,8},{24,16},{32,56},{40,32},{48,40},{56,48},{64,88... | collective-permute-start | bytes 417800 | tf_op jit(solution)/shard_map/ppermute | solution.py:337
  30.1 9.1 %collective-permute-start.13 = (bf16[1152,128]{1,0:T(8,128)(2,1)S(1)}, bf16[1152,128]{1,0:T(8,128)(2,1)S(1)}, u32[]{:S(2)}, u32[]{:S(2)}) collective-permute-start(bf16[1152,128]{1,0:T(8,128)(2,1)S(1)} %get-tuple-element.20.h2.b0), channel_id=1, source_target_pairs={{0,8},{8,16},{16,24},{24,0},{32,40},{40,48},{48,56},{56,32},{64,72... | collective-permute-start | bytes 884744 | tf_op jit(solution)/shard_map/ppermute | solution.py:346
  32.4 16.9 %collective-permute-start.12 = (bf16[1152,128]{1,0:T(8,128)(2,1)S(1)}, bf16[1152,128]{1,0:T(8,128)(2,1)S(1)}, u32[]{:S(2)}, u32[]{:S(2)}) collective-permute-start(bf16[1152,128]{1,0:T(8,128)(2,1)S(1)} %get-tuple-element.20.h2.b0), channel_id=1, source_target_pairs={{0,24},{8,0},{16,8},{24,16},{32,56},{40,32},{48,40},{56,48},{64,88... | collective-permute-start | bytes 884744 | tf_op jit(solution)/shard_map/ppermute | solution.py:346
  32.6 16.7 %collective-permute-start.11 = (bf16[1152,128]{1,0:T(8,128)(2,1)S(1)}, bf16[1152,128]{1,0:T(8,128)(2,1)S(1)}, u32[]{:S(2)}, u32[]{:S(2)}) collective-permute-start(bf16[1152,128]{1,0:T(8,128)(2,1)S(1)} %get-tuple-element.20.h2.b0), channel_id=1, source_target_pairs={{0,16},{8,24},{16,0},{24,8},{32,48},{40,56},{48,32},{56,40},{64,80... | collective-permute-start | bytes 884744 | tf_op jit(solution)/shard_map/ppermute | solution.py:346
  36.3 13.1 %collective-permute-start.15 = (bf16[1152,128]{1,0:T(8,128)(2,1)S(1)}, bf16[1152,128]{1,0:T(8,128)(2,1)S(1)}, u32[]{:S(2)}, u32[]{:S(2)}) collective-permute-start(bf16[1152,128]{1,0:T(8,128)(2,1)S(1)} %constant_dynamic-update-slice_fusion.20.h1.a0), channel_id=1, source_target_pairs={{0,192},{8,200},{16,208},{24,216},{32,224},{40,232},{48,240},{56,2... | collective-permute-start | bytes 884744 | tf_op jit(solution)/shard_map/ppermute | solution.py:345
  37.1 12.2 %collective-permute-start.14 = (bf16[1152,128]{1,0:T(8,128)(2,1)S(1)}, bf16[1152,128]{1,0:T(8,128)(2,1)S(1)}, u32[]{:S(2)}, u32[]{:S(2)}) collective-permute-start(bf16[1152,128]{1,0:T(8,128)(2,1)S(1)} %constant_dynamic-update-slice_fusion.20.h1.a0), channel_id=1, source_target_pairs={{0,64},{8,72},{16,80},{24,88},{32,96},{40,104},{48,112},{56,120},{... | collective-permute-start | bytes 884744 | tf_op jit(solution)/shard_map/ppermute | solution.py:345
  39.2 10.1 %collective-permute-start.7 = (bf16[1152,128]{1,0:T(8,128)(2,1)S(1)}, bf16[1152,128]{1,0:T(8,128)(2,1)S(1)}, u32[]{:S(2)}, u32[]{:S(2)}) collective-permute-start(bf16[1152,128]{1,0:T(8,128)(2,1)S(1)} %constant_dynamic-update-slice_fusion.20.h1.a0), channel_id=1, source_target_pairs={{0,128},{8,136},{16,144},{24,152},{32,160},{40,168},{48,176},{56,1... | collective-permute-start | bytes 884744 | tf_op jit(solution)/shard_map/ppermute | solution.py:345
  50.6 26.8 %collective-permute-start.17 = (bf16[32,32,256]{2,1,0:T(8,128)(2,1)S(1)}, bf16[32,32,256]{2,1,0:T(8,128)(2,1)S(1)}, u32[]{:S(2)}, u32[]{:S(2)}) collective-permute-start(bf16[32,32,256]{2,1,0:T(8,128)(2,1)S(1)} %shard_map.72), channel_id=1, source_target_pairs={{0,1},{1,0},{2,3},{3,2},{4,5},{5,4},{6,7},{7,6},{8,9},{9,8},{10,11... | collective-permute-start | bytes 1572872 | tf_op jit(solution)/shard_map/ppermute | solution.py:366
  77.2 2.1 %collective-permute-start.16 = (bf16[256,1152]{1,0:T(8,128)(2,1)S(1)}, bf16[256,1152]{1,0:T(8,128)(2,1)S(1)}, u32[]{:S(2)}, u32[]{:S(2)}) collective-permute-start(bf16[256,1152]{1,0:T(8,128)(2,1)S(1)} %get-tuple-element.19), channel_id=1, source_target_pairs={{0,1},{1,0},{2,3},{3,2},{4,5},{5,4},{6,7},{7,6},{8,9},{9,8},{10,11... | collective-permute-start | bytes 1769480 | tf_op jit(solution)/shard_map/ppermute | solution.py:364

commit v3 on v2

v3 whole, which is shorter than its diff:
```python
import math

import jax
import jax.numpy as jnp
from jax import lax
from jax.experimental import pallas as pl
from jax.experimental.pallas import tpu as pltpu
from jax.sharding import PartitionSpec as P

GROUP = 8
HD = 128
SINK = 64
RECENT = 1024
PAGE = 16
ROWS = 256
HALF = 128
QUART = 64
META = 16
FIRST = 2 * QUART + META
CHUNK = 512
WIDE = 2
PASSED = 8 * 2 * QUART + 2 * SINK
NEG = -1e30
SCALE = math.log2(math.e) / math.sqrt(HD)
F32 = jnp.float32
BF16 = jnp.bfloat16


def ctx_of(x, z, y):
    return (x % 4) * 8 + (z % 2) * 4 + (y % 4)


CHIPS = [(x, z, y) for x in range(4) for z in range(2) for y in range(4)]
CORE_SWAP = [(i, i ^ 1) for i in range(8)]
Z_SWAP = [(ctx_of(x, z, y), ctx_of(x, z + 1, y)) for x, z, y in CHIPS]
FOUR_ON = [(i, i + 4) for i in range(28)]
X_SHIFT = {s: [(ctx_of(x, z, y), ctx_of(x + s, z, y)) for x, z, y in CHIPS] for s in (1, 2, 3)}
Y_SHIFT = {s: [(ctx_of(x, z, y), ctx_of(x, z, y + s)) for x, z, y in CHIPS] for s in (1, 2, 3)}


def nt_dot(a, b):
    return lax.dot_general(a, b, (((1,), (1,)), ((), ())), preferred_element_type=F32)


def iota(shape, axis):
    return lax.broadcasted_iota(jnp.int32, shape, axis)


def fold(state, q, k, v, left=None, right=None):
    s = nt_dot(q, k)
    if left is not None:
        s = jnp.concatenate([s[:, :HD] + left, s[:, HD:]], axis=1) if s.shape[1] > HD else s + left
    if right is not None:
        s = jnp.concatenate([s[:, :-HD], s[:, -HD:] + right], axis=1)
    high = jnp.max(s, axis=1, keepdims=True)
    top = jnp.broadcast_to(high, (ROWS, HD)) if state is None else jnp.maximum(state[0], high)
    p = jnp.exp2((s - jnp.concatenate([top] * (s.shape[1] // HD), axis=1)) * SCALE).astype(BF16)
    up = jnp.dot(p, v, preferred_element_type=F32)
    if state is None:
        return top, up[:, HD:], up[:, :HD]
    keep = jnp.exp2((state[0] - top) * SCALE)
    return top, state[1] * keep + up[:, HD:], state[2] * keep + up[:, :HD]


def put_keys(k_s, v_s, at, ref, first, rows, gap):
    k_s[pl.ds(at, rows), 0:HD] = ref[first:first + rows, :]
    v_s[pl.ds(at, rows), 0:HD] = ref[first + gap:first + gap + rows, :]


def put_first(k_s, v_s, at, ref):
    for n in range(8):
        put_keys(k_s, v_s, at + n * QUART, ref, n * FIRST, QUART, QUART)


def put_second(k_s, v_s, at, ref):
    for n in range(8):
        put_keys(k_s, v_s, at + n * QUART, ref, n * 2 * QUART, QUART, QUART)


def put_bias(k_s, v_s, bias):
    lane = iota(bias.shape, 1)
    k_s[:, HD:] = jnp.where(lane == 0, bias, 0.0).astype(BF16)
    v_s[:, HD:] = jnp.ones(bias.shape, BF16)


def range_bias(sc, shape, chunks):
    x, y, z, c = sc[0], sc[1], sc[2], sc[4]
    n = iota(shape, 0)
    outer, far = (n >> 7) & 3, (n >> 6) & 1
    which = n >> 9
    dx, dy = outer, outer
    for i, (fixed_x, fixed_y) in enumerate(chunks):
        if fixed_x is not None:
            dx = jnp.where(which == i, fixed_x, dx)
        else:
            dy = jnp.where(which == i, fixed_y, dy)
    zz = jnp.where(far == 0, z, 1 - z)
    block = ((x - dx) & 3) * 8 + zz * 4 + ((y - dy) & 3)
    return jnp.where(block <= c, 0.0, NEG)


def load_head(q_a, q_b, flag, a):
    cols = slice(a * HD, (a + 1) * HD)
    q = jnp.where(flag == 1, q_a[:, cols], q_b[:, cols])
    one = jnp.where(iota((ROWS, HD), 1) == 0, 1.0, 0.0).astype(BF16)
    return jnp.concatenate([q, one], axis=1)


def near_kernel(sc, q_own, q_other, h1, h2, m_out, l_out, o_out, kr, vr):
    core, is_r = sc[3], sc[5]
    put_first(kr, vr, 0, h1)
    put_second(kr, vr, CHUNK, h2)
    put_bias(kr, vr, range_bias(sc, (2 * CHUNK, HD), ((0, None), (None, 0))))
    row = iota((ROWS, HD), 0)
    lane = iota((ROWS, HD), 1)
    key = core * HALF + lane
    first = jnp.where((lane < QUART) & (key > row), NEG, 0.0)
    second = jnp.where((lane < QUART) & (key + QUART > row), NEG, 0.0)

    def heads(i):
        at = [WIDE * i + u for u in range(WIDE)]
        q = [load_head(q_own, q_other, is_r, a) for a in at]
        state = [fold(None, q[u], kr[0:CHUNK, :], vr[0:CHUNK, :], left=first) for u in range(WIDE)]
        state = [fold(state[u], q[u], kr[CHUNK:, :], vr[CHUNK:, :], left=second) for u in range(WIDE)]
        for u in range(WIDE):
            m_out[at[u]], l_out[at[u]], o_out[at[u]] = state[u]

    for i in range(GROUP // WIDE):
        heads(i)


def middle_kernel(sc, q_own, q_other, x1, x3, y1, y3, m_in, l_in, o_in, m_out, l_out, o_out, kr, vr):
    is_r = sc[5]
    put_first(kr, vr, 0, x1)
    put_first(kr, vr, CHUNK, x3)
    put_second(kr, vr, 2 * CHUNK, y1)
    put_second(kr, vr, 3 * CHUNK, y3)
    put_bias(kr, vr, range_bias(sc, (4 * CHUNK, HD), ((1, None), (3, None), (None, 1), (None, 3))))

    def heads(i):
        at = [WIDE * i + u for u in range(WIDE)]
        q = [load_head(q_own, q_other, is_r, a) for a in at]
        state = [(m_in[a], l_in[a], o_in[a]) for a in at]
        for n in range(4):
            rows = slice(n * CHUNK, (n + 1) * CHUNK)
            state = [fold(state[u], q[u], kr[rows, :], vr[rows, :]) for u in range(WIDE)]
        for u in range(WIDE):
            m_out[at[u]], l_out[at[u]], o_out[at[u]] = state[u]

    for i in range(GROUP // WIDE):
        heads(i)


def finish(state):
    m, l, o = state
    return o / l, m * SCALE + jnp.log2(l)


def last_kernel(sc, q_own, q_other, x2, y1, y2, y3, pas, far, sink, m_in, l_in, o_in, keep, keep_lse, send,
                kr, vr, kp, vp, lse_s):
    core, c, is_r = sc[3], sc[4], sc[5]
    put_first(kr, vr, 0, x2)
    put_second(kr, vr, CHUNK, y2)
    put_bias(kr, vr, range_bias(sc, (2 * CHUNK, HD), ((2, None), (None, 2))))
    put_keys(kp, vp, 0, pas, 0, HALF, HALF)
    for n, ref in enumerate((y1, y2, y3)):
        put_keys(kp, vp, (n + 1) * HALF, ref, PASSED, HALF, HALF)
    kp[4 * HALF:5 * HALF, :] = jnp.zeros((HALF, 2 * HD), BF16)
    vp[4 * HALF:5 * HALF, :] = jnp.zeros((HALF, 2 * HD), BF16)
    put_keys(kp, vp, 4 * HALF, sink, 0, SINK, SINK)
    put_keys(kp, vp, 5 * HALF, far, 0, HALF, HALF)
    slot = iota((6 * HALF, HD), 0) >> 7
    put_bias(kp, vp, jnp.where((slot - (slot >> 2) <= c) | (slot == 4), 0.0, NEG))
    row = iota((ROWS, HD), 0)
    lane = iota((ROWS, HD), 1)
    key = core * HALF + lane
    own = jnp.where(key > row, NEG, 0.0)
    edge = jnp.where(key <= row, NEG, 0.0)
    seen = (core == 0) & (lane < SINK) & (c * ROWS + row - lane >= RECENT)
    sink_bias = jnp.where(seen, 0.0, NEG)
    lse_s[...] = jnp.zeros((ROWS, HD), F32)
    keep_lse[...] = jnp.zeros((ROWS, HD), F32)

    def heads(i):
        at = [WIDE * i + u for u in range(WIDE)]
        qp = [load_head(q_other, q_own, is_r, a) for a in at]
        qr = [load_head(q_own, q_other, is_r, a) for a in at]
        sr = [(m_in[a], l_in[a], o_in[a]) for a in at]
        sr = [fold(sr[u], qr[u], kr[0:CHUNK, :], vr[0:CHUNK, :]) for u in range(WIDE)]
        sp = [fold(None, qp[u], kp[0:4 * HALF, :], vp[0:4 * HALF, :], left=own) for u in range(WIDE)]
        sr = [fold(sr[u], qr[u], kr[CHUNK:, :], vr[CHUNK:, :]) for u in range(WIDE)]
        sp = [fold(sp[u], qp[u], kp[4 * HALF:, :], vp[4 * HALF:, :], left=sink_bias, right=edge) for u in range(WIDE)]
        for u in range(WIDE):
            cols = slice(at[u] * HD, (at[u] + 1) * HD)
            out_r, lse_r = finish(sr[u])
            out_p, lse_p = finish(sp[u])
            keep[:, cols] = jnp.where(is_r == 1, out_r, out_p).astype(BF16)
            send[:, cols] = jnp.where(is_r == 1, out_p, out_r).astype(BF16)
            keep_lse[...] = jnp.where(lane == at[u], jnp.where(is_r == 1, lse_r, lse_p), keep_lse[...])
            lse_s[...] = jnp.where(lane == at[u], jnp.where(is_r == 1, lse_p, lse_r), lse_s[...])

    for i in range(GROUP // WIDE):
        heads(i)
    lse = lse_s[...]
    high = lse.astype(BF16).astype(F32)
    mid = (lse - high).astype(BF16).astype(F32)
    low = lse - high - mid
    parts = high + pltpu.roll(mid, GROUP, 1) + pltpu.roll(low, 2 * GROUP, 1)
    send[:, GROUP * HD:] = parts.astype(BF16)


def merge_kernel(keep, keep_lse, got, out_ref):
    ext = got[:, GROUP * HD:].astype(F32)
    lse = ext + pltpu.roll(ext, HD - GROUP, 1) + pltpu.roll(ext, HD - 2 * GROUP, 1)
    lane = iota((ROWS, HD), 1)
    gap = jnp.where(lane < GROUP, lse - keep_lse[...], 0.0)
    weight = 1.0 / (1.0 + jnp.exp2(jnp.clip(gap, -126.0, 126.0)))
    for a in range(GROUP):
        cols = slice(a * HD, (a + 1) * HD)
        w = weight[:, a:a + 1]
        mine, theirs = keep[:, cols].astype(F32), got[:, cols].astype(F32)
        out_ref[:, cols] = (theirs + w * (mine - theirs)).astype(BF16)


def pages_kernel(sc, a0, a1, a2, a3, b0, b1, b2, b3, out_ref):
    x, y, z, c = sc[0], sc[1], sc[2], sc[4]
    first = (a0, a1, a2, a3)
    second = (b0, b1, b2, b3)
    row = iota((2 * PAGE, HD), 0)
    lane = iota((2 * PAGE, HD), 1)
    same_row = (lane & (PAGE - 1)) == (row & (PAGE - 1))
    want = (2 * c + (row >> 4)).astype(F32)
    for dx in range(4):
        for d in range(4):
            for col in range(2):
                f, at = first[dx], (d * 2 + col) * FIRST
                s, on = second[d], (dx * 2 + col) * 2 * QUART
                code = jnp.concatenate([f[at + 2 * QUART:at + FIRST, :]] * 2, axis=0).astype(F32)
                select = jnp.where(same_row & (code == want), 1.0, 0.0).astype(BF16)
                zz = z if col == 0 else 1 - z
                block = ((x - dx) & 3) * 8 + zz * 4 + ((y - d) & 3)
                for part in range(2):
                    k1 = f[at + part * QUART:at + (part + 1) * QUART, :]
                    k2 = s[on + part * QUART:on + (part + 1) * QUART, :]
                    pages = jnp.dot(select, jnp.concatenate([k1, k2], axis=0), preferred_element_type=F32)
                    out_ref[block, :, part * HD:(part + 1) * HD] = pages.astype(BF16)


VMEM_SPEC = pl.BlockSpec(memory_space=pltpu.VMEM)
SMEM_SPEC = pl.BlockSpec(memory_space=pltpu.SMEM)


def call(kernel, out_shape, scratch, flops, sc, *args):
    many = isinstance(out_shape, tuple)
    specs = ([SMEM_SPEC] if sc is not None else []) + [VMEM_SPEC] * len(args)
    operands = ([sc] if sc is not None else []) + list(args)
    return pl.pallas_call(
        kernel,
        out_shape=out_shape,
        in_specs=specs,
        out_specs=(VMEM_SPEC,) * len(out_shape) if many else VMEM_SPEC,
        scratch_shapes=scratch,
        compiler_params=pltpu.CompilerParams(vmem_limit_bytes=24 * 1024 * 1024),
        cost_estimate=pl.CostEstimate(flops=flops, bytes_accessed=4 << 20, transcendentals=flops // 512),
    )(*operands)


def keys(rows):
    return [pltpu.VMEM((rows, 2 * HD), BF16), pltpu.VMEM((rows, 2 * HD), BF16)]


def shards(q, k, v, head_kind, page_owner):
    c = lax.axis_index("ctx")
    tp = lax.axis_index("tp")
    x, z, y = c // 8, (c // 4) % 2, c % 4
    core = tp % 2
    is_r = lax.dynamic_index_in_dim(head_kind, tp, 0, keepdims=False) == 1
    sc = jnp.stack([x, y, z, core, c, is_r.astype(jnp.int32), tp, tp]).astype(jnp.int32)

    low = jnp.concatenate([k[:HALF], v[:HALF]])
    high = jnp.concatenate([k[HALF:], v[HALF:]])
    stay = jnp.where(core == 0, low, high)
    came = lax.ppermute(jnp.where(core == 0, high, low), "tp", CORE_SWAP)
    q_other = lax.ppermute(q, "tp", CORE_SWAP)
    ret = jnp.where(is_r, stay, came)
    pas = jnp.where(is_r, came, stay)

    earlier = lax.iota(jnp.int32, 16)[None, :] < lax.iota(jnp.int32, 16)[:, None]
    rank = jnp.sum(((page_owner[:, None] == page_owner[None, :]) & earlier).astype(jnp.int32), axis=1)
    code = page_owner * 2 + rank
    code = jnp.where(core == 0, code[:8], code[8:]).astype(BF16)
    meta = jnp.broadcast_to(jnp.repeat(code, PAGE)[None, :], (META, HD))

    r1 = jnp.concatenate([ret[:QUART], ret[HALF:HALF + QUART], meta])
    r2 = jnp.concatenate([ret[QUART:HALF], ret[HALF + QUART:]])
    sink = jnp.concatenate([pas[:SINK], pas[HALF:HALF + SINK]])
    theirs = lax.ppermute(jnp.concatenate([r1, r2, sink]), "ctx", Z_SWAP)
    theirs, q_other = lax.optimization_barrier((theirs, q_other))
    far = lax.ppermute(pas, "ctx", FOUR_ON)
    r1 = jnp.concatenate([r1, theirs[:FIRST]])
    r2 = jnp.concatenate([r2, theirs[FIRST:FIRST + HALF]])
    sink = jnp.where(z == 0, sink, theirs[FIRST + HALF:])

    along_x = jnp.concatenate([r2, sink])
    ys = {s: lax.ppermute(r1, "ctx", Y_SHIFT[s]) for s in (1, 3)}
    xs = {s: lax.ppermute(along_x, "ctx", X_SHIFT[s]) for s in (1, 3)}
    r1_late, x_late, far = lax.optimization_barrier((r1, along_x, far))
    ys[2] = lax.ppermute(r1_late, "ctx", Y_SHIFT[2])
    xs[2] = lax.ppermute(x_late, "ctx", X_SHIFT[2])
    h1 = jnp.concatenate([r1] + [ys[s] for s in (1, 2, 3)])
    for s in (1, 2, 3):
        sink = jnp.where(x == s, xs[s][2 * HALF:], sink)
    h2 = jnp.concatenate([r2] + [xs[s][:2 * HALF] for s in (1, 2, 3)] + [sink])

    a = {0: h1} | {s: lax.ppermute(h1, "ctx", X_SHIFT[s]) for s in (1, 3, 2)}
    b = {0: h2} | {
        s: lax.ppermute(jnp.concatenate([h2, jnp.where(y + s < 4, pas, far)]), "ctx", Y_SHIFT[s]) for s in (1, 3, 2)
    }

    state = (jax.ShapeDtypeStruct((GROUP, ROWS, HD), F32),) * 3
    unit = 2 * 2048 * 256 * 512
    now = call(near_kernel, state, keys(2 * CHUNK), 4 * unit, sc, q, q_other, h1, h2)
    now = call(middle_kernel, state, keys(4 * CHUNK), 8 * unit, sc, q, q_other, a[1], a[3], b[1], b[3], *now)
    for s in (1, 2, 3):
        sink = jnp.where(y == s, b[s][8 * HALF:8 * HALF + 2 * SINK], sink)
    keep, keep_lse, send = call(
        last_kernel,
        (
            jax.ShapeDtypeStruct((ROWS, GROUP * HD), BF16),
            jax.ShapeDtypeStruct((ROWS, HD), F32),
            jax.ShapeDtypeStruct((ROWS, (GROUP + 1) * HD), BF16),
        ),
        keys(2 * CHUNK) + keys(6 * HALF) + [pltpu.VMEM((ROWS, HD), F32)],
        7 * unit, sc, q, q_other, a[2], b[1], b[2], b[3], pas, far, sink, *now)

    got = lax.ppermute(send, "tp", CORE_SWAP)
    sc, _ = lax.optimization_barrier((sc, send))
    pages = call(
        pages_kernel, jax.ShapeDtypeStruct((32, 2 * PAGE, 2 * HD), BF16), [], unit // 4,
        sc, *[a[s] for s in range(4)], *[b[s] for s in range(4)])
    got_pages = lax.ppermute(pages, "tp", CORE_SWAP)
    attn_out = call(
        merge_kernel, jax.ShapeDtypeStruct((ROWS, GROUP * HD), BF16), [], unit // 4, None, keep, keep_lse, got)
    decode_cache = jnp.where(is_r, pages + got_pages, jnp.zeros((), BF16)).reshape(64, PAGE, 2 * HD)
    return attn_out, decode_cache


def solution(mesh):
    return jax.shard_map(
        shards,
        mesh=mesh,
        in_specs=(P("ctx", "tp"), P("ctx", "tp"), P("ctx", "tp"), P(), P("ctx")),
        out_specs=(P("ctx", "tp"), P("ctx", None, "tp")),
        check_vma=False,
    )
```

time: 81.1 us -> 80.9 us (level)
  the two profiles are of different devices: /device:TPU:21 before, /device:TPU:33 now
where the time goes in v3:
time: 80.9 us; the launch traced here: 80.7 us
  starting transfers between devices  39.2 us (48%)
  Pallas kernels  21.1 us (26%)
  waiting for transfers between devices  14.8 us (18%)
  local copies, waits for them, and re-layouts  2.69 us (3%)
  between operations  1.58 us (2%)
  other arithmetic  1.38 us (2%)
    pallas_call x5, Pallas kernels, call(): pl.pallas_call(kernel, out_shape=out_shape, in_specs=specs, out_specs=(VM...  21.1 us
    ppermute x1, starting transfers between devices, shards(): got_pages = lax.ppermute(pages, 'tp', CORE_SWAP)  12.4 us
    ppermute x1, starting transfers between devices, shards(): far = lax.ppermute(pas, 'ctx', FOUR_ON)  7.92 us
    ppermute x1, waiting for transfers between devices, shards(): theirs = lax.ppermute(jnp.concatenate([r1, r2, sink]), 'ctx', Z_SWAP)  7.21 us
    ppermute x2, starting transfers between devices, shards(): xs = {s: lax.ppermute(along_x, 'ctx', X_SHIFT[s]) for s in (1, 3)}  5.1 us
    ppermute x3, starting transfers between devices, shards(): lax.ppermute(jnp.concatenate([h2, jnp.where(y + s < 4, pas, far)]), 'ctx'...  3.5 us
    ppermute x3, starting transfers between devices, shards(): a = {0: h1} | {s: lax.ppermute(h1, 'ctx', X_SHIFT[s]) for s in (1, 3, 2)}  3.42 us
    ppermute x1, waiting for transfers between devices, shards(): ys[2] = lax.ppermute(r1_late, 'ctx', Y_SHIFT[2])  3.07 us
  transfers between devices with their start and end apart: 18, of which 5 were waited for; matrix products, arithmetic and copies ran while one was open for 3% of the time, Pallas kernels for 13%

profile of v3, /device:TPU:33, one launch (start us, length us, event | category | flops | bytes accessed | tf_op | source)
XLA Modules:
  0.0 80.7 jit_solution(5488372085937898594)
XLA Ops:
  0.6 0.8 %fusion.9 = (bf16[128,128]{1,0:T(8,128)(2,1)S(1)}, bf16[128,128]{1,0:T(8,128)(2,1)S(1)}, bf16[128,128]{1,0:T(8,128)(2,1)S(1)}, bf16[128,128]{1,0:T(8,128)(2,1)S(1)}) fusion(bf16[256,128]{1,0:T(8,128)(2,1)} %param.6, bf16[256,128]{1,0:T(8,128)(2,1)} %param.7), kind=kLoop, calls=%fused_computation.69 | loop fusion | bytes 262144 | tf_op jit(solution)/shard_map/slice | solution.py:280
  1.5 0.8 collective-permute-start
  2.3 0.1 collective-permute-start.2
  2.4 0.2 convert_reduce_fusion
  2.8 0.7 copy-done.2
  3.5 0.6 dynamic_slice.4
  5.0 7.9 %collective-permute-start.4 = (bf16[256,128]{1,0:T(8,128)(2,1)S(1)}, bf16[256,128]{1,0:T(8,128)(2,1)S(1)}, u32[]{:S(2)}, u32[]{:S(2)}) collective-permute-start(bf16[256,128]{1,0:T(8,128)(2,1)S(1)} %get-tuple-element.34.pas), channel_id=1, source_target_pairs={{0,32},{8,40},{16,48},{24,56},{32,64},{40,72},{48,80},{56,88},{64,... | collective-permute-start | bytes 196616 | tf_op jit(solution)/shard_map/ppermute | solution.py:299
  13.0 0.4 collective-permute-start.1
  13.4 7.2 %collective-permute-done.1 = bf16[400,128]{1,0:T(8,128)(2,1)S(1)} collective-permute-done((bf16[400,128]{1,0:T(8,128)(2,1)S(1)}, bf16[400,128]{1,0:T(8,128)(2,1)S(1)}, u32[]{:S(2)}, u32[]{:S(2)}) %collective-permute-start.1) | collective-permute-done | bytes 102432 | tf_op jit(solution)/shard_map/ppermute | solution.py:297
  20.7 1.4 %collective-permute-start.3 = (bf16[288,128]{1,0:T(8,128)(2,1)S(1)}, bf16[288,128]{1,0:T(8,128)(2,1)S(1)}, u32[]{:S(2)}, u32[]{:S(2)}) collective-permute-start(bf16[288,128]{1,0:T(8,128)(2,1)S(1)} %pad_maximum_fusion.1), channel_id=1, source_target_pairs={{0,8},{8,16},{16,24},{24,0},{32,40},{40,48},{48,56},{56,32},{64,72... | collective-permute-start | bytes 221192 | tf_op jit(solution)/shard_map/ppermute | solution.py:305
  22.1 1.3 %collective-permute-start.8 = (bf16[384,128]{1,0:T(8,128)(2,1)S(1)}, bf16[384,128]{1,0:T(8,128)(2,1)S(1)}, u32[]{:S(2)}, u32[]{:S(2)}) collective-permute-start(bf16[384,128]{1,0:T(8,128)(2,1)S(1)} %pad_maximum_fusion), channel_id=1, source_target_pairs={{0,64},{8,72},{16,80},{24,88},{32,96},{40,104},{48,112},{56,120},{... | collective-permute-start | bytes 294920 | tf_op jit(solution)/shard_map/ppermute | solution.py:306
  23.4 3.8 %collective-permute-start.10 = (bf16[384,128]{1,0:T(8,128)(2,1)S(1)}, bf16[384,128]{1,0:T(8,128)(2,1)S(1)}, u32[]{:S(2)}, u32[]{:S(2)}) collective-permute-start(bf16[384,128]{1,0:T(8,128)(2,1)S(1)} %pad_maximum_fusion), channel_id=1, source_target_pairs={{0,192},{8,200},{16,208},{24,216},{32,224},{40,232},{48,240},{56,2... | collective-permute-start | bytes 294920 | tf_op jit(solution)/shard_map/ppermute | solution.py:306
  27.2 1.5 %collective-permute-start.6 = (bf16[288,128]{1,0:T(8,128)(2,1)S(1)}, bf16[288,128]{1,0:T(8,128)(2,1)S(1)}, u32[]{:S(2)}, u32[]{:S(2)}) collective-permute-start(bf16[288,128]{1,0:T(8,128)(2,1)S(1)} %pad_maximum_fusion.1), channel_id=1, source_target_pairs={{0,24},{8,0},{16,8},{24,16},{32,56},{40,32},{48,40},{56,48},{64,88... | collective-permute-start | bytes 221192 | tf_op jit(solution)/shard_map/ppermute | solution.py:305
  28.6 1.1 %collective-permute-start.9 = (bf16[384,128]{1,0:T(8,128)(2,1)S(1)}, bf16[384,128]{1,0:T(8,128)(2,1)S(1)}, u32[]{:S(2)}, u32[]{:S(2)}) collective-permute-start(bf16[384,128]{1,0:T(8,128)(2,1)S(1)} %pad_maximum_fusion), channel_id=1, source_target_pairs={{0,128},{8,136},{16,144},{24,152},{32,160},{40,168},{48,176},{56,1... | collective-permute-start | bytes 294920 | tf_op jit(solution)/shard_map/ppermute | solution.py:309
  29.7 1.6 %collective-permute-start.5 = (bf16[288,128]{1,0:T(8,128)(2,1)S(1)}, bf16[288,128]{1,0:T(8,128)(2,1)S(1)}, u32[]{:S(2)}, u32[]{:S(2)}) collective-permute-start(bf16[288,128]{1,0:T(8,128)(2,1)S(1)} %pad_maximum_fusion.1), channel_id=1, source_target_pairs={{0,16},{8,24},{16,0},{24,8},{32,48},{40,56},{48,32},{56,40},{64,80... | collective-permute-start | bytes 221192 | tf_op jit(solution)/shard_map/ppermute | solution.py:308
  31.4 3.1 %collective-permute-done.5 = bf16[288,128]{1,0:T(8,128)(2,1)S(1)} collective-permute-done((bf16[288,128]{1,0:T(8,128)(2,1)S(1)}, bf16[288,128]{1,0:T(8,128)(2,1)S(1)}, u32[]{:S(2)}, u32[]{:S(2)}) %collective-permute-start.5) | collective-permute-done | bytes 73760 | tf_op jit(solution)/shard_map/ppermute | solution.py:308
  34.5 0.9 %collective-permute-start.14 = (bf16[1152,128]{1,0:T(8,128)(2,1)S(1)}, bf16[1152,128]{1,0:T(8,128)(2,1)S(1)}, u32[]{:S(2)}, u32[]{:S(2)}) collective-permute-start(bf16[1152,128]{1,0:T(8,128)(2,1)S(1)} %constant_dynamic-update-slice_fusion.7.h1.a0), channel_id=1, source_target_pairs={{0,64},{8,72},{16,80},{24,88},{32,96},{40,104},{48,112},{56,120},{... | collective-permute-start | bytes 884744 | tf_op jit(solution)/shard_map/ppermute | solution.py:315
  35.4 1.8 %collective-permute-start.15 = (bf16[1152,128]{1,0:T(8,128)(2,1)S(1)}, bf16[1152,128]{1,0:T(8,128)(2,1)S(1)}, u32[]{:S(2)}, u32[]{:S(2)}) collective-permute-start(bf16[1152,128]{1,0:T(8,128)(2,1)S(1)} %constant_dynamic-update-slice_fusion.7.h1.a0), channel_id=1, source_target_pairs={{0,192},{8,200},{16,208},{24,216},{32,224},{40,232},{48,240},{56,2... | collective-permute-start | bytes 884744 | tf_op jit(solution)/shard_map/ppermute | solution.py:315
  37.2 0.7 collective-permute-start.7
  38.2 1.7 %collective-permute-start.13 = (bf16[1408,128]{1,0:T(8,128)(2,1)S(1)}, bf16[1408,128]{1,0:T(8,128)(2,1)S(1)}, u32[]{:S(2)}, u32[]{:S(2)}) collective-permute-start(bf16[1408,128]{1,0:T(8,128)(2,1)S(1)} %constant_dynamic-update-slice_fusion.30), channel_id=1, source_target_pairs={{0,24},{8,0},{16,8},{24,16},{32,56},{40,32},{48,40},{56,48},{64,88... | collective-permute-start | bytes 1081352 | tf_op jit(solution)/shard_map/ppermute | solution.py:317
  40.0 0.3 collective-permute-start.11
  40.2 3.8 %shard_map.68 = (f32[8,256,128]{2,1,0:T(8,128)S(1)}, f32[8,256,128]{2,1,0:T(8,128)S(1)}, f32[8,256,128]{2,1,0:T(8,128)S(1)}) custom-call(s32[8]{0:T(128)S(1)} %stack.33.sc, bf16[256,1024]{1,0:T(8,128)(2,1)S(1)} %copy-done, bf16[256,1024]{1,0:T(8,128)(2,1)S(1)} %collective-permute-done.2.q_other, ...), custom_call_target="tpu_custom_call" | custom-call | flops 2147483648 | bytes 4194304 | tf_op jit(solution)/shard_map/pallas_call | solution.py:257
  44.1 1.5 %collective-permute-start.12 = (bf16[1408,128]{1,0:T(8,128)(2,1)S(1)}, bf16[1408,128]{1,0:T(8,128)(2,1)S(1)}, u32[]{:S(2)}, u32[]{:S(2)}) collective-permute-start(bf16[1408,128]{1,0:T(8,128)(2,1)S(1)} %constant_dynamic-update-slice_fusion.22), channel_id=1, source_target_pairs={{0,16},{8,24},{16,0},{24,8},{32,48},{40,56},{48,32},{56,40},{64,80... | collective-permute-start | bytes 1081352 | tf_op jit(solution)/shard_map/ppermute | solution.py:317
  45.6 2.4 %collective-permute-done.11.y1.b1 = bf16[1408,128]{1,0:T(8,128)(2,1)S(1)} collective-permute-done((bf16[1408,128]{1,0:T(8,128)(2,1)S(1)}, bf16[1408,128]{1,0:T(8,128)(2,1)S(1)}, u32[]{:S(2)}, u32[]{:S(2)}) %collective-permute-start.11) | collective-permute-done | bytes 360480 | tf_op jit(solution)/shard_map/ppermute | solution.py:317
  48.0 7.0 %shard_map.69 = (f32[8,256,128]{2,1,0:T(8,128)S(1)}, f32[8,256,128]{2,1,0:T(8,128)S(1)}, f32[8,256,128]{2,1,0:T(8,128)S(1)}) custom-call(s32[8]{0:T(128)S(1)} %stack.33.sc, bf16[256,1024]{1,0:T(8,128)(2,1)S(1)} %copy-done, bf16[256,1024]{1,0:T(8,128)(2,1)S(1)} %collective-permute-done.2.q_other, bf16[1152,128]{1,0:T(8,128)(2,1)S(1)} %collective-permute-done.14.x1.a1, ...), custom_call_target="tpu_custom_call" | custom-call | flops 4294967296 | bytes 4194304 | tf_op jit(solution)/shard_map/pallas_call | solution.py:257
  55.0 0.6 collective-permute-done.12.y2.b2
  55.7 7.8 %shard_map.70 = (bf16[256,1024]{1,0:T(8,128)(2,1)S(1)}, f32[256,128]{1,0:T(8,128)S(1)}, bf16[256,1152]{1,0:T(8,128)(2,1)S(1)}) custom-call(s32[8]{0:T(128)S(1)} %stack.33.sc, bf16[256,1024]{1,0:T(8,128)(2,1)S(1)} %copy-done, bf16[256,1024]{1,0:T(8,128)(2,1)S(1)} %collective-permute-done.2.q_other, bf16[1152,128]{1,0:T(8,128)(2,1)S(1)} %collective-permute-done.7.x2.a2, ...), custom_call_target="tpu_custom_call" | custom-call | flops 3758096384 | bytes 4194304 | tf_op jit(solution)/shard_map/pallas_call | solution.py:257
  63.5 1.2 %shard_map.72 = bf16[32,32,256]{2,1,0:T(8,128)(2,1)S(1)} custom-call(s32[8]{0:T(128)S(1)} %stack.33.sc, bf16[1152,128]{1,0:T(8,128)(2,1)S(1)} %constant_dynamic-update-slice_fusion.7.h1.a0, bf16[1152,128]{1,0:T(8,128)(2,1)S(1)} %collective-permute-done.14.x1.a1, bf16[1152,128]{1,0:T(8,128)(2,1)S(1)} %collective-permute-done.7.x2.a2, ...), custom_call_target="tpu_custom_call" | custom-call | flops 134217728 | bytes 4194304 | tf_op jit(solution)/shard_map/pallas_call | solution.py:257
  64.7 12.4 %collective-permute-start.17 = (bf16[32,32,256]{2,1,0:T(8,128)(2,1)S(1)}, bf16[32,32,256]{2,1,0:T(8,128)(2,1)S(1)}, u32[]{:S(2)}, u32[]{:S(2)}) collective-permute-start(bf16[32,32,256]{2,1,0:T(8,128)(2,1)S(1)} %shard_map.72), channel_id=1, source_target_pairs={{0,1},{1,0},{2,3},{3,2},{4,5},{5,4},{6,7},{7,6},{8,9},{9,8},{10,11... | collective-permute-start | bytes 1572872 | tf_op jit(solution)/shard_map/ppermute | solution.py:341
  77.1 1.4 %collective-permute-done.17 = bf16[32,32,256]{2,1,0:T(8,128)(2,1)S(1)} collective-permute-done((bf16[32,32,256]{2,1,0:T(8,128)(2,1)S(1)}, bf16[32,32,256]{2,1,0:T(8,128)(2,1)S(1)}, u32[]{:S(2)}, u32[]{:S(2)}) %collective-permute-start.17) | collective-permute-done | bytes 524320 | tf_op jit(solution)/shard_map/ppermute | solution.py:341
  78.6 0.8 %add_select_fusion = bf16[32,32,256]{2,1,0:T(8,128)(2,1)} fusion(bf16[32,32,256]{2,1,0:T(8,128)(2,1)S(1)} %shard_map.72, bf16[32,32,256]{2,1,0:T(8,128)(2,1)S(1)} %collective-permute-done.17, pred[]{:T(512)} %bitcast.6), kind=kLoop, calls=%fused_computation | loop fusion | flops 524288 | bytes 1572865 | tf_op jit(solution)/shard_map/jit(_where)/select_n | solution.py:344
  79.4 1.3 %shard_map.71 = bf16[256,1024]{1,0:T(8,128)(2,1)} custom-call(bf16[256,1024]{1,0:T(8,128)(2,1)S(1)} %get-tuple-element.28.keep, f32[256,128]{1,0:T(8,128)S(1)} %get-tuple-element.29.keep_lse, bf16[256,1152]{1,0:T(8,128)(2,1)S(1)} %collective-permute-done.16.got), custom_call_target="tpu_custom_call" | custom-call | flops 134217728 | bytes 4194304 | tf_op jit(solution)/shard_map/pallas_call | solution.py:257
  (54 shorter events, 1.0 us)
Async XLA Ops:
  1.5 0.9 %copy-start.1 = (s32[16]{0:T(128)S(1)}, s32[16]{0:T(128)}, u32[]{:S(2)}) copy-start(s32[16]{0:T(128)} %param.9) | copy-start | bytes 196
  1.5 3.4 %collective-permute-start = (bf16[256,128]{1,0:T(8,128)(2,1)S(1)}, bf16[256,128]{1,0:T(8,128)(2,1)S(1)}, u32[]{:S(2)}, u32[]{:S(2)}) collective-permute-start(bf16[256,128]{1,0:T(8,128)(2,1)S(1)} %broadcast_select_fusion), channel_id=1, source_target_pairs={{0,1},{1,0},{2,3},{3,2},{4,5},{5,4},{6,7},{7,6},{8,9},{9,8},{10,11... | collective-permute-start | bytes 196616 | tf_op jit(solution)/shard_map/ppermute | solution.py:283
  2.3 18.3 %collective-permute-start.2 = (bf16[256,1024]{1,0:T(8,128)(2,1)}, bf16[256,1024]{1,0:T(8,128)(2,1)S(1)}, u32[]{:S(2)}, u32[]{:S(2)}) collective-permute-start(bf16[256,1024]{1,0:T(8,128)(2,1)} %q_own.5), channel_id=1, source_target_pairs={{0,1},{1,0},{2,3},{3,2},{4,5},{5,4},{6,7},{7,6},{8,9},{9,8},{10,11... | collective-permute-start | bytes 1572872 | tf_op jit(solution)/shard_map/ppermute | solution.py:284
  2.8 0.7 copy-start.2
  5.0 23.6 %collective-permute-start.4 = (bf16[256,128]{1,0:T(8,128)(2,1)S(1)}, bf16[256,128]{1,0:T(8,128)(2,1)S(1)}, u32[]{:S(2)}, u32[]{:S(2)}) collective-permute-start(bf16[256,128]{1,0:T(8,128)(2,1)S(1)} %get-tuple-element.34.pas), channel_id=1, source_target_pairs={{0,32},{8,40},{16,48},{24,56},{32,64},{40,72},{48,80},{56,88},{64,... | collective-permute-start | bytes 196616 | tf_op jit(solution)/shard_map/ppermute | solution.py:299
  13.0 7.6 %collective-permute-start.1 = (bf16[400,128]{1,0:T(8,128)(2,1)S(1)}, bf16[400,128]{1,0:T(8,128)(2,1)S(1)}, u32[]{:S(2)}, u32[]{:S(2)}) collective-permute-start(bf16[400,128]{1,0:T(8,128)(2,1)S(1)} %constant_dynamic-update-slice_fusion), channel_id=1, source_target_pairs={{0,32},{8,40},{16,48},{24,56},{32,0},{40,8},{48,16},{56,24},{64,96... | collective-permute-start | bytes 307208 | tf_op jit(solution)/shard_map/ppermute | solution.py:297
  20.7 9.1 %collective-permute-start.3 = (bf16[288,128]{1,0:T(8,128)(2,1)S(1)}, bf16[288,128]{1,0:T(8,128)(2,1)S(1)}, u32[]{:S(2)}, u32[]{:S(2)}) collective-permute-start(bf16[288,128]{1,0:T(8,128)(2,1)S(1)} %pad_maximum_fusion.1), channel_id=1, source_target_pairs={{0,8},{8,16},{16,24},{24,0},{32,40},{40,48},{48,56},{56,32},{64,72... | collective-permute-start | bytes 221192 | tf_op jit(solution)/shard_map/ppermute | solution.py:305
  22.1 15.2 %collective-permute-start.8 = (bf16[384,128]{1,0:T(8,128)(2,1)S(1)}, bf16[384,128]{1,0:T(8,128)(2,1)S(1)}, u32[]{:S(2)}, u32[]{:S(2)}) collective-permute-start(bf16[384,128]{1,0:T(8,128)(2,1)S(1)} %pad_maximum_fusion), channel_id=1, source_target_pairs={{0,64},{8,72},{16,80},{24,88},{32,96},{40,104},{48,112},{56,120},{... | collective-permute-start | bytes 294920 | tf_op jit(solution)/shard_map/ppermute | solution.py:306
  23.4 14.6 %collective-permute-start.10 = (bf16[384,128]{1,0:T(8,128)(2,1)S(1)}, bf16[384,128]{1,0:T(8,128)(2,1)S(1)}, u32[]{:S(2)}, u32[]{:S(2)}) collective-permute-start(bf16[384,128]{1,0:T(8,128)(2,1)S(1)} %pad_maximum_fusion), channel_id=1, source_target_pairs={{0,192},{8,200},{16,208},{24,216},{32,224},{40,232},{48,240},{56,2... | collective-permute-start | bytes 294920 | tf_op jit(solution)/shard_map/ppermute | solution.py:306
  27.2 7.3 %collective-permute-start.6 = (bf16[288,128]{1,0:T(8,128)(2,1)S(1)}, bf16[288,128]{1,0:T(8,128)(2,1)S(1)}, u32[]{:S(2)}, u32[]{:S(2)}) collective-permute-start(bf16[288,128]{1,0:T(8,128)(2,1)S(1)} %pad_maximum_fusion.1), channel_id=1, source_target_pairs={{0,24},{8,0},{16,8},{24,16},{32,56},{40,32},{48,40},{56,48},{64,88... | collective-permute-start | bytes 221192 | tf_op jit(solution)/shard_map/ppermute | solution.py:305
  28.6 9.3 %collective-permute-start.9 = (bf16[384,128]{1,0:T(8,128)(2,1)S(1)}, bf16[384,128]{1,0:T(8,128)(2,1)S(1)}, u32[]{:S(2)}, u32[]{:S(2)}) collective-permute-start(bf16[384,128]{1,0:T(8,128)(2,1)S(1)} %pad_maximum_fusion), channel_id=1, source_target_pairs={{0,128},{8,136},{16,144},{24,152},{32,160},{40,168},{48,176},{56,1... | collective-permute-start | bytes 294920 | tf_op jit(solution)/shard_map/ppermute | solution.py:309
  29.7 4.7 %collective-permute-start.5 = (bf16[288,128]{1,0:T(8,128)(2,1)S(1)}, bf16[288,128]{1,0:T(8,128)(2,1)S(1)}, u32[]{:S(2)}, u32[]{:S(2)}) collective-permute-start(bf16[288,128]{1,0:T(8,128)(2,1)S(1)} %pad_maximum_fusion.1), channel_id=1, source_target_pairs={{0,16},{8,24},{16,0},{24,8},{32,48},{40,56},{48,32},{56,40},{64,80... | collective-permute-start | bytes 221192 | tf_op jit(solution)/shard_map/ppermute | solution.py:308
  34.5 9.6 %collective-permute-start.14 = (bf16[1152,128]{1,0:T(8,128)(2,1)S(1)}, bf16[1152,128]{1,0:T(8,128)(2,1)S(1)}, u32[]{:S(2)}, u32[]{:S(2)}) collective-permute-start(bf16[1152,128]{1,0:T(8,128)(2,1)S(1)} %constant_dynamic-update-slice_fusion.7.h1.a0), channel_id=1, source_target_pairs={{0,64},{8,72},{16,80},{24,88},{32,96},{40,104},{48,112},{56,120},{... | collective-permute-start | bytes 884744 | tf_op jit(solution)/shard_map/ppermute | solution.py:315
  35.4 10.2 %collective-permute-start.15 = (bf16[1152,128]{1,0:T(8,128)(2,1)S(1)}, bf16[1152,128]{1,0:T(8,128)(2,1)S(1)}, u32[]{:S(2)}, u32[]{:S(2)}) collective-permute-start(bf16[1152,128]{1,0:T(8,128)(2,1)S(1)} %constant_dynamic-update-slice_fusion.7.h1.a0), channel_id=1, source_target_pairs={{0,192},{8,200},{16,208},{24,216},{32,224},{40,232},{48,240},{56,2... | collective-permute-start | bytes 884744 | tf_op jit(solution)/shard_map/ppermute | solution.py:315
  37.2 18.4 %collective-permute-start.7 = (bf16[1152,128]{1,0:T(8,128)(2,1)S(1)}, bf16[1152,128]{1,0:T(8,128)(2,1)S(1)}, u32[]{:S(2)}, u32[]{:S(2)}) collective-permute-start(bf16[1152,128]{1,0:T(8,128)(2,1)S(1)} %constant_dynamic-update-slice_fusion.7.h1.a0), channel_id=1, source_target_pairs={{0,128},{8,136},{16,144},{24,152},{32,160},{40,168},{48,176},{56,1... | collective-permute-start | bytes 884744 | tf_op jit(solution)/shard_map/ppermute | solution.py:315
  38.1 2.1 %copy-start = (bf16[256,1024]{1,0:T(8,128)(2,1)S(1)}, bf16[256,1024]{1,0:T(8,128)(2,1)}, u32[]{:S(2)}) copy-start(bf16[256,1024]{1,0:T(8,128)(2,1)} %q_own.5) | copy-start | bytes 1572868
  38.2 7.4 %collective-permute-start.13 = (bf16[1408,128]{1,0:T(8,128)(2,1)S(1)}, bf16[1408,128]{1,0:T(8,128)(2,1)S(1)}, u32[]{:S(2)}, u32[]{:S(2)}) collective-permute-start(bf16[1408,128]{1,0:T(8,128)(2,1)S(1)} %constant_dynamic-update-slice_fusion.30), channel_id=1, source_target_pairs={{0,24},{8,0},{16,8},{24,16},{32,56},{40,32},{48,40},{56,48},{64,88... | collective-permute-start | bytes 1081352 | tf_op jit(solution)/shard_map/ppermute | solution.py:317
  40.0 8.0 %collective-permute-start.11 = (bf16[1408,128]{1,0:T(8,128)(2,1)S(1)}, bf16[1408,128]{1,0:T(8,128)(2,1)S(1)}, u32[]{:S(2)}, u32[]{:S(2)}) collective-permute-start(bf16[1408,128]{1,0:T(8,128)(2,1)S(1)} %constant_dynamic-update-slice_fusion.14), channel_id=1, source_target_pairs={{0,8},{8,16},{16,24},{24,0},{32,40},{40,48},{48,56},{56,32},{64,72... | collective-permute-start | bytes 1081352 | tf_op jit(solution)/shard_map/ppermute | solution.py:317
  44.1 11.5 %collective-permute-start.12 = (bf16[1408,128]{1,0:T(8,128)(2,1)S(1)}, bf16[1408,128]{1,0:T(8,128)(2,1)S(1)}, u32[]{:S(2)}, u32[]{:S(2)}) collective-permute-start(bf16[1408,128]{1,0:T(8,128)(2,1)S(1)} %constant_dynamic-update-slice_fusion.22), channel_id=1, source_target_pairs={{0,16},{8,24},{16,0},{24,8},{32,48},{40,56},{48,32},{56,40},{64,80... | collective-permute-start | bytes 1081352 | tf_op jit(solution)/shard_map/ppermute | solution.py:317
  64.7 13.9 %collective-permute-start.17 = (bf16[32,32,256]{2,1,0:T(8,128)(2,1)S(1)}, bf16[32,32,256]{2,1,0:T(8,128)(2,1)S(1)}, u32[]{:S(2)}, u32[]{:S(2)}) collective-permute-start(bf16[32,32,256]{2,1,0:T(8,128)(2,1)S(1)} %shard_map.72), channel_id=1, source_target_pairs={{0,1},{1,0},{2,3},{3,2},{4,5},{5,4},{6,7},{7,6},{8,9},{9,8},{10,11... | collective-permute-start | bytes 1572872 | tf_op jit(solution)/shard_map/ppermute | solution.py:341
  77.0 2.4 %collective-permute-start.16 = (bf16[256,1152]{1,0:T(8,128)(2,1)S(1)}, bf16[256,1152]{1,0:T(8,128)(2,1)S(1)}, u32[]{:S(2)}, u32[]{:S(2)}) collective-permute-start(bf16[256,1152]{1,0:T(8,128)(2,1)S(1)} %get-tuple-element.30), channel_id=1, source_target_pairs={{0,1},{1,0},{2,3},{3,2},{4,5},{5,4},{6,7},{7,6},{8,9},{9,8},{10,11... | collective-permute-start | bytes 1769480 | tf_op jit(solution)/shard_map/ppermute | solution.py:336

commit v4 on v3

--- a/solution.py
+++ b/solution.py
@@ -16,10 +16,10 @@
 HALF = 128
 QUART = 64
 META = 16
-FIRST = 2 * QUART + META
+PAIR = 2 * QUART
 CHUNK = 512
 WIDE = 2
-PASSED = 8 * 2 * QUART + 2 * SINK
+PASSED = 2 * PAIR + META
 NEG = -1e30
 SCALE = math.log2(math.e) / math.sqrt(HD)
 F32 = jnp.float32
@@ -67,14 +67,9 @@
     v_s[pl.ds(at, rows), 0:HD] = ref[first + gap:first + gap + rows, :]
 
 
-def put_first(k_s, v_s, at, ref):
+def put_ranges(k_s, v_s, at, ref):
     for n in range(8):
-        put_keys(k_s, v_s, at + n * QUART, ref, n * FIRST, QUART, QUART)
-
-
-def put_second(k_s, v_s, at, ref):
-    for n in range(8):
-        put_keys(k_s, v_s, at + n * QUART, ref, n * 2 * QUART, QUART, QUART)
+        put_keys(k_s, v_s, at + n * QUART, ref, n * PAIR, QUART, QUART)
 
 
 def put_bias(k_s, v_s, bias):
@@ -106,24 +101,36 @@
     return jnp.concatenate([q, one], axis=1)
 
 
-def near_kernel(sc, q_own, q_other, h1, h2, m_out, l_out, o_out, kr, vr):
-    core, is_r = sc[3], sc[5]
-    put_first(kr, vr, 0, h1)
-    put_second(kr, vr, CHUNK, h2)
+def near_kernel(sc, q_own, q_other, pas, y1, y2, y3, far, h1, h2, mp_out, lp_out, op_out, m_out, l_out, o_out,
+                kp, vp, kr, vr):
+    core, c, is_r = sc[3], sc[4], sc[5]
+    put_keys(kp, vp, 0, pas, 0, HALF, HALF)
+    for n, ref in enumerate((y1, y2, y3)):
+        put_keys(kp, vp, (n + 1) * HALF, ref, PASSED, HALF, HALF)
+    put_keys(kp, vp, 4 * HALF, far, 0, HALF, HALF)
+    put_bias(kp, vp, jnp.where((iota((5 * HALF, HD), 0) >> 7) <= c, 0.0, NEG))
+    put_ranges(kr, vr, 0, h1)
+    put_ranges(kr, vr, CHUNK, h2)
     put_bias(kr, vr, range_bias(sc, (2 * CHUNK, HD), ((0, None), (None, 0))))
     row = iota((ROWS, HD), 0)
     lane = iota((ROWS, HD), 1)
     key = core * HALF + lane
+    own = jnp.where(key > row, NEG, 0.0)
+    edge = jnp.where(key <= row, NEG, 0.0)
     first = jnp.where((lane < QUART) & (key > row), NEG, 0.0)
     second = jnp.where((lane < QUART) & (key + QUART > row), NEG, 0.0)
 
     def heads(i):
         at = [WIDE * i + u for u in range(WIDE)]
+        qp = [load_head(q_other, q_own, is_r, a) for a in at]
         q = [load_head(q_own, q_other, is_r, a) for a in at]
-        state = [fold(None, q[u], kr[0:CHUNK, :], vr[0:CHUNK, :], left=first) for u in range(WIDE)]
-        state = [fold(state[u], q[u], kr[CHUNK:, :], vr[CHUNK:, :], left=second) for u in range(WIDE)]
+        sr = [fold(None, q[u], kr[0:CHUNK, :], vr[0:CHUNK, :], left=first) for u in range(WIDE)]
+        sp = [fold(None, qp[u], kp[0:3 * HALF, :], vp[0:3 * HALF, :], left=own) for u in range(WIDE)]
+        sr = [fold(sr[u], q[u], kr[CHUNK:, :], vr[CHUNK:, :], left=second) for u in range(WIDE)]
+        sp = [fold(sp[u], qp[u], kp[3 * HALF:, :], vp[3 * HALF:, :], right=edge) for u in range(WIDE)]
         for u in range(WIDE):
-            m_out[at[u]], l_out[at[u]], o_out[at[u]] = state[u]
+            m_out[at[u]], l_out[at[u]], o_out[at[u]] = sr[u]
+            mp_out[at[u]], lp_out[at[u]], op_out[at[u]] = sp[u]
 
     for i in range(GROUP // WIDE):
         heads(i)
@@ -131,10 +138,10 @@
 
 def middle_kernel(sc, q_own, q_other, x1, x3, y1, y3, m_in, l_in, o_in, m_out, l_out, o_out, kr, vr):
     is_r = sc[5]
-    put_first(kr, vr, 0, x1)
-    put_first(kr, vr, CHUNK, x3)
-    put_second(kr, vr, 2 * CHUNK, y1)
-    put_second(kr, vr, 3 * CHUNK, y3)
+    put_ranges(kr, vr, 0, x1)
+    put_ranges(kr, vr, CHUNK, x3)
+    put_ranges(kr, vr, 2 * CHUNK, y1)
+    put_ranges(kr, vr, 3 * CHUNK, y3)
     put_bias(kr, vr, range_bias(sc, (4 * CHUNK, HD), ((1, None), (3, None), (None, 1), (None, 3))))
 
     def heads(i):
@@ -156,26 +163,18 @@
     return o / l, m * SCALE + jnp.log2(l)
 
 
-def last_kernel(sc, q_own, q_other, x2, y1, y2, y3, pas, far, sink, m_in, l_in, o_in, keep, keep_lse, send,
-                kr, vr, kp, vp, lse_s):
+def last_kernel(sc, q_own, q_other, x2, y2, sink, m_in, l_in, o_in, mp_in, lp_in, op_in, keep, keep_lse, send,
+                kr, vr, ks, vs, lse_s):
     core, c, is_r = sc[3], sc[4], sc[5]
-    put_first(kr, vr, 0, x2)
-    put_second(kr, vr, CHUNK, y2)
+    put_ranges(kr, vr, 0, x2)
+    put_ranges(kr, vr, CHUNK, y2)
     put_bias(kr, vr, range_bias(sc, (2 * CHUNK, HD), ((2, None), (None, 2))))
-    put_keys(kp, vp, 0, pas, 0, HALF, HALF)
-    for n, ref in enumerate((y1, y2, y3)):
-        put_keys(kp, vp, (n + 1) * HALF, ref, PASSED, HALF, HALF)
-    kp[4 * HALF:5 * HALF, :] = jnp.zeros((HALF, 2 * HD), BF16)
-    vp[4 * HALF:5 * HALF, :] = jnp.zeros((HALF, 2 * HD), BF16)
-    put_keys(kp, vp, 4 * HALF, sink, 0, SINK, SINK)
-    put_keys(kp, vp, 5 * HALF, far, 0, HALF, HALF)
-    slot = iota((6 * HALF, HD), 0) >> 7
-    put_bias(kp, vp, jnp.where((slot - (slot >> 2) <= c) | (slot == 4), 0.0, NEG))
+    ks[...] = jnp.zeros((HALF, 2 * HD), BF16)
+    vs[...] = jnp.zeros((HALF, 2 * HD), BF16)
+    put_keys(ks, vs, 0, sink, 0, SINK, SINK)
+    put_bias(ks, vs, jnp.zeros((HALF, HD), F32))
     row = iota((ROWS, HD), 0)
     lane = iota((ROWS, HD), 1)
-    key = core * HALF + lane
-    own = jnp.where(key > row, NEG, 0.0)
-    edge = jnp.where(key <= row, NEG, 0.0)
     seen = (core == 0) & (lane < SINK) & (c * ROWS + row - lane >= RECENT)
     sink_bias = jnp.where(seen, 0.0, NEG)
     lse_s[...] = jnp.zeros((ROWS, HD), F32)
@@ -186,10 +185,10 @@
         qp = [load_head(q_other, q_own, is_r, a) for a in at]
         qr = [load_head(q_own, q_other, is_r, a) for a in at]
         sr = [(m_in[a], l_in[a], o_in[a]) for a in at]
+        sp = [(mp_in[a], lp_in[a], op_in[a]) for a in at]
         sr = [fold(sr[u], qr[u], kr[0:CHUNK, :], vr[0:CHUNK, :]) for u in range(WIDE)]
-        sp = [fold(None, qp[u], kp[0:4 * HALF, :], vp[0:4 * HALF, :], left=own) for u in range(WIDE)]
+        sp = [fold(sp[u], qp[u], ks[...], vs[...], left=sink_bias) for u in range(WIDE)]
         sr = [fold(sr[u], qr[u], kr[CHUNK:, :], vr[CHUNK:, :]) for u in range(WIDE)]
-        sp = [fold(sp[u], qp[u], kp[4 * HALF:, :], vp[4 * HALF:, :], left=sink_bias, right=edge) for u in range(WIDE)]
         for u in range(WIDE):
             cols = slice(at[u] * HD, (at[u] + 1) * HD)
             out_r, lse_r = finish(sr[u])
@@ -230,12 +229,14 @@
     lane = iota((2 * PAGE, HD), 1)
     same_row = (lane & (PAGE - 1)) == (row & (PAGE - 1))
     want = (2 * c + (row >> 4)).astype(F32)
+    codes = [f[8 * PAIR:8 * PAIR + META, :].astype(F32) for f in first]
     for dx in range(4):
         for d in range(4):
             for col in range(2):
-                f, at = first[dx], (d * 2 + col) * FIRST
-                s, on = second[d], (dx * 2 + col) * 2 * QUART
-                code = jnp.concatenate([f[at + 2 * QUART:at + FIRST, :]] * 2, axis=0).astype(F32)
+                n = d * 2 + col
+                f, at = first[dx], n * PAIR
+                s, on = second[d], (dx * 2 + col) * PAIR
+                code = codes[dx][n:n + 1, :]
                 select = jnp.where(same_row & (code == want), 1.0, 0.0).astype(BF16)
                 zz = z if col == 0 else 1 - z
                 block = ((x - dx) & 3) * 8 + zz * 4 + ((y - d) & 3)
@@ -291,38 +292,49 @@
     code = jnp.where(core == 0, code[:8], code[8:]).astype(BF16)
     meta = jnp.broadcast_to(jnp.repeat(code, PAGE)[None, :], (META, HD))
 
-    r1 = jnp.concatenate([ret[:QUART], ret[HALF:HALF + QUART], meta])
+    r1 = jnp.concatenate([ret[:QUART], ret[HALF:HALF + QUART]])
     r2 = jnp.concatenate([ret[QUART:HALF], ret[HALF + QUART:]])
     sink = jnp.concatenate([pas[:SINK], pas[HALF:HALF + SINK]])
-    theirs = lax.ppermute(jnp.concatenate([r1, r2, sink]), "ctx", Z_SWAP)
+    mine = jnp.concatenate([r1, r2, sink, meta])
+    theirs = lax.ppermute(mine, "ctx", Z_SWAP)
     theirs, q_other = lax.optimization_barrier((theirs, q_other))
-    far = lax.ppermute(pas, "ctx", FOUR_ON)
-    r1 = jnp.concatenate([r1, theirs[:FIRST]])
-    r2 = jnp.concatenate([r2, theirs[FIRST:FIRST + HALF]])
-    sink = jnp.where(z == 0, sink, theirs[FIRST + HALF:])
+    far = lax.ppermute(jnp.concatenate([pas, mine[-META:]]), "ctx", FOUR_ON)[:2 * HALF]
+    r1 = jnp.concatenate([r1, theirs[:PAIR]])
+    r2 = jnp.concatenate([r2, theirs[PAIR:2 * PAIR]])
+    sink = jnp.where(z == 0, sink, theirs[2 * PAIR:2 * PAIR + 2 * SINK])
+    line = iota((META, HD), 0)
+    meta = jnp.where((line & 1) == 0, meta, theirs[2 * PAIR + 2 * SINK:])
 
     along_x = jnp.concatenate([r2, sink])
-    ys = {s: lax.ppermute(r1, "ctx", Y_SHIFT[s]) for s in (1, 3)}
-    xs = {s: lax.ppermute(along_x, "ctx", X_SHIFT[s]) for s in (1, 3)}
-    r1_late, x_late, far = lax.optimization_barrier((r1, along_x, far))
-    ys[2] = lax.ppermute(r1_late, "ctx", Y_SHIFT[2])
-    xs[2] = lax.ppermute(x_late, "ctx", X_SHIFT[2])
-    h1 = jnp.concatenate([r1] + [ys[s] for s in (1, 2, 3)])
+    xs = {s: lax.ppermute(along_x, "ctx", X_SHIFT[s]) for s in (1, 3, 2)}
+    ys = {
+        s: lax.ppermute(jnp.concatenate([r1, meta, jnp.where(y + s < 4, pas, far)]), "ctx", Y_SHIFT[s])
+        for s in (1, 3, 2)
+    }
     for s in (1, 2, 3):
-        sink = jnp.where(x == s, xs[s][2 * HALF:], sink)
-    h2 = jnp.concatenate([r2] + [xs[s][:2 * HALF] for s in (1, 2, 3)] + [sink])
-
-    a = {0: h1} | {s: lax.ppermute(h1, "ctx", X_SHIFT[s]) for s in (1, 3, 2)}
-    b = {0: h2} | {
-        s: lax.ppermute(jnp.concatenate([h2, jnp.where(y + s < 4, pas, far)]), "ctx", Y_SHIFT[s]) for s in (1, 3, 2)
-    }
-
+        meta = jnp.where((line >> 1) == s, ys[s][2 * PAIR:2 * PAIR + META], meta)
+        sink = jnp.where(x == s, xs[s][2 * PAIR:], sink)
+    h1 = jnp.concatenate([r1] + [ys[s][:2 * PAIR] for s in (1, 2, 3)] + [meta])
+    h2 = jnp.concatenate([r2] + [xs[s][:2 * PAIR] for s in (1, 2, 3)] + [sink])
+
+    a = {0: h1} | {s: lax.ppermute(h1, "ctx", X_SHIFT[s]) for s in (1, 3)}
+    b = {0: h2} | {s: lax.ppermute(h2, "ctx", Y_SHIFT[s]) for s in (1, 3)}
     state = (jax.ShapeDtypeStruct((GROUP, ROWS, HD), F32),) * 3
     unit = 2 * 2048 * 256 * 512
-    now = call(near_kernel, state, keys(2 * CHUNK), 4 * unit, sc, q, q_other, h1, h2)
-    now = call(middle_kernel, state, keys(4 * CHUNK), 8 * unit, sc, q, q_other, a[1], a[3], b[1], b[3], *now)
+    now = call(
+        near_kernel, state + state, keys(5 * HALF) + keys(2 * CHUNK), 7 * unit,
+        sc, q, q_other, pas, ys[1], ys[2], ys[3], far, h1, h2)
+    h1_late, h2_late, *now = lax.optimization_barrier((h1, h2, *now))
+    now_p, now_r = now[:3], now[3:]
+    a[2] = lax.ppermute(h1_late, "ctx", X_SHIFT[2])
+    b[2] = lax.ppermute(h2_late, "ctx", Y_SHIFT[2])
+    now_r = call(middle_kernel, state, keys(4 * CHUNK), 8 * unit, sc, q, q_other, a[1], a[3], b[1], b[3], *now_r)
     for s in (1, 2, 3):
-        sink = jnp.where(y == s, b[s][8 * HALF:8 * HALF + 2 * SINK], sink)
+        sink = jnp.where(y == s, b[s][8 * PAIR:], sink)
+    pages = call(
+        pages_kernel, jax.ShapeDtypeStruct((32, 2 * PAGE, 2 * HD), BF16), [], unit // 4,
+        sc, *[a[s] for s in range(4)], *[b[s] for s in range(4)])
+    got_pages = lax.ppermute(pages, "tp", CORE_SWAP)
     keep, keep_lse, send = call(
         last_kernel,
         (
@@ -330,15 +342,10 @@
             jax.ShapeDtypeStruct((ROWS, HD), F32),
             jax.ShapeDtypeStruct((ROWS, (GROUP + 1) * HD), BF16),
         ),
-        keys(2 * CHUNK) + keys(6 * HALF) + [pltpu.VMEM((ROWS, HD), F32)],
-        7 * unit, sc, q, q_other, a[2], b[1], b[2], b[3], pas, far, sink, *now)
+        keys(2 * CHUNK) + keys(HALF) + [pltpu.VMEM((ROWS, HD), F32)],
+        5 * unit, sc, q, q_other, a[2], b[2], sink, *now_r, *now_p)
 
     got = lax.ppermute(send, "tp", CORE_SWAP)
-    sc, _ = lax.optimization_barrier((sc, send))
-    pages = call(
-        pages_kernel, jax.ShapeDtypeStruct((32, 2 * PAGE, 2 * HD), BF16), [], unit // 4,
-        sc, *[a[s] for s in range(4)], *[b[s] for s in range(4)])
-    got_pages = lax.ppermute(pages, "tp", CORE_SWAP)
     attn_out = call(
         merge_kernel, jax.ShapeDtypeStruct((ROWS, GROUP * HD), BF16), [], unit // 4, None, keep, keep_lse, got)
     decode_cache = jnp.where(is_r, pages + got_pages, jnp.zeros((), BF16)).reshape(64, PAGE, 2 * HD)

time: 80.9 us -> 69.4 us (0.86)
  waiting for transfers between devices: 14.8 us -> 2.73 us
  starting transfers between devices: 39.2 us -> 36.7 us
  Pallas kernels: 21.1 us -> 22.9 us
    ppermute x14, waiting for transfers between devices: 13.3 us -> 1.6 us  [the longest x1 0.96 us: shards(): theirs = lax.ppermute(mine, 'ctx', Z_SWAP)]
    ppermute x1, starting transfers between devices: 12.4 us -> 7.2 us  [shards(): got_pages = lax.ppermute(pages, 'tp', CORE_SWAP)]
    ppermute x14, starting transfers between devices: 25.9 us -> 28.5 us  [the longest x2 6.17 us: shards(): a = {0: h1} | {s: lax.ppermute(h1, 'ctx', X_SHIFT[s]) for s in (1, 3)}]
    pallas_call x5, Pallas kernels: 21.1 us -> 22.9 us  [call(): pl.pallas_call(kernel, out_shape=out_shape, in_specs=specs, out_specs=(VM...]
    ppermute x1, waiting for transfers between devices: 1.44 us -> 0.01 us  [shards(): got_pages = lax.ppermute(pages, 'tp', CORE_SWAP)]
    ppermute x1, waiting for transfers between devices: 0.01 us -> 1.13 us  [shards(): got = lax.ppermute(send, 'tp', CORE_SWAP)]
  transfers between devices with their start and end apart: 18 -> 18, of which waited for: 5 -> 3; matrix products, arithmetic and copies ran while one was open for 3% -> 4% of each run, Pallas kernels for 13% -> 30%
where the time goes in v4:
time: 69.4 us; the launch traced here: 68.6 us
  starting transfers between devices  36.7 us (53%)
  Pallas kernels  22.9 us (33%)
  local copies, waits for them, and re-layouts  3.16 us (5%)
  waiting for transfers between devices  2.73 us (4%)
  other arithmetic  1.56 us (2%)
  between operations  1.48 us (2%)
    pallas_call x5, Pallas kernels, call(): pl.pallas_call(kernel, out_shape=out_shape, in_specs=specs, out_specs=(VM...  22.9 us
    ppermute x1, starting transfers between devices, shards(): got_pages = lax.ppermute(pages, 'tp', CORE_SWAP)  7.2 us
    ppermute x2, starting transfers between devices, shards(): a = {0: h1} | {s: lax.ppermute(h1, 'ctx', X_SHIFT[s]) for s in (1, 3)}  6.17 us
    ppermute x1, starting transfers between devices, shards(): theirs = lax.ppermute(mine, 'ctx', Z_SWAP)  6.1 us
    ppermute x3, starting transfers between devices, shards(): lax.ppermute(jnp.concatenate([r1, meta, jnp.where(y + s < 4, pas, far)]),...  5.83 us
    ppermute x3, starting transfers between devices, shards(): xs = {s: lax.ppermute(along_x, 'ctx', X_SHIFT[s]) for s in (1, 3, 2)}  4.89 us
    ppermute x1, starting transfers between devices, shards(): a[2] = lax.ppermute(h1_late, 'ctx', X_SHIFT[2])  1.99 us
    ppermute x1, starting transfers between devices, shards(): lax.ppermute(jnp.concatenate([pas, mine[-META:]]), 'ctx', FOUR_ON)  1.94 us
  transfers between devices with their start and end apart: 18, of which 3 were waited for; matrix products, arithmetic and copies ran while one was open for 4% of the time, Pallas kernels for 30%

profile of v4, /device:TPU:33, one launch (start us, length us, event | category | flops | bytes accessed | tf_op | source)
XLA Modules:
  0.0 68.6 jit_solution(1273540947139819262)
XLA Ops:
  0.6 0.8 %fusion.16 = (bf16[128,128]{1,0:T(8,128)(2,1)S(1)}, bf16[128,128]{1,0:T(8,128)(2,1)S(1)}, bf16[128,128]{1,0:T(8,128)(2,1)S(1)}, bf16[128,128]{1,0:T(8,128)(2,1)S(1)}) fusion(bf16[256,128]{1,0:T(8,128)(2,1)} %param.6, bf16[256,128]{1,0:T(8,128)(2,1)} %param.7), kind=kLoop, calls=%fused_computation.71 | loop fusion | bytes 262144 | tf_op jit(solution)/shard_map/slice | solution.py:281
  1.5 0.8 %collective-permute-start = (bf16[256,128]{1,0:T(8,128)(2,1)S(1)}, bf16[256,128]{1,0:T(8,128)(2,1)S(1)}, u32[]{:S(2)}, u32[]{:S(2)}) collective-permute-start(bf16[256,128]{1,0:T(8,128)(2,1)S(1)} %broadcast_select_fusion), channel_id=1, source_target_pairs={{0,1},{1,0},{2,3},{3,2},{4,5},{5,4},{6,7},{7,6},{8,9},{9,8},{10,11... | collective-permute-start | bytes 196616 | tf_op jit(solution)/shard_map/ppermute | solution.py:284
  2.3 0.1 collective-permute-start.2
  2.4 0.6 copy-done.1
  3.0 0.2 convert_reduce_fusion
  3.5 0.7 copy-done.2
  4.1 0.6 dynamic_slice.4
  5.5 6.1 %collective-permute-start.1 = (bf16[400,128]{1,0:T(8,128)(2,1)S(1)}, bf16[400,128]{1,0:T(8,128)(2,1)S(1)}, u32[]{:S(2)}, u32[]{:S(2)}) collective-permute-start(bf16[400,128]{1,0:T(8,128)(2,1)S(1)} %constant_dynamic-update-slice_fusion), channel_id=1, source_target_pairs={{0,32},{8,40},{16,48},{24,56},{32,0},{40,8},{48,16},{56,24},{64,96... | collective-permute-start | bytes 307208 | tf_op jit(solution)/shard_map/ppermute | solution.py:299
  11.7 1.9 %collective-permute-start.3 = (bf16[272,128]{1,0:T(8,128)(2,1)S(1)}, bf16[272,128]{1,0:T(8,128)(2,1)S(1)}, u32[]{:S(2)}, u32[]{:S(2)}) collective-permute-start(bf16[272,128]{1,0:T(8,128)(2,1)S(1)} %pad_maximum_fusion.1), channel_id=1, source_target_pairs={{0,32},{8,40},{16,48},{24,56},{32,64},{40,72},{48,80},{56,88},{64,... | collective-permute-start | bytes 208904 | tf_op jit(solution)/shard_map/ppermute | solution.py:301
  13.6 1.0 %collective-permute-done.1 = bf16[400,128]{1,0:T(8,128)(2,1)S(1)} collective-permute-done((bf16[400,128]{1,0:T(8,128)(2,1)S(1)}, bf16[400,128]{1,0:T(8,128)(2,1)S(1)}, u32[]{:S(2)}, u32[]{:S(2)}) %collective-permute-start.1) | collective-permute-done | bytes 102432 | tf_op jit(solution)/shard_map/ppermute | solution.py:299
  14.6 1.3 %collective-permute-start.7 = (bf16[384,128]{1,0:T(8,128)(2,1)S(1)}, bf16[384,128]{1,0:T(8,128)(2,1)S(1)}, u32[]{:S(2)}, u32[]{:S(2)}) collective-permute-start(bf16[384,128]{1,0:T(8,128)(2,1)S(1)} %pad_maximum_fusion), channel_id=1, source_target_pairs={{0,64},{8,72},{16,80},{24,88},{32,96},{40,104},{48,112},{56,120},{... | collective-permute-start | bytes 294920 | tf_op jit(solution)/shard_map/ppermute | solution.py:309
  15.9 2.5 %collective-permute-start.8 = (bf16[384,128]{1,0:T(8,128)(2,1)S(1)}, bf16[384,128]{1,0:T(8,128)(2,1)S(1)}, u32[]{:S(2)}, u32[]{:S(2)}) collective-permute-start(bf16[384,128]{1,0:T(8,128)(2,1)S(1)} %pad_maximum_fusion), channel_id=1, source_target_pairs={{0,128},{8,136},{16,144},{24,152},{32,160},{40,168},{48,176},{56,1... | collective-permute-start | bytes 294920 | tf_op jit(solution)/shard_map/ppermute | solution.py:309
  18.4 1.2 %collective-permute-start.9 = (bf16[384,128]{1,0:T(8,128)(2,1)S(1)}, bf16[384,128]{1,0:T(8,128)(2,1)S(1)}, u32[]{:S(2)}, u32[]{:S(2)}) collective-permute-start(bf16[384,128]{1,0:T(8,128)(2,1)S(1)} %pad_maximum_fusion), channel_id=1, source_target_pairs={{0,192},{8,200},{16,208},{24,216},{32,224},{40,232},{48,240},{56,2... | collective-permute-start | bytes 294920 | tf_op jit(solution)/shard_map/ppermute | solution.py:309
  19.7 3.0 %collective-permute-start.5 = (bf16[528,128]{1,0:T(8,128)(2,1)S(1)}, bf16[528,128]{1,0:T(8,128)(2,1)S(1)}, u32[]{:S(2)}, u32[]{:S(2)}) collective-permute-start(bf16[528,128]{1,0:T(8,128)(2,1)S(1)} %constant_dynamic-update-slice_fusion.12), channel_id=1, source_target_pairs={{0,16},{8,24},{16,0},{24,8},{32,48},{40,56},{48,32},{56,40},{64,80... | collective-permute-start | bytes 405512 | tf_op jit(solution)/shard_map/ppermute | solution.py:311
  22.7 0.5 collective-permute-start.4
  23.2 2.4 %collective-permute-start.6 = (bf16[528,128]{1,0:T(8,128)(2,1)S(1)}, bf16[528,128]{1,0:T(8,128)(2,1)S(1)}, u32[]{:S(2)}, u32[]{:S(2)}) collective-permute-start(bf16[528,128]{1,0:T(8,128)(2,1)S(1)} %constant_dynamic-update-slice_fusion.17), channel_id=1, source_target_pairs={{0,24},{8,0},{16,8},{24,16},{32,56},{40,32},{48,40},{56,48},{64,88... | collective-permute-start | bytes 405512 | tf_op jit(solution)/shard_map/ppermute | solution.py:311
  25.7 0.1 collective-permute-start.12
  25.8 1.4 %collective-permute-start.13 = (bf16[1152,128]{1,0:T(8,128)(2,1)S(1)}, bf16[1152,128]{1,0:T(8,128)(2,1)S(1)}, u32[]{:S(2)}, u32[]{:S(2)}) collective-permute-start(bf16[1152,128]{1,0:T(8,128)(2,1)S(1)} %get-tuple-element.33.h2.b0), channel_id=1, source_target_pairs={{0,8},{8,16},{16,24},{24,0},{32,40},{40,48},{48,56},{56,32},{64,72... | collective-permute-start | bytes 884744 | tf_op jit(solution)/shard_map/ppermute | solution.py:321
  27.2 0.6 collective-permute-done.4.y1
  28.0 4.8 %collective-permute-start.14 = (bf16[1040,128]{1,0:T(8,128)(2,1)S(1)}, bf16[1040,128]{1,0:T(8,128)(2,1)S(1)}, u32[]{:S(2)}, u32[]{:S(2)}) collective-permute-start(bf16[1040,128]{1,0:T(8,128)(2,1)S(1)} %constant_dynamic-update-slice_fusion.22.h1.a0), channel_id=1, source_target_pairs={{0,64},{8,72},{16,80},{24,88},{32,96},{40,104},{48,112},{56,120},{... | collective-permute-start | bytes 798728 | tf_op jit(solution)/shard_map/ppermute | solution.py:320
  32.9 1.3 %collective-permute-start.15 = (bf16[1040,128]{1,0:T(8,128)(2,1)S(1)}, bf16[1040,128]{1,0:T(8,128)(2,1)S(1)}, u32[]{:S(2)}, u32[]{:S(2)}) collective-permute-start(bf16[1040,128]{1,0:T(8,128)(2,1)S(1)} %constant_dynamic-update-slice_fusion.22.h1.a0), channel_id=1, source_target_pairs={{0,192},{8,200},{16,208},{24,216},{32,224},{40,232},{48,240},{56,2... | collective-permute-start | bytes 798728 | tf_op jit(solution)/shard_map/ppermute | solution.py:320
  34.2 6.8 %shard_map.68 = (f32[8,256,128]{2,1,0:T(8,128)S(1)}, f32[8,256,128]{2,1,0:T(8,128)S(1)}, f32[8,256,128]{2,1,0:T(8,128)S(1)}, f32[8,256,128]{2,1,0:T(8,128)S(1)},...) custom-call(s32[8]{0:T(128)S(1)} %stack.33.sc, bf16[256,1024]{1,0:T(8,128)(2,1)S(1)} %copy-done, ...), custom_call_target="tpu_custom_call" | custom-call | flops 3758096384 | bytes 4194304 | tf_op jit(solution)/shard_map/pallas_call | solution.py:258
  41.0 0.1 collective-permute-start.11
  41.1 2.0 %collective-permute-start.10 = (bf16[1040,128]{1,0:T(8,128)(2,1)S(1)}, bf16[1040,128]{1,0:T(8,128)(2,1)S(1)}, u32[]{:S(2)}, u32[]{:S(2)}) collective-permute-start(bf16[1040,128]{1,0:T(8,128)(2,1)S(1)} %constant_dynamic-update-slice_fusion.22.h1.a0), channel_id=1, source_target_pairs={{0,128},{8,136},{16,144},{24,152},{32,160},{40,168},{48,176},{56,1... | collective-permute-start | bytes 798728 | tf_op jit(solution)/shard_map/ppermute | solution.py:329
  43.1 7.2 %shard_map.69 = (f32[8,256,128]{2,1,0:T(8,128)S(1)}, f32[8,256,128]{2,1,0:T(8,128)S(1)}, f32[8,256,128]{2,1,0:T(8,128)S(1)}) custom-call(s32[8]{0:T(128)S(1)} %stack.33.sc, bf16[256,1024]{1,0:T(8,128)(2,1)S(1)} %copy-done, bf16[256,1024]{1,0:T(8,128)(2,1)S(1)} %collective-permute-done.2.q_other, bf16[1040,128]{1,0:T(8,128)(2,1)S(1)} %collective-permute-done.14.x1.a1, ...), custom_call_target="tpu_custom_call" | custom-call | flops 4294967296 | bytes 4194304 | tf_op jit(solution)/shard_map/pallas_call | solution.py:258
  50.3 1.2 %shard_map.72 = bf16[32,32,256]{2,1,0:T(8,128)(2,1)S(1)} custom-call(s32[8]{0:T(128)S(1)} %stack.33.sc, bf16[1040,128]{1,0:T(8,128)(2,1)S(1)} %constant_dynamic-update-slice_fusion.22.h1.a0, bf16[1040,128]{1,0:T(8,128)(2,1)S(1)} %collective-permute-done.14.x1.a1, bf16[1040,128]{1,0:T(8,128)(2,1)S(1)} %collective-permute-done.10.x2.a2, ...), custom_call_target="tpu_custom_call" | custom-call | flops 134217728 | bytes 4194304 | tf_op jit(solution)/shard_map/pallas_call | solution.py:258
  51.5 7.2 %collective-permute-start.17 = (bf16[32,32,256]{2,1,0:T(8,128)(2,1)S(1)}, bf16[32,32,256]{2,1,0:T(8,128)(2,1)S(1)}, u32[]{:S(2)}, u32[]{:S(2)}) collective-permute-start(bf16[32,32,256]{2,1,0:T(8,128)(2,1)S(1)} %shard_map.72), channel_id=1, source_target_pairs={{0,1},{1,0},{2,3},{3,2},{4,5},{5,4},{6,7},{7,6},{8,9},{9,8},{10,11... | collective-permute-start | bytes 1572872 | tf_op jit(solution)/shard_map/ppermute | solution.py:337
  58.8 6.5 %shard_map.70 = (bf16[256,1024]{1,0:T(8,128)(2,1)S(1)}, f32[256,128]{1,0:T(8,128)S(1)}, bf16[256,1152]{1,0:T(8,128)(2,1)S(1)}) custom-call(s32[8]{0:T(128)S(1)} %stack.33.sc, bf16[256,1024]{1,0:T(8,128)(2,1)S(1)} %copy-done, bf16[256,1024]{1,0:T(8,128)(2,1)S(1)} %collective-permute-done.2.q_other, bf16[1040,128]{1,0:T(8,128)(2,1)S(1)} %collective-permute-done.10.x2.a2, ...), custom_call_target="tpu_custom_call" | custom-call | flops 2684354560 | bytes 4194304 | tf_op jit(solution)/shard_map/pallas_call | solution.py:258
  65.2 0.1 collective-permute-start.16
  65.3 0.8 %add_select_fusion = bf16[32,32,256]{2,1,0:T(8,128)(2,1)} fusion(bf16[32,32,256]{2,1,0:T(8,128)(2,1)S(1)} %shard_map.72, bf16[32,32,256]{2,1,0:T(8,128)(2,1)S(1)} %collective-permute-done.17, pred[]{:T(512)} %bitcast.6), kind=kLoop, calls=%fused_computation | loop fusion | flops 524288 | bytes 1572865 | tf_op jit(solution)/shard_map/jit(_where)/select_n | solution.py:351
  66.2 1.1 %collective-permute-done.16.got = bf16[256,1152]{1,0:T(8,128)(2,1)S(1)} collective-permute-done((bf16[256,1152]{1,0:T(8,128)(2,1)S(1)}, bf16[256,1152]{1,0:T(8,128)(2,1)S(1)}, u32[]{:S(2)}, u32[]{:S(2)}) %collective-permute-start.16) | collective-permute-done | bytes 589856 | tf_op jit(solution)/shard_map/ppermute | solution.py:348
  67.3 1.3 %shard_map.71 = bf16[256,1024]{1,0:T(8,128)(2,1)} custom-call(bf16[256,1024]{1,0:T(8,128)(2,1)S(1)} %get-tuple-element.43.keep, f32[256,128]{1,0:T(8,128)S(1)} %get-tuple-element.44.keep_lse, bf16[256,1152]{1,0:T(8,128)(2,1)S(1)} %collective-permute-done.16.got), custom_call_target="tpu_custom_call" | custom-call | flops 134217728 | bytes 4194304 | tf_op jit(solution)/shard_map/pallas_call | solution.py:258
  (55 shorter events, 1.0 us)
Async XLA Ops:
  1.5 3.9 %collective-permute-start = (bf16[256,128]{1,0:T(8,128)(2,1)S(1)}, bf16[256,128]{1,0:T(8,128)(2,1)S(1)}, u32[]{:S(2)}, u32[]{:S(2)}) collective-permute-start(bf16[256,128]{1,0:T(8,128)(2,1)S(1)} %broadcast_select_fusion), channel_id=1, source_target_pairs={{0,1},{1,0},{2,3},{3,2},{4,5},{5,4},{6,7},{7,6},{8,9},{9,8},{10,11... | collective-permute-start | bytes 196616 | tf_op jit(solution)/shard_map/ppermute | solution.py:284
  2.3 12.3 %collective-permute-start.2 = (bf16[256,1024]{1,0:T(8,128)(2,1)}, bf16[256,1024]{1,0:T(8,128)(2,1)S(1)}, u32[]{:S(2)}, u32[]{:S(2)}) collective-permute-start(bf16[256,1024]{1,0:T(8,128)(2,1)} %q_own.5), channel_id=1, source_target_pairs={{0,1},{1,0},{2,3},{3,2},{4,5},{5,4},{6,7},{7,6},{8,9},{9,8},{10,11... | collective-permute-start | bytes 1572872 | tf_op jit(solution)/shard_map/ppermute | solution.py:285
  2.4 0.7 copy-start.1
  3.5 0.7 copy-start.2
  5.5 9.0 %collective-permute-start.1 = (bf16[400,128]{1,0:T(8,128)(2,1)S(1)}, bf16[400,128]{1,0:T(8,128)(2,1)S(1)}, u32[]{:S(2)}, u32[]{:S(2)}) collective-permute-start(bf16[400,128]{1,0:T(8,128)(2,1)S(1)} %constant_dynamic-update-slice_fusion), channel_id=1, source_target_pairs={{0,32},{8,40},{16,48},{24,56},{32,0},{40,8},{48,16},{56,24},{64,96... | collective-permute-start | bytes 307208 | tf_op jit(solution)/shard_map/ppermute | solution.py:299
  11.7 8.0 %collective-permute-start.3 = (bf16[272,128]{1,0:T(8,128)(2,1)S(1)}, bf16[272,128]{1,0:T(8,128)(2,1)S(1)}, u32[]{:S(2)}, u32[]{:S(2)}) collective-permute-start(bf16[272,128]{1,0:T(8,128)(2,1)S(1)} %pad_maximum_fusion.1), channel_id=1, source_target_pairs={{0,32},{8,40},{16,48},{24,56},{32,64},{40,72},{48,80},{56,88},{64,... | collective-permute-start | bytes 208904 | tf_op jit(solution)/shard_map/ppermute | solution.py:301
  14.6 8.6 %collective-permute-start.7 = (bf16[384,128]{1,0:T(8,128)(2,1)S(1)}, bf16[384,128]{1,0:T(8,128)(2,1)S(1)}, u32[]{:S(2)}, u32[]{:S(2)}) collective-permute-start(bf16[384,128]{1,0:T(8,128)(2,1)S(1)} %pad_maximum_fusion), channel_id=1, source_target_pairs={{0,64},{8,72},{16,80},{24,88},{32,96},{40,104},{48,112},{56,120},{... | collective-permute-start | bytes 294920 | tf_op jit(solution)/shard_map/ppermute | solution.py:309
  15.9 9.7 %collective-permute-start.8 = (bf16[384,128]{1,0:T(8,128)(2,1)S(1)}, bf16[384,128]{1,0:T(8,128)(2,1)S(1)}, u32[]{:S(2)}, u32[]{:S(2)}) collective-permute-start(bf16[384,128]{1,0:T(8,128)(2,1)S(1)} %pad_maximum_fusion), channel_id=1, source_target_pairs={{0,128},{8,136},{16,144},{24,152},{32,160},{40,168},{48,176},{56,1... | collective-permute-start | bytes 294920 | tf_op jit(solution)/shard_map/ppermute | solution.py:309
  18.4 7.3 %collective-permute-start.9 = (bf16[384,128]{1,0:T(8,128)(2,1)S(1)}, bf16[384,128]{1,0:T(8,128)(2,1)S(1)}, u32[]{:S(2)}, u32[]{:S(2)}) collective-permute-start(bf16[384,128]{1,0:T(8,128)(2,1)S(1)} %pad_maximum_fusion), channel_id=1, source_target_pairs={{0,192},{8,200},{16,208},{24,216},{32,224},{40,232},{48,240},{56,2... | collective-permute-start | bytes 294920 | tf_op jit(solution)/shard_map/ppermute | solution.py:309
  19.7 8.2 %collective-permute-start.5 = (bf16[528,128]{1,0:T(8,128)(2,1)S(1)}, bf16[528,128]{1,0:T(8,128)(2,1)S(1)}, u32[]{:S(2)}, u32[]{:S(2)}) collective-permute-start(bf16[528,128]{1,0:T(8,128)(2,1)S(1)} %constant_dynamic-update-slice_fusion.12), channel_id=1, source_target_pairs={{0,16},{8,24},{16,0},{24,8},{32,48},{40,56},{48,32},{56,40},{64,80... | collective-permute-start | bytes 405512 | tf_op jit(solution)/shard_map/ppermute | solution.py:311
  22.7 5.1 %collective-permute-start.4 = (bf16[528,128]{1,0:T(8,128)(2,1)S(1)}, bf16[528,128]{1,0:T(8,128)(2,1)S(1)}, u32[]{:S(2)}, u32[]{:S(2)}) collective-permute-start(bf16[528,128]{1,0:T(8,128)(2,1)S(1)} %get-tuple-element.56), channel_id=1, source_target_pairs={{0,8},{8,16},{16,24},{24,0},{32,40},{40,48},{48,56},{56,32},{64,72... | collective-permute-start | bytes 405512 | tf_op jit(solution)/shard_map/ppermute | solution.py:311
  23.2 11.0 %copy-start = (bf16[256,1024]{1,0:T(8,128)(2,1)S(1)}, bf16[256,1024]{1,0:T(8,128)(2,1)}, u32[]{:S(2)}) copy-start(bf16[256,1024]{1,0:T(8,128)(2,1)} %q_own.5) | copy-start | bytes 1572868
  23.2 4.7 %collective-permute-start.6 = (bf16[528,128]{1,0:T(8,128)(2,1)S(1)}, bf16[528,128]{1,0:T(8,128)(2,1)S(1)}, u32[]{:S(2)}, u32[]{:S(2)}) collective-permute-start(bf16[528,128]{1,0:T(8,128)(2,1)S(1)} %constant_dynamic-update-slice_fusion.17), channel_id=1, source_target_pairs={{0,24},{8,0},{16,8},{24,16},{32,56},{40,32},{48,40},{56,48},{64,88... | collective-permute-start | bytes 405512 | tf_op jit(solution)/shard_map/ppermute | solution.py:311
  25.7 15.4 %collective-permute-start.12 = (bf16[1152,128]{1,0:T(8,128)(2,1)S(1)}, bf16[1152,128]{1,0:T(8,128)(2,1)S(1)}, u32[]{:S(2)}, u32[]{:S(2)}) collective-permute-start(bf16[1152,128]{1,0:T(8,128)(2,1)S(1)} %get-tuple-element.33.h2.b0), channel_id=1, source_target_pairs={{0,24},{8,0},{16,8},{24,16},{32,56},{40,32},{48,40},{56,48},{64,88... | collective-permute-start | bytes 884744 | tf_op jit(solution)/shard_map/ppermute | solution.py:321
  25.8 17.3 %collective-permute-start.13 = (bf16[1152,128]{1,0:T(8,128)(2,1)S(1)}, bf16[1152,128]{1,0:T(8,128)(2,1)S(1)}, u32[]{:S(2)}, u32[]{:S(2)}) collective-permute-start(bf16[1152,128]{1,0:T(8,128)(2,1)S(1)} %get-tuple-element.33.h2.b0), channel_id=1, source_target_pairs={{0,8},{8,16},{16,24},{24,0},{32,40},{40,48},{48,56},{56,32},{64,72... | collective-permute-start | bytes 884744 | tf_op jit(solution)/shard_map/ppermute | solution.py:321
  28.0 15.1 %collective-permute-start.14 = (bf16[1040,128]{1,0:T(8,128)(2,1)S(1)}, bf16[1040,128]{1,0:T(8,128)(2,1)S(1)}, u32[]{:S(2)}, u32[]{:S(2)}) collective-permute-start(bf16[1040,128]{1,0:T(8,128)(2,1)S(1)} %constant_dynamic-update-slice_fusion.22.h1.a0), channel_id=1, source_target_pairs={{0,64},{8,72},{16,80},{24,88},{32,96},{40,104},{48,112},{56,120},{... | collective-permute-start | bytes 798728 | tf_op jit(solution)/shard_map/ppermute | solution.py:320
  32.9 10.2 %collective-permute-start.15 = (bf16[1040,128]{1,0:T(8,128)(2,1)S(1)}, bf16[1040,128]{1,0:T(8,128)(2,1)S(1)}, u32[]{:S(2)}, u32[]{:S(2)}) collective-permute-start(bf16[1040,128]{1,0:T(8,128)(2,1)S(1)} %constant_dynamic-update-slice_fusion.22.h1.a0), channel_id=1, source_target_pairs={{0,192},{8,200},{16,208},{24,216},{32,224},{40,232},{48,240},{56,2... | collective-permute-start | bytes 798728 | tf_op jit(solution)/shard_map/ppermute | solution.py:320
  41.0 9.3 %collective-permute-start.11 = (bf16[1152,128]{1,0:T(8,128)(2,1)S(1)}, bf16[1152,128]{1,0:T(8,128)(2,1)S(1)}, u32[]{:S(2)}, u32[]{:S(2)}) collective-permute-start(bf16[1152,128]{1,0:T(8,128)(2,1)S(1)} %get-tuple-element.33.h2.b0), channel_id=1, source_target_pairs={{0,16},{8,24},{16,0},{24,8},{32,48},{40,56},{48,32},{56,40},{64,80... | collective-permute-start | bytes 884744 | tf_op jit(solution)/shard_map/ppermute | solution.py:330
  41.1 9.2 %collective-permute-start.10 = (bf16[1040,128]{1,0:T(8,128)(2,1)S(1)}, bf16[1040,128]{1,0:T(8,128)(2,1)S(1)}, u32[]{:S(2)}, u32[]{:S(2)}) collective-permute-start(bf16[1040,128]{1,0:T(8,128)(2,1)S(1)} %constant_dynamic-update-slice_fusion.22.h1.a0), channel_id=1, source_target_pairs={{0,128},{8,136},{16,144},{24,152},{32,160},{40,168},{48,176},{56,1... | collective-permute-start | bytes 798728 | tf_op jit(solution)/shard_map/ppermute | solution.py:329
  51.5 13.8 %collective-permute-start.17 = (bf16[32,32,256]{2,1,0:T(8,128)(2,1)S(1)}, bf16[32,32,256]{2,1,0:T(8,128)(2,1)S(1)}, u32[]{:S(2)}, u32[]{:S(2)}) collective-permute-start(bf16[32,32,256]{2,1,0:T(8,128)(2,1)S(1)} %shard_map.72), channel_id=1, source_target_pairs={{0,1},{1,0},{2,3},{3,2},{4,5},{5,4},{6,7},{7,6},{8,9},{9,8},{10,11... | collective-permute-start | bytes 1572872 | tf_op jit(solution)/shard_map/ppermute | solution.py:337
  65.2 2.1 %collective-permute-start.16 = (bf16[256,1152]{1,0:T(8,128)(2,1)S(1)}, bf16[256,1152]{1,0:T(8,128)(2,1)S(1)}, u32[]{:S(2)}, u32[]{:S(2)}) collective-permute-start(bf16[256,1152]{1,0:T(8,128)(2,1)S(1)} %get-tuple-element.45), channel_id=1, source_target_pairs={{0,1},{1,0},{2,3},{3,2},{4,5},{5,4},{6,7},{7,6},{8,9},{9,8},{10,11... | collective-permute-start | bytes 1769480 | tf_op jit(solution)/shard_map/ppermute | solution.py:348

commit v5 on v4

--- a/solution.py
+++ b/solution.py
@@ -14,12 +14,9 @@
 PAGE = 16
 ROWS = 256
 HALF = 128
-QUART = 64
 META = 16
-PAIR = 2 * QUART
 CHUNK = 512
 WIDE = 2
-PASSED = 2 * PAIR + META
 NEG = -1e30
 SCALE = math.log2(math.e) / math.sqrt(HD)
 F32 = jnp.float32
@@ -34,8 +31,20 @@
 CORE_SWAP = [(i, i ^ 1) for i in range(8)]
 Z_SWAP = [(ctx_of(x, z, y), ctx_of(x, z + 1, y)) for x, z, y in CHIPS]
 FOUR_ON = [(i, i + 4) for i in range(28)]
-X_SHIFT = {s: [(ctx_of(x, z, y), ctx_of(x + s, z, y)) for x, z, y in CHIPS] for s in (1, 2, 3)}
 Y_SHIFT = {s: [(ctx_of(x, z, y), ctx_of(x, z, y + s)) for x, z, y in CHIPS] for s in (1, 2, 3)}
+
+
+def two_ways(s, along_y):
+    pairs = []
+    for x, z, y in CHIPS:
+        for tp in range(8):
+            there = ctx_of(x, z, y + s) if tp % 2 == along_y else ctx_of(x + s, z, y)
+            pairs.append((ctx_of(x, z, y) * 8 + tp, there * 8 + tp))
+    return pairs
+
+
+STAGE_1 = {s: two_ways(s, 0) for s in (1, 2, 3)}
+STAGE_2 = {s: two_ways(s, 1) for s in (1, 2, 3)}
 
 
 def nt_dot(a, b):
@@ -69,7 +78,7 @@
 
 def put_ranges(k_s, v_s, at, ref):
     for n in range(8):
-        put_keys(k_s, v_s, at + n * QUART, ref, n * PAIR, QUART, QUART)
+        put_keys(k_s, v_s, at + n * HALF, ref, n * ROWS, HALF, HALF)
 
 
 def put_bias(k_s, v_s, bias):
@@ -78,20 +87,20 @@
     v_s[:, HD:] = jnp.ones(bias.shape, BF16)
 
 
-def range_bias(sc, shape, chunks):
-    x, y, z, c = sc[0], sc[1], sc[2], sc[4]
-    n = iota(shape, 0)
-    outer, far = (n >> 7) & 3, (n >> 6) & 1
-    which = n >> 9
-    dx, dy = outer, outer
-    for i, (fixed_x, fixed_y) in enumerate(chunks):
-        if fixed_x is not None:
-            dx = jnp.where(which == i, fixed_x, dx)
-        else:
-            dy = jnp.where(which == i, fixed_y, dy)
+def range_of(sc, inner, outer, far):
+    x, y, z, core = sc[0], sc[1], sc[2], sc[3]
+    dx = jnp.where(core == 0, outer, inner)
+    dy = jnp.where(core == 0, inner, outer)
     zz = jnp.where(far == 0, z, 1 - z)
-    block = ((x - dx) & 3) * 8 + zz * 4 + ((y - dy) & 3)
-    return jnp.where(block <= c, 0.0, NEG)
+    return ((x - dx) & 3) * 8 + zz * 4 + ((y - dy) & 3)
+
+
+def range_bias(sc, outers):
+    n = iota((len(outers) * 8 * HALF, HD), 0)
+    outer = jnp.full(n.shape, outers[0], jnp.int32)
+    for i, distance in enumerate(outers[1:], 1):
+        outer = jnp.where(n >> 10 == i, distance, outer)
+    return jnp.where(range_of(sc, (n >> 8) & 3, outer, (n >> 7) & 1) <= sc[4], 0.0, NEG)
 
 
 def load_head(q_a, q_b, flag, a):
@@ -101,48 +110,51 @@
     return jnp.concatenate([q, one], axis=1)
 
 
-def near_kernel(sc, q_own, q_other, pas, y1, y2, y3, far, h1, h2, mp_out, lp_out, op_out, m_out, l_out, o_out,
-                kp, vp, kr, vr):
+def near_kernel(sc, q_own, q_other, here, m_out, l_out, o_out, kr, vr):
+    core, is_r = sc[3], sc[5]
+    put_ranges(kr, vr, 0, here)
+    put_bias(kr, vr, range_bias(sc, (0,)))
+    own = jnp.where(core * HALF + iota((ROWS, HD), 1) > iota((ROWS, HD), 0), NEG, 0.0)
+
+    def heads(i):
+        at = [WIDE * i + u for u in range(WIDE)]
+        q = [load_head(q_own, q_other, is_r, a) for a in at]
+        state = [fold(None, q[u], kr[0:CHUNK, :], vr[0:CHUNK, :], left=own) for u in range(WIDE)]
+        state = [fold(state[u], q[u], kr[CHUNK:, :], vr[CHUNK:, :]) for u in range(WIDE)]
+        for u in range(WIDE):
+            m_out[at[u]], l_out[at[u]], o_out[at[u]] = state[u]
+
+    for i in range(GROUP // WIDE):
+        heads(i)
+
+
+def passing_kernel(sc, q_own, q_other, pas, p1, p2, p3, far, m_out, l_out, o_out, kp, vp):
     core, c, is_r = sc[3], sc[4], sc[5]
-    put_keys(kp, vp, 0, pas, 0, HALF, HALF)
-    for n, ref in enumerate((y1, y2, y3)):
-        put_keys(kp, vp, (n + 1) * HALF, ref, PASSED, HALF, HALF)
-    put_keys(kp, vp, 4 * HALF, far, 0, HALF, HALF)
+    for n, ref in enumerate((pas, p1, p2, p3, far)):
+        put_keys(kp, vp, n * HALF, ref, 0, HALF, HALF)
     put_bias(kp, vp, jnp.where((iota((5 * HALF, HD), 0) >> 7) <= c, 0.0, NEG))
-    put_ranges(kr, vr, 0, h1)
-    put_ranges(kr, vr, CHUNK, h2)
-    put_bias(kr, vr, range_bias(sc, (2 * CHUNK, HD), ((0, None), (None, 0))))
     row = iota((ROWS, HD), 0)
-    lane = iota((ROWS, HD), 1)
-    key = core * HALF + lane
+    key = core * HALF + iota((ROWS, HD), 1)
     own = jnp.where(key > row, NEG, 0.0)
     edge = jnp.where(key <= row, NEG, 0.0)
-    first = jnp.where((lane < QUART) & (key > row), NEG, 0.0)
-    second = jnp.where((lane < QUART) & (key + QUART > row), NEG, 0.0)
 
     def heads(i):
         at = [WIDE * i + u for u in range(WIDE)]
-        qp = [load_head(q_other, q_own, is_r, a) for a in at]
-        q = [load_head(q_own, q_other, is_r, a) for a in at]
-        sr = [fold(None, q[u], kr[0:CHUNK, :], vr[0:CHUNK, :], left=first) for u in range(WIDE)]
-        sp = [fold(None, qp[u], kp[0:3 * HALF, :], vp[0:3 * HALF, :], left=own) for u in range(WIDE)]
-        sr = [fold(sr[u], q[u], kr[CHUNK:, :], vr[CHUNK:, :], left=second) for u in range(WIDE)]
-        sp = [fold(sp[u], qp[u], kp[3 * HALF:, :], vp[3 * HALF:, :], right=edge) for u in range(WIDE)]
+        q = [load_head(q_other, q_own, is_r, a) for a in at]
+        state = [fold(None, q[u], kp[0:3 * HALF, :], vp[0:3 * HALF, :], left=own) for u in range(WIDE)]
+        state = [fold(state[u], q[u], kp[3 * HALF:, :], vp[3 * HALF:, :], right=edge) for u in range(WIDE)]
         for u in range(WIDE):
-            m_out[at[u]], l_out[at[u]], o_out[at[u]] = sr[u]
-            mp_out[at[u]], lp_out[at[u]], op_out[at[u]] = sp[u]
+            m_out[at[u]], l_out[at[u]], o_out[at[u]] = state[u]
 
     for i in range(GROUP // WIDE):
         heads(i)
 
 
-def middle_kernel(sc, q_own, q_other, x1, x3, y1, y3, m_in, l_in, o_in, m_out, l_out, o_out, kr, vr):
+def middle_kernel(sc, q_own, q_other, r1, r3, m_in, l_in, o_in, m_out, l_out, o_out, kr, vr):
     is_r = sc[5]
-    put_ranges(kr, vr, 0, x1)
-    put_ranges(kr, vr, CHUNK, x3)
-    put_ranges(kr, vr, 2 * CHUNK, y1)
-    put_ranges(kr, vr, 3 * CHUNK, y3)
-    put_bias(kr, vr, range_bias(sc, (4 * CHUNK, HD), ((1, None), (3, None), (None, 1), (None, 3))))
+    put_ranges(kr, vr, 0, r1)
+    put_ranges(kr, vr, 8 * HALF, r3)
+    put_bias(kr, vr, range_bias(sc, (1, 3)))
 
     def heads(i):
         at = [WIDE * i + u for u in range(WIDE)]
@@ -163,12 +175,11 @@
     return o / l, m * SCALE + jnp.log2(l)
 
 
-def last_kernel(sc, q_own, q_other, x2, y2, sink, m_in, l_in, o_in, mp_in, lp_in, op_in, keep, keep_lse, send,
+def last_kernel(sc, q_own, q_other, r2, sink, m_in, l_in, o_in, mp_in, lp_in, op_in, keep, keep_lse, send,
                 kr, vr, ks, vs, lse_s):
     core, c, is_r = sc[3], sc[4], sc[5]
-    put_ranges(kr, vr, 0, x2)
-    put_ranges(kr, vr, CHUNK, y2)
-    put_bias(kr, vr, range_bias(sc, (2 * CHUNK, HD), ((2, None), (None, 2))))
+    put_ranges(kr, vr, 0, r2)
+    put_bias(kr, vr, range_bias(sc, (2,)))
     ks[...] = jnp.zeros((HALF, 2 * HD), BF16)
     vs[...] = jnp.zeros((HALF, 2 * HD), BF16)
     put_keys(ks, vs, 0, sink, 0, SINK, SINK)
@@ -221,30 +232,21 @@
         out_ref[:, cols] = (theirs + w * (mine - theirs)).astype(BF16)
 
 
-def pages_kernel(sc, a0, a1, a2, a3, b0, b1, b2, b3, out_ref):
-    x, y, z, c = sc[0], sc[1], sc[2], sc[4]
-    first = (a0, a1, a2, a3)
-    second = (b0, b1, b2, b3)
+def pages_kernel(sc, r0, r1, r2, r3, out_ref):
+    c = sc[4]
     row = iota((2 * PAGE, HD), 0)
     lane = iota((2 * PAGE, HD), 1)
     same_row = (lane & (PAGE - 1)) == (row & (PAGE - 1))
     want = (2 * c + (row >> 4)).astype(F32)
-    codes = [f[8 * PAIR:8 * PAIR + META, :].astype(F32) for f in first]
-    for dx in range(4):
-        for d in range(4):
-            for col in range(2):
-                n = d * 2 + col
-                f, at = first[dx], n * PAIR
-                s, on = second[d], (dx * 2 + col) * PAIR
-                code = codes[dx][n:n + 1, :]
-                select = jnp.where(same_row & (code == want), 1.0, 0.0).astype(BF16)
-                zz = z if col == 0 else 1 - z
-                block = ((x - dx) & 3) * 8 + zz * 4 + ((y - d) & 3)
-                for part in range(2):
-                    k1 = f[at + part * QUART:at + (part + 1) * QUART, :]
-                    k2 = s[on + part * QUART:on + (part + 1) * QUART, :]
-                    pages = jnp.dot(select, jnp.concatenate([k1, k2], axis=0), preferred_element_type=F32)
-                    out_ref[block, :, part * HD:(part + 1) * HD] = pages.astype(BF16)
+    for outer, ref in enumerate((r0, r1, r2, r3)):
+        codes = ref[8 * ROWS:8 * ROWS + META, :].astype(F32)
+        for n in range(8):
+            select = jnp.where(same_row & (codes[n:n + 1, :] == want), 1.0, 0.0).astype(BF16)
+            block = range_of(sc, n >> 1, outer, n & 1)
+            for part in range(2):
+                at = n * ROWS + part * HALF
+                pages = jnp.dot(select, ref[at:at + HALF, :], preferred_element_type=F32)
+                out_ref[block, :, part * HD:(part + 1) * HD] = pages.astype(BF16)
 
 
 VMEM_SPEC = pl.BlockSpec(memory_space=pltpu.VMEM)
@@ -292,48 +294,41 @@
     code = jnp.where(core == 0, code[:8], code[8:]).astype(BF16)
     meta = jnp.broadcast_to(jnp.repeat(code, PAGE)[None, :], (META, HD))
 
-    r1 = jnp.concatenate([ret[:QUART], ret[HALF:HALF + QUART]])
-    r2 = jnp.concatenate([ret[QUART:HALF], ret[HALF + QUART:]])
     sink = jnp.concatenate([pas[:SINK], pas[HALF:HALF + SINK]])
-    mine = jnp.concatenate([r1, r2, sink, meta])
-    theirs = lax.ppermute(mine, "ctx", Z_SWAP)
+    theirs = lax.ppermute(jnp.concatenate([ret, sink, meta]), "ctx", Z_SWAP)
     theirs, q_other = lax.optimization_barrier((theirs, q_other))
-    far = lax.ppermute(jnp.concatenate([pas, mine[-META:]]), "ctx", FOUR_ON)[:2 * HALF]
-    r1 = jnp.concatenate([r1, theirs[:PAIR]])
-    r2 = jnp.concatenate([r2, theirs[PAIR:2 * PAIR]])
-    sink = jnp.where(z == 0, sink, theirs[2 * PAIR:2 * PAIR + 2 * SINK])
+    both = jnp.concatenate([ret, theirs[:ROWS]])
+    sink = jnp.where(z == 0, sink, theirs[ROWS:ROWS + 2 * SINK])
     line = iota((META, HD), 0)
-    meta = jnp.where((line & 1) == 0, meta, theirs[2 * PAIR + 2 * SINK:])
-
-    along_x = jnp.concatenate([r2, sink])
-    xs = {s: lax.ppermute(along_x, "ctx", X_SHIFT[s]) for s in (1, 3, 2)}
-    ys = {
-        s: lax.ppermute(jnp.concatenate([r1, meta, jnp.where(y + s < 4, pas, far)]), "ctx", Y_SHIFT[s])
-        for s in (1, 3, 2)
-    }
+    meta = jnp.where((line & 1) == 0, meta, theirs[ROWS + 2 * SINK:])
+
+    axes = ("ctx", "tp")
+    message = jnp.concatenate([both, sink, meta])
+    got = {s: lax.ppermute(message, axes, STAGE_1[s]) for s in (1, 3, 2)}
     for s in (1, 2, 3):
-        meta = jnp.where((line >> 1) == s, ys[s][2 * PAIR:2 * PAIR + META], meta)
-        sink = jnp.where(x == s, xs[s][2 * PAIR:], sink)
-    h1 = jnp.concatenate([r1] + [ys[s][:2 * PAIR] for s in (1, 2, 3)] + [meta])
-    h2 = jnp.concatenate([r2] + [xs[s][:2 * PAIR] for s in (1, 2, 3)] + [sink])
-
-    a = {0: h1} | {s: lax.ppermute(h1, "ctx", X_SHIFT[s]) for s in (1, 3)}
-    b = {0: h2} | {s: lax.ppermute(h2, "ctx", Y_SHIFT[s]) for s in (1, 3)}
+        meta = jnp.where((line >> 1) == s, got[s][2 * ROWS + 2 * SINK:], meta)
+        sink = jnp.where(y == s, got[s][2 * ROWS:2 * ROWS + 2 * SINK], sink)
+    message = jnp.concatenate([both] + [got[s][:2 * ROWS] for s in (1, 2, 3)] + [meta, sink])
+
+    far = lax.ppermute(jnp.concatenate([pas, theirs[-META:]]), "ctx", FOUR_ON)[:ROWS]
+
+    r = {0: message} | {s: lax.ppermute(message, axes, STAGE_2[s]) for s in (1, 3)}
+    p = {s: lax.ppermute(jnp.where(y + s < 4, pas, far), "ctx", Y_SHIFT[s]) for s in (1, 3, 2)}
+
     state = (jax.ShapeDtypeStruct((GROUP, ROWS, HD), F32),) * 3
     unit = 2 * 2048 * 256 * 512
-    now = call(
-        near_kernel, state + state, keys(5 * HALF) + keys(2 * CHUNK), 7 * unit,
-        sc, q, q_other, pas, ys[1], ys[2], ys[3], far, h1, h2)
-    h1_late, h2_late, *now = lax.optimization_barrier((h1, h2, *now))
-    now_p, now_r = now[:3], now[3:]
-    a[2] = lax.ppermute(h1_late, "ctx", X_SHIFT[2])
-    b[2] = lax.ppermute(h2_late, "ctx", Y_SHIFT[2])
-    now_r = call(middle_kernel, state, keys(4 * CHUNK), 8 * unit, sc, q, q_other, a[1], a[3], b[1], b[3], *now_r)
+    now = call(near_kernel, state, keys(8 * HALF), 4 * unit, sc, q, q_other, message)
+    late, sc_p, *now = lax.optimization_barrier((message, sc, *now))
+    r[2] = lax.ppermute(late, axes, STAGE_2[2])
+    now_p = call(passing_kernel, state, keys(5 * HALF), 3 * unit, sc_p, q, q_other, pas, p[1], p[2], p[3], far)
+    sc_m, now_p0 = lax.optimization_barrier((sc_p, now_p[0]))
+    now = call(middle_kernel, state, keys(16 * HALF), 8 * unit, sc_m, q, q_other, r[1], r[3], *now)
+    sc_l, now_0 = lax.optimization_barrier((sc_m, now[0]))
     for s in (1, 2, 3):
-        sink = jnp.where(y == s, b[s][8 * PAIR:], sink)
+        sink = jnp.where(x == s, r[s][8 * ROWS + META:], sink)
     pages = call(
         pages_kernel, jax.ShapeDtypeStruct((32, 2 * PAGE, 2 * HD), BF16), [], unit // 4,
-        sc, *[a[s] for s in range(4)], *[b[s] for s in range(4)])
+        sc_l, *[r[s] for s in range(4)])
     got_pages = lax.ppermute(pages, "tp", CORE_SWAP)
     keep, keep_lse, send = call(
         last_kernel,
@@ -342,8 +337,8 @@
             jax.ShapeDtypeStruct((ROWS, HD), F32),
             jax.ShapeDtypeStruct((ROWS, (GROUP + 1) * HD), BF16),
         ),
-        keys(2 * CHUNK) + keys(HALF) + [pltpu.VMEM((ROWS, HD), F32)],
-        5 * unit, sc, q, q_other, a[2], b[2], sink, *now_r, *now_p)
+        keys(8 * HALF) + keys(HALF) + [pltpu.VMEM((ROWS, HD), F32)],
+        5 * unit, sc_l, q, q_other, r[2], sink, now_0, *now[1:], now_p0, *now_p[1:])
 
     got = lax.ppermute(send, "tp", CORE_SWAP)
     attn_out = call(

time: 69.4 us -> 72.3 us (1.042)
  local copies, waits for them, and re-layouts: 3.16 us -> 5.9 us
  starting transfers between devices: 36.7 us -> 34.3 us
  waiting for transfers between devices: 2.73 us -> 4.07 us
  Pallas kernels: 22.9 us -> 24.1 us
    unnamed x18 -> x21, local copies, waits for them, and re-layouts: 1.46 us -> 4.22 us
    ppermute x14 -> x11, starting transfers between devices: 28.5 us -> 25.9 us  [the longest x1 6.99 us: shards(): lax.ppermute(jnp.concatenate([pas, theirs[-META:]]), 'ctx', FOUR_ON)[:ROWS]]
    ppermute x14 -> x11, waiting for transfers between devices: 1.6 us -> 2.93 us  [the longest x1 2.9 us: shards(): theirs = lax.ppermute(jnp.concatenate([ret, sink, meta]), 'ctx', Z_SWAP)]
    pallas_call x5 -> x6, Pallas kernels: 22.9 us -> 24.1 us  [call(): pl.pallas_call(kernel, out_shape=out_shape, in_specs=specs, out_specs=(VM...]
  transfers between devices with their start and end apart: 18 -> 15, of which waited for: 3 -> 2; matrix products, arithmetic and copies ran while one was open for 4% -> 4% of each run, Pallas kernels for 30% -> 30%
where the time goes in v5:
time: 72.3 us; the launch traced here: 72.1 us
  starting transfers between devices  34.3 us (47%)
  Pallas kernels  24.1 us (33%)
  local copies, waits for them, and re-layouts  5.9 us (8%)
  waiting for transfers between devices  4.07 us (6%)
  other arithmetic  2.12 us (3%)
  between operations  1.56 us (2%)
    pallas_call x6, Pallas kernels, call(): pl.pallas_call(kernel, out_shape=out_shape, in_specs=specs, out_specs=(VM...  24.1 us
    ppermute x1, starting transfers between devices, shards(): got_pages = lax.ppermute(pages, 'tp', CORE_SWAP)  7.43 us
    ppermute x1, starting transfers between devices, shards(): lax.ppermute(jnp.concatenate([pas, theirs[-META:]]), 'ctx', FOUR_ON)[:ROWS]  6.99 us
    ppermute x1, starting transfers between devices, shards(): theirs = lax.ppermute(jnp.concatenate([ret, sink, meta]), 'ctx', Z_SWAP)  6.1 us
    ppermute x3, starting transfers between devices, shards(): got = {s: lax.ppermute(message, axes, STAGE_1[s]) for s in (1, 3, 2)}  4.92 us
    unnamed x21, local copies, waits for them, and re-layouts  4.22 us
    ppermute x3, starting transfers between devices, shards(): lax.ppermute(jnp.where(y + s < 4, pas, far), 'ctx', Y_SHIFT[s])  3.63 us
    ppermute x1, waiting for transfers between devices, shards(): theirs = lax.ppermute(jnp.concatenate([ret, sink, meta]), 'ctx', Z_SWAP)  2.9 us
  transfers between devices with their start and end apart: 15, of which 2 were waited for; matrix products, arithmetic and copies ran while one was open for 4% of the time, Pallas kernels for 30%

profile of v5, /device:TPU:33, one launch (start us, length us, event | category | flops | bytes accessed | tf_op | source)
XLA Modules:
  0.0 72.1 jit_solution(16745490819122711011)
XLA Ops:
  0.6 0.8 %fusion.15 = (bf16[128,128]{1,0:T(8,128)(2,1)S(1)}, bf16[128,128]{1,0:T(8,128)(2,1)S(1)}, bf16[128,128]{1,0:T(8,128)(2,1)S(1)}, bf16[128,128]{1,0:T(8,128)(2,1)S(1)}) fusion(bf16[256,128]{1,0:T(8,128)(2,1)} %param.6, bf16[256,128]{1,0:T(8,128)(2,1)} %param.7), kind=kLoop, calls=%fused_computation.45 | loop fusion | bytes 262144 | tf_op jit(solution)/shard_map/slice | solution.py:283
  1.5 0.8 %collective-permute-start = (bf16[256,128]{1,0:T(8,128)(2,1)S(1)}, bf16[256,128]{1,0:T(8,128)(2,1)S(1)}, u32[]{:S(2)}, u32[]{:S(2)}) collective-permute-start(bf16[256,128]{1,0:T(8,128)(2,1)S(1)} %broadcast_select_fusion.3), channel_id=1, source_target_pairs={{0,1},{1,0},{2,3},{3,2},{4,5},{5,4},{6,7},{7,6},{8,9},{9,8},{10,11... | collective-permute-start | bytes 196616 | tf_op jit(solution)/shard_map/ppermute | solution.py:286
  2.3 0.1 collective-permute-start.2
  2.4 0.7 copy-done.7
  3.0 0.2 convert_reduce_fusion
  3.4 0.6 copy-done.8
  4.0 0.6 dynamic_slice.4
  5.4 6.1 %collective-permute-start.1 = (bf16[400,128]{1,0:T(8,128)(2,1)S(1)}, bf16[400,128]{1,0:T(8,128)(2,1)S(1)}, u32[]{:S(2)}, u32[]{:S(2)}) collective-permute-start(bf16[400,128]{1,0:T(8,128)(2,1)S(1)} %pad_maximum_fusion.1), channel_id=1, source_target_pairs={{0,32},{8,40},{16,48},{24,56},{32,0},{40,8},{48,16},{56,24},{64,96... | collective-permute-start | bytes 307208 | tf_op jit(solution)/shard_map/ppermute | solution.py:298
  11.5 2.9 %collective-permute-done.1 = bf16[400,128]{1,0:T(8,128)(2,1)S(1)} collective-permute-done((bf16[400,128]{1,0:T(8,128)(2,1)S(1)}, bf16[400,128]{1,0:T(8,128)(2,1)S(1)}, u32[]{:S(2)}, u32[]{:S(2)}) %collective-permute-start.1) | collective-permute-done | bytes 102432 | tf_op jit(solution)/shard_map/ppermute | solution.py:298
  14.5 1.3 %collective-permute-start.3 = (bf16[656,128]{1,0:T(8,128)(2,1)S(1)}, bf16[656,128]{1,0:T(8,128)(2,1)S(1)}, u32[]{:S(2)}, u32[]{:S(2)}) collective-permute-start(bf16[656,128]{1,0:T(8,128)(2,1)S(1)} %pad_maximum_fusion), channel_id=1, source_target_pairs={{0,8},{1,65},{2,10},{3,67},{4,12},{5,69},{6,14},{7,71},{8,16},{9,7... | collective-permute-start | bytes 503816 | tf_op jit(solution)/shard_map/ppermute | solution.py:307
  15.9 2.5 %collective-permute-start.4 = (bf16[656,128]{1,0:T(8,128)(2,1)S(1)}, bf16[656,128]{1,0:T(8,128)(2,1)S(1)}, u32[]{:S(2)}, u32[]{:S(2)}) collective-permute-start(bf16[656,128]{1,0:T(8,128)(2,1)S(1)} %pad_maximum_fusion), channel_id=1, source_target_pairs={{0,16},{1,129},{2,18},{3,131},{4,20},{5,133},{6,22},{7,135},{8,24}... | collective-permute-start | bytes 503816 | tf_op jit(solution)/shard_map/ppermute | solution.py:307
  18.4 1.2 %collective-permute-start.5 = (bf16[656,128]{1,0:T(8,128)(2,1)S(1)}, bf16[656,128]{1,0:T(8,128)(2,1)S(1)}, u32[]{:S(2)}, u32[]{:S(2)}) collective-permute-start(bf16[656,128]{1,0:T(8,128)(2,1)S(1)} %pad_maximum_fusion), channel_id=1, source_target_pairs={{0,24},{1,193},{2,26},{3,195},{4,28},{5,197},{6,30},{7,199},{8,0},... | collective-permute-start | bytes 503816 | tf_op jit(solution)/shard_map/ppermute | solution.py:307
  19.5 7.0 %collective-permute-start.6 = (bf16[272,128]{1,0:T(8,128)(2,1)S(1)}, bf16[272,128]{1,0:T(8,128)(2,1)S(1)}, u32[]{:S(2)}, u32[]{:S(2)}) collective-permute-start(bf16[272,128]{1,0:T(8,128)(2,1)S(1)} %pad_maximum_fusion.2), channel_id=1, source_target_pairs={{0,32},{8,40},{16,48},{24,56},{32,64},{40,72},{48,80},{56,88},{64,... | collective-permute-start | bytes 208904 | tf_op jit(solution)/shard_map/ppermute | solution.py:313
  26.8 1.4 %collective-permute-start.10 = (bf16[2192,128]{1,0:T(8,128)(2,1)S(1)}, bf16[2192,128]{1,0:T(8,128)(2,1)S(1)}, u32[]{:S(2)}, u32[]{:S(2)}) collective-permute-start(bf16[2192,128]{1,0:T(8,128)(2,1)S(1)} %get-tuple-element.38.here.r0), channel_id=1, source_target_pairs={{0,64},{1,9},{2,66},{3,11},{4,68},{5,13},{6,70},{7,15},{8,72},{9,1... | collective-permute-start | bytes 1683464 | tf_op jit(solution)/shard_map/ppermute | solution.py:315
  28.1 1.5 %collective-permute-start.11 = (bf16[2192,128]{1,0:T(8,128)(2,1)S(1)}, bf16[2192,128]{1,0:T(8,128)(2,1)S(1)}, u32[]{:S(2)}, u32[]{:S(2)}) collective-permute-start(bf16[2192,128]{1,0:T(8,128)(2,1)S(1)} %get-tuple-element.38.here.r0), channel_id=1, source_target_pairs={{0,192},{1,25},{2,194},{3,27},{4,196},{5,29},{6,198},{7,31},{8,200... | collective-permute-start | bytes 1683464 | tf_op jit(solution)/shard_map/ppermute | solution.py:315
  29.7 0.7 broadcast_select_fusion
  30.3 2.6 %collective-permute-start.8 = (bf16[256,128]{1,0:T(8,128)(2,1)}, bf16[256,128]{1,0:T(8,128)(2,1)}, u32[]{:S(2)}, u32[]{:S(2)}) collective-permute-start(bf16[256,128]{1,0:T(8,128)(2,1)} %get-tuple-element.54), channel_id=1, source_target_pairs={{0,16},{8,24},{16,0},{24,8},{32,48},{40,56},{48,32},{56,40},{64,80... | collective-permute-start | bytes 196616 | tf_op jit(solution)/shard_map/ppermute | solution.py:316
  32.9 1.1 %collective-permute-start.9 = (bf16[256,128]{1,0:T(8,128)(2,1)}, bf16[256,128]{1,0:T(8,128)(2,1)}, u32[]{:S(2)}, u32[]{:S(2)}) collective-permute-start(bf16[256,128]{1,0:T(8,128)(2,1)} %get-tuple-element.53), channel_id=1, source_target_pairs={{0,24},{8,0},{16,8},{24,16},{32,56},{40,32},{48,40},{56,48},{64,88... | collective-permute-start | bytes 196616 | tf_op jit(solution)/shard_map/ppermute | solution.py:316
  34.0 3.7 %shard_map.68 = (f32[8,256,128]{2,1,0:T(8,128)S(1)}, f32[8,256,128]{2,1,0:T(8,128)S(1)}, f32[8,256,128]{2,1,0:T(8,128)S(1)}) custom-call(s32[8]{0:T(128)S(1)} %stack.33.sc, bf16[256,1024]{1,0:T(8,128)(2,1)S(1)} %copy-done, bf16[256,1024]{1,0:T(8,128)(2,1)S(1)} %collective-permute-done.2.q_other, bf16[2192,128]{1,0:T(8,128)(2,1)S(1)} %get-tuple-element.38.here.r0), custom_call_target="tpu_custom_call" | custom-call | flops 2147483648 | bytes 4194304 | tf_op jit(solution)/shard_map/pallas_call | solution.py:260
  37.7 1.0 %copy-done.1 = f32[8,256,128]{2,1,0:T(8,128)} copy-done((f32[8,256,128]{2,1,0:T(8,128)}, f32[8,256,128]{2,1,0:T(8,128)S(1)}, u32[]{:S(2)}) %copy-start.1) | copy-done | bytes 1048600
  38.7 1.0 %copy-done.3 = f32[8,256,128]{2,1,0:T(8,128)} copy-done((f32[8,256,128]{2,1,0:T(8,128)}, f32[8,256,128]{2,1,0:T(8,128)S(1)}, u32[]{:S(2)}) %copy-start.3) | copy-done | bytes 1048600
  39.7 1.0 %copy-done.5 = f32[8,256,128]{2,1,0:T(8,128)} copy-done((f32[8,256,128]{2,1,0:T(8,128)}, f32[8,256,128]{2,1,0:T(8,128)S(1)}, u32[]{:S(2)}) %copy-start.5) | copy-done | bytes 1048600
  40.6 1.4 %collective-permute-start.12 = (bf16[2192,128]{1,0:T(8,128)(2,1)S(1)}, bf16[2192,128]{1,0:T(8,128)(2,1)S(1)}, u32[]{:S(2)}, u32[]{:S(2)}) collective-permute-start(bf16[2192,128]{1,0:T(8,128)(2,1)S(1)} %get-tuple-element.38.here.r0), channel_id=1, source_target_pairs={{0,128},{1,17},{2,130},{3,19},{4,132},{5,21},{6,134},{7,23},{8,136... | collective-permute-start | bytes 1683464 | tf_op jit(solution)/shard_map/ppermute | solution.py:322
  42.1 4.4 %shard_map.69 = (f32[8,256,128]{2,1,0:T(8,128)S(1)}, f32[8,256,128]{2,1,0:T(8,128)S(1)}, f32[8,256,128]{2,1,0:T(8,128)S(1)}) custom-call(s32[8]{0:T(128)S(1)} %stack.33.sc, bf16[256,1024]{1,0:T(8,128)(2,1)S(1)} %copy-done, bf16[256,1024]{1,0:T(8,128)(2,1)S(1)} %collective-permute-done.2.q_other, bf16[256,128]{1,0:T(8,128)(2,1)S(1)} %get-tuple-element.52.pas, ...), custom_call_target="tpu_custom_call" | custom-call | flops 1610612736 | bytes 4194304 | tf_op jit(solution)/shard_map/pallas_call | solution.py:260
  46.5 7.1 %shard_map.70 = (f32[8,256,128]{2,1,0:T(8,128)S(1)}, f32[8,256,128]{2,1,0:T(8,128)S(1)}, f32[8,256,128]{2,1,0:T(8,128)S(1)}) custom-call(s32[8]{0:T(128)S(1)} %stack.33.sc, bf16[256,1024]{1,0:T(8,128)(2,1)S(1)} %copy-done, bf16[256,1024]{1,0:T(8,128)(2,1)S(1)} %collective-permute-done.2.q_other, bf16[2192,128]{1,0:T(8,128)(2,1)S(1)} %collective-permute-done.10.r1, ...), custom_call_target="tpu_custom_call" | custom-call | flops 4294967296 | bytes 4194304 | tf_op jit(solution)/shard_map/pallas_call | solution.py:260
  53.6 1.2 %shard_map.73 = bf16[32,32,256]{2,1,0:T(8,128)(2,1)S(1)} custom-call(s32[8]{0:T(128)S(1)} %stack.33.sc, bf16[2192,128]{1,0:T(8,128)(2,1)S(1)} %get-tuple-element.38.here.r0, bf16[2192,128]{1,0:T(8,128)(2,1)S(1)} %collective-permute-done.10.r1, bf16[2192,128]{1,0:T(8,128)(2,1)S(1)} %collective-permute-done.12.r2, bf16[2192,128]{1,0:T(8,128)(2,1)S(1)} %collective-permute-done.11.r3), custom_call_target="tpu_custom_call" | custom-call | flops 134217728 | bytes 4194304 | tf_op jit(solution)/shard_map/pallas_call | solution.py:260
  54.8 7.4 %collective-permute-start.14 = (bf16[32,32,256]{2,1,0:T(8,128)(2,1)S(1)}, bf16[32,32,256]{2,1,0:T(8,128)(2,1)S(1)}, u32[]{:S(2)}, u32[]{:S(2)}) collective-permute-start(bf16[32,32,256]{2,1,0:T(8,128)(2,1)S(1)} %shard_map.73), channel_id=1, source_target_pairs={{0,1},{1,0},{2,3},{3,2},{4,5},{5,4},{6,7},{7,6},{8,9},{9,8},{10,11... | collective-permute-start | bytes 1572872 | tf_op jit(solution)/shard_map/ppermute | solution.py:332
  62.3 6.5 %shard_map.71 = (bf16[256,1024]{1,0:T(8,128)(2,1)S(1)}, f32[256,128]{1,0:T(8,128)S(1)}, bf16[256,1152]{1,0:T(8,128)(2,1)S(1)}) custom-call(s32[8]{0:T(128)S(1)} %stack.33.sc, bf16[256,1024]{1,0:T(8,128)(2,1)S(1)} %copy-done, bf16[256,1024]{1,0:T(8,128)(2,1)S(1)} %collective-permute-done.2.q_other, bf16[2192,128]{1,0:T(8,128)(2,1)S(1)} %collective-permute-done.12.r2, ...), custom_call_target="tpu_custom_call" | custom-call | flops 2684354560 | bytes 4194304 | tf_op jit(solution)/shard_map/pallas_call | solution.py:260
  68.7 0.1 collective-permute-start.13
  68.8 0.9 %add_select_fusion = bf16[32,32,256]{2,1,0:T(8,128)(2,1)} fusion(bf16[32,32,256]{2,1,0:T(8,128)(2,1)S(1)} %shard_map.73, bf16[32,32,256]{2,1,0:T(8,128)(2,1)S(1)} %collective-permute-done.14, pred[]{:T(512)} %bitcast), kind=kLoop, calls=%fused_computation | loop fusion | flops 524288 | bytes 1572865 | tf_op jit(solution)/shard_map/jit(_where)/select_n | solution.py:346
  69.7 1.1 %collective-permute-done.13.got = bf16[256,1152]{1,0:T(8,128)(2,1)S(1)} collective-permute-done((bf16[256,1152]{1,0:T(8,128)(2,1)S(1)}, bf16[256,1152]{1,0:T(8,128)(2,1)S(1)}, u32[]{:S(2)}, u32[]{:S(2)}) %collective-permute-start.13) | collective-permute-done | bytes 589856 | tf_op jit(solution)/shard_map/ppermute | solution.py:343
  70.8 1.3 %shard_map.72 = bf16[256,1024]{1,0:T(8,128)(2,1)} custom-call(bf16[256,1024]{1,0:T(8,128)(2,1)S(1)} %get-tuple-element.45.keep, f32[256,128]{1,0:T(8,128)S(1)} %get-tuple-element.46.keep_lse, bf16[256,1152]{1,0:T(8,128)(2,1)S(1)} %collective-permute-done.13.got), custom_call_target="tpu_custom_call" | custom-call | flops 134217728 | bytes 4194304 | tf_op jit(solution)/shard_map/pallas_call | solution.py:260
  (51 shorter events, 0.8 us)
Async XLA Ops:
  1.5 3.8 %collective-permute-start = (bf16[256,128]{1,0:T(8,128)(2,1)S(1)}, bf16[256,128]{1,0:T(8,128)(2,1)S(1)}, u32[]{:S(2)}, u32[]{:S(2)}) collective-permute-start(bf16[256,128]{1,0:T(8,128)(2,1)S(1)} %broadcast_select_fusion.3), channel_id=1, source_target_pairs={{0,1},{1,0},{2,3},{3,2},{4,5},{5,4},{6,7},{7,6},{8,9},{9,8},{10,11... | collective-permute-start | bytes 196616 | tf_op jit(solution)/shard_map/ppermute | solution.py:286
  2.3 12.1 %collective-permute-start.2 = (bf16[256,1024]{1,0:T(8,128)(2,1)}, bf16[256,1024]{1,0:T(8,128)(2,1)S(1)}, u32[]{:S(2)}, u32[]{:S(2)}) collective-permute-start(bf16[256,1024]{1,0:T(8,128)(2,1)} %q_own.7), channel_id=1, source_target_pairs={{0,1},{1,0},{2,3},{3,2},{4,5},{5,4},{6,7},{7,6},{8,9},{9,8},{10,11... | collective-permute-start | bytes 1572872 | tf_op jit(solution)/shard_map/ppermute | solution.py:287
  2.4 0.7 copy-start.7
  3.4 0.7 copy-start.8
  5.4 9.0 %collective-permute-start.1 = (bf16[400,128]{1,0:T(8,128)(2,1)S(1)}, bf16[400,128]{1,0:T(8,128)(2,1)S(1)}, u32[]{:S(2)}, u32[]{:S(2)}) collective-permute-start(bf16[400,128]{1,0:T(8,128)(2,1)S(1)} %pad_maximum_fusion.1), channel_id=1, source_target_pairs={{0,32},{8,40},{16,48},{24,56},{32,0},{40,8},{48,16},{56,24},{64,96... | collective-permute-start | bytes 307208 | tf_op jit(solution)/shard_map/ppermute | solution.py:298
  14.5 12.0 %collective-permute-start.3 = (bf16[656,128]{1,0:T(8,128)(2,1)S(1)}, bf16[656,128]{1,0:T(8,128)(2,1)S(1)}, u32[]{:S(2)}, u32[]{:S(2)}) collective-permute-start(bf16[656,128]{1,0:T(8,128)(2,1)S(1)} %pad_maximum_fusion), channel_id=1, source_target_pairs={{0,8},{1,65},{2,10},{3,67},{4,12},{5,69},{6,14},{7,71},{8,16},{9,7... | collective-permute-start | bytes 503816 | tf_op jit(solution)/shard_map/ppermute | solution.py:307
  15.9 10.7 %collective-permute-start.4 = (bf16[656,128]{1,0:T(8,128)(2,1)S(1)}, bf16[656,128]{1,0:T(8,128)(2,1)S(1)}, u32[]{:S(2)}, u32[]{:S(2)}) collective-permute-start(bf16[656,128]{1,0:T(8,128)(2,1)S(1)} %pad_maximum_fusion), channel_id=1, source_target_pairs={{0,16},{1,129},{2,18},{3,131},{4,20},{5,133},{6,22},{7,135},{8,24}... | collective-permute-start | bytes 503816 | tf_op jit(solution)/shard_map/ppermute | solution.py:307
  18.4 8.2 %collective-permute-start.5 = (bf16[656,128]{1,0:T(8,128)(2,1)S(1)}, bf16[656,128]{1,0:T(8,128)(2,1)S(1)}, u32[]{:S(2)}, u32[]{:S(2)}) collective-permute-start(bf16[656,128]{1,0:T(8,128)(2,1)S(1)} %pad_maximum_fusion), channel_id=1, source_target_pairs={{0,24},{1,193},{2,26},{3,195},{4,28},{5,197},{6,30},{7,199},{8,0},... | collective-permute-start | bytes 503816 | tf_op jit(solution)/shard_map/ppermute | solution.py:307
  19.5 10.1 %collective-permute-start.6 = (bf16[272,128]{1,0:T(8,128)(2,1)S(1)}, bf16[272,128]{1,0:T(8,128)(2,1)S(1)}, u32[]{:S(2)}, u32[]{:S(2)}) collective-permute-start(bf16[272,128]{1,0:T(8,128)(2,1)S(1)} %pad_maximum_fusion.2), channel_id=1, source_target_pairs={{0,32},{8,40},{16,48},{24,56},{32,64},{40,72},{48,80},{56,88},{64,... | collective-permute-start | bytes 208904 | tf_op jit(solution)/shard_map/ppermute | solution.py:313
  26.6 7.4 %copy-start = (bf16[256,1024]{1,0:T(8,128)(2,1)S(1)}, bf16[256,1024]{1,0:T(8,128)(2,1)}, u32[]{:S(2)}) copy-start(bf16[256,1024]{1,0:T(8,128)(2,1)} %q_own.7) | copy-start | bytes 1572868
  26.8 19.7 %collective-permute-start.10 = (bf16[2192,128]{1,0:T(8,128)(2,1)S(1)}, bf16[2192,128]{1,0:T(8,128)(2,1)S(1)}, u32[]{:S(2)}, u32[]{:S(2)}) collective-permute-start(bf16[2192,128]{1,0:T(8,128)(2,1)S(1)} %get-tuple-element.38.here.r0), channel_id=1, source_target_pairs={{0,64},{1,9},{2,66},{3,11},{4,68},{5,13},{6,70},{7,15},{8,72},{9,1... | collective-permute-start | bytes 1683464 | tf_op jit(solution)/shard_map/ppermute | solution.py:315
  28.1 18.3 %collective-permute-start.11 = (bf16[2192,128]{1,0:T(8,128)(2,1)S(1)}, bf16[2192,128]{1,0:T(8,128)(2,1)S(1)}, u32[]{:S(2)}, u32[]{:S(2)}) collective-permute-start(bf16[2192,128]{1,0:T(8,128)(2,1)S(1)} %get-tuple-element.38.here.r0), channel_id=1, source_target_pairs={{0,192},{1,25},{2,194},{3,27},{4,196},{5,29},{6,198},{7,31},{8,200... | collective-permute-start | bytes 1683464 | tf_op jit(solution)/shard_map/ppermute | solution.py:315
  30.3 10.3 %collective-permute-start.7 = (bf16[256,128]{1,0:T(8,128)(2,1)S(1)}, bf16[256,128]{1,0:T(8,128)(2,1)S(1)}, u32[]{:S(2)}, u32[]{:S(2)}) collective-permute-start(bf16[256,128]{1,0:T(8,128)(2,1)S(1)} %get-tuple-element.55), channel_id=1, source_target_pairs={{0,8},{8,16},{16,24},{24,0},{32,40},{40,48},{48,56},{56,32},{64,72... | collective-permute-start | bytes 196616 | tf_op jit(solution)/shard_map/ppermute | solution.py:316
  30.3 11.7 %collective-permute-start.8 = (bf16[256,128]{1,0:T(8,128)(2,1)}, bf16[256,128]{1,0:T(8,128)(2,1)}, u32[]{:S(2)}, u32[]{:S(2)}) collective-permute-start(bf16[256,128]{1,0:T(8,128)(2,1)} %get-tuple-element.54), channel_id=1, source_target_pairs={{0,16},{8,24},{16,0},{24,8},{32,48},{40,56},{48,32},{56,40},{64,80... | collective-permute-start | bytes 196616 | tf_op jit(solution)/shard_map/ppermute | solution.py:316
  32.9 9.2 %collective-permute-start.9 = (bf16[256,128]{1,0:T(8,128)(2,1)}, bf16[256,128]{1,0:T(8,128)(2,1)}, u32[]{:S(2)}, u32[]{:S(2)}) collective-permute-start(bf16[256,128]{1,0:T(8,128)(2,1)} %get-tuple-element.53), channel_id=1, source_target_pairs={{0,24},{8,0},{16,8},{24,16},{32,56},{40,32},{48,40},{56,48},{64,88... | collective-permute-start | bytes 196616 | tf_op jit(solution)/shard_map/ppermute | solution.py:316
  37.7 1.0 %copy-start.1 = (f32[8,256,128]{2,1,0:T(8,128)}, f32[8,256,128]{2,1,0:T(8,128)S(1)}, u32[]{:S(2)}) copy-start(f32[8,256,128]{2,1,0:T(8,128)S(1)} %get-tuple-element.33.m_in) | copy-start | bytes 3145732
  38.7 1.0 %copy-start.3 = (f32[8,256,128]{2,1,0:T(8,128)}, f32[8,256,128]{2,1,0:T(8,128)S(1)}, u32[]{:S(2)}) copy-start(f32[8,256,128]{2,1,0:T(8,128)S(1)} %get-tuple-element.34.l_in) | copy-start | bytes 3145732
  39.7 1.0 %copy-start.5 = (f32[8,256,128]{2,1,0:T(8,128)}, f32[8,256,128]{2,1,0:T(8,128)S(1)}, u32[]{:S(2)}) copy-start(f32[8,256,128]{2,1,0:T(8,128)S(1)} %get-tuple-element.35.o_in) | copy-start | bytes 3145732
  40.6 13.0 %collective-permute-start.12 = (bf16[2192,128]{1,0:T(8,128)(2,1)S(1)}, bf16[2192,128]{1,0:T(8,128)(2,1)S(1)}, u32[]{:S(2)}, u32[]{:S(2)}) collective-permute-start(bf16[2192,128]{1,0:T(8,128)(2,1)S(1)} %get-tuple-element.38.here.r0), channel_id=1, source_target_pairs={{0,128},{1,17},{2,130},{3,19},{4,132},{5,21},{6,134},{7,23},{8,136... | collective-permute-start | bytes 1683464 | tf_op jit(solution)/shard_map/ppermute | solution.py:322
  42.1 4.4 %copy-start.2 = (f32[8,256,128]{2,1,0:T(8,128)S(1)}, f32[8,256,128]{2,1,0:T(8,128)}, u32[]{:S(2)}) copy-start(f32[8,256,128]{2,1,0:T(8,128)} %copy-done.1) | copy-start | bytes 3145732
  42.1 4.4 %copy-start.4 = (f32[8,256,128]{2,1,0:T(8,128)S(1)}, f32[8,256,128]{2,1,0:T(8,128)}, u32[]{:S(2)}) copy-start(f32[8,256,128]{2,1,0:T(8,128)} %copy-done.3) | copy-start | bytes 3145732
  42.1 4.4 %copy-start.6 = (f32[8,256,128]{2,1,0:T(8,128)S(1)}, f32[8,256,128]{2,1,0:T(8,128)}, u32[]{:S(2)}) copy-start(f32[8,256,128]{2,1,0:T(8,128)} %copy-done.5) | copy-start | bytes 3145732
  54.8 14.0 %collective-permute-start.14 = (bf16[32,32,256]{2,1,0:T(8,128)(2,1)S(1)}, bf16[32,32,256]{2,1,0:T(8,128)(2,1)S(1)}, u32[]{:S(2)}, u32[]{:S(2)}) collective-permute-start(bf16[32,32,256]{2,1,0:T(8,128)(2,1)S(1)} %shard_map.73), channel_id=1, source_target_pairs={{0,1},{1,0},{2,3},{3,2},{4,5},{5,4},{6,7},{7,6},{8,9},{9,8},{10,11... | collective-permute-start | bytes 1572872 | tf_op jit(solution)/shard_map/ppermute | solution.py:332
  68.7 2.1 %collective-permute-start.13 = (bf16[256,1152]{1,0:T(8,128)(2,1)S(1)}, bf16[256,1152]{1,0:T(8,128)(2,1)S(1)}, u32[]{:S(2)}, u32[]{:S(2)}) collective-permute-start(bf16[256,1152]{1,0:T(8,128)(2,1)S(1)} %get-tuple-element.47), channel_id=1, source_target_pairs={{0,1},{1,0},{2,3},{3,2},{4,5},{5,4},{6,7},{7,6},{8,9},{9,8},{10,11... | collective-permute-start | bytes 1769480 | tf_op jit(solution)/shard_map/ppermute | solution.py:343

commit v6 on v5

--- a/solution.py
+++ b/solution.py
@@ -110,26 +110,11 @@
     return jnp.concatenate([q, one], axis=1)
 
 
-def near_kernel(sc, q_own, q_other, here, m_out, l_out, o_out, kr, vr):
-    core, is_r = sc[3], sc[5]
+def near_kernel(sc, q_own, q_other, here, pas, p1, p2, p3, far, mp_out, lp_out, op_out, m_out, l_out, o_out,
+                kp, vp, kr, vr):
+    core, c, is_r = sc[3], sc[4], sc[5]
     put_ranges(kr, vr, 0, here)
     put_bias(kr, vr, range_bias(sc, (0,)))
-    own = jnp.where(core * HALF + iota((ROWS, HD), 1) > iota((ROWS, HD), 0), NEG, 0.0)
-
-    def heads(i):
-        at = [WIDE * i + u for u in range(WIDE)]
-        q = [load_head(q_own, q_other, is_r, a) for a in at]
-        state = [fold(None, q[u], kr[0:CHUNK, :], vr[0:CHUNK, :], left=own) for u in range(WIDE)]
-        state = [fold(state[u], q[u], kr[CHUNK:, :], vr[CHUNK:, :]) for u in range(WIDE)]
-        for u in range(WIDE):
-            m_out[at[u]], l_out[at[u]], o_out[at[u]] = state[u]
-
-    for i in range(GROUP // WIDE):
-        heads(i)
-
-
-def passing_kernel(sc, q_own, q_other, pas, p1, p2, p3, far, m_out, l_out, o_out, kp, vp):
-    core, c, is_r = sc[3], sc[4], sc[5]
     for n, ref in enumerate((pas, p1, p2, p3, far)):
         put_keys(kp, vp, n * HALF, ref, 0, HALF, HALF)
     put_bias(kp, vp, jnp.where((iota((5 * HALF, HD), 0) >> 7) <= c, 0.0, NEG))
@@ -140,11 +125,15 @@
 
     def heads(i):
         at = [WIDE * i + u for u in range(WIDE)]
-        q = [load_head(q_other, q_own, is_r, a) for a in at]
-        state = [fold(None, q[u], kp[0:3 * HALF, :], vp[0:3 * HALF, :], left=own) for u in range(WIDE)]
-        state = [fold(state[u], q[u], kp[3 * HALF:, :], vp[3 * HALF:, :], right=edge) for u in range(WIDE)]
+        qp = [load_head(q_other, q_own, is_r, a) for a in at]
+        q = [load_head(q_own, q_other, is_r, a) for a in at]
+        sr = [fold(None, q[u], kr[0:CHUNK, :], vr[0:CHUNK, :], left=own) for u in range(WIDE)]
+        sp = [fold(None, qp[u], kp[0:3 * HALF, :], vp[0:3 * HALF, :], left=own) for u in range(WIDE)]
+        sr = [fold(sr[u], q[u], kr[CHUNK:, :], vr[CHUNK:, :]) for u in range(WIDE)]
+        sp = [fold(sp[u], qp[u], kp[3 * HALF:, :], vp[3 * HALF:, :], right=edge) for u in range(WIDE)]
         for u in range(WIDE):
-            m_out[at[u]], l_out[at[u]], o_out[at[u]] = state[u]
+            m_out[at[u]], l_out[at[u]], o_out[at[u]] = sr[u]
+            mp_out[at[u]], lp_out[at[u]], op_out[at[u]] = sp[u]
 
     for i in range(GROUP // WIDE):
         heads(i)
@@ -295,8 +284,10 @@
     meta = jnp.broadcast_to(jnp.repeat(code, PAGE)[None, :], (META, HD))
 
     sink = jnp.concatenate([pas[:SINK], pas[HALF:HALF + SINK]])
-    theirs = lax.ppermute(jnp.concatenate([ret, sink, meta]), "ctx", Z_SWAP)
-    theirs, q_other = lax.optimization_barrier((theirs, q_other))
+    message = jnp.concatenate([ret, sink, meta])
+    theirs = lax.ppermute(message, "ctx", Z_SWAP)
+    far = lax.ppermute(jnp.concatenate([pas, message[-META:]]), "ctx", FOUR_ON)[:ROWS]
+    theirs, far, q_other = lax.optimization_barrier((theirs, far, q_other))
     both = jnp.concatenate([ret, theirs[:ROWS]])
     sink = jnp.where(z == 0, sink, theirs[ROWS:ROWS + 2 * SINK])
     line = iota((META, HD), 0)
@@ -305,25 +296,25 @@
     axes = ("ctx", "tp")
     message = jnp.concatenate([both, sink, meta])
     got = {s: lax.ppermute(message, axes, STAGE_1[s]) for s in (1, 3, 2)}
+    pas, far, got[1] = lax.optimization_barrier((pas, far, got[1]))
+    p = {s: lax.ppermute(jnp.where(y + s < 4, pas, far), "ctx", Y_SHIFT[s]) for s in (1, 3, 2)}
+
     for s in (1, 2, 3):
         meta = jnp.where((line >> 1) == s, got[s][2 * ROWS + 2 * SINK:], meta)
         sink = jnp.where(y == s, got[s][2 * ROWS:2 * ROWS + 2 * SINK], sink)
     message = jnp.concatenate([both] + [got[s][:2 * ROWS] for s in (1, 2, 3)] + [meta, sink])
 
-    far = lax.ppermute(jnp.concatenate([pas, theirs[-META:]]), "ctx", FOUR_ON)[:ROWS]
-
     r = {0: message} | {s: lax.ppermute(message, axes, STAGE_2[s]) for s in (1, 3)}
-    p = {s: lax.ppermute(jnp.where(y + s < 4, pas, far), "ctx", Y_SHIFT[s]) for s in (1, 3, 2)}
-
     state = (jax.ShapeDtypeStruct((GROUP, ROWS, HD), F32),) * 3
     unit = 2 * 2048 * 256 * 512
-    now = call(near_kernel, state, keys(8 * HALF), 4 * unit, sc, q, q_other, message)
-    late, sc_p, *now = lax.optimization_barrier((message, sc, *now))
+    now = call(
+        near_kernel, state + state, keys(5 * HALF) + keys(8 * HALF), 7 * unit,
+        sc, q, q_other, message, pas, p[1], p[2], p[3], far)
+    late, *now = lax.optimization_barrier((message, *now))
+    now_p, now = now[:3], now[3:]
     r[2] = lax.ppermute(late, axes, STAGE_2[2])
-    now_p = call(passing_kernel, state, keys(5 * HALF), 3 * unit, sc_p, q, q_other, pas, p[1], p[2], p[3], far)
-    sc_m, now_p0 = lax.optimization_barrier((sc_p, now_p[0]))
-    now = call(middle_kernel, state, keys(16 * HALF), 8 * unit, sc_m, q, q_other, r[1], r[3], *now)
-    sc_l, now_0 = lax.optimization_barrier((sc_m, now[0]))
+    now = call(middle_kernel, state, keys(16 * HALF), 8 * unit, sc, q, q_other, r[1], r[3], *now)
+    sc_l, now_0 = lax.optimization_barrier((sc, now[0]))
     for s in (1, 2, 3):
         sink = jnp.where(x == s, r[s][8 * ROWS + META:], sink)
     pages = call(
@@ -338,7 +329,7 @@
             jax.ShapeDtypeStruct((ROWS, (GROUP + 1) * HD), BF16),
         ),
         keys(8 * HALF) + keys(HALF) + [pltpu.VMEM((ROWS, HD), F32)],
-        5 * unit, sc_l, q, q_other, r[2], sink, now_0, *now[1:], now_p0, *now_p[1:])
+        5 * unit, sc_l, q, q_other, r[2], sink, now_0, *now[1:], *now_p)
 
     got = lax.ppermute(send, "tp", CORE_SWAP)
     attn_out = call(

time: 72.3 us -> 79.9 us (1.11); the launches traced: 72.1 us -> 78.5 us
  local copies, waits for them, and re-layouts: 5.9 us -> 12 us
  waiting for transfers between devices: 4.07 us -> 10 us
  starting transfers between devices: 34.3 us -> 30.5 us
  Pallas kernels: 24.1 us -> 22.4 us
    unnamed x21 -> x33, local copies, waits for them, and re-layouts: 4.22 us -> 10.3 us
    ppermute x2, starting transfers between devices: 13.1 us -> 8.3 us  [the longest x1 7.92 us: shards(): lax.ppermute(jnp.concatenate([pas, message[-META:]]), 'ctx', FOUR_ON)[:ROWS]]
    ppermute x2, waiting for transfers between devices: 2.91 us -> 7.21 us  [the longest x1 6.28 us: shards(): theirs = lax.ppermute(message, 'ctx', Z_SWAP)]
    ppermute x3, starting transfers between devices: 4.92 us -> 7.38 us  [shards(): got = {s: lax.ppermute(message, axes, STAGE_1[s]) for s in (1, 3, 2)}]
    pallas_call x6 -> x5, Pallas kernels: 24.1 us -> 22.4 us  [call(): pl.pallas_call(kernel, out_shape=out_shape, in_specs=specs, out_specs=(VM...]
    ppermute x3, waiting for transfers between devices: 0.01 us -> 1.27 us  [shards(): lax.ppermute(jnp.where(y + s < 4, pas, far), 'ctx', Y_SHIFT[s])]
    ppermute x1, starting transfers between devices: 1.42 us -> 0.19 us  [shards(): r[2] = lax.ppermute(late, axes, STAGE_2[2])]
    ppermute x1, starting transfers between devices: 7.43 us -> 6.49 us  [shards(): got_pages = lax.ppermute(pages, 'tp', CORE_SWAP)]
  transfers between devices with their start and end apart: 15 -> 15, of which waited for: 2 -> 5; matrix products, arithmetic and copies ran while one was open for 4% -> 4% of each run, Pallas kernels for 30% -> 25%
where the time goes in v6:
time: 79.9 us; the launch traced here: 78.5 us
  starting transfers between devices  30.5 us (38%)
  Pallas kernels  22.4 us (28%)
  local copies, waits for them, and re-layouts  12 us (15%)
  waiting for transfers between devices  10 us (13%)
  other arithmetic  2.1 us (3%)
  between operations  1.54 us (2%)
    pallas_call x5, Pallas kernels, call(): pl.pallas_call(kernel, out_shape=out_shape, in_specs=specs, out_specs=(VM...  22.4 us
    unnamed x33, local copies, waits for them, and re-layouts  10.3 us
    ppermute x1, starting transfers between devices, shards(): lax.ppermute(jnp.concatenate([pas, message[-META:]]), 'ctx', FOUR_ON)[:ROWS]  7.92 us
    ppermute x3, starting transfers between devices, shards(): got = {s: lax.ppermute(message, axes, STAGE_1[s]) for s in (1, 3, 2)}  7.38 us
    ppermute x1, starting transfers between devices, shards(): got_pages = lax.ppermute(pages, 'tp', CORE_SWAP)  6.49 us
    ppermute x1, waiting for transfers between devices, shards(): theirs = lax.ppermute(message, 'ctx', Z_SWAP)  6.28 us
    ppermute x3, starting transfers between devices, shards(): lax.ppermute(jnp.where(y + s < 4, pas, far), 'ctx', Y_SHIFT[s])  4.38 us
    ppermute x2, starting transfers between devices, shards(): lax.ppermute(message, axes, STAGE_2[s])  2.75 us
  transfers between devices with their start and end apart: 15, of which 5 were waited for; matrix products, arithmetic and copies ran while one was open for 4% of the time, Pallas kernels for 25%

profile of v6, /device:TPU:33, one launch (start us, length us, event | category | flops | bytes accessed | tf_op | source)
XLA Modules:
  0.0 78.5 jit_solution(1787454589367258340)
XLA Ops:
  0.6 0.8 %fusion.12 = (bf16[128,128]{1,0:T(8,128)(2,1)S(1)}, bf16[128,128]{1,0:T(8,128)(2,1)S(1)}, bf16[128,128]{1,0:T(8,128)(2,1)S(1)}, bf16[128,128]{1,0:T(8,128)(2,1)S(1)}) fusion(bf16[256,128]{1,0:T(8,128)(2,1)} %param.6, bf16[256,128]{1,0:T(8,128)(2,1)} %param.7), kind=kLoop, calls=%fused_computation.42 | loop fusion | bytes 262144 | tf_op jit(solution)/shard_map/slice | solution.py:272
  1.5 0.8 collective-permute-start
  2.8 0.7 copy-done.14
  4.8 7.9 %collective-permute-start.2 = (bf16[272,128]{1,0:T(8,128)(2,1)S(1)}, bf16[272,128]{1,0:T(8,128)(2,1)S(1)}, u32[]{:S(2)}, u32[]{:S(2)}) collective-permute-start(bf16[272,128]{1,0:T(8,128)(2,1)S(1)} %pad_maximum_fusion.2), channel_id=1, source_target_pairs={{0,32},{8,40},{16,48},{24,56},{32,64},{40,72},{48,80},{56,88},{64,... | collective-permute-start | bytes 208904 | tf_op jit(solution)/shard_map/ppermute | solution.py:289
  13.1 0.9 %collective-permute-done.2 = bf16[272,128]{1,0:T(8,128)(2,1)S(1)} collective-permute-done((bf16[272,128]{1,0:T(8,128)(2,1)S(1)}, bf16[272,128]{1,0:T(8,128)(2,1)S(1)}, u32[]{:S(2)}, u32[]{:S(2)}) %collective-permute-start.2) | collective-permute-done | bytes 69664 | tf_op jit(solution)/shard_map/ppermute | solution.py:289
  14.1 6.3 %collective-permute-done.1 = bf16[400,128]{1,0:T(8,128)(2,1)S(1)} collective-permute-done((bf16[400,128]{1,0:T(8,128)(2,1)S(1)}, bf16[400,128]{1,0:T(8,128)(2,1)S(1)}, u32[]{:S(2)}, u32[]{:S(2)}) %collective-permute-start.1) | collective-permute-done | bytes 102432 | tf_op jit(solution)/shard_map/ppermute | solution.py:288
  20.5 1.3 %collective-permute-start.4 = (bf16[656,128]{1,0:T(8,128)(2,1)S(1)}, bf16[656,128]{1,0:T(8,128)(2,1)S(1)}, u32[]{:S(2)}, u32[]{:S(2)}) collective-permute-start(bf16[656,128]{1,0:T(8,128)(2,1)S(1)} %pad_maximum_fusion), channel_id=1, source_target_pairs={{0,8},{1,65},{2,10},{3,67},{4,12},{5,69},{6,14},{7,71},{8,16},{9,7... | collective-permute-start | bytes 503816 | tf_op jit(solution)/shard_map/ppermute | solution.py:298
  21.8 5.0 %collective-permute-start.5 = (bf16[656,128]{1,0:T(8,128)(2,1)S(1)}, bf16[656,128]{1,0:T(8,128)(2,1)S(1)}, u32[]{:S(2)}, u32[]{:S(2)}) collective-permute-start(bf16[656,128]{1,0:T(8,128)(2,1)S(1)} %pad_maximum_fusion), channel_id=1, source_target_pairs={{0,16},{1,129},{2,18},{3,131},{4,20},{5,133},{6,22},{7,135},{8,24}... | collective-permute-start | bytes 503816 | tf_op jit(solution)/shard_map/ppermute | solution.py:298
  26.8 1.1 %collective-permute-start.6 = (bf16[656,128]{1,0:T(8,128)(2,1)S(1)}, bf16[656,128]{1,0:T(8,128)(2,1)S(1)}, u32[]{:S(2)}, u32[]{:S(2)}) collective-permute-start(bf16[656,128]{1,0:T(8,128)(2,1)S(1)} %pad_maximum_fusion), channel_id=1, source_target_pairs={{0,24},{1,193},{2,26},{3,195},{4,28},{5,197},{6,30},{7,199},{8,0},... | collective-permute-start | bytes 503816 | tf_op jit(solution)/shard_map/ppermute | solution.py:298
  28.3 0.6 broadcast_select_fusion
  28.9 2.9 %collective-permute-start.10 = (bf16[256,128]{1,0:T(8,128)(2,1)}, bf16[256,128]{1,0:T(8,128)(2,1)S(1)}, u32[]{:S(2)}, u32[]{:S(2)}) collective-permute-start(bf16[256,128]{1,0:T(8,128)(2,1)} %get-tuple-element.62), channel_id=1, source_target_pairs={{0,16},{8,24},{16,0},{24,8},{32,48},{40,56},{48,32},{56,40},{64,80... | collective-permute-start | bytes 196616 | tf_op jit(solution)/shard_map/ppermute | solution.py:300
  31.8 0.8 collective-permute-start.11
  32.6 0.7 collective-permute-start.9
  34.0 2.3 %collective-permute-start.8 = (bf16[2192,128]{1,0:T(8,128)(2,1)S(1)}, bf16[2192,128]{1,0:T(8,128)(2,1)S(1)}, u32[]{:S(2)}, u32[]{:S(2)}) collective-permute-start(bf16[2192,128]{1,0:T(8,128)(2,1)S(1)} %get-tuple-element.46.here.r0), channel_id=1, source_target_pairs={{0,192},{1,25},{2,194},{3,27},{4,196},{5,29},{6,198},{7,31},{8,200... | collective-permute-start | bytes 1683464 | tf_op jit(solution)/shard_map/ppermute | solution.py:307
  36.4 1.3 %collective-permute-done.9.p1 = bf16[256,128]{1,0:T(8,128)(2,1)S(1)} collective-permute-done((bf16[256,128]{1,0:T(8,128)(2,1)S(1)}, bf16[256,128]{1,0:T(8,128)(2,1)S(1)}, u32[]{:S(2)}, u32[]{:S(2)}) %collective-permute-start.9) | collective-permute-done | bytes 65568 | tf_op jit(solution)/shard_map/ppermute | solution.py:300
  37.6 6.6 %shard_map.68 = (f32[8,256,128]{2,1,0:T(8,128)S(1)}, f32[8,256,128]{2,1,0:T(8,128)S(1)}, f32[8,256,128]{2,1,0:T(8,128)S(1)}, f32[8,256,128]{2,1,0:T(8,128)S(1)},...) custom-call(s32[8]{0:T(128)S(1)} %stack.33.sc, bf16[256,1024]{1,0:T(8,128)(2,1)S(1)} %copy-done, ...), custom_call_target="tpu_custom_call" | custom-call | flops 3758096384 | bytes 4194304 | tf_op jit(solution)/shard_map/pallas_call | solution.py:249
  44.3 1.0 %copy-done.1 = f32[8,256,128]{2,1,0:T(8,128)} copy-done((f32[8,256,128]{2,1,0:T(8,128)}, f32[8,256,128]{2,1,0:T(8,128)S(1)}, u32[]{:S(2)}) %copy-start.1) | copy-done | bytes 1048600
  45.3 1.0 %copy-done.3 = f32[8,256,128]{2,1,0:T(8,128)} copy-done((f32[8,256,128]{2,1,0:T(8,128)}, f32[8,256,128]{2,1,0:T(8,128)S(1)}, u32[]{:S(2)}) %copy-start.3) | copy-done | bytes 1048600
  46.2 1.0 %copy-done.5 = f32[8,256,128]{2,1,0:T(8,128)} copy-done((f32[8,256,128]{2,1,0:T(8,128)}, f32[8,256,128]{2,1,0:T(8,128)S(1)}, u32[]{:S(2)}) %copy-start.5) | copy-done | bytes 1048600
  47.2 1.0 %copy-done.7 = f32[8,256,128]{2,1,0:T(8,128)} copy-done((f32[8,256,128]{2,1,0:T(8,128)}, f32[8,256,128]{2,1,0:T(8,128)S(1)}, u32[]{:S(2)}) %copy-start.7) | copy-done | bytes 1048600
  48.2 1.0 %copy-done.9 = f32[8,256,128]{2,1,0:T(8,128)} copy-done((f32[8,256,128]{2,1,0:T(8,128)}, f32[8,256,128]{2,1,0:T(8,128)S(1)}, u32[]{:S(2)}) %copy-start.9) | copy-done | bytes 1048600
  49.2 1.0 %copy-done.11 = f32[8,256,128]{2,1,0:T(8,128)} copy-done((f32[8,256,128]{2,1,0:T(8,128)}, f32[8,256,128]{2,1,0:T(8,128)S(1)}, u32[]{:S(2)}) %copy-start.11) | copy-done | bytes 1048600
  50.4 1.2 %copy-done.8 = f32[8,256,128]{2,1,0:T(8,128)S(1)} copy-done((f32[8,256,128]{2,1,0:T(8,128)S(1)}, f32[8,256,128]{2,1,0:T(8,128)}, u32[]{:S(2)}) %copy-start.8) | copy-done | bytes 1048600
  51.7 1.2 %copy-done.10 = f32[8,256,128]{2,1,0:T(8,128)S(1)} copy-done((f32[8,256,128]{2,1,0:T(8,128)S(1)}, f32[8,256,128]{2,1,0:T(8,128)}, u32[]{:S(2)}) %copy-start.10) | copy-done | bytes 1048600
  52.9 1.2 %copy-done.12 = f32[8,256,128]{2,1,0:T(8,128)S(1)} copy-done((f32[8,256,128]{2,1,0:T(8,128)S(1)}, f32[8,256,128]{2,1,0:T(8,128)}, u32[]{:S(2)}) %copy-start.12) | copy-done | bytes 1048600
  54.1 6.9 %shard_map.69 = (f32[8,256,128]{2,1,0:T(8,128)S(1)}, f32[8,256,128]{2,1,0:T(8,128)S(1)}, f32[8,256,128]{2,1,0:T(8,128)S(1)}) custom-call(s32[8]{0:T(128)S(1)} %stack.33.sc, bf16[256,1024]{1,0:T(8,128)(2,1)S(1)} %copy-done, bf16[256,1024]{1,0:T(8,128)(2,1)S(1)} %collective-permute-done.3.q_other, bf16[2192,128]{1,0:T(8,128)(2,1)S(1)} %collective-permute-done.7.r1, ...), custom_call_target="tpu_custom_call" | custom-call | flops 4294967296 | bytes 4194304 | tf_op jit(solution)/shard_map/pallas_call | solution.py:249
  61.0 1.2 %shard_map.72 = bf16[32,32,256]{2,1,0:T(8,128)(2,1)S(1)} custom-call(s32[8]{0:T(128)S(1)} %stack.33.sc, bf16[2192,128]{1,0:T(8,128)(2,1)S(1)} %get-tuple-element.46.here.r0, bf16[2192,128]{1,0:T(8,128)(2,1)S(1)} %collective-permute-done.7.r1, bf16[2192,128]{1,0:T(8,128)(2,1)S(1)} %collective-permute-done.12.r2, bf16[2192,128]{1,0:T(8,128)(2,1)S(1)} %collective-permute-done.8.r3), custom_call_target="tpu_custom_call" | custom-call | flops 134217728 | bytes 4194304 | tf_op jit(solution)/shard_map/pallas_call | solution.py:249
  62.2 6.5 %collective-permute-start.14 = (bf16[32,32,256]{2,1,0:T(8,128)(2,1)S(1)}, bf16[32,32,256]{2,1,0:T(8,128)(2,1)S(1)}, u32[]{:S(2)}, u32[]{:S(2)}) collective-permute-start(bf16[32,32,256]{2,1,0:T(8,128)(2,1)S(1)} %shard_map.72), channel_id=1, source_target_pairs={{0,1},{1,0},{2,3},{3,2},{4,5},{5,4},{6,7},{7,6},{8,9},{9,8},{10,11... | collective-permute-start | bytes 1572872 | tf_op jit(solution)/shard_map/ppermute | solution.py:323
  68.8 6.4 %shard_map.70 = (bf16[256,1024]{1,0:T(8,128)(2,1)S(1)}, f32[256,128]{1,0:T(8,128)S(1)}, bf16[256,1152]{1,0:T(8,128)(2,1)S(1)}) custom-call(s32[8]{0:T(128)S(1)} %stack.33.sc, bf16[256,1024]{1,0:T(8,128)(2,1)S(1)} %copy-done, bf16[256,1024]{1,0:T(8,128)(2,1)S(1)} %collective-permute-done.3.q_other, bf16[2192,128]{1,0:T(8,128)(2,1)S(1)} %collective-permute-done.12.r2, ...), custom_call_target="tpu_custom_call" | custom-call | flops 2684354560 | bytes 4194304 | tf_op jit(solution)/shard_map/pallas_call | solution.py:249
  75.3 0.8 %add_select_fusion = bf16[32,32,256]{2,1,0:T(8,128)(2,1)} fusion(bf16[32,32,256]{2,1,0:T(8,128)(2,1)S(1)} %shard_map.72, bf16[32,32,256]{2,1,0:T(8,128)(2,1)S(1)} %collective-permute-done.14, pred[]{:T(512)} %bitcast.6), kind=kLoop, calls=%fused_computation | loop fusion | flops 524288 | bytes 1572865 | tf_op jit(solution)/shard_map/jit(_where)/select_n | solution.py:337
  76.1 1.1 %collective-permute-done.13.got = bf16[256,1152]{1,0:T(8,128)(2,1)S(1)} collective-permute-done((bf16[256,1152]{1,0:T(8,128)(2,1)S(1)}, bf16[256,1152]{1,0:T(8,128)(2,1)S(1)}, u32[]{:S(2)}, u32[]{:S(2)}) %collective-permute-start.13) | collective-permute-done | bytes 589856 | tf_op jit(solution)/shard_map/ppermute | solution.py:334
  77.3 1.3 %shard_map.71 = bf16[256,1024]{1,0:T(8,128)(2,1)} custom-call(bf16[256,1024]{1,0:T(8,128)(2,1)S(1)} %get-tuple-element.53.keep, f32[256,128]{1,0:T(8,128)S(1)} %get-tuple-element.54.keep_lse, bf16[256,1152]{1,0:T(8,128)(2,1)S(1)} %collective-permute-done.13.got), custom_call_target="tpu_custom_call" | custom-call | flops 134217728 | bytes 4194304 | tf_op jit(solution)/shard_map/pallas_call | solution.py:249
  (63 shorter events, 3.2 us)
Async XLA Ops:
  1.5 0.9 %copy-start.13 = (s32[16]{0:T(128)S(1)}, s32[16]{0:T(128)}, u32[]{:S(2)}) copy-start(s32[16]{0:T(128)} %param.9) | copy-start | bytes 196
  1.5 3.2 %collective-permute-start = (bf16[256,128]{1,0:T(8,128)(2,1)S(1)}, bf16[256,128]{1,0:T(8,128)(2,1)S(1)}, u32[]{:S(2)}, u32[]{:S(2)}) collective-permute-start(bf16[256,128]{1,0:T(8,128)(2,1)S(1)} %broadcast_select_fusion.3), channel_id=1, source_target_pairs={{0,1},{1,0},{2,3},{3,2},{4,5},{5,4},{6,7},{7,6},{8,9},{9,8},{10,11... | collective-permute-start | bytes 196616 | tf_op jit(solution)/shard_map/ppermute | solution.py:275
  2.3 18.1 %collective-permute-start.3 = (bf16[256,1024]{1,0:T(8,128)(2,1)}, bf16[256,1024]{1,0:T(8,128)(2,1)S(1)}, u32[]{:S(2)}, u32[]{:S(2)}) collective-permute-start(bf16[256,1024]{1,0:T(8,128)(2,1)} %q_own.5), channel_id=1, source_target_pairs={{0,1},{1,0},{2,3},{3,2},{4,5},{5,4},{6,7},{7,6},{8,9},{9,8},{10,11... | collective-permute-start | bytes 1572872 | tf_op jit(solution)/shard_map/ppermute | solution.py:276
  2.8 0.7 copy-start.14
  4.8 9.3 %collective-permute-start.2 = (bf16[272,128]{1,0:T(8,128)(2,1)S(1)}, bf16[272,128]{1,0:T(8,128)(2,1)S(1)}, u32[]{:S(2)}, u32[]{:S(2)}) collective-permute-start(bf16[272,128]{1,0:T(8,128)(2,1)S(1)} %pad_maximum_fusion.2), channel_id=1, source_target_pairs={{0,32},{8,40},{16,48},{24,56},{32,64},{40,72},{48,80},{56,88},{64,... | collective-permute-start | bytes 208904 | tf_op jit(solution)/shard_map/ppermute | solution.py:289
  12.7 7.6 %collective-permute-start.1 = (bf16[400,128]{1,0:T(8,128)(2,1)S(1)}, bf16[400,128]{1,0:T(8,128)(2,1)S(1)}, u32[]{:S(2)}, u32[]{:S(2)}) collective-permute-start(bf16[400,128]{1,0:T(8,128)(2,1)S(1)} %pad_maximum_fusion.1), channel_id=1, source_target_pairs={{0,32},{8,40},{16,48},{24,56},{32,0},{40,8},{48,16},{56,24},{64,96... | collective-permute-start | bytes 307208 | tf_op jit(solution)/shard_map/ppermute | solution.py:288
  20.5 7.8 %collective-permute-start.4 = (bf16[656,128]{1,0:T(8,128)(2,1)S(1)}, bf16[656,128]{1,0:T(8,128)(2,1)S(1)}, u32[]{:S(2)}, u32[]{:S(2)}) collective-permute-start(bf16[656,128]{1,0:T(8,128)(2,1)S(1)} %pad_maximum_fusion), channel_id=1, source_target_pairs={{0,8},{1,65},{2,10},{3,67},{4,12},{5,69},{6,14},{7,71},{8,16},{9,7... | collective-permute-start | bytes 503816 | tf_op jit(solution)/shard_map/ppermute | solution.py:298
  21.8 11.5 %collective-permute-start.5 = (bf16[656,128]{1,0:T(8,128)(2,1)S(1)}, bf16[656,128]{1,0:T(8,128)(2,1)S(1)}, u32[]{:S(2)}, u32[]{:S(2)}) collective-permute-start(bf16[656,128]{1,0:T(8,128)(2,1)S(1)} %pad_maximum_fusion), channel_id=1, source_target_pairs={{0,16},{1,129},{2,18},{3,131},{4,20},{5,133},{6,22},{7,135},{8,24}... | collective-permute-start | bytes 503816 | tf_op jit(solution)/shard_map/ppermute | solution.py:298
  26.8 6.6 %collective-permute-start.6 = (bf16[656,128]{1,0:T(8,128)(2,1)S(1)}, bf16[656,128]{1,0:T(8,128)(2,1)S(1)}, u32[]{:S(2)}, u32[]{:S(2)}) collective-permute-start(bf16[656,128]{1,0:T(8,128)(2,1)S(1)} %pad_maximum_fusion), channel_id=1, source_target_pairs={{0,24},{1,193},{2,26},{3,195},{4,28},{5,197},{6,30},{7,199},{8,0},... | collective-permute-start | bytes 503816 | tf_op jit(solution)/shard_map/ppermute | solution.py:298
  28.9 7.4 %collective-permute-start.10 = (bf16[256,128]{1,0:T(8,128)(2,1)}, bf16[256,128]{1,0:T(8,128)(2,1)S(1)}, u32[]{:S(2)}, u32[]{:S(2)}) collective-permute-start(bf16[256,128]{1,0:T(8,128)(2,1)} %get-tuple-element.62), channel_id=1, source_target_pairs={{0,16},{8,24},{16,0},{24,8},{32,48},{40,56},{48,32},{56,40},{64,80... | collective-permute-start | bytes 196616 | tf_op jit(solution)/shard_map/ppermute | solution.py:300
  31.8 4.5 %collective-permute-start.11 = (bf16[256,128]{1,0:T(8,128)(2,1)S(1)}, bf16[256,128]{1,0:T(8,128)(2,1)S(1)}, u32[]{:S(2)}, u32[]{:S(2)}) collective-permute-start(bf16[256,128]{1,0:T(8,128)(2,1)S(1)} %get-tuple-element.61), channel_id=1, source_target_pairs={{0,24},{8,0},{16,8},{24,16},{32,56},{40,32},{48,40},{56,48},{64,88... | collective-permute-start | bytes 196616 | tf_op jit(solution)/shard_map/ppermute | solution.py:300
  32.6 5.0 %collective-permute-start.9 = (bf16[256,128]{1,0:T(8,128)(2,1)S(1)}, bf16[256,128]{1,0:T(8,128)(2,1)S(1)}, u32[]{:S(2)}, u32[]{:S(2)}) collective-permute-start(bf16[256,128]{1,0:T(8,128)(2,1)S(1)} %get-tuple-element.63), channel_id=1, source_target_pairs={{0,8},{8,16},{16,24},{24,0},{32,40},{40,48},{48,56},{56,32},{64,72... | collective-permute-start | bytes 196616 | tf_op jit(solution)/shard_map/ppermute | solution.py:300
  33.3 4.3 %copy-start = (bf16[256,1024]{1,0:T(8,128)(2,1)S(1)}, bf16[256,1024]{1,0:T(8,128)(2,1)}, u32[]{:S(2)}) copy-start(bf16[256,1024]{1,0:T(8,128)(2,1)} %q_own.5) | copy-start | bytes 1572868
  33.5 16.9 %collective-permute-start.7 = (bf16[2192,128]{1,0:T(8,128)(2,1)S(1)}, bf16[2192,128]{1,0:T(8,128)(2,1)S(1)}, u32[]{:S(2)}, u32[]{:S(2)}) collective-permute-start(bf16[2192,128]{1,0:T(8,128)(2,1)S(1)} %get-tuple-element.46.here.r0), channel_id=1, source_target_pairs={{0,64},{1,9},{2,66},{3,11},{4,68},{5,13},{6,70},{7,15},{8,72},{9,1... | collective-permute-start | bytes 1683464 | tf_op jit(solution)/shard_map/ppermute | solution.py:307
  34.0 16.4 %collective-permute-start.8 = (bf16[2192,128]{1,0:T(8,128)(2,1)S(1)}, bf16[2192,128]{1,0:T(8,128)(2,1)S(1)}, u32[]{:S(2)}, u32[]{:S(2)}) collective-permute-start(bf16[2192,128]{1,0:T(8,128)(2,1)S(1)} %get-tuple-element.46.here.r0), channel_id=1, source_target_pairs={{0,192},{1,25},{2,194},{3,27},{4,196},{5,29},{6,198},{7,31},{8,200... | collective-permute-start | bytes 1683464 | tf_op jit(solution)/shard_map/ppermute | solution.py:307
  44.3 1.0 %copy-start.1 = (f32[8,256,128]{2,1,0:T(8,128)}, f32[8,256,128]{2,1,0:T(8,128)S(1)}, u32[]{:S(2)}) copy-start(f32[8,256,128]{2,1,0:T(8,128)S(1)} %get-tuple-element.50.mp_in) | copy-start | bytes 3145732
  45.3 1.0 %copy-start.3 = (f32[8,256,128]{2,1,0:T(8,128)}, f32[8,256,128]{2,1,0:T(8,128)S(1)}, u32[]{:S(2)}) copy-start(f32[8,256,128]{2,1,0:T(8,128)S(1)} %get-tuple-element.51.lp_in) | copy-start | bytes 3145732
  46.2 1.0 %copy-start.5 = (f32[8,256,128]{2,1,0:T(8,128)}, f32[8,256,128]{2,1,0:T(8,128)S(1)}, u32[]{:S(2)}) copy-start(f32[8,256,128]{2,1,0:T(8,128)S(1)} %get-tuple-element.52.op_in) | copy-start | bytes 3145732
  47.2 1.0 %copy-start.7 = (f32[8,256,128]{2,1,0:T(8,128)}, f32[8,256,128]{2,1,0:T(8,128)S(1)}, u32[]{:S(2)}) copy-start(f32[8,256,128]{2,1,0:T(8,128)S(1)} %get-tuple-element.41.m_in) | copy-start | bytes 3145732
  48.2 1.0 %copy-start.9 = (f32[8,256,128]{2,1,0:T(8,128)}, f32[8,256,128]{2,1,0:T(8,128)S(1)}, u32[]{:S(2)}) copy-start(f32[8,256,128]{2,1,0:T(8,128)S(1)} %get-tuple-element.42.l_in) | copy-start | bytes 3145732
  49.2 1.0 %copy-start.11 = (f32[8,256,128]{2,1,0:T(8,128)}, f32[8,256,128]{2,1,0:T(8,128)S(1)}, u32[]{:S(2)}) copy-start(f32[8,256,128]{2,1,0:T(8,128)S(1)} %get-tuple-element.43.o_in) | copy-start | bytes 3145732
  50.2 10.8 %collective-permute-start.12 = (bf16[2192,128]{1,0:T(8,128)(2,1)S(1)}, bf16[2192,128]{1,0:T(8,128)(2,1)S(1)}, u32[]{:S(2)}, u32[]{:S(2)}) collective-permute-start(bf16[2192,128]{1,0:T(8,128)(2,1)S(1)} %get-tuple-element.46.here.r0), channel_id=1, source_target_pairs={{0,128},{1,17},{2,130},{3,19},{4,132},{5,21},{6,134},{7,23},{8,136... | collective-permute-start | bytes 1683464 | tf_op jit(solution)/shard_map/ppermute | solution.py:315
  50.4 1.2 %copy-start.8 = (f32[8,256,128]{2,1,0:T(8,128)S(1)}, f32[8,256,128]{2,1,0:T(8,128)}, u32[]{:S(2)}) copy-start(f32[8,256,128]{2,1,0:T(8,128)} %copy-done.7) | copy-start | bytes 3145732
  51.7 1.2 %copy-start.10 = (f32[8,256,128]{2,1,0:T(8,128)S(1)}, f32[8,256,128]{2,1,0:T(8,128)}, u32[]{:S(2)}) copy-start(f32[8,256,128]{2,1,0:T(8,128)} %copy-done.9) | copy-start | bytes 3145732
  52.9 1.2 %copy-start.12 = (f32[8,256,128]{2,1,0:T(8,128)S(1)}, f32[8,256,128]{2,1,0:T(8,128)}, u32[]{:S(2)}) copy-start(f32[8,256,128]{2,1,0:T(8,128)} %copy-done.11) | copy-start | bytes 3145732
  54.1 14.7 %copy-start.6 = (f32[8,256,128]{2,1,0:T(8,128)S(1)}, f32[8,256,128]{2,1,0:T(8,128)}, u32[]{:S(2)}) copy-start(f32[8,256,128]{2,1,0:T(8,128)} %copy-done.5) | copy-start | bytes 3145732
  61.0 7.7 %copy-start.2 = (f32[8,256,128]{2,1,0:T(8,128)S(1)}, f32[8,256,128]{2,1,0:T(8,128)}, u32[]{:S(2)}) copy-start(f32[8,256,128]{2,1,0:T(8,128)} %copy-done.1) | copy-start | bytes 3145732
  61.0 7.7 %copy-start.4 = (f32[8,256,128]{2,1,0:T(8,128)S(1)}, f32[8,256,128]{2,1,0:T(8,128)}, u32[]{:S(2)}) copy-start(f32[8,256,128]{2,1,0:T(8,128)} %copy-done.3) | copy-start | bytes 3145732
  62.2 13.0 %collective-permute-start.14 = (bf16[32,32,256]{2,1,0:T(8,128)(2,1)S(1)}, bf16[32,32,256]{2,1,0:T(8,128)(2,1)S(1)}, u32[]{:S(2)}, u32[]{:S(2)}) collective-permute-start(bf16[32,32,256]{2,1,0:T(8,128)(2,1)S(1)} %shard_map.72), channel_id=1, source_target_pairs={{0,1},{1,0},{2,3},{3,2},{4,5},{5,4},{6,7},{7,6},{8,9},{9,8},{10,11... | collective-permute-start | bytes 1572872 | tf_op jit(solution)/shard_map/ppermute | solution.py:323
  75.2 2.1 %collective-permute-start.13 = (bf16[256,1152]{1,0:T(8,128)(2,1)S(1)}, bf16[256,1152]{1,0:T(8,128)(2,1)S(1)}, u32[]{:S(2)}, u32[]{:S(2)}) collective-permute-start(bf16[256,1152]{1,0:T(8,128)(2,1)S(1)} %get-tuple-element.55), channel_id=1, source_target_pairs={{0,1},{1,0},{2,3},{3,2},{4,5},{5,4},{6,7},{7,6},{8,9},{9,8},{10,11... | collective-permute-start | bytes 1769480 | tf_op jit(solution)/shard_map/ppermute | solution.py:334

commit v7 on v5

--- a/solution.py
+++ b/solution.py
@@ -30,7 +30,7 @@
 CHIPS = [(x, z, y) for x in range(4) for z in range(2) for y in range(4)]
 CORE_SWAP = [(i, i ^ 1) for i in range(8)]
 Z_SWAP = [(ctx_of(x, z, y), ctx_of(x, z + 1, y)) for x, z, y in CHIPS]
-FOUR_ON = [(i, i + 4) for i in range(28)]
+X_STEP = [(ctx_of(x, 0, y), ctx_of(x + 1, 0, y)) for x in range(3) for y in range(4)]
 Y_SHIFT = {s: [(ctx_of(x, z, y), ctx_of(x, z, y + s)) for x, z, y in CHIPS] for s in (1, 2, 3)}
 
 
@@ -110,7 +110,17 @@
     return jnp.concatenate([q, one], axis=1)
 
 
-def near_kernel(sc, q_own, q_other, here, m_out, l_out, o_out, kr, vr):
+def pack(m, l):
+    return jnp.where(iota((ROWS, HD), 1) < HD // 2, m, l)
+
+
+def unpack(both):
+    low = iota((ROWS, HD), 1) < HD // 2
+    turned = pltpu.roll(both, HD // 2, 1)
+    return jnp.where(low, both, turned), jnp.where(low, turned, both)
+
+
+def near_kernel(sc, q_own, q_other, here, ml_out, o_out, kr, vr):
     core, is_r = sc[3], sc[5]
     put_ranges(kr, vr, 0, here)
     put_bias(kr, vr, range_bias(sc, (0,)))
@@ -122,49 +132,7 @@
         state = [fold(None, q[u], kr[0:CHUNK, :], vr[0:CHUNK, :], left=own) for u in range(WIDE)]
         state = [fold(state[u], q[u], kr[CHUNK:, :], vr[CHUNK:, :]) for u in range(WIDE)]
         for u in range(WIDE):
-            m_out[at[u]], l_out[at[u]], o_out[at[u]] = state[u]
-
-    for i in range(GROUP // WIDE):
-        heads(i)
-
-
-def passing_kernel(sc, q_own, q_other, pas, p1, p2, p3, far, m_out, l_out, o_out, kp, vp):
-    core, c, is_r = sc[3], sc[4], sc[5]
-    for n, ref in enumerate((pas, p1, p2, p3, far)):
-        put_keys(kp, vp, n * HALF, ref, 0, HALF, HALF)
-    put_bias(kp, vp, jnp.where((iota((5 * HALF, HD), 0) >> 7) <= c, 0.0, NEG))
-    row = iota((ROWS, HD), 0)
-    key = core * HALF + iota((ROWS, HD), 1)
-    own = jnp.where(key > row, NEG, 0.0)
-    edge = jnp.where(key <= row, NEG, 0.0)
-
-    def heads(i):
-        at = [WIDE * i + u for u in range(WIDE)]
-        q = [load_head(q_other, q_own, is_r, a) for a in at]
-        state = [fold(None, q[u], kp[0:3 * HALF, :], vp[0:3 * HALF, :], left=own) for u in range(WIDE)]
-        state = [fold(state[u], q[u], kp[3 * HALF:, :], vp[3 * HALF:, :], right=edge) for u in range(WIDE)]
-        for u in range(WIDE):
-            m_out[at[u]], l_out[at[u]], o_out[at[u]] = state[u]
-
-    for i in range(GROUP // WIDE):
-        heads(i)
-
-
-def middle_kernel(sc, q_own, q_other, r1, r3, m_in, l_in, o_in, m_out, l_out, o_out, kr, vr):
-    is_r = sc[5]
-    put_ranges(kr, vr, 0, r1)
-    put_ranges(kr, vr, 8 * HALF, r3)
-    put_bias(kr, vr, range_bias(sc, (1, 3)))
-
-    def heads(i):
-        at = [WIDE * i + u for u in range(WIDE)]
-        q = [load_head(q_own, q_other, is_r, a) for a in at]
-        state = [(m_in[a], l_in[a], o_in[a]) for a in at]
-        for n in range(4):
-            rows = slice(n * CHUNK, (n + 1) * CHUNK)
-            state = [fold(state[u], q[u], kr[rows, :], vr[rows, :]) for u in range(WIDE)]
-        for u in range(WIDE):
-            m_out[at[u]], l_out[at[u]], o_out[at[u]] = state[u]
+            ml_out[at[u]], o_out[at[u]] = pack(*state[u][:2]), state[u][2]
 
     for i in range(GROUP // WIDE):
         heads(i)
@@ -175,17 +143,25 @@
     return o / l, m * SCALE + jnp.log2(l)
 
 
-def last_kernel(sc, q_own, q_other, r2, sink, m_in, l_in, o_in, mp_in, lp_in, op_in, keep, keep_lse, send,
-                kr, vr, ks, vs, lse_s):
+def rest_kernel(sc, q_own, q_other, r1, r3, r2, sink, pas, p1, p2, p3, far, ml_in, o_in, keep, keep_lse, send,
+                kr, vr, kp, vp, lse_s):
     core, c, is_r = sc[3], sc[4], sc[5]
-    put_ranges(kr, vr, 0, r2)
-    put_bias(kr, vr, range_bias(sc, (2,)))
-    ks[...] = jnp.zeros((HALF, 2 * HD), BF16)
-    vs[...] = jnp.zeros((HALF, 2 * HD), BF16)
-    put_keys(ks, vs, 0, sink, 0, SINK, SINK)
-    put_bias(ks, vs, jnp.zeros((HALF, HD), F32))
+    for n, ref in enumerate((r1, r3, r2)):
+        put_ranges(kr, vr, n * 8 * HALF, ref)
+    put_bias(kr, vr, range_bias(sc, (1, 3, 2)))
+    for n, ref in enumerate((pas, p1, p2, p3)):
+        put_keys(kp, vp, n * HALF, ref, 0, HALF, HALF)
+    kp[4 * HALF:5 * HALF, :] = jnp.zeros((HALF, 2 * HD), BF16)
+    vp[4 * HALF:5 * HALF, :] = jnp.zeros((HALF, 2 * HD), BF16)
+    put_keys(kp, vp, 4 * HALF, sink, 0, SINK, SINK)
+    put_keys(kp, vp, 5 * HALF, far, 0, HALF, HALF)
+    slot = iota((6 * HALF, HD), 0) >> 7
+    put_bias(kp, vp, jnp.where((slot - (slot >> 2) <= c) | (slot == 4), 0.0, NEG))
     row = iota((ROWS, HD), 0)
     lane = iota((ROWS, HD), 1)
+    key = core * HALF + lane
+    own = jnp.where(key > row, NEG, 0.0)
+    edge = jnp.where(key <= row, NEG, 0.0)
     seen = (core == 0) & (lane < SINK) & (c * ROWS + row - lane >= RECENT)
     sink_bias = jnp.where(seen, 0.0, NEG)
     lse_s[...] = jnp.zeros((ROWS, HD), F32)
@@ -195,11 +171,14 @@
         at = [WIDE * i + u for u in range(WIDE)]
         qp = [load_head(q_other, q_own, is_r, a) for a in at]
         qr = [load_head(q_own, q_other, is_r, a) for a in at]
-        sr = [(m_in[a], l_in[a], o_in[a]) for a in at]
-        sp = [(mp_in[a], lp_in[a], op_in[a]) for a in at]
-        sr = [fold(sr[u], qr[u], kr[0:CHUNK, :], vr[0:CHUNK, :]) for u in range(WIDE)]
-        sp = [fold(sp[u], qp[u], ks[...], vs[...], left=sink_bias) for u in range(WIDE)]
-        sr = [fold(sr[u], qr[u], kr[CHUNK:, :], vr[CHUNK:, :]) for u in range(WIDE)]
+        sr = [(*unpack(ml_in[a]), o_in[a]) for a in at]
+        for n in range(6):
+            rows = slice(n * CHUNK, (n + 1) * CHUNK)
+            sr = [fold(sr[u], qr[u], kr[rows, :], vr[rows, :]) for u in range(WIDE)]
+            if n == 1:
+                sp = [fold(None, qp[u], kp[0:4 * HALF, :], vp[0:4 * HALF, :], left=own) for u in range(WIDE)]
+            if n == 3:
+                sp = [fold(sp[u], qp[u], kp[4 * HALF:, :], vp[4 * HALF:, :], left=sink_bias, right=edge) for u in range(WIDE)]
         for u in range(WIDE):
             cols = slice(at[u] * HD, (at[u] + 1) * HD)
             out_r, lse_r = finish(sr[u])
@@ -263,7 +242,7 @@
         in_specs=specs,
         out_specs=(VMEM_SPEC,) * len(out_shape) if many else VMEM_SPEC,
         scratch_shapes=scratch,
-        compiler_params=pltpu.CompilerParams(vmem_limit_bytes=24 * 1024 * 1024),
+        compiler_params=pltpu.CompilerParams(vmem_limit_bytes=16 * 1024 * 1024),
         cost_estimate=pl.CostEstimate(flops=flops, bytes_accessed=4 << 20, transcendentals=flops // 512),
     )(*operands)
 
@@ -294,51 +273,47 @@
     code = jnp.where(core == 0, code[:8], code[8:]).astype(BF16)
     meta = jnp.broadcast_to(jnp.repeat(code, PAGE)[None, :], (META, HD))
 
-    sink = jnp.concatenate([pas[:SINK], pas[HALF:HALF + SINK]])
-    theirs = lax.ppermute(jnp.concatenate([ret, sink, meta]), "ctx", Z_SWAP)
+    theirs = lax.ppermute(jnp.concatenate([ret, pas, meta]), "ctx", Z_SWAP)
     theirs, q_other = lax.optimization_barrier((theirs, q_other))
+    from_x = lax.ppermute(theirs[ROWS:2 * ROWS], "ctx", X_STEP)
     both = jnp.concatenate([ret, theirs[:ROWS]])
-    sink = jnp.where(z == 0, sink, theirs[ROWS:ROWS + 2 * SINK])
+    low = jnp.where(z == 0, pas, theirs[ROWS:2 * ROWS])
+    sink = jnp.concatenate([low[:SINK], low[HALF:HALF + SINK]])
     line = iota((META, HD), 0)
-    meta = jnp.where((line & 1) == 0, meta, theirs[ROWS + 2 * SINK:])
+    meta = jnp.where((line & 1) == 0, meta, theirs[2 * ROWS:])
 
     axes = ("ctx", "tp")
     message = jnp.concatenate([both, sink, meta])
     got = {s: lax.ppermute(message, axes, STAGE_1[s]) for s in (1, 3, 2)}
+    pas, from_x, got[1] = lax.optimization_barrier((pas, from_x, got[1]))
+    far = jnp.where(z == 1, theirs[ROWS:2 * ROWS], from_x)
+    p = {s: lax.ppermute(jnp.where(y + s < 4, pas, far), "ctx", Y_SHIFT[s]) for s in (1, 3, 2)}
+
     for s in (1, 2, 3):
         meta = jnp.where((line >> 1) == s, got[s][2 * ROWS + 2 * SINK:], meta)
         sink = jnp.where(y == s, got[s][2 * ROWS:2 * ROWS + 2 * SINK], sink)
     message = jnp.concatenate([both] + [got[s][:2 * ROWS] for s in (1, 2, 3)] + [meta, sink])
 
-    far = lax.ppermute(jnp.concatenate([pas, theirs[-META:]]), "ctx", FOUR_ON)[:ROWS]
-
-    r = {0: message} | {s: lax.ppermute(message, axes, STAGE_2[s]) for s in (1, 3)}
-    p = {s: lax.ppermute(jnp.where(y + s < 4, pas, far), "ctx", Y_SHIFT[s]) for s in (1, 3, 2)}
-
-    state = (jax.ShapeDtypeStruct((GROUP, ROWS, HD), F32),) * 3
+    r = {0: message} | {s: lax.ppermute(message, axes, STAGE_2[s]) for s in (1, 3, 2)}
+    state = (jax.ShapeDtypeStruct((GROUP, ROWS, HD), F32),) * 2
     unit = 2 * 2048 * 256 * 512
-    now = call(near_kernel, state, keys(8 * HALF), 4 * unit, sc, q, q_other, message)
-    late, sc_p, *now = lax.optimization_barrier((message, sc, *now))
-    r[2] = lax.ppermute(late, axes, STAGE_2[2])
-    now_p = call(passing_kernel, state, keys(5 * HALF), 3 * unit, sc_p, q, q_other, pas, p[1], p[2], p[3], far)
-    sc_m, now_p0 = lax.optimization_barrier((sc_p, now_p[0]))
-    now = call(middle_kernel, state, keys(16 * HALF), 8 * unit, sc_m, q, q_other, r[1], r[3], *now)
-    sc_l, now_0 = lax.optimization_barrier((sc_m, now[0]))
+    now_ml, now_o = call(near_kernel, state, keys(8 * HALF), 4 * unit, sc, q, q_other, message)
     for s in (1, 2, 3):
         sink = jnp.where(x == s, r[s][8 * ROWS + META:], sink)
+    sc_l, now_ml = lax.optimization_barrier((sc, now_ml))
     pages = call(
         pages_kernel, jax.ShapeDtypeStruct((32, 2 * PAGE, 2 * HD), BF16), [], unit // 4,
         sc_l, *[r[s] for s in range(4)])
     got_pages = lax.ppermute(pages, "tp", CORE_SWAP)
     keep, keep_lse, send = call(
-        last_kernel,
+        rest_kernel,
         (
             jax.ShapeDtypeStruct((ROWS, GROUP * HD), BF16),
             jax.ShapeDtypeStruct((ROWS, HD), F32),
             jax.ShapeDtypeStruct((ROWS, (GROUP + 1) * HD), BF16),
         ),
-        keys(8 * HALF) + keys(HALF) + [pltpu.VMEM((ROWS, HD), F32)],
-        5 * unit, sc_l, q, q_other, r[2], sink, now_0, *now[1:], now_p0, *now_p[1:])
+        keys(24 * HALF) + keys(6 * HALF) + [pltpu.VMEM((ROWS, HD), F32)],
+        16 * unit, sc_l, q, q_other, r[1], r[3], r[2], sink, pas, p[1], p[2], p[3], far, now_ml, now_o)
 
     got = lax.ppermute(send, "tp", CORE_SWAP)
     attn_out = call(

time: 72.3 us -> 71.1 us (0.983)
  waiting for transfers between devices: 4.07 us -> 15.9 us
  starting transfers between devices: 34.3 us -> 28.8 us
  Pallas kernels: 24.1 us -> 20.2 us
  local copies, waits for them, and re-layouts: 5.9 us -> 2.32 us
    ppermute x2 -> x3, waiting for transfers between devices: 0.01 us -> 5.45 us  [shards(): lax.ppermute(message, axes, STAGE_2[s])]
    ppermute x3 -> x2, starting transfers between devices: 14.5 us -> 9.2 us  [the longest x1 6.1 us: shards(): theirs = lax.ppermute(jnp.concatenate([ret, pas, meta]), 'ctx', Z_SWAP)]
    pallas_call x6 -> x4, Pallas kernels: 24.1 us -> 20.2 us  [call(): pl.pallas_call(kernel, out_shape=out_shape, in_specs=specs, out_specs=(VM...]
    ppermute x3 -> x2, waiting for transfers between devices: 2.91 us -> 6.48 us  [the longest x1 6.47 us: shards(): theirs = lax.ppermute(jnp.concatenate([ret, pas, meta]), 'ctx', Z_SWAP)]
    unnamed x21 -> x11, local copies, waits for them, and re-layouts: 4.22 us -> 0.66 us
    ppermute x3, waiting for transfers between devices: 0.01 us -> 3.21 us  [shards(): got = {s: lax.ppermute(message, axes, STAGE_1[s]) for s in (1, 3, 2)}]
    ppermute x1, starting transfers between devices: 7.43 us -> 5.71 us  [shards(): got_pages = lax.ppermute(pages, 'tp', CORE_SWAP)]
    ppermute x2 -> x3, starting transfers between devices: 2.9 us -> 4.27 us  [shards(): lax.ppermute(message, axes, STAGE_2[s])]
  transfers between devices with their start and end apart: 15 -> 15, of which waited for: 2 -> 5; matrix products, arithmetic and copies ran while one was open for 4% -> 3% of each run, Pallas kernels for 30% -> 27%
where the time goes in v7:
time: 71.1 us; the launch traced here: 70.3 us
  starting transfers between devices  28.8 us (41%)
  Pallas kernels  20.2 us (28%)
  waiting for transfers between devices  15.9 us (22%)
  local copies, waits for them, and re-layouts  2.32 us (3%)
  other arithmetic  1.52 us (2%)
  between operations  1.48 us (2%)
    pallas_call x4, Pallas kernels, call(): pl.pallas_call(kernel, out_shape=out_shape, in_specs=specs, out_specs=(VM...  20.2 us
    ppermute x1, waiting for transfers between devices, shards(): theirs = lax.ppermute(jnp.concatenate([ret, pas, meta]), 'ctx', Z_SWAP)  6.47 us
    ppermute x1, starting transfers between devices, shards(): theirs = lax.ppermute(jnp.concatenate([ret, pas, meta]), 'ctx', Z_SWAP)  6.1 us
    ppermute x1, starting transfers between devices, shards(): got_pages = lax.ppermute(pages, 'tp', CORE_SWAP)  5.71 us
    ppermute x3, waiting for transfers between devices, shards(): lax.ppermute(message, axes, STAGE_2[s])  5.45 us
    ppermute x3, starting transfers between devices, shards(): got = {s: lax.ppermute(message, axes, STAGE_1[s]) for s in (1, 3, 2)}  4.63 us
    ppermute x3, starting transfers between devices, shards(): lax.ppermute(message, axes, STAGE_2[s])  4.27 us
    ppermute x3, starting transfers between devices, shards(): lax.ppermute(jnp.where(y + s < 4, pas, far), 'ctx', Y_SHIFT[s])  3.68 us
  transfers between devices with their start and end apart: 15, of which 5 were waited for; matrix products, arithmetic and copies ran while one was open for 3% of the time, Pallas kernels for 27%

profile of v7, /device:TPU:33, one launch (start us, length us, event | category | flops | bytes accessed | tf_op | source)
XLA Modules:
  0.0 70.3 jit_solution(1033325884172567580)
XLA Ops:
  0.6 0.8 %fusion.11 = (bf16[128,128]{1,0:T(8,128)(2,1)S(1)}, bf16[128,128]{1,0:T(8,128)(2,1)S(1)}, bf16[128,128]{1,0:T(8,128)(2,1)S(1)}, bf16[128,128]{1,0:T(8,128)(2,1)S(1)}) fusion(bf16[256,128]{1,0:T(8,128)(2,1)} %param.6, bf16[256,128]{1,0:T(8,128)(2,1)} %param.7), kind=kLoop, calls=%fused_computation.46 | loop fusion | bytes 262144 | tf_op jit(solution)/shard_map/slice | solution.py:262
  1.5 0.8 %collective-permute-start = (bf16[256,128]{1,0:T(8,128)(2,1)S(1)}, bf16[256,128]{1,0:T(8,128)(2,1)S(1)}, u32[]{:S(2)}, u32[]{:S(2)}) collective-permute-start(bf16[256,128]{1,0:T(8,128)(2,1)S(1)} %broadcast_select_fusion.5), channel_id=1, source_target_pairs={{0,1},{1,0},{2,3},{3,2},{4,5},{5,4},{6,7},{7,6},{8,9},{9,8},{10,11... | collective-permute-start | bytes 196616 | tf_op jit(solution)/shard_map/ppermute | solution.py:265
  2.3 0.1 collective-permute-start.2
  2.4 0.2 convert_reduce_fusion
  2.7 0.1 broadcast_in_dim.19
  2.8 0.6 copy-done.2
  3.4 0.6 dynamic_slice.4
  4.7 6.1 %collective-permute-start.1 = (bf16[528,128]{1,0:T(8,128)(2,1)S(1)}, bf16[528,128]{1,0:T(8,128)(2,1)S(1)}, u32[]{:S(2)}, u32[]{:S(2)}) collective-permute-start(bf16[528,128]{1,0:T(8,128)(2,1)S(1)} %pad_maximum_fusion), channel_id=1, source_target_pairs={{0,32},{8,40},{16,48},{24,56},{32,0},{40,8},{48,16},{56,24},{64,96... | collective-permute-start | bytes 405512 | tf_op jit(solution)/shard_map/ppermute | solution.py:276
  10.8 6.5 %collective-permute-done.1 = bf16[528,128]{1,0:T(8,128)(2,1)S(1)} collective-permute-done((bf16[528,128]{1,0:T(8,128)(2,1)S(1)}, bf16[528,128]{1,0:T(8,128)(2,1)S(1)}, u32[]{:S(2)}, u32[]{:S(2)}) %collective-permute-start.1) | collective-permute-done | bytes 135200 | tf_op jit(solution)/shard_map/ppermute | solution.py:276
  17.4 1.2 %collective-permute-start.4 = (bf16[656,128]{1,0:T(8,128)(2,1)S(1)}, bf16[656,128]{1,0:T(8,128)(2,1)S(1)}, u32[]{:S(2)}, u32[]{:S(2)}) collective-permute-start(bf16[656,128]{1,0:T(8,128)(2,1)S(1)} %constant_dynamic-update-slice_fusion), channel_id=1, source_target_pairs={{0,8},{1,65},{2,10},{3,67},{4,12},{5,69},{6,14},{7,71},{8,16},{9,7... | collective-permute-start | bytes 503816 | tf_op jit(solution)/shard_map/ppermute | solution.py:287
  18.7 3.1 %collective-permute-start.3 = (bf16[256,128]{1,0:T(8,128)(2,1)S(1)}, bf16[256,128]{1,0:T(8,128)(2,1)S(1)}, u32[]{:S(2)}, u32[]{:S(2)}) collective-permute-start(bf16[256,128]{1,0:T(8,128)(2,1)S(1)} %get-tuple-element.35), channel_id=1, source_target_pairs={{0,64},{8,72},{16,80},{24,88},{64,128},{72,136},{80,144},{88,152},... | collective-permute-start | bytes 196616 | tf_op jit(solution)/shard_map/ppermute | solution.py:278
  21.8 1.5 %collective-permute-start.5 = (bf16[656,128]{1,0:T(8,128)(2,1)S(1)}, bf16[656,128]{1,0:T(8,128)(2,1)S(1)}, u32[]{:S(2)}, u32[]{:S(2)}) collective-permute-start(bf16[656,128]{1,0:T(8,128)(2,1)S(1)} %constant_dynamic-update-slice_fusion), channel_id=1, source_target_pairs={{0,16},{1,129},{2,18},{3,131},{4,20},{5,133},{6,22},{7,135},{8,24}... | collective-permute-start | bytes 503816 | tf_op jit(solution)/shard_map/ppermute | solution.py:287
  23.3 1.9 %collective-permute-start.6 = (bf16[656,128]{1,0:T(8,128)(2,1)S(1)}, bf16[656,128]{1,0:T(8,128)(2,1)S(1)}, u32[]{:S(2)}, u32[]{:S(2)}) collective-permute-start(bf16[656,128]{1,0:T(8,128)(2,1)S(1)} %constant_dynamic-update-slice_fusion), channel_id=1, source_target_pairs={{0,24},{1,193},{2,26},{3,195},{4,28},{5,197},{6,30},{7,199},{8,0},... | collective-permute-start | bytes 503816 | tf_op jit(solution)/shard_map/ppermute | solution.py:287
  25.3 3.2 %collective-permute-done.5 = bf16[656,128]{1,0:T(8,128)(2,1)S(1)} collective-permute-done((bf16[656,128]{1,0:T(8,128)(2,1)S(1)}, bf16[656,128]{1,0:T(8,128)(2,1)S(1)}, u32[]{:S(2)}, u32[]{:S(2)}) %collective-permute-start.5) | collective-permute-done | bytes 167968 | tf_op jit(solution)/shard_map/ppermute | solution.py:287
  28.6 0.1 constant_dynamic-update-slice_fusion.5
  28.7 1.1 %collective-permute-start.7 = (bf16[2192,128]{1,0:T(8,128)(2,1)S(1)}, bf16[2192,128]{1,0:T(8,128)(2,1)S(1)}, u32[]{:S(2)}, u32[]{:S(2)}) collective-permute-start(bf16[2192,128]{1,0:T(8,128)(2,1)S(1)} %get-tuple-element.28.here.r0), channel_id=1, source_target_pairs={{0,64},{1,9},{2,66},{3,11},{4,68},{5,13},{6,70},{7,15},{8,72},{9,1... | collective-permute-start | bytes 1683464 | tf_op jit(solution)/shard_map/ppermute | solution.py:297
  29.8 1.8 %collective-permute-start.8 = (bf16[2192,128]{1,0:T(8,128)(2,1)S(1)}, bf16[2192,128]{1,0:T(8,128)(2,1)S(1)}, u32[]{:S(2)}, u32[]{:S(2)}) collective-permute-start(bf16[2192,128]{1,0:T(8,128)(2,1)S(1)} %get-tuple-element.28.here.r0), channel_id=1, source_target_pairs={{0,192},{1,25},{2,194},{3,27},{4,196},{5,29},{6,198},{7,31},{8,200... | collective-permute-start | bytes 1683464 | tf_op jit(solution)/shard_map/ppermute | solution.py:297
  31.5 1.4 %collective-permute-start.9 = (bf16[2192,128]{1,0:T(8,128)(2,1)S(1)}, bf16[2192,128]{1,0:T(8,128)(2,1)S(1)}, u32[]{:S(2)}, u32[]{:S(2)}) collective-permute-start(bf16[2192,128]{1,0:T(8,128)(2,1)S(1)} %get-tuple-element.28.here.r0), channel_id=1, source_target_pairs={{0,128},{1,17},{2,130},{3,19},{4,132},{5,21},{6,134},{7,23},{8,136... | collective-permute-start | bytes 1683464 | tf_op jit(solution)/shard_map/ppermute | solution.py:297
  33.0 0.1 stack.33.sc
  33.0 3.7 %shard_map.68 = (f32[8,256,128]{2,1,0:T(8,128)S(1)}, f32[8,256,128]{2,1,0:T(8,128)S(1)}) custom-call(s32[8]{0:T(128)S(1)} %stack.33.sc, bf16[256,1024]{1,0:T(8,128)(2,1)S(1)} %copy-done, bf16[256,1024]{1,0:T(8,128)(2,1)S(1)} %collective-permute-done.2.q_other, bf16[2192,128]{1,0:T(8,128)(2,1)S(1)} %get-tuple-element.28.here.r0), custom_call_target="tpu_custom_call" | custom-call | flops 2147483648 | bytes 4194304 | tf_op jit(solution)/shard_map/pallas_call | solution.py:239
  36.8 0.6 collective-permute-start.10
  37.4 1.3 %collective-permute-start.11 = (bf16[256,128]{1,0:T(8,128)(2,1)S(1)}, bf16[256,128]{1,0:T(8,128)(2,1)S(1)}, u32[]{:S(2)}, u32[]{:S(2)}) collective-permute-start(bf16[256,128]{1,0:T(8,128)(2,1)S(1)} %get-tuple-element.37), channel_id=1, source_target_pairs={{0,16},{8,24},{16,0},{24,8},{32,48},{40,56},{48,32},{56,40},{64,80... | collective-permute-start | bytes 196616 | tf_op jit(solution)/shard_map/ppermute | solution.py:290
  38.7 1.8 %collective-permute-start.12 = (bf16[256,128]{1,0:T(8,128)(2,1)S(1)}, bf16[256,128]{1,0:T(8,128)(2,1)S(1)}, u32[]{:S(2)}, u32[]{:S(2)}) collective-permute-start(bf16[256,128]{1,0:T(8,128)(2,1)S(1)} %get-tuple-element.26), channel_id=1, source_target_pairs={{0,24},{8,0},{16,8},{24,16},{32,56},{40,32},{48,40},{56,48},{64,88... | collective-permute-start | bytes 196616 | tf_op jit(solution)/shard_map/ppermute | solution.py:290
  40.5 4.3 %collective-permute-done.8.r3 = bf16[2192,128]{1,0:T(8,128)(2,1)S(1)} collective-permute-done((bf16[2192,128]{1,0:T(8,128)(2,1)S(1)}, bf16[2192,128]{1,0:T(8,128)(2,1)S(1)}, u32[]{:S(2)}, u32[]{:S(2)}) %collective-permute-start.8) | collective-permute-done | bytes 561184 | tf_op jit(solution)/shard_map/ppermute | solution.py:297
  44.8 1.2 %collective-permute-done.9.r2 = bf16[2192,128]{1,0:T(8,128)(2,1)S(1)} collective-permute-done((bf16[2192,128]{1,0:T(8,128)(2,1)S(1)}, bf16[2192,128]{1,0:T(8,128)(2,1)S(1)}, u32[]{:S(2)}, u32[]{:S(2)}) %collective-permute-start.9) | collective-permute-done | bytes 561184 | tf_op jit(solution)/shard_map/ppermute | solution.py:297
  45.9 1.2 %shard_map.71 = bf16[32,32,256]{2,1,0:T(8,128)(2,1)S(1)} custom-call(s32[8]{0:T(128)S(1)} %stack.33.sc, bf16[2192,128]{1,0:T(8,128)(2,1)S(1)} %get-tuple-element.28.here.r0, bf16[2192,128]{1,0:T(8,128)(2,1)S(1)} %collective-permute-done.7.r1, bf16[2192,128]{1,0:T(8,128)(2,1)S(1)} %collective-permute-done.9.r2, bf16[2192,128]{1,0:T(8,128)(2,1)S(1)} %collective-permute-done.8.r3), custom_call_target="tpu_custom_call" | custom-call | flops 134217728 | bytes 4194304 | tf_op jit(solution)/shard_map/pallas_call | solution.py:239
  47.1 5.7 %collective-permute-start.14 = (bf16[32,32,256]{2,1,0:T(8,128)(2,1)S(1)}, bf16[32,32,256]{2,1,0:T(8,128)(2,1)S(1)}, u32[]{:S(2)}, u32[]{:S(2)}) collective-permute-start(bf16[32,32,256]{2,1,0:T(8,128)(2,1)S(1)} %shard_map.71), channel_id=1, source_target_pairs={{0,1},{1,0},{2,3},{3,2},{4,5},{5,4},{6,7},{7,6},{8,9},{9,8},{10,11... | collective-permute-start | bytes 1572872 | tf_op jit(solution)/shard_map/ppermute | solution.py:307
  52.9 14.1 %shard_map.69 = (bf16[256,1024]{1,0:T(8,128)(2,1)S(1)}, f32[256,128]{1,0:T(8,128)S(1)}, bf16[256,1152]{1,0:T(8,128)(2,1)S(1)}) custom-call(s32[8]{0:T(128)S(1)} %stack.33.sc, bf16[256,1024]{1,0:T(8,128)(2,1)S(1)} %copy-done, bf16[256,1024]{1,0:T(8,128)(2,1)S(1)} %collective-permute-done.2.q_other, bf16[2192,128]{1,0:T(8,128)(2,1)S(1)} %collective-permute-done.7.r1, ...), custom_call_target="tpu_custom_call" | custom-call | flops 8589934592 | bytes 4194304 | tf_op jit(solution)/shard_map/pallas_call | solution.py:239
  67.0 0.5 collective-permute-start.13
  67.5 0.8 %add_select_fusion = bf16[32,32,256]{2,1,0:T(8,128)(2,1)} fusion(bf16[32,32,256]{2,1,0:T(8,128)(2,1)S(1)} %shard_map.71, bf16[32,32,256]{2,1,0:T(8,128)(2,1)S(1)} %collective-permute-done.14, pred[]{:T(512)} %bitcast.6), kind=kLoop, calls=%fused_computation | loop fusion | flops 524288 | bytes 1572865 | tf_op jit(solution)/shard_map/jit(_where)/select_n | solution.py:321
  68.3 0.8 %collective-permute-done.13.got = bf16[256,1152]{1,0:T(8,128)(2,1)S(1)} collective-permute-done((bf16[256,1152]{1,0:T(8,128)(2,1)S(1)}, bf16[256,1152]{1,0:T(8,128)(2,1)S(1)}, u32[]{:S(2)}, u32[]{:S(2)}) %collective-permute-start.13) | collective-permute-done | bytes 589856 | tf_op jit(solution)/shard_map/ppermute | solution.py:318
  69.1 1.2 %shard_map.70 = bf16[256,1024]{1,0:T(8,128)(2,1)} custom-call(bf16[256,1024]{1,0:T(8,128)(2,1)S(1)} %get-tuple-element.23.keep, f32[256,128]{1,0:T(8,128)S(1)} %get-tuple-element.24.keep_lse, bf16[256,1152]{1,0:T(8,128)(2,1)S(1)} %collective-permute-done.13.got), custom_call_target="tpu_custom_call" | custom-call | flops 134217728 | bytes 4194304 | tf_op jit(solution)/shard_map/pallas_call | solution.py:239
  (37 shorter events, 0.6 us)
Async XLA Ops:
  1.5 0.9 %copy-start.1 = (s32[16]{0:T(128)S(1)}, s32[16]{0:T(128)}, u32[]{:S(2)}) copy-start(s32[16]{0:T(128)} %param.9) | copy-start | bytes 196
  1.5 3.1 %collective-permute-start = (bf16[256,128]{1,0:T(8,128)(2,1)S(1)}, bf16[256,128]{1,0:T(8,128)(2,1)S(1)}, u32[]{:S(2)}, u32[]{:S(2)}) collective-permute-start(bf16[256,128]{1,0:T(8,128)(2,1)S(1)} %broadcast_select_fusion.5), channel_id=1, source_target_pairs={{0,1},{1,0},{2,3},{3,2},{4,5},{5,4},{6,7},{7,6},{8,9},{9,8},{10,11... | collective-permute-start | bytes 196616 | tf_op jit(solution)/shard_map/ppermute | solution.py:265
  2.3 15.0 %collective-permute-start.2 = (bf16[256,1024]{1,0:T(8,128)(2,1)}, bf16[256,1024]{1,0:T(8,128)(2,1)S(1)}, u32[]{:S(2)}, u32[]{:S(2)}) collective-permute-start(bf16[256,1024]{1,0:T(8,128)(2,1)} %q_own.3), channel_id=1, source_target_pairs={{0,1},{1,0},{2,3},{3,2},{4,5},{5,4},{6,7},{7,6},{8,9},{9,8},{10,11... | collective-permute-start | bytes 1572872 | tf_op jit(solution)/shard_map/ppermute | solution.py:266
  2.7 0.7 copy-start.2
  4.7 12.6 %collective-permute-start.1 = (bf16[528,128]{1,0:T(8,128)(2,1)S(1)}, bf16[528,128]{1,0:T(8,128)(2,1)S(1)}, u32[]{:S(2)}, u32[]{:S(2)}) collective-permute-start(bf16[528,128]{1,0:T(8,128)(2,1)S(1)} %pad_maximum_fusion), channel_id=1, source_target_pairs={{0,32},{8,40},{16,48},{24,56},{32,0},{40,8},{48,16},{56,24},{64,96... | collective-permute-start | bytes 405512 | tf_op jit(solution)/shard_map/ppermute | solution.py:276
  17.4 7.8 %collective-permute-start.4 = (bf16[656,128]{1,0:T(8,128)(2,1)S(1)}, bf16[656,128]{1,0:T(8,128)(2,1)S(1)}, u32[]{:S(2)}, u32[]{:S(2)}) collective-permute-start(bf16[656,128]{1,0:T(8,128)(2,1)S(1)} %constant_dynamic-update-slice_fusion), channel_id=1, source_target_pairs={{0,8},{1,65},{2,10},{3,67},{4,12},{5,69},{6,14},{7,71},{8,16},{9,7... | collective-permute-start | bytes 503816 | tf_op jit(solution)/shard_map/ppermute | solution.py:287
  18.7 6.5 %collective-permute-start.3 = (bf16[256,128]{1,0:T(8,128)(2,1)S(1)}, bf16[256,128]{1,0:T(8,128)(2,1)S(1)}, u32[]{:S(2)}, u32[]{:S(2)}) collective-permute-start(bf16[256,128]{1,0:T(8,128)(2,1)S(1)} %get-tuple-element.35), channel_id=1, source_target_pairs={{0,64},{8,72},{16,80},{24,88},{64,128},{72,136},{80,144},{88,152},... | collective-permute-start | bytes 196616 | tf_op jit(solution)/shard_map/ppermute | solution.py:278
  21.8 6.7 %collective-permute-start.5 = (bf16[656,128]{1,0:T(8,128)(2,1)S(1)}, bf16[656,128]{1,0:T(8,128)(2,1)S(1)}, u32[]{:S(2)}, u32[]{:S(2)}) collective-permute-start(bf16[656,128]{1,0:T(8,128)(2,1)S(1)} %constant_dynamic-update-slice_fusion), channel_id=1, source_target_pairs={{0,16},{1,129},{2,18},{3,131},{4,20},{5,133},{6,22},{7,135},{8,24}... | collective-permute-start | bytes 503816 | tf_op jit(solution)/shard_map/ppermute | solution.py:287
  23.3 5.2 %collective-permute-start.6 = (bf16[656,128]{1,0:T(8,128)(2,1)S(1)}, bf16[656,128]{1,0:T(8,128)(2,1)S(1)}, u32[]{:S(2)}, u32[]{:S(2)}) collective-permute-start(bf16[656,128]{1,0:T(8,128)(2,1)S(1)} %constant_dynamic-update-slice_fusion), channel_id=1, source_target_pairs={{0,24},{1,193},{2,26},{3,195},{4,28},{5,197},{6,30},{7,199},{8,0},... | collective-permute-start | bytes 503816 | tf_op jit(solution)/shard_map/ppermute | solution.py:287
  25.3 7.8 %copy-start = (bf16[256,1024]{1,0:T(8,128)(2,1)S(1)}, bf16[256,1024]{1,0:T(8,128)(2,1)}, u32[]{:S(2)}) copy-start(bf16[256,1024]{1,0:T(8,128)(2,1)} %q_own.3) | copy-start | bytes 1572868
  28.7 10.0 %collective-permute-start.7 = (bf16[2192,128]{1,0:T(8,128)(2,1)S(1)}, bf16[2192,128]{1,0:T(8,128)(2,1)S(1)}, u32[]{:S(2)}, u32[]{:S(2)}) collective-permute-start(bf16[2192,128]{1,0:T(8,128)(2,1)S(1)} %get-tuple-element.28.here.r0), channel_id=1, source_target_pairs={{0,64},{1,9},{2,66},{3,11},{4,68},{5,13},{6,70},{7,15},{8,72},{9,1... | collective-permute-start | bytes 1683464 | tf_op jit(solution)/shard_map/ppermute | solution.py:297
  29.8 15.0 %collective-permute-start.8 = (bf16[2192,128]{1,0:T(8,128)(2,1)S(1)}, bf16[2192,128]{1,0:T(8,128)(2,1)S(1)}, u32[]{:S(2)}, u32[]{:S(2)}) collective-permute-start(bf16[2192,128]{1,0:T(8,128)(2,1)S(1)} %get-tuple-element.28.here.r0), channel_id=1, source_target_pairs={{0,192},{1,25},{2,194},{3,27},{4,196},{5,29},{6,198},{7,31},{8,200... | collective-permute-start | bytes 1683464 | tf_op jit(solution)/shard_map/ppermute | solution.py:297
  31.5 14.4 %collective-permute-start.9 = (bf16[2192,128]{1,0:T(8,128)(2,1)S(1)}, bf16[2192,128]{1,0:T(8,128)(2,1)S(1)}, u32[]{:S(2)}, u32[]{:S(2)}) collective-permute-start(bf16[2192,128]{1,0:T(8,128)(2,1)S(1)} %get-tuple-element.28.here.r0), channel_id=1, source_target_pairs={{0,128},{1,17},{2,130},{3,19},{4,132},{5,21},{6,134},{7,23},{8,136... | collective-permute-start | bytes 1683464 | tf_op jit(solution)/shard_map/ppermute | solution.py:297
  36.8 16.1 %collective-permute-start.10 = (bf16[256,128]{1,0:T(8,128)(2,1)S(1)}, bf16[256,128]{1,0:T(8,128)(2,1)S(1)}, u32[]{:S(2)}, u32[]{:S(2)}) collective-permute-start(bf16[256,128]{1,0:T(8,128)(2,1)S(1)} %get-tuple-element.38), channel_id=1, source_target_pairs={{0,8},{8,16},{16,24},{24,0},{32,40},{40,48},{48,56},{56,32},{64,72... | collective-permute-start | bytes 196616 | tf_op jit(solution)/shard_map/ppermute | solution.py:290
  37.4 15.5 %collective-permute-start.11 = (bf16[256,128]{1,0:T(8,128)(2,1)S(1)}, bf16[256,128]{1,0:T(8,128)(2,1)S(1)}, u32[]{:S(2)}, u32[]{:S(2)}) collective-permute-start(bf16[256,128]{1,0:T(8,128)(2,1)S(1)} %get-tuple-element.37), channel_id=1, source_target_pairs={{0,16},{8,24},{16,0},{24,8},{32,48},{40,56},{48,32},{56,40},{64,80... | collective-permute-start | bytes 196616 | tf_op jit(solution)/shard_map/ppermute | solution.py:290
  38.7 14.2 %collective-permute-start.12 = (bf16[256,128]{1,0:T(8,128)(2,1)S(1)}, bf16[256,128]{1,0:T(8,128)(2,1)S(1)}, u32[]{:S(2)}, u32[]{:S(2)}) collective-permute-start(bf16[256,128]{1,0:T(8,128)(2,1)S(1)} %get-tuple-element.26), channel_id=1, source_target_pairs={{0,24},{8,0},{16,8},{24,16},{32,56},{40,32},{48,40},{56,48},{64,88... | collective-permute-start | bytes 196616 | tf_op jit(solution)/shard_map/ppermute | solution.py:290
  47.1 20.3 %collective-permute-start.14 = (bf16[32,32,256]{2,1,0:T(8,128)(2,1)S(1)}, bf16[32,32,256]{2,1,0:T(8,128)(2,1)S(1)}, u32[]{:S(2)}, u32[]{:S(2)}) collective-permute-start(bf16[32,32,256]{2,1,0:T(8,128)(2,1)S(1)} %shard_map.71), channel_id=1, source_target_pairs={{0,1},{1,0},{2,3},{3,2},{4,5},{5,4},{6,7},{7,6},{8,9},{9,8},{10,11... | collective-permute-start | bytes 1572872 | tf_op jit(solution)/shard_map/ppermute | solution.py:307
  67.0 2.1 %collective-permute-start.13 = (bf16[256,1152]{1,0:T(8,128)(2,1)S(1)}, bf16[256,1152]{1,0:T(8,128)(2,1)S(1)}, u32[]{:S(2)}, u32[]{:S(2)}) collective-permute-start(bf16[256,1152]{1,0:T(8,128)(2,1)S(1)} %get-tuple-element.25), channel_id=1, source_target_pairs={{0,1},{1,0},{2,3},{3,2},{4,5},{5,4},{6,7},{7,6},{8,9},{9,8},{10,11... | collective-permute-start | bytes 1769480 | tf_op jit(solution)/shard_map/ppermute | solution.py:318

commit v8 on v7

--- a/solution.py
+++ b/solution.py
@@ -81,12 +81,6 @@
         put_keys(k_s, v_s, at + n * HALF, ref, n * ROWS, HALF, HALF)
 
 
-def put_bias(k_s, v_s, bias):
-    lane = iota(bias.shape, 1)
-    k_s[:, HD:] = jnp.where(lane == 0, bias, 0.0).astype(BF16)
-    v_s[:, HD:] = jnp.ones(bias.shape, BF16)
-
-
 def range_of(sc, inner, outer, far):
     x, y, z, core = sc[0], sc[1], sc[2], sc[3]
     dx = jnp.where(core == 0, outer, inner)
@@ -95,12 +89,20 @@
     return ((x - dx) & 3) * 8 + zz * 4 + ((y - dy) & 3)
 
 
-def range_bias(sc, outers):
-    n = iota((len(outers) * 8 * HALF, HD), 0)
-    outer = jnp.full(n.shape, outers[0], jnp.int32)
-    for i, distance in enumerate(outers[1:], 1):
-        outer = jnp.where(n >> 10 == i, distance, outer)
-    return jnp.where(range_of(sc, (n >> 8) & 3, outer, (n >> 7) & 1) <= sc[4], 0.0, NEG)
+def put_range_bias(k_s, v_s, sc, outers):
+    first = jnp.where(iota((HALF, HD), 1) == 0, 1.0, 0.0)
+    for i, outer in enumerate(outers):
+        for n in range(8):
+            bias = jnp.where(range_of(sc, n >> 1, outer, n & 1) <= sc[4], 0.0, NEG)
+            k_s[pl.ds((i * 8 + n) * HALF, HALF), HD:] = (first * bias).astype(BF16)
+    v_s[:, HD:] = jnp.ones((len(outers) * 8 * HALF, HD), BF16)
+
+
+def put_slot_bias(k_s, v_s, biases):
+    first = jnp.where(iota((HALF, HD), 1) == 0, 1.0, 0.0)
+    for i, bias in enumerate(biases):
+        k_s[pl.ds(i * HALF, HALF), HD:] = (first * bias).astype(BF16)
+    v_s[:, HD:] = jnp.ones((len(biases) * HALF, HD), BF16)
 
 
 def load_head(q_a, q_b, flag, a):
@@ -120,19 +122,29 @@
     return jnp.where(low, both, turned), jnp.where(low, turned, both)
 
 
-def near_kernel(sc, q_own, q_other, here, ml_out, o_out, kr, vr):
-    core, is_r = sc[3], sc[5]
+def near_kernel(sc, q_own, q_other, here, pas, p1, p2, p3, far, mlp_out, op_out, ml_out, o_out, kp, vp, kr, vr):
+    core, c, is_r = sc[3], sc[4], sc[5]
     put_ranges(kr, vr, 0, here)
-    put_bias(kr, vr, range_bias(sc, (0,)))
-    own = jnp.where(core * HALF + iota((ROWS, HD), 1) > iota((ROWS, HD), 0), NEG, 0.0)
+    put_range_bias(kr, vr, sc, (0,))
+    for n, ref in enumerate((pas, p1, p2, p3, far)):
+        put_keys(kp, vp, n * HALF, ref, 0, HALF, HALF)
+    put_slot_bias(kp, vp, [jnp.where(n <= c, 0.0, NEG) for n in range(5)])
+    row = iota((ROWS, HD), 0)
+    key = core * HALF + iota((ROWS, HD), 1)
+    own = jnp.where(key > row, NEG, 0.0)
+    edge = jnp.where(key <= row, NEG, 0.0)
 
     def heads(i):
         at = [WIDE * i + u for u in range(WIDE)]
+        qp = [load_head(q_other, q_own, is_r, a) for a in at]
         q = [load_head(q_own, q_other, is_r, a) for a in at]
-        state = [fold(None, q[u], kr[0:CHUNK, :], vr[0:CHUNK, :], left=own) for u in range(WIDE)]
-        state = [fold(state[u], q[u], kr[CHUNK:, :], vr[CHUNK:, :]) for u in range(WIDE)]
+        sr = [fold(None, q[u], kr[0:CHUNK, :], vr[0:CHUNK, :], left=own) for u in range(WIDE)]
+        sp = [fold(None, qp[u], kp[0:3 * HALF, :], vp[0:3 * HALF, :], left=own) for u in range(WIDE)]
+        sr = [fold(sr[u], q[u], kr[CHUNK:, :], vr[CHUNK:, :]) for u in range(WIDE)]
+        sp = [fold(sp[u], qp[u], kp[3 * HALF:, :], vp[3 * HALF:, :], right=edge) for u in range(WIDE)]
         for u in range(WIDE):
-            ml_out[at[u]], o_out[at[u]] = pack(*state[u][:2]), state[u][2]
+            ml_out[at[u]], o_out[at[u]] = pack(*sr[u][:2]), sr[u][2]
+            mlp_out[at[u]], op_out[at[u]] = pack(*sp[u][:2]), sp[u][2]
 
     for i in range(GROUP // WIDE):
         heads(i)
@@ -143,25 +155,18 @@
     return o / l, m * SCALE + jnp.log2(l)
 
 
-def rest_kernel(sc, q_own, q_other, r1, r3, r2, sink, pas, p1, p2, p3, far, ml_in, o_in, keep, keep_lse, send,
-                kr, vr, kp, vp, lse_s):
+def rest_kernel(sc, q_own, q_other, r1, r3, r2, sink, mlp_in, op_in, ml_in, o_in, keep, keep_lse, send,
+                kr, vr, ks, vs, lse_s):
     core, c, is_r = sc[3], sc[4], sc[5]
     for n, ref in enumerate((r1, r3, r2)):
         put_ranges(kr, vr, n * 8 * HALF, ref)
-    put_bias(kr, vr, range_bias(sc, (1, 3, 2)))
-    for n, ref in enumerate((pas, p1, p2, p3)):
-        put_keys(kp, vp, n * HALF, ref, 0, HALF, HALF)
-    kp[4 * HALF:5 * HALF, :] = jnp.zeros((HALF, 2 * HD), BF16)
-    vp[4 * HALF:5 * HALF, :] = jnp.zeros((HALF, 2 * HD), BF16)
-    put_keys(kp, vp, 4 * HALF, sink, 0, SINK, SINK)
-    put_keys(kp, vp, 5 * HALF, far, 0, HALF, HALF)
-    slot = iota((6 * HALF, HD), 0) >> 7
-    put_bias(kp, vp, jnp.where((slot - (slot >> 2) <= c) | (slot == 4), 0.0, NEG))
+    put_range_bias(kr, vr, sc, (1, 3, 2))
+    ks[...] = jnp.zeros((HALF, 2 * HD), BF16)
+    vs[...] = jnp.zeros((HALF, 2 * HD), BF16)
+    put_keys(ks, vs, 0, sink, 0, SINK, SINK)
+    put_slot_bias(ks, vs, [0.0])
     row = iota((ROWS, HD), 0)
     lane = iota((ROWS, HD), 1)
-    key = core * HALF + lane
-    own = jnp.where(key > row, NEG, 0.0)
-    edge = jnp.where(key <= row, NEG, 0.0)
     seen = (core == 0) & (lane < SINK) & (c * ROWS + row - lane >= RECENT)
     sink_bias = jnp.where(seen, 0.0, NEG)
     lse_s[...] = jnp.zeros((ROWS, HD), F32)
@@ -172,13 +177,12 @@
         qp = [load_head(q_other, q_own, is_r, a) for a in at]
         qr = [load_head(q_own, q_other, is_r, a) for a in at]
         sr = [(*unpack(ml_in[a]), o_in[a]) for a in at]
+        sp = [(*unpack(mlp_in[a]), op_in[a]) for a in at]
         for n in range(6):
             rows = slice(n * CHUNK, (n + 1) * CHUNK)
             sr = [fold(sr[u], qr[u], kr[rows, :], vr[rows, :]) for u in range(WIDE)]
-            if n == 1:
-                sp = [fold(None, qp[u], kp[0:4 * HALF, :], vp[0:4 * HALF, :], left=own) for u in range(WIDE)]
-            if n == 3:
-                sp = [fold(sp[u], qp[u], kp[4 * HALF:, :], vp[4 * HALF:, :], left=sink_bias, right=edge) for u in range(WIDE)]
+            if n == 2:
+                sp = [fold(sp[u], qp[u], ks[...], vs[...], left=sink_bias) for u in range(WIDE)]
         for u in range(WIDE):
             cols = slice(at[u] * HD, (at[u] + 1) * HD)
             out_r, lse_r = finish(sr[u])
@@ -297,7 +301,9 @@
     r = {0: message} | {s: lax.ppermute(message, axes, STAGE_2[s]) for s in (1, 3, 2)}
     state = (jax.ShapeDtypeStruct((GROUP, ROWS, HD), F32),) * 2
     unit = 2 * 2048 * 256 * 512
-    now_ml, now_o = call(near_kernel, state, keys(8 * HALF), 4 * unit, sc, q, q_other, message)
+    *now_p, now_ml, now_o = call(
+        near_kernel, state + state, keys(5 * HALF) + keys(8 * HALF), 60 * unit,
+        sc, q, q_other, message, pas, p[1], p[2], p[3], far)
     for s in (1, 2, 3):
         sink = jnp.where(x == s, r[s][8 * ROWS + META:], sink)
     sc_l, now_ml = lax.optimization_barrier((sc, now_ml))
@@ -312,8 +318,8 @@
             jax.ShapeDtypeStruct((ROWS, HD), F32),
             jax.ShapeDtypeStruct((ROWS, (GROUP + 1) * HD), BF16),
         ),
-        keys(24 * HALF) + keys(6 * HALF) + [pltpu.VMEM((ROWS, HD), F32)],
-        16 * unit, sc_l, q, q_other, r[1], r[3], r[2], sink, pas, p[1], p[2], p[3], far, now_ml, now_o)
+        keys(24 * HALF) + keys(HALF) + [pltpu.VMEM((ROWS, HD), F32)],
+        13 * unit, sc_l, q, q_other, r[1], r[3], r[2], sink, *now_p, now_ml, now_o)
 
     got = lax.ppermute(send, "tp", CORE_SWAP)
     attn_out = call(

time: 71.1 us -> 68.7 us (0.966)
  waiting for transfers between devices: 15.9 us -> 14 us
  Pallas kernels: 20.2 us -> 21.8 us
  starting transfers between devices: 28.8 us -> 27.4 us
    ppermute x3, waiting for transfers between devices: 3.21 us -> 0.01 us  [shards(): got = {s: lax.ppermute(message, axes, STAGE_1[s]) for s in (1, 3, 2)}]
    pallas_call x4, Pallas kernels: 20.2 us -> 21.8 us  [call(): pl.pallas_call(kernel, out_shape=out_shape, in_specs=specs, out_specs=(VM...]
    ppermute x1, starting transfers between devices: 5.71 us -> 4.33 us  [shards(): got_pages = lax.ppermute(pages, 'tp', CORE_SWAP)]
    ppermute x3, starting transfers between devices: 3.68 us -> 5.06 us  [shards(): lax.ppermute(jnp.where(y + s < 4, pas, far), 'ctx', Y_SHIFT[s])]
    ppermute x3, starting transfers between devices: 4.27 us -> 3.25 us  [shards(): lax.ppermute(message, axes, STAGE_2[s])]
    ppermute x3, waiting for transfers between devices: 5.45 us -> 6.38 us  [shards(): lax.ppermute(message, axes, STAGE_2[s])]
  transfers between devices with their start and end apart: 15 -> 15, of which waited for: 5 -> 3; matrix products, arithmetic and copies ran while one was open for 3% -> 3% of each run, Pallas kernels for 27% -> 28%
where the time goes in v8:
time: 68.7 us; the launch traced here: 68.5 us
  starting transfers between devices  27.4 us (40%)
  Pallas kernels  21.8 us (32%)
  waiting for transfers between devices  14 us (20%)
  local copies, waits for them, and re-layouts  2.32 us (3%)
  other arithmetic  1.54 us (2%)
  between operations  1.47 us (2%)
    pallas_call x4, Pallas kernels, call(): pl.pallas_call(kernel, out_shape=out_shape, in_specs=specs, out_specs=(VM...  21.8 us
    ppermute x1, waiting for transfers between devices, shards(): theirs = lax.ppermute(jnp.concatenate([ret, pas, meta]), 'ctx', Z_SWAP)  6.47 us
    ppermute x3, waiting for transfers between devices, shards(): lax.ppermute(message, axes, STAGE_2[s])  6.38 us
    ppermute x1, starting transfers between devices, shards(): theirs = lax.ppermute(jnp.concatenate([ret, pas, meta]), 'ctx', Z_SWAP)  6.1 us
    ppermute x3, starting transfers between devices, shards(): lax.ppermute(jnp.where(y + s < 4, pas, far), 'ctx', Y_SHIFT[s])  5.06 us
    ppermute x3, starting transfers between devices, shards(): got = {s: lax.ppermute(message, axes, STAGE_1[s]) for s in (1, 3, 2)}  4.63 us
    ppermute x1, starting transfers between devices, shards(): got_pages = lax.ppermute(pages, 'tp', CORE_SWAP)  4.33 us
    ppermute x3, starting transfers between devices, shards(): lax.ppermute(message, axes, STAGE_2[s])  3.25 us
  transfers between devices with their start and end apart: 15, of which 3 were waited for; matrix products, arithmetic and copies ran while one was open for 3% of the time, Pallas kernels for 28%

profile of v8, /device:TPU:33, one launch (start us, length us, event | category | flops | bytes accessed | tf_op | source)
XLA Modules:
  0.0 68.5 jit_solution(3851731350266100048)
XLA Ops:
  0.6 0.8 %fusion.11 = (bf16[128,128]{1,0:T(8,128)(2,1)S(1)}, bf16[128,128]{1,0:T(8,128)(2,1)S(1)}, bf16[128,128]{1,0:T(8,128)(2,1)S(1)}, bf16[128,128]{1,0:T(8,128)(2,1)S(1)}) fusion(bf16[256,128]{1,0:T(8,128)(2,1)} %param.6, bf16[256,128]{1,0:T(8,128)(2,1)} %param.7), kind=kLoop, calls=%fused_computation.46 | loop fusion | bytes 262144 | tf_op jit(solution)/shard_map/slice | solution.py:266
  1.5 0.8 %collective-permute-start = (bf16[256,128]{1,0:T(8,128)(2,1)S(1)}, bf16[256,128]{1,0:T(8,128)(2,1)S(1)}, u32[]{:S(2)}, u32[]{:S(2)}) collective-permute-start(bf16[256,128]{1,0:T(8,128)(2,1)S(1)} %broadcast_select_fusion.5), channel_id=1, source_target_pairs={{0,1},{1,0},{2,3},{3,2},{4,5},{5,4},{6,7},{7,6},{8,9},{9,8},{10,11... | collective-permute-start | bytes 196616 | tf_op jit(solution)/shard_map/ppermute | solution.py:269
  2.3 0.1 collective-permute-start.2
  2.4 0.2 convert_reduce_fusion
  2.6 0.1 fusion.5
  2.7 0.1 broadcast_in_dim.19
  2.8 0.6 copy-done.2
  3.4 0.6 dynamic_slice.4
  4.7 6.1 %collective-permute-start.1 = (bf16[528,128]{1,0:T(8,128)(2,1)S(1)}, bf16[528,128]{1,0:T(8,128)(2,1)S(1)}, u32[]{:S(2)}, u32[]{:S(2)}) collective-permute-start(bf16[528,128]{1,0:T(8,128)(2,1)S(1)} %pad_maximum_fusion), channel_id=1, source_target_pairs={{0,32},{8,40},{16,48},{24,56},{32,0},{40,8},{48,16},{56,24},{64,96... | collective-permute-start | bytes 405512 | tf_op jit(solution)/shard_map/ppermute | solution.py:280
  10.8 6.5 %collective-permute-done.1 = bf16[528,128]{1,0:T(8,128)(2,1)S(1)} collective-permute-done((bf16[528,128]{1,0:T(8,128)(2,1)S(1)}, bf16[528,128]{1,0:T(8,128)(2,1)S(1)}, u32[]{:S(2)}, u32[]{:S(2)}) %collective-permute-start.1) | collective-permute-done | bytes 135200 | tf_op jit(solution)/shard_map/ppermute | solution.py:280
  17.4 0.1 constant_dynamic-update-slice_fusion
  17.4 1.2 %collective-permute-start.4 = (bf16[656,128]{1,0:T(8,128)(2,1)S(1)}, bf16[656,128]{1,0:T(8,128)(2,1)S(1)}, u32[]{:S(2)}, u32[]{:S(2)}) collective-permute-start(bf16[656,128]{1,0:T(8,128)(2,1)S(1)} %constant_dynamic-update-slice_fusion), channel_id=1, source_target_pairs={{0,8},{1,65},{2,10},{3,67},{4,12},{5,69},{6,14},{7,71},{8,16},{9,7... | collective-permute-start | bytes 503816 | tf_op jit(solution)/shard_map/ppermute | solution.py:291
  18.7 0.1 stack.33.sc
  18.8 3.1 %collective-permute-start.3 = (bf16[256,128]{1,0:T(8,128)(2,1)S(1)}, bf16[256,128]{1,0:T(8,128)(2,1)S(1)}, u32[]{:S(2)}, u32[]{:S(2)}) collective-permute-start(bf16[256,128]{1,0:T(8,128)(2,1)S(1)} %get-tuple-element.39), channel_id=1, source_target_pairs={{0,64},{8,72},{16,80},{24,88},{64,128},{72,136},{80,144},{88,152},... | collective-permute-start | bytes 196616 | tf_op jit(solution)/shard_map/ppermute | solution.py:282
  21.9 1.5 %collective-permute-start.5 = (bf16[656,128]{1,0:T(8,128)(2,1)S(1)}, bf16[656,128]{1,0:T(8,128)(2,1)S(1)}, u32[]{:S(2)}, u32[]{:S(2)}) collective-permute-start(bf16[656,128]{1,0:T(8,128)(2,1)S(1)} %constant_dynamic-update-slice_fusion), channel_id=1, source_target_pairs={{0,16},{1,129},{2,18},{3,131},{4,20},{5,133},{6,22},{7,135},{8,24}... | collective-permute-start | bytes 503816 | tf_op jit(solution)/shard_map/ppermute | solution.py:291
  23.4 1.9 %collective-permute-start.6 = (bf16[656,128]{1,0:T(8,128)(2,1)S(1)}, bf16[656,128]{1,0:T(8,128)(2,1)S(1)}, u32[]{:S(2)}, u32[]{:S(2)}) collective-permute-start(bf16[656,128]{1,0:T(8,128)(2,1)S(1)} %constant_dynamic-update-slice_fusion), channel_id=1, source_target_pairs={{0,24},{1,193},{2,26},{3,195},{4,28},{5,197},{6,30},{7,199},{8,0},... | collective-permute-start | bytes 503816 | tf_op jit(solution)/shard_map/ppermute | solution.py:291
  25.4 1.4 %collective-permute-start.7 = (bf16[256,128]{1,0:T(8,128)(2,1)S(1)}, bf16[256,128]{1,0:T(8,128)(2,1)S(1)}, u32[]{:S(2)}, u32[]{:S(2)}) collective-permute-start(bf16[256,128]{1,0:T(8,128)(2,1)S(1)} %get-tuple-element.42), channel_id=1, source_target_pairs={{0,8},{8,16},{16,24},{24,0},{32,40},{40,48},{48,56},{56,32},{64,72... | collective-permute-start | bytes 196616 | tf_op jit(solution)/shard_map/ppermute | solution.py:294
  26.8 2.6 %collective-permute-start.8 = (bf16[256,128]{1,0:T(8,128)(2,1)S(1)}, bf16[256,128]{1,0:T(8,128)(2,1)S(1)}, u32[]{:S(2)}, u32[]{:S(2)}) collective-permute-start(bf16[256,128]{1,0:T(8,128)(2,1)S(1)} %get-tuple-element.41), channel_id=1, source_target_pairs={{0,16},{8,24},{16,0},{24,8},{32,48},{40,56},{48,32},{56,40},{64,80... | collective-permute-start | bytes 196616 | tf_op jit(solution)/shard_map/ppermute | solution.py:294
  29.4 1.1 %collective-permute-start.9 = (bf16[256,128]{1,0:T(8,128)(2,1)S(1)}, bf16[256,128]{1,0:T(8,128)(2,1)S(1)}, u32[]{:S(2)}, u32[]{:S(2)}) collective-permute-start(bf16[256,128]{1,0:T(8,128)(2,1)S(1)} %get-tuple-element.30), channel_id=1, source_target_pairs={{0,24},{8,0},{16,8},{24,16},{32,56},{40,32},{48,40},{56,48},{64,88... | collective-permute-start | bytes 196616 | tf_op jit(solution)/shard_map/ppermute | solution.py:294
  30.5 0.1 constant_dynamic-update-slice_fusion.5
  30.7 0.5 collective-permute-start.10
  31.1 2.3 %collective-permute-start.11 = (bf16[2192,128]{1,0:T(8,128)(2,1)S(1)}, bf16[2192,128]{1,0:T(8,128)(2,1)S(1)}, u32[]{:S(2)}, u32[]{:S(2)}) collective-permute-start(bf16[2192,128]{1,0:T(8,128)(2,1)S(1)} %get-tuple-element.32.here.r0), channel_id=1, source_target_pairs={{0,192},{1,25},{2,194},{3,27},{4,196},{5,29},{6,198},{7,31},{8,200... | collective-permute-start | bytes 1683464 | tf_op jit(solution)/shard_map/ppermute | solution.py:301
  33.4 0.5 collective-permute-start.12
  33.9 6.4 %shard_map.68 = (f32[8,256,128]{2,1,0:T(8,128)S(1)}, f32[8,256,128]{2,1,0:T(8,128)S(1)}, f32[8,256,128]{2,1,0:T(8,128)S(1)}, f32[8,256,128]{2,1,0:T(8,128)S(1)}) custom-call(s32[8]{0:T(128)S(1)} %stack.33.sc, bf16[256,1024]{1,0:T(8,128)(2,1)S(1)} %copy-done, bf16[256,1024]{1,0:T(8,128)(2,1)S(1)} %collective-permute-done.2.q_other, ...), custom_call_target="tpu_custom_call" | custom-call | flops 32212254720 | bytes 4194304 | tf_op jit(solution)/shard_map/pallas_call | solution.py:243
  40.3 6.4 %collective-permute-done.10.r1 = bf16[2192,128]{1,0:T(8,128)(2,1)S(1)} collective-permute-done((bf16[2192,128]{1,0:T(8,128)(2,1)S(1)}, bf16[2192,128]{1,0:T(8,128)(2,1)S(1)}, u32[]{:S(2)}, u32[]{:S(2)}) %collective-permute-start.10) | collective-permute-done | bytes 561184 | tf_op jit(solution)/shard_map/ppermute | solution.py:301
  46.7 1.2 %shard_map.71 = bf16[32,32,256]{2,1,0:T(8,128)(2,1)S(1)} custom-call(s32[8]{0:T(128)S(1)} %stack.33.sc, bf16[2192,128]{1,0:T(8,128)(2,1)S(1)} %get-tuple-element.32.here.r0, bf16[2192,128]{1,0:T(8,128)(2,1)S(1)} %collective-permute-done.10.r1, bf16[2192,128]{1,0:T(8,128)(2,1)S(1)} %collective-permute-done.12.r2, bf16[2192,128]{1,0:T(8,128)(2,1)S(1)} %collective-permute-done.11.r3), custom_call_target="tpu_custom_call" | custom-call | flops 134217728 | bytes 4194304 | tf_op jit(solution)/shard_map/pallas_call | solution.py:243
  47.9 4.3 %collective-permute-start.14 = (bf16[32,32,256]{2,1,0:T(8,128)(2,1)S(1)}, bf16[32,32,256]{2,1,0:T(8,128)(2,1)S(1)}, u32[]{:S(2)}, u32[]{:S(2)}) collective-permute-start(bf16[32,32,256]{2,1,0:T(8,128)(2,1)S(1)} %shard_map.71), channel_id=1, source_target_pairs={{0,1},{1,0},{2,3},{3,2},{4,5},{5,4},{6,7},{7,6},{8,9},{9,8},{10,11... | collective-permute-start | bytes 1572872 | tf_op jit(solution)/shard_map/ppermute | solution.py:313
  52.2 12.9 %shard_map.69 = (bf16[256,1024]{1,0:T(8,128)(2,1)S(1)}, f32[256,128]{1,0:T(8,128)S(1)}, bf16[256,1152]{1,0:T(8,128)(2,1)S(1)}) custom-call(s32[8]{0:T(128)S(1)} %stack.33.sc, bf16[256,1024]{1,0:T(8,128)(2,1)S(1)} %copy-done, bf16[256,1024]{1,0:T(8,128)(2,1)S(1)} %collective-permute-done.2.q_other, bf16[2192,128]{1,0:T(8,128)(2,1)S(1)} %collective-permute-done.10.r1, ...), custom_call_target="tpu_custom_call" | custom-call | flops 6979321856 | bytes 4194304 | tf_op jit(solution)/shard_map/pallas_call | solution.py:243
  65.2 0.1 collective-permute-start.13
  65.3 0.9 %add_select_fusion = bf16[32,32,256]{2,1,0:T(8,128)(2,1)} fusion(bf16[32,32,256]{2,1,0:T(8,128)(2,1)S(1)} %shard_map.71, bf16[32,32,256]{2,1,0:T(8,128)(2,1)S(1)} %collective-permute-done.14, pred[]{:T(512)} %bitcast.6), kind=kLoop, calls=%fused_computation | loop fusion | flops 524288 | bytes 1572865 | tf_op jit(solution)/shard_map/jit(_where)/select_n | solution.py:327
  66.2 1.1 %collective-permute-done.13.got = bf16[256,1152]{1,0:T(8,128)(2,1)S(1)} collective-permute-done((bf16[256,1152]{1,0:T(8,128)(2,1)S(1)}, bf16[256,1152]{1,0:T(8,128)(2,1)S(1)}, u32[]{:S(2)}, u32[]{:S(2)}) %collective-permute-start.13) | collective-permute-done | bytes 589856 | tf_op jit(solution)/shard_map/ppermute | solution.py:324
  67.3 1.2 %shard_map.70 = bf16[256,1024]{1,0:T(8,128)(2,1)} custom-call(bf16[256,1024]{1,0:T(8,128)(2,1)S(1)} %get-tuple-element.27.keep, f32[256,128]{1,0:T(8,128)S(1)} %get-tuple-element.28.keep_lse, bf16[256,1152]{1,0:T(8,128)(2,1)S(1)} %collective-permute-done.13.got), custom_call_target="tpu_custom_call" | custom-call | flops 134217728 | bytes 4194304 | tf_op jit(solution)/shard_map/pallas_call | solution.py:243
  (37 shorter events, 0.5 us)
Async XLA Ops:
  1.5 0.9 %copy-start.1 = (s32[16]{0:T(128)S(1)}, s32[16]{0:T(128)}, u32[]{:S(2)}) copy-start(s32[16]{0:T(128)} %param.9) | copy-start | bytes 196
  1.5 3.1 %collective-permute-start = (bf16[256,128]{1,0:T(8,128)(2,1)S(1)}, bf16[256,128]{1,0:T(8,128)(2,1)S(1)}, u32[]{:S(2)}, u32[]{:S(2)}) collective-permute-start(bf16[256,128]{1,0:T(8,128)(2,1)S(1)} %broadcast_select_fusion.5), channel_id=1, source_target_pairs={{0,1},{1,0},{2,3},{3,2},{4,5},{5,4},{6,7},{7,6},{8,9},{9,8},{10,11... | collective-permute-start | bytes 196616 | tf_op jit(solution)/shard_map/ppermute | solution.py:269
  2.3 15.0 %collective-permute-start.2 = (bf16[256,1024]{1,0:T(8,128)(2,1)}, bf16[256,1024]{1,0:T(8,128)(2,1)S(1)}, u32[]{:S(2)}, u32[]{:S(2)}) collective-permute-start(bf16[256,1024]{1,0:T(8,128)(2,1)} %q_own.3), channel_id=1, source_target_pairs={{0,1},{1,0},{2,3},{3,2},{4,5},{5,4},{6,7},{7,6},{8,9},{9,8},{10,11... | collective-permute-start | bytes 1572872 | tf_op jit(solution)/shard_map/ppermute | solution.py:270
  2.7 0.7 copy-start.2
  4.7 12.6 %collective-permute-start.1 = (bf16[528,128]{1,0:T(8,128)(2,1)S(1)}, bf16[528,128]{1,0:T(8,128)(2,1)S(1)}, u32[]{:S(2)}, u32[]{:S(2)}) collective-permute-start(bf16[528,128]{1,0:T(8,128)(2,1)S(1)} %pad_maximum_fusion), channel_id=1, source_target_pairs={{0,32},{8,40},{16,48},{24,56},{32,0},{40,8},{48,16},{56,24},{64,96... | collective-permute-start | bytes 405512 | tf_op jit(solution)/shard_map/ppermute | solution.py:280
  17.4 7.9 %collective-permute-start.4 = (bf16[656,128]{1,0:T(8,128)(2,1)S(1)}, bf16[656,128]{1,0:T(8,128)(2,1)S(1)}, u32[]{:S(2)}, u32[]{:S(2)}) collective-permute-start(bf16[656,128]{1,0:T(8,128)(2,1)S(1)} %constant_dynamic-update-slice_fusion), channel_id=1, source_target_pairs={{0,8},{1,65},{2,10},{3,67},{4,12},{5,69},{6,14},{7,71},{8,16},{9,7... | collective-permute-start | bytes 503816 | tf_op jit(solution)/shard_map/ppermute | solution.py:291
  18.8 6.5 %collective-permute-start.3 = (bf16[256,128]{1,0:T(8,128)(2,1)S(1)}, bf16[256,128]{1,0:T(8,128)(2,1)S(1)}, u32[]{:S(2)}, u32[]{:S(2)}) collective-permute-start(bf16[256,128]{1,0:T(8,128)(2,1)S(1)} %get-tuple-element.39), channel_id=1, source_target_pairs={{0,64},{8,72},{16,80},{24,88},{64,128},{72,136},{80,144},{88,152},... | collective-permute-start | bytes 196616 | tf_op jit(solution)/shard_map/ppermute | solution.py:282
  21.9 8.6 %collective-permute-start.5 = (bf16[656,128]{1,0:T(8,128)(2,1)S(1)}, bf16[656,128]{1,0:T(8,128)(2,1)S(1)}, u32[]{:S(2)}, u32[]{:S(2)}) collective-permute-start(bf16[656,128]{1,0:T(8,128)(2,1)S(1)} %constant_dynamic-update-slice_fusion), channel_id=1, source_target_pairs={{0,16},{1,129},{2,18},{3,131},{4,20},{5,133},{6,22},{7,135},{8,24}... | collective-permute-start | bytes 503816 | tf_op jit(solution)/shard_map/ppermute | solution.py:291
  23.4 7.1 %collective-permute-start.6 = (bf16[656,128]{1,0:T(8,128)(2,1)S(1)}, bf16[656,128]{1,0:T(8,128)(2,1)S(1)}, u32[]{:S(2)}, u32[]{:S(2)}) collective-permute-start(bf16[656,128]{1,0:T(8,128)(2,1)S(1)} %constant_dynamic-update-slice_fusion), channel_id=1, source_target_pairs={{0,24},{1,193},{2,26},{3,195},{4,28},{5,197},{6,30},{7,199},{8,0},... | collective-permute-start | bytes 503816 | tf_op jit(solution)/shard_map/ppermute | solution.py:291
  25.4 8.6 %copy-start = (bf16[256,1024]{1,0:T(8,128)(2,1)S(1)}, bf16[256,1024]{1,0:T(8,128)(2,1)}, u32[]{:S(2)}) copy-start(bf16[256,1024]{1,0:T(8,128)(2,1)} %q_own.3) | copy-start | bytes 1572868
  25.4 8.0 %collective-permute-start.7 = (bf16[256,128]{1,0:T(8,128)(2,1)S(1)}, bf16[256,128]{1,0:T(8,128)(2,1)S(1)}, u32[]{:S(2)}, u32[]{:S(2)}) collective-permute-start(bf16[256,128]{1,0:T(8,128)(2,1)S(1)} %get-tuple-element.42), channel_id=1, source_target_pairs={{0,8},{8,16},{16,24},{24,0},{32,40},{40,48},{48,56},{56,32},{64,72... | collective-permute-start | bytes 196616 | tf_op jit(solution)/shard_map/ppermute | solution.py:294
  26.8 7.2 %collective-permute-start.8 = (bf16[256,128]{1,0:T(8,128)(2,1)S(1)}, bf16[256,128]{1,0:T(8,128)(2,1)S(1)}, u32[]{:S(2)}, u32[]{:S(2)}) collective-permute-start(bf16[256,128]{1,0:T(8,128)(2,1)S(1)} %get-tuple-element.41), channel_id=1, source_target_pairs={{0,16},{8,24},{16,0},{24,8},{32,48},{40,56},{48,32},{56,40},{64,80... | collective-permute-start | bytes 196616 | tf_op jit(solution)/shard_map/ppermute | solution.py:294
  29.4 4.6 %collective-permute-start.9 = (bf16[256,128]{1,0:T(8,128)(2,1)S(1)}, bf16[256,128]{1,0:T(8,128)(2,1)S(1)}, u32[]{:S(2)}, u32[]{:S(2)}) collective-permute-start(bf16[256,128]{1,0:T(8,128)(2,1)S(1)} %get-tuple-element.30), channel_id=1, source_target_pairs={{0,24},{8,0},{16,8},{24,16},{32,56},{40,32},{48,40},{56,48},{64,88... | collective-permute-start | bytes 196616 | tf_op jit(solution)/shard_map/ppermute | solution.py:294
  30.7 16.0 %collective-permute-start.10 = (bf16[2192,128]{1,0:T(8,128)(2,1)S(1)}, bf16[2192,128]{1,0:T(8,128)(2,1)S(1)}, u32[]{:S(2)}, u32[]{:S(2)}) collective-permute-start(bf16[2192,128]{1,0:T(8,128)(2,1)S(1)} %get-tuple-element.32.here.r0), channel_id=1, source_target_pairs={{0,64},{1,9},{2,66},{3,11},{4,68},{5,13},{6,70},{7,15},{8,72},{9,1... | collective-permute-start | bytes 1683464 | tf_op jit(solution)/shard_map/ppermute | solution.py:301
  31.1 15.6 %collective-permute-start.11 = (bf16[2192,128]{1,0:T(8,128)(2,1)S(1)}, bf16[2192,128]{1,0:T(8,128)(2,1)S(1)}, u32[]{:S(2)}, u32[]{:S(2)}) collective-permute-start(bf16[2192,128]{1,0:T(8,128)(2,1)S(1)} %get-tuple-element.32.here.r0), channel_id=1, source_target_pairs={{0,192},{1,25},{2,194},{3,27},{4,196},{5,29},{6,198},{7,31},{8,200... | collective-permute-start | bytes 1683464 | tf_op jit(solution)/shard_map/ppermute | solution.py:301
  33.4 13.3 %collective-permute-start.12 = (bf16[2192,128]{1,0:T(8,128)(2,1)S(1)}, bf16[2192,128]{1,0:T(8,128)(2,1)S(1)}, u32[]{:S(2)}, u32[]{:S(2)}) collective-permute-start(bf16[2192,128]{1,0:T(8,128)(2,1)S(1)} %get-tuple-element.32.here.r0), channel_id=1, source_target_pairs={{0,128},{1,17},{2,130},{3,19},{4,132},{5,21},{6,134},{7,23},{8,136... | collective-permute-start | bytes 1683464 | tf_op jit(solution)/shard_map/ppermute | solution.py:301
  47.9 17.4 %collective-permute-start.14 = (bf16[32,32,256]{2,1,0:T(8,128)(2,1)S(1)}, bf16[32,32,256]{2,1,0:T(8,128)(2,1)S(1)}, u32[]{:S(2)}, u32[]{:S(2)}) collective-permute-start(bf16[32,32,256]{2,1,0:T(8,128)(2,1)S(1)} %shard_map.71), channel_id=1, source_target_pairs={{0,1},{1,0},{2,3},{3,2},{4,5},{5,4},{6,7},{7,6},{8,9},{9,8},{10,11... | collective-permute-start | bytes 1572872 | tf_op jit(solution)/shard_map/ppermute | solution.py:313
  65.2 2.1 %collective-permute-start.13 = (bf16[256,1152]{1,0:T(8,128)(2,1)S(1)}, bf16[256,1152]{1,0:T(8,128)(2,1)S(1)}, u32[]{:S(2)}, u32[]{:S(2)}) collective-permute-start(bf16[256,1152]{1,0:T(8,128)(2,1)S(1)} %get-tuple-element.29), channel_id=1, source_target_pairs={{0,1},{1,0},{2,3},{3,2},{4,5},{5,4},{6,7},{7,6},{8,9},{9,8},{10,11... | collective-permute-start | bytes 1769480 | tf_op jit(solution)/shard_map/ppermute | solution.py:324

commit v9 on v8

--- a/solution.py
+++ b/solution.py
@@ -150,17 +150,31 @@
         heads(i)
 
 
-def finish(state):
-    m, l, o = state
-    return o / l, m * SCALE + jnp.log2(l)
-
-
-def rest_kernel(sc, q_own, q_other, r1, r3, r2, sink, mlp_in, op_in, ml_in, o_in, keep, keep_lse, send,
-                kr, vr, ks, vs, lse_s):
+def middle_kernel(sc, q_own, q_other, r1, r3, ml_in, o_in, ml_out, o_out, kr, vr):
+    is_r = sc[5]
+    put_ranges(kr, vr, 0, r1)
+    put_ranges(kr, vr, 8 * HALF, r3)
+    put_range_bias(kr, vr, sc, (1, 3))
+
+    def heads(i):
+        at = [WIDE * i + u for u in range(WIDE)]
+        q = [load_head(q_own, q_other, is_r, a) for a in at]
+        state = [(*unpack(ml_in[a]), o_in[a]) for a in at]
+        for n in range(4):
+            rows = slice(n * CHUNK, (n + 1) * CHUNK)
+            state = [fold(state[u], q[u], kr[rows, :], vr[rows, :]) for u in range(WIDE)]
+        for u in range(WIDE):
+            ml_out[at[u]], o_out[at[u]] = pack(*state[u][:2]), state[u][2]
+
+    for i in range(GROUP // WIDE):
+        heads(i)
+
+
+def last_kernel(sc, q_own, q_other, r2, sink, mlp_in, op_in, ml_in, o_in, keep, keep_ml, send,
+                kr, vr, ks, vs, mlr_s, mlp_s):
     core, c, is_r = sc[3], sc[4], sc[5]
-    for n, ref in enumerate((r1, r3, r2)):
-        put_ranges(kr, vr, n * 8 * HALF, ref)
-    put_range_bias(kr, vr, sc, (1, 3, 2))
+    put_ranges(kr, vr, 0, r2)
+    put_range_bias(kr, vr, sc, (2,))
     ks[...] = jnp.zeros((HALF, 2 * HD), BF16)
     vs[...] = jnp.zeros((HALF, 2 * HD), BF16)
     put_keys(ks, vs, 0, sink, 0, SINK, SINK)
@@ -169,8 +183,8 @@
     lane = iota((ROWS, HD), 1)
     seen = (core == 0) & (lane < SINK) & (c * ROWS + row - lane >= RECENT)
     sink_bias = jnp.where(seen, 0.0, NEG)
-    lse_s[...] = jnp.zeros((ROWS, HD), F32)
-    keep_lse[...] = jnp.zeros((ROWS, HD), F32)
+    mlr_s[...] = jnp.zeros((ROWS, HD), F32)
+    mlp_s[...] = jnp.zeros((ROWS, HD), F32)
 
     def heads(i):
         at = [WIDE * i + u for u in range(WIDE)]
@@ -178,41 +192,42 @@
         qr = [load_head(q_own, q_other, is_r, a) for a in at]
         sr = [(*unpack(ml_in[a]), o_in[a]) for a in at]
         sp = [(*unpack(mlp_in[a]), op_in[a]) for a in at]
-        for n in range(6):
-            rows = slice(n * CHUNK, (n + 1) * CHUNK)
-            sr = [fold(sr[u], qr[u], kr[rows, :], vr[rows, :]) for u in range(WIDE)]
-            if n == 2:
-                sp = [fold(sp[u], qp[u], ks[...], vs[...], left=sink_bias) for u in range(WIDE)]
+        sr = [fold(sr[u], qr[u], kr[0:CHUNK, :], vr[0:CHUNK, :]) for u in range(WIDE)]
+        sp = [fold(sp[u], qp[u], ks[...], vs[...], left=sink_bias) for u in range(WIDE)]
+        sr = [fold(sr[u], qr[u], kr[CHUNK:, :], vr[CHUNK:, :]) for u in range(WIDE)]
         for u in range(WIDE):
             cols = slice(at[u] * HD, (at[u] + 1) * HD)
-            out_r, lse_r = finish(sr[u])
-            out_p, lse_p = finish(sp[u])
-            keep[:, cols] = jnp.where(is_r == 1, out_r, out_p).astype(BF16)
-            send[:, cols] = jnp.where(is_r == 1, out_p, out_r).astype(BF16)
-            keep_lse[...] = jnp.where(lane == at[u], jnp.where(is_r == 1, lse_r, lse_p), keep_lse[...])
-            lse_s[...] = jnp.where(lane == at[u], jnp.where(is_r == 1, lse_p, lse_r), lse_s[...])
+            keep[:, cols] = jnp.where(is_r == 1, sr[u][2], sp[u][2]).astype(BF16)
+            send[:, cols] = jnp.where(is_r == 1, sp[u][2], sr[u][2]).astype(BF16)
+            for ref, (m, l, _) in ((mlr_s, sr[u]), (mlp_s, sp[u])):
+                ref[...] = jnp.where(lane == at[u], m, jnp.where(lane == at[u] + GROUP, l, ref[...]))
 
     for i in range(GROUP // WIDE):
         heads(i)
-    lse = lse_s[...]
-    high = lse.astype(BF16).astype(F32)
-    mid = (lse - high).astype(BF16).astype(F32)
-    low = lse - high - mid
-    parts = high + pltpu.roll(mid, GROUP, 1) + pltpu.roll(low, 2 * GROUP, 1)
+    keep_ml[...] = jnp.where(is_r == 1, mlr_s[...], mlp_s[...])
+    ml = jnp.where(is_r == 1, mlp_s[...], mlr_s[...])
+    high = ml.astype(BF16).astype(F32)
+    mid = (ml - high).astype(BF16).astype(F32)
+    low = ml - high - mid
+    parts = high + pltpu.roll(mid, 2 * GROUP, 1) + pltpu.roll(low, 4 * GROUP, 1)
     send[:, GROUP * HD:] = parts.astype(BF16)
 
 
-def merge_kernel(keep, keep_lse, got, out_ref):
+def merge_kernel(keep, keep_ml, got, out_ref):
     ext = got[:, GROUP * HD:].astype(F32)
-    lse = ext + pltpu.roll(ext, HD - GROUP, 1) + pltpu.roll(ext, HD - 2 * GROUP, 1)
-    lane = iota((ROWS, HD), 1)
-    gap = jnp.where(lane < GROUP, lse - keep_lse[...], 0.0)
-    weight = 1.0 / (1.0 + jnp.exp2(jnp.clip(gap, -126.0, 126.0)))
+    theirs = ext + pltpu.roll(ext, HD - 2 * GROUP, 1) + pltpu.roll(ext, HD - 4 * GROUP, 1)
+    mine = keep_ml[...]
+    used = iota((ROWS, HD), 1) < GROUP
+    m0, m1 = jnp.where(used, mine, 0.0), jnp.where(used, theirs, 0.0)
+    l0, l1 = pltpu.roll(mine, HD - GROUP, 1), pltpu.roll(theirs, HD - GROUP, 1)
+    top = jnp.maximum(m0, m1)
+    w0, w1 = jnp.exp2((m0 - top) * SCALE), jnp.exp2((m1 - top) * SCALE)
+    scale = 1.0 / jnp.where(used, l0 * w0 + l1 * w1, 1.0)
+    w0, w1 = w0 * scale, w1 * scale
     for a in range(GROUP):
         cols = slice(a * HD, (a + 1) * HD)
-        w = weight[:, a:a + 1]
-        mine, theirs = keep[:, cols].astype(F32), got[:, cols].astype(F32)
-        out_ref[:, cols] = (theirs + w * (mine - theirs)).astype(BF16)
+        out = keep[:, cols].astype(F32) * w0[:, a:a + 1] + got[:, cols].astype(F32) * w1[:, a:a + 1]
+        out_ref[:, cols] = out.astype(BF16)
 
 
 def pages_kernel(sc, r0, r1, r2, r3, out_ref):
@@ -306,24 +321,26 @@
         sc, q, q_other, message, pas, p[1], p[2], p[3], far)
     for s in (1, 2, 3):
         sink = jnp.where(x == s, r[s][8 * ROWS + META:], sink)
+    now_ml, now_o = call(
+        middle_kernel, state, keys(16 * HALF), 8 * unit, sc, q, q_other, r[1], r[3], now_ml, now_o)
     sc_l, now_ml = lax.optimization_barrier((sc, now_ml))
     pages = call(
         pages_kernel, jax.ShapeDtypeStruct((32, 2 * PAGE, 2 * HD), BF16), [], unit // 4,
         sc_l, *[r[s] for s in range(4)])
     got_pages = lax.ppermute(pages, "tp", CORE_SWAP)
-    keep, keep_lse, send = call(
-        rest_kernel,
+    keep, keep_ml, send = call(
+        last_kernel,
         (
             jax.ShapeDtypeStruct((ROWS, GROUP * HD), BF16),
             jax.ShapeDtypeStruct((ROWS, HD), F32),
             jax.ShapeDtypeStruct((ROWS, (GROUP + 1) * HD), BF16),
         ),
-        keys(24 * HALF) + keys(HALF) + [pltpu.VMEM((ROWS, HD), F32)],
-        13 * unit, sc_l, q, q_other, r[1], r[3], r[2], sink, *now_p, now_ml, now_o)
+        keys(8 * HALF) + keys(HALF) + [pltpu.VMEM((ROWS, HD), F32)] * 2,
+        5 * unit, sc_l, q, q_other, r[2], sink, *now_p, now_ml, now_o)
 
     got = lax.ppermute(send, "tp", CORE_SWAP)
     attn_out = call(
-        merge_kernel, jax.ShapeDtypeStruct((ROWS, GROUP * HD), BF16), [], unit // 4, None, keep, keep_lse, got)
+        merge_kernel, jax.ShapeDtypeStruct((ROWS, GROUP * HD), BF16), [], unit // 4, None, keep, keep_ml, got)
     decode_cache = jnp.where(is_r, pages + got_pages, jnp.zeros((), BF16)).reshape(64, PAGE, 2 * HD)
     return attn_out, decode_cache
 

time: 68.7 us -> 72.6 us (1.057)
  the two profiles are of different devices: /device:TPU:33 before, /device:TPU:39 now
where the time goes in v9:
time: 72.6 us; the launch traced here: 72.4 us
  starting transfers between devices  27.6 us (38%)
  Pallas kernels  25.9 us (36%)
  waiting for transfers between devices  13.6 us (19%)
  local copies, waits for them, and re-layouts  2.32 us (3%)
  other arithmetic  1.52 us (2%)
  between operations  1.48 us (2%)
    pallas_call x5, Pallas kernels, call(): pl.pallas_call(kernel, out_shape=out_shape, in_specs=specs, out_specs=(VM...  25.9 us
    ppermute x1, waiting for transfers between devices, shards(): theirs = lax.ppermute(jnp.concatenate([ret, pas, meta]), 'ctx', Z_SWAP)  6.47 us
    ppermute x1, starting transfers between devices, shards(): theirs = lax.ppermute(jnp.concatenate([ret, pas, meta]), 'ctx', Z_SWAP)  6.1 us
    ppermute x3, waiting for transfers between devices, shards(): lax.ppermute(message, axes, STAGE_2[s])  5.79 us
    ppermute x1, starting transfers between devices, shards(): got_pages = lax.ppermute(pages, 'tp', CORE_SWAP)  5.77 us
    ppermute x3, starting transfers between devices, shards(): lax.ppermute(jnp.where(y + s < 4, pas, far), 'ctx', Y_SHIFT[s])  5.68 us
    ppermute x3, starting transfers between devices, shards(): got = {s: lax.ppermute(message, axes, STAGE_1[s]) for s in (1, 3, 2)}  3.98 us
    ppermute x3, starting transfers between devices, shards(): lax.ppermute(message, axes, STAGE_2[s])  3.8 us
  transfers between devices with their start and end apart: 15, of which 5 were waited for; matrix products, arithmetic and copies ran while one was open for 3% of the time, Pallas kernels for 32%

profile of v9, /device:TPU:39, one launch (start us, length us, event | category | flops | bytes accessed | tf_op | source)
XLA Modules:
  0.0 72.4 jit_solution(7598281992168315002)
XLA Ops:
  0.6 0.8 %fusion.11 = (bf16[128,128]{1,0:T(8,128)(2,1)S(1)}, bf16[128,128]{1,0:T(8,128)(2,1)S(1)}, bf16[128,128]{1,0:T(8,128)(2,1)S(1)}, bf16[128,128]{1,0:T(8,128)(2,1)S(1)}) fusion(bf16[256,128]{1,0:T(8,128)(2,1)} %param.6, bf16[256,128]{1,0:T(8,128)(2,1)} %param.7), kind=kLoop, calls=%fused_computation.46 | loop fusion | bytes 262144 | tf_op jit(solution)/shard_map/slice | solution.py:281
  1.5 0.8 %collective-permute-start = (bf16[256,128]{1,0:T(8,128)(2,1)S(1)}, bf16[256,128]{1,0:T(8,128)(2,1)S(1)}, u32[]{:S(2)}, u32[]{:S(2)}) collective-permute-start(bf16[256,128]{1,0:T(8,128)(2,1)S(1)} %broadcast_select_fusion.5), channel_id=1, source_target_pairs={{0,1},{1,0},{2,3},{3,2},{4,5},{5,4},{6,7},{7,6},{8,9},{9,8},{10,11... | collective-permute-start | bytes 196616 | tf_op jit(solution)/shard_map/ppermute | solution.py:284
  2.3 0.1 collective-permute-start.2
  2.4 0.2 convert_reduce_fusion
  2.7 0.1 broadcast_in_dim.19
  2.8 0.6 copy-done.2
  3.4 0.6 dynamic_slice.4
  4.7 6.1 %collective-permute-start.1 = (bf16[528,128]{1,0:T(8,128)(2,1)S(1)}, bf16[528,128]{1,0:T(8,128)(2,1)S(1)}, u32[]{:S(2)}, u32[]{:S(2)}) collective-permute-start(bf16[528,128]{1,0:T(8,128)(2,1)S(1)} %pad_maximum_fusion), channel_id=1, source_target_pairs={{0,32},{8,40},{16,48},{24,56},{32,0},{40,8},{48,16},{56,24},{64,96... | collective-permute-start | bytes 405512 | tf_op jit(solution)/shard_map/ppermute | solution.py:295
  10.8 6.5 %collective-permute-done.1 = bf16[528,128]{1,0:T(8,128)(2,1)S(1)} collective-permute-done((bf16[528,128]{1,0:T(8,128)(2,1)S(1)}, bf16[528,128]{1,0:T(8,128)(2,1)S(1)}, u32[]{:S(2)}, u32[]{:S(2)}) %collective-permute-start.1) | collective-permute-done | bytes 135200 | tf_op jit(solution)/shard_map/ppermute | solution.py:295
  17.4 0.2 collective-permute-start.4
  17.7 0.1 stack.33.sc
  17.7 1.3 %collective-permute-start.3 = (bf16[256,128]{1,0:T(8,128)(2,1)S(1)}, bf16[256,128]{1,0:T(8,128)(2,1)S(1)}, u32[]{:S(2)}, u32[]{:S(2)}) collective-permute-start(bf16[256,128]{1,0:T(8,128)(2,1)S(1)} %get-tuple-element.43), channel_id=1, source_target_pairs={{0,64},{8,72},{16,80},{24,88},{64,128},{72,136},{80,144},{88,152},... | collective-permute-start | bytes 196616 | tf_op jit(solution)/shard_map/ppermute | solution.py:297
  19.1 3.8 %collective-permute-start.5 = (bf16[656,128]{1,0:T(8,128)(2,1)S(1)}, bf16[656,128]{1,0:T(8,128)(2,1)S(1)}, u32[]{:S(2)}, u32[]{:S(2)}) collective-permute-start(bf16[656,128]{1,0:T(8,128)(2,1)S(1)} %constant_dynamic-update-slice_fusion), channel_id=1, source_target_pairs={{0,16},{1,129},{2,18},{3,131},{4,20},{5,133},{6,22},{7,135},{8,24}... | collective-permute-start | bytes 503816 | tf_op jit(solution)/shard_map/ppermute | solution.py:306
  22.8 0.2 collective-permute-done.3
  23.1 3.0 %collective-permute-start.10 = (bf16[256,128]{1,0:T(8,128)(2,1)S(1)}, bf16[256,128]{1,0:T(8,128)(2,1)S(1)}, u32[]{:S(2)}, u32[]{:S(2)}) collective-permute-start(bf16[256,128]{1,0:T(8,128)(2,1)S(1)} %get-tuple-element.45), channel_id=1, source_target_pairs={{0,16},{8,24},{16,0},{24,8},{32,48},{40,56},{48,32},{56,40},{64,80... | collective-permute-start | bytes 196616 | tf_op jit(solution)/shard_map/ppermute | solution.py:309
  26.1 0.4 collective-permute-start.9
  26.5 2.3 %collective-permute-start.11 = (bf16[256,128]{1,0:T(8,128)(2,1)S(1)}, bf16[256,128]{1,0:T(8,128)(2,1)S(1)}, u32[]{:S(2)}, u32[]{:S(2)}) collective-permute-start(bf16[256,128]{1,0:T(8,128)(2,1)S(1)} %get-tuple-element.34), channel_id=1, source_target_pairs={{0,24},{8,0},{16,8},{24,16},{32,56},{40,32},{48,40},{56,48},{64,88... | collective-permute-start | bytes 196616 | tf_op jit(solution)/shard_map/ppermute | solution.py:309
  28.9 0.1 constant_dynamic-update-slice_fusion.5
  29.0 0.9 %collective-permute-start.7 = (bf16[2192,128]{1,0:T(8,128)(2,1)S(1)}, bf16[2192,128]{1,0:T(8,128)(2,1)S(1)}, u32[]{:S(2)}, u32[]{:S(2)}) collective-permute-start(bf16[2192,128]{1,0:T(8,128)(2,1)S(1)} %get-tuple-element.36.here.r0), channel_id=1, source_target_pairs={{0,64},{1,9},{2,66},{3,11},{4,68},{5,13},{6,70},{7,15},{8,72},{9,1... | collective-permute-start | bytes 1683464 | tf_op jit(solution)/shard_map/ppermute | solution.py:316
  29.9 1.9 %collective-permute-start.8 = (bf16[2192,128]{1,0:T(8,128)(2,1)S(1)}, bf16[2192,128]{1,0:T(8,128)(2,1)S(1)}, u32[]{:S(2)}, u32[]{:S(2)}) collective-permute-start(bf16[2192,128]{1,0:T(8,128)(2,1)S(1)} %get-tuple-element.36.here.r0), channel_id=1, source_target_pairs={{0,192},{1,25},{2,194},{3,27},{4,196},{5,29},{6,198},{7,31},{8,200... | collective-permute-start | bytes 1683464 | tf_op jit(solution)/shard_map/ppermute | solution.py:316
  31.8 1.1 %collective-permute-start.12 = (bf16[2192,128]{1,0:T(8,128)(2,1)S(1)}, bf16[2192,128]{1,0:T(8,128)(2,1)S(1)}, u32[]{:S(2)}, u32[]{:S(2)}) collective-permute-start(bf16[2192,128]{1,0:T(8,128)(2,1)S(1)} %get-tuple-element.36.here.r0), channel_id=1, source_target_pairs={{0,128},{1,17},{2,130},{3,19},{4,132},{5,21},{6,134},{7,23},{8,136... | collective-permute-start | bytes 1683464 | tf_op jit(solution)/shard_map/ppermute | solution.py:316
  32.9 6.4 %shard_map.68 = (f32[8,256,128]{2,1,0:T(8,128)S(1)}, f32[8,256,128]{2,1,0:T(8,128)S(1)}, f32[8,256,128]{2,1,0:T(8,128)S(1)}, f32[8,256,128]{2,1,0:T(8,128)S(1)}) custom-call(s32[8]{0:T(128)S(1)} %stack.33.sc, bf16[256,1024]{1,0:T(8,128)(2,1)S(1)} %copy-done, bf16[256,1024]{1,0:T(8,128)(2,1)S(1)} %collective-permute-done.2.q_other, ...), custom_call_target="tpu_custom_call" | custom-call | flops 32212254720 | bytes 4194304 | tf_op jit(solution)/shard_map/pallas_call | solution.py:258
  39.2 0.5 collective-permute-done.7.r1
  39.7 5.3 %collective-permute-done.8.r3 = bf16[2192,128]{1,0:T(8,128)(2,1)S(1)} collective-permute-done((bf16[2192,128]{1,0:T(8,128)(2,1)S(1)}, bf16[2192,128]{1,0:T(8,128)(2,1)S(1)}, u32[]{:S(2)}, u32[]{:S(2)}) %collective-permute-start.8) | collective-permute-done | bytes 561184 | tf_op jit(solution)/shard_map/ppermute | solution.py:316
  45.0 6.8 %shard_map.69 = (f32[8,256,128]{2,1,0:T(8,128)S(1)}, f32[8,256,128]{2,1,0:T(8,128)S(1)}) custom-call(s32[8]{0:T(128)S(1)} %stack.33.sc, bf16[256,1024]{1,0:T(8,128)(2,1)S(1)} %copy-done, bf16[256,1024]{1,0:T(8,128)(2,1)S(1)} %collective-permute-done.2.q_other, bf16[2192,128]{1,0:T(8,128)(2,1)S(1)} %collective-permute-done.7.r1, ...), custom_call_target="tpu_custom_call" | custom-call | flops 4294967296 | bytes 4194304 | tf_op jit(solution)/shard_map/pallas_call | solution.py:258
  51.9 1.4 %shard_map.72 = bf16[32,32,256]{2,1,0:T(8,128)(2,1)S(1)} custom-call(s32[8]{0:T(128)S(1)} %stack.33.sc, bf16[2192,128]{1,0:T(8,128)(2,1)S(1)} %get-tuple-element.36.here.r0, bf16[2192,128]{1,0:T(8,128)(2,1)S(1)} %collective-permute-done.7.r1, bf16[2192,128]{1,0:T(8,128)(2,1)S(1)} %collective-permute-done.12.r2, bf16[2192,128]{1,0:T(8,128)(2,1)S(1)} %collective-permute-done.8.r3), custom_call_target="tpu_custom_call" | custom-call | flops 134217728 | bytes 4194304 | tf_op jit(solution)/shard_map/pallas_call | solution.py:258
  53.3 5.8 %collective-permute-start.14 = (bf16[32,32,256]{2,1,0:T(8,128)(2,1)S(1)}, bf16[32,32,256]{2,1,0:T(8,128)(2,1)S(1)}, u32[]{:S(2)}, u32[]{:S(2)}) collective-permute-start(bf16[32,32,256]{2,1,0:T(8,128)(2,1)S(1)} %shard_map.72), channel_id=1, source_target_pairs={{0,1},{1,0},{2,3},{3,2},{4,5},{5,4},{6,7},{7,6},{8,9},{9,8},{10,11... | collective-permute-start | bytes 1572872 | tf_op jit(solution)/shard_map/ppermute | solution.py:330
  59.1 9.7 %shard_map.70 = (bf16[256,1024]{1,0:T(8,128)(2,1)S(1)}, f32[256,128]{1,0:T(8,128)S(1)}, bf16[256,1152]{1,0:T(8,128)(2,1)S(1)}) custom-call(s32[8]{0:T(128)S(1)} %stack.33.sc, bf16[256,1024]{1,0:T(8,128)(2,1)S(1)} %copy-done, bf16[256,1024]{1,0:T(8,128)(2,1)S(1)} %collective-permute-done.2.q_other, bf16[2192,128]{1,0:T(8,128)(2,1)S(1)} %collective-permute-done.12.r2, ...), custom_call_target="tpu_custom_call" | custom-call | flops 2684354560 | bytes 4194304 | tf_op jit(solution)/shard_map/pallas_call | solution.py:258
  68.8 0.1 collective-permute-start.13
  68.9 0.8 %add_select_fusion = bf16[32,32,256]{2,1,0:T(8,128)(2,1)} fusion(bf16[32,32,256]{2,1,0:T(8,128)(2,1)S(1)} %shard_map.72, bf16[32,32,256]{2,1,0:T(8,128)(2,1)S(1)} %collective-permute-done.14, pred[]{:T(512)} %bitcast.6), kind=kLoop, calls=%fused_computation | loop fusion | flops 524288 | bytes 1572865 | tf_op jit(solution)/shard_map/jit(_where)/select_n | solution.py:344
  69.7 1.1 %collective-permute-done.13.got = bf16[256,1152]{1,0:T(8,128)(2,1)S(1)} collective-permute-done((bf16[256,1152]{1,0:T(8,128)(2,1)S(1)}, bf16[256,1152]{1,0:T(8,128)(2,1)S(1)}, u32[]{:S(2)}, u32[]{:S(2)}) %collective-permute-start.13) | collective-permute-done | bytes 589856 | tf_op jit(solution)/shard_map/ppermute | solution.py:341
  70.8 1.6 %shard_map.71 = bf16[256,1024]{1,0:T(8,128)(2,1)} custom-call(bf16[256,1024]{1,0:T(8,128)(2,1)S(1)} %get-tuple-element.31.keep, f32[256,128]{1,0:T(8,128)S(1)} %get-tuple-element.32.keep_ml, bf16[256,1152]{1,0:T(8,128)(2,1)S(1)} %collective-permute-done.13.got), custom_call_target="tpu_custom_call" | custom-call | flops 134217728 | bytes 4194304 | tf_op jit(solution)/shard_map/pallas_call | solution.py:258
  (38 shorter events, 0.6 us)
Async XLA Ops:
  1.5 0.9 %copy-start.1 = (s32[16]{0:T(128)S(1)}, s32[16]{0:T(128)}, u32[]{:S(2)}) copy-start(s32[16]{0:T(128)} %param.9) | copy-start | bytes 196
  1.5 3.1 %collective-permute-start = (bf16[256,128]{1,0:T(8,128)(2,1)S(1)}, bf16[256,128]{1,0:T(8,128)(2,1)S(1)}, u32[]{:S(2)}, u32[]{:S(2)}) collective-permute-start(bf16[256,128]{1,0:T(8,128)(2,1)S(1)} %broadcast_select_fusion.5), channel_id=1, source_target_pairs={{0,1},{1,0},{2,3},{3,2},{4,5},{5,4},{6,7},{7,6},{8,9},{9,8},{10,11... | collective-permute-start | bytes 196616 | tf_op jit(solution)/shard_map/ppermute | solution.py:284
  2.3 15.0 %collective-permute-start.2 = (bf16[256,1024]{1,0:T(8,128)(2,1)}, bf16[256,1024]{1,0:T(8,128)(2,1)S(1)}, u32[]{:S(2)}, u32[]{:S(2)}) collective-permute-start(bf16[256,1024]{1,0:T(8,128)(2,1)} %q_own.5), channel_id=1, source_target_pairs={{0,1},{1,0},{2,3},{3,2},{4,5},{5,4},{6,7},{7,6},{8,9},{9,8},{10,11... | collective-permute-start | bytes 1572872 | tf_op jit(solution)/shard_map/ppermute | solution.py:285
  2.7 0.7 copy-start.2
  4.7 12.6 %collective-permute-start.1 = (bf16[528,128]{1,0:T(8,128)(2,1)S(1)}, bf16[528,128]{1,0:T(8,128)(2,1)S(1)}, u32[]{:S(2)}, u32[]{:S(2)}) collective-permute-start(bf16[528,128]{1,0:T(8,128)(2,1)S(1)} %pad_maximum_fusion), channel_id=1, source_target_pairs={{0,32},{8,40},{16,48},{24,56},{32,0},{40,8},{48,16},{56,24},{64,96... | collective-permute-start | bytes 405512 | tf_op jit(solution)/shard_map/ppermute | solution.py:295
  17.4 5.6 %collective-permute-start.4 = (bf16[656,128]{1,0:T(8,128)(2,1)S(1)}, bf16[656,128]{1,0:T(8,128)(2,1)S(1)}, u32[]{:S(2)}, u32[]{:S(2)}) collective-permute-start(bf16[656,128]{1,0:T(8,128)(2,1)S(1)} %constant_dynamic-update-slice_fusion), channel_id=1, source_target_pairs={{0,8},{1,65},{2,10},{3,67},{4,12},{5,69},{6,14},{7,71},{8,16},{9,7... | collective-permute-start | bytes 503816 | tf_op jit(solution)/shard_map/ppermute | solution.py:306
  17.7 5.3 %collective-permute-start.3 = (bf16[256,128]{1,0:T(8,128)(2,1)S(1)}, bf16[256,128]{1,0:T(8,128)(2,1)S(1)}, u32[]{:S(2)}, u32[]{:S(2)}) collective-permute-start(bf16[256,128]{1,0:T(8,128)(2,1)S(1)} %get-tuple-element.43), channel_id=1, source_target_pairs={{0,64},{8,72},{16,80},{24,88},{64,128},{72,136},{80,144},{88,152},... | collective-permute-start | bytes 196616 | tf_op jit(solution)/shard_map/ppermute | solution.py:297
  19.1 9.8 %collective-permute-start.5 = (bf16[656,128]{1,0:T(8,128)(2,1)S(1)}, bf16[656,128]{1,0:T(8,128)(2,1)S(1)}, u32[]{:S(2)}, u32[]{:S(2)}) collective-permute-start(bf16[656,128]{1,0:T(8,128)(2,1)S(1)} %constant_dynamic-update-slice_fusion), channel_id=1, source_target_pairs={{0,16},{1,129},{2,18},{3,131},{4,20},{5,133},{6,22},{7,135},{8,24}... | collective-permute-start | bytes 503816 | tf_op jit(solution)/shard_map/ppermute | solution.py:306
  22.8 6.1 %collective-permute-start.6 = (bf16[656,128]{1,0:T(8,128)(2,1)S(1)}, bf16[656,128]{1,0:T(8,128)(2,1)S(1)}, u32[]{:S(2)}, u32[]{:S(2)}) collective-permute-start(bf16[656,128]{1,0:T(8,128)(2,1)S(1)} %constant_dynamic-update-slice_fusion), channel_id=1, source_target_pairs={{0,24},{1,193},{2,26},{3,195},{4,28},{5,197},{6,30},{7,199},{8,0},... | collective-permute-start | bytes 503816 | tf_op jit(solution)/shard_map/ppermute | solution.py:306
  23.1 9.7 %copy-start = (bf16[256,1024]{1,0:T(8,128)(2,1)S(1)}, bf16[256,1024]{1,0:T(8,128)(2,1)}, u32[]{:S(2)}) copy-start(bf16[256,1024]{1,0:T(8,128)(2,1)} %q_own.5) | copy-start | bytes 1572868
  23.1 8.7 %collective-permute-start.10 = (bf16[256,128]{1,0:T(8,128)(2,1)S(1)}, bf16[256,128]{1,0:T(8,128)(2,1)S(1)}, u32[]{:S(2)}, u32[]{:S(2)}) collective-permute-start(bf16[256,128]{1,0:T(8,128)(2,1)S(1)} %get-tuple-element.45), channel_id=1, source_target_pairs={{0,16},{8,24},{16,0},{24,8},{32,48},{40,56},{48,32},{56,40},{64,80... | collective-permute-start | bytes 196616 | tf_op jit(solution)/shard_map/ppermute | solution.py:309
  26.1 6.7 %collective-permute-start.9 = (bf16[256,128]{1,0:T(8,128)(2,1)S(1)}, bf16[256,128]{1,0:T(8,128)(2,1)S(1)}, u32[]{:S(2)}, u32[]{:S(2)}) collective-permute-start(bf16[256,128]{1,0:T(8,128)(2,1)S(1)} %get-tuple-element.46), channel_id=1, source_target_pairs={{0,8},{8,16},{16,24},{24,0},{32,40},{40,48},{48,56},{56,32},{64,72... | collective-permute-start | bytes 196616 | tf_op jit(solution)/shard_map/ppermute | solution.py:309
  26.5 6.3 %collective-permute-start.11 = (bf16[256,128]{1,0:T(8,128)(2,1)S(1)}, bf16[256,128]{1,0:T(8,128)(2,1)S(1)}, u32[]{:S(2)}, u32[]{:S(2)}) collective-permute-start(bf16[256,128]{1,0:T(8,128)(2,1)S(1)} %get-tuple-element.34), channel_id=1, source_target_pairs={{0,24},{8,0},{16,8},{24,16},{32,56},{40,32},{48,40},{56,48},{64,88... | collective-permute-start | bytes 196616 | tf_op jit(solution)/shard_map/ppermute | solution.py:309
  29.0 10.7 %collective-permute-start.7 = (bf16[2192,128]{1,0:T(8,128)(2,1)S(1)}, bf16[2192,128]{1,0:T(8,128)(2,1)S(1)}, u32[]{:S(2)}, u32[]{:S(2)}) collective-permute-start(bf16[2192,128]{1,0:T(8,128)(2,1)S(1)} %get-tuple-element.36.here.r0), channel_id=1, source_target_pairs={{0,64},{1,9},{2,66},{3,11},{4,68},{5,13},{6,70},{7,15},{8,72},{9,1... | collective-permute-start | bytes 1683464 | tf_op jit(solution)/shard_map/ppermute | solution.py:316
  29.9 15.1 %collective-permute-start.8 = (bf16[2192,128]{1,0:T(8,128)(2,1)S(1)}, bf16[2192,128]{1,0:T(8,128)(2,1)S(1)}, u32[]{:S(2)}, u32[]{:S(2)}) collective-permute-start(bf16[2192,128]{1,0:T(8,128)(2,1)S(1)} %get-tuple-element.36.here.r0), channel_id=1, source_target_pairs={{0,192},{1,25},{2,194},{3,27},{4,196},{5,29},{6,198},{7,31},{8,200... | collective-permute-start | bytes 1683464 | tf_op jit(solution)/shard_map/ppermute | solution.py:316
  31.8 20.1 %collective-permute-start.12 = (bf16[2192,128]{1,0:T(8,128)(2,1)S(1)}, bf16[2192,128]{1,0:T(8,128)(2,1)S(1)}, u32[]{:S(2)}, u32[]{:S(2)}) collective-permute-start(bf16[2192,128]{1,0:T(8,128)(2,1)S(1)} %get-tuple-element.36.here.r0), channel_id=1, source_target_pairs={{0,128},{1,17},{2,130},{3,19},{4,132},{5,21},{6,134},{7,23},{8,136... | collective-permute-start | bytes 1683464 | tf_op jit(solution)/shard_map/ppermute | solution.py:316
  53.3 15.6 %collective-permute-start.14 = (bf16[32,32,256]{2,1,0:T(8,128)(2,1)S(1)}, bf16[32,32,256]{2,1,0:T(8,128)(2,1)S(1)}, u32[]{:S(2)}, u32[]{:S(2)}) collective-permute-start(bf16[32,32,256]{2,1,0:T(8,128)(2,1)S(1)} %shard_map.72), channel_id=1, source_target_pairs={{0,1},{1,0},{2,3},{3,2},{4,5},{5,4},{6,7},{7,6},{8,9},{9,8},{10,11... | collective-permute-start | bytes 1572872 | tf_op jit(solution)/shard_map/ppermute | solution.py:330
  68.8 2.1 %collective-permute-start.13 = (bf16[256,1152]{1,0:T(8,128)(2,1)S(1)}, bf16[256,1152]{1,0:T(8,128)(2,1)S(1)}, u32[]{:S(2)}, u32[]{:S(2)}) collective-permute-start(bf16[256,1152]{1,0:T(8,128)(2,1)S(1)} %get-tuple-element.33), channel_id=1, source_target_pairs={{0,1},{1,0},{2,3},{3,2},{4,5},{5,4},{6,7},{7,6},{8,9},{9,8},{10,11... | collective-permute-start | bytes 1769480 | tf_op jit(solution)/shard_map/ppermute | solution.py:341

commit v10 on v9

--- a/solution.py
+++ b/solution.py
@@ -15,7 +15,7 @@
 ROWS = 256
 HALF = 128
 META = 16
-CHUNK = 512
+CHUNK = 1024
 WIDE = 2
 NEG = -1e30
 SCALE = math.log2(math.e) / math.sqrt(HD)
@@ -112,17 +112,8 @@
     return jnp.concatenate([q, one], axis=1)
 
 
-def pack(m, l):
-    return jnp.where(iota((ROWS, HD), 1) < HD // 2, m, l)
-
-
-def unpack(both):
-    low = iota((ROWS, HD), 1) < HD // 2
-    turned = pltpu.roll(both, HD // 2, 1)
-    return jnp.where(low, both, turned), jnp.where(low, turned, both)
-
-
-def near_kernel(sc, q_own, q_other, here, pas, p1, p2, p3, far, mlp_out, op_out, ml_out, o_out, kp, vp, kr, vr):
+def near_kernel(sc, q_own, q_other, here, pas, p1, p2, p3, far, mp_out, lp_out, op_out,
+                m_out, l_out, o_out, kp, vp, kr, vr):
     core, c, is_r = sc[3], sc[4], sc[5]
     put_ranges(kr, vr, 0, here)
     put_range_bias(kr, vr, sc, (0,))
@@ -138,19 +129,17 @@
         at = [WIDE * i + u for u in range(WIDE)]
         qp = [load_head(q_other, q_own, is_r, a) for a in at]
         q = [load_head(q_own, q_other, is_r, a) for a in at]
-        sr = [fold(None, q[u], kr[0:CHUNK, :], vr[0:CHUNK, :], left=own) for u in range(WIDE)]
-        sp = [fold(None, qp[u], kp[0:3 * HALF, :], vp[0:3 * HALF, :], left=own) for u in range(WIDE)]
-        sr = [fold(sr[u], q[u], kr[CHUNK:, :], vr[CHUNK:, :]) for u in range(WIDE)]
-        sp = [fold(sp[u], qp[u], kp[3 * HALF:, :], vp[3 * HALF:, :], right=edge) for u in range(WIDE)]
+        sp = [fold(None, qp[u], kp[...], vp[...], left=own, right=edge) for u in range(WIDE)]
+        sr = [fold(None, q[u], kr[...], vr[...], left=own) for u in range(WIDE)]
         for u in range(WIDE):
-            ml_out[at[u]], o_out[at[u]] = pack(*sr[u][:2]), sr[u][2]
-            mlp_out[at[u]], op_out[at[u]] = pack(*sp[u][:2]), sp[u][2]
+            m_out[at[u]], l_out[at[u]], o_out[at[u]] = sr[u]
+            mp_out[at[u]], lp_out[at[u]], op_out[at[u]] = sp[u]
 
     for i in range(GROUP // WIDE):
         heads(i)
 
 
-def middle_kernel(sc, q_own, q_other, r1, r3, ml_in, o_in, ml_out, o_out, kr, vr):
+def middle_kernel(sc, q_own, q_other, r1, r3, m_in, l_in, o_in, m_out, l_out, o_out, kr, vr):
     is_r = sc[5]
     put_ranges(kr, vr, 0, r1)
     put_ranges(kr, vr, 8 * HALF, r3)
@@ -159,18 +148,18 @@
     def heads(i):
         at = [WIDE * i + u for u in range(WIDE)]
         q = [load_head(q_own, q_other, is_r, a) for a in at]
-        state = [(*unpack(ml_in[a]), o_in[a]) for a in at]
-        for n in range(4):
+        state = [(m_in[a], l_in[a], o_in[a]) for a in at]
+        for n in range(2):
             rows = slice(n * CHUNK, (n + 1) * CHUNK)
             state = [fold(state[u], q[u], kr[rows, :], vr[rows, :]) for u in range(WIDE)]
         for u in range(WIDE):
-            ml_out[at[u]], o_out[at[u]] = pack(*state[u][:2]), state[u][2]
+            m_out[at[u]], l_out[at[u]], o_out[at[u]] = state[u]
 
     for i in range(GROUP // WIDE):
         heads(i)
 
 
-def last_kernel(sc, q_own, q_other, r2, sink, mlp_in, op_in, ml_in, o_in, keep, keep_ml, send,
+def last_kernel(sc, q_own, q_other, r2, sink, mp_in, lp_in, op_in, m_in, l_in, o_in, keep, keep_ml, send,
                 kr, vr, ks, vs, mlr_s, mlp_s):
     core, c, is_r = sc[3], sc[4], sc[5]
     put_ranges(kr, vr, 0, r2)
@@ -190,11 +179,10 @@
         at = [WIDE * i + u for u in range(WIDE)]
         qp = [load_head(q_other, q_own, is_r, a) for a in at]
         qr = [load_head(q_own, q_other, is_r, a) for a in at]
-        sr = [(*unpack(ml_in[a]), o_in[a]) for a in at]
-        sp = [(*unpack(mlp_in[a]), op_in[a]) for a in at]
-        sr = [fold(sr[u], qr[u], kr[0:CHUNK, :], vr[0:CHUNK, :]) for u in range(WIDE)]
+        sr = [(m_in[a], l_in[a], o_in[a]) for a in at]
+        sp = [(mp_in[a], lp_in[a], op_in[a]) for a in at]
         sp = [fold(sp[u], qp[u], ks[...], vs[...], left=sink_bias) for u in range(WIDE)]
-        sr = [fold(sr[u], qr[u], kr[CHUNK:, :], vr[CHUNK:, :]) for u in range(WIDE)]
+        sr = [fold(sr[u], qr[u], kr[...], vr[...]) for u in range(WIDE)]
         for u in range(WIDE):
             cols = slice(at[u] * HD, (at[u] + 1) * HD)
             keep[:, cols] = jnp.where(is_r == 1, sr[u][2], sp[u][2]).astype(BF16)
@@ -275,7 +263,7 @@
     tp = lax.axis_index("tp")
     x, z, y = c // 8, (c // 4) % 2, c % 4
     core = tp % 2
-    is_r = lax.dynamic_index_in_dim(head_kind, tp, 0, keepdims=False) == 1
+    is_r = jnp.sum(jnp.where(lax.iota(jnp.int32, head_kind.shape[0]) == tp, head_kind, 0)) == 1
     sc = jnp.stack([x, y, z, core, c, is_r.astype(jnp.int32), tp, tp]).astype(jnp.int32)
 
     low = jnp.concatenate([k[:HALF], v[:HALF]])
@@ -314,16 +302,16 @@
     message = jnp.concatenate([both] + [got[s][:2 * ROWS] for s in (1, 2, 3)] + [meta, sink])
 
     r = {0: message} | {s: lax.ppermute(message, axes, STAGE_2[s]) for s in (1, 3, 2)}
-    state = (jax.ShapeDtypeStruct((GROUP, ROWS, HD), F32),) * 2
+    state = (jax.ShapeDtypeStruct((GROUP, ROWS, HD), F32),) * 3
     unit = 2 * 2048 * 256 * 512
-    *now_p, now_ml, now_o = call(
+    *now_p, now_m, now_l, now_o = call(
         near_kernel, state + state, keys(5 * HALF) + keys(8 * HALF), 60 * unit,
         sc, q, q_other, message, pas, p[1], p[2], p[3], far)
     for s in (1, 2, 3):
         sink = jnp.where(x == s, r[s][8 * ROWS + META:], sink)
-    now_ml, now_o = call(
-        middle_kernel, state, keys(16 * HALF), 8 * unit, sc, q, q_other, r[1], r[3], now_ml, now_o)
-    sc_l, now_ml = lax.optimization_barrier((sc, now_ml))
+    now_m, now_l, now_o = call(
+        middle_kernel, state, keys(16 * HALF), 8 * unit, sc, q, q_other, r[1], r[3], now_m, now_l, now_o)
+    sc_l, now_m = lax.optimization_barrier((sc, now_m))
     pages = call(
         pages_kernel, jax.ShapeDtypeStruct((32, 2 * PAGE, 2 * HD), BF16), [], unit // 4,
         sc_l, *[r[s] for s in range(4)])
@@ -336,7 +324,7 @@
             jax.ShapeDtypeStruct((ROWS, (GROUP + 1) * HD), BF16),
         ),
         keys(8 * HALF) + keys(HALF) + [pltpu.VMEM((ROWS, HD), F32)] * 2,
-        5 * unit, sc_l, q, q_other, r[2], sink, *now_p, now_ml, now_o)
+        5 * unit, sc_l, q, q_other, r[2], sink, *now_p, now_m, now_l, now_o)
 
     got = lax.ppermute(send, "tp", CORE_SWAP)
     attn_out = call(

time: 72.6 us -> 68.2 us (0.939)
  Pallas kernels: 25.9 us -> 21.6 us
    pallas_call x5, Pallas kernels: 25.9 us -> 21.6 us  [call(): pl.pallas_call(kernel, out_shape=out_shape, in_specs=specs, out_specs=(VM...]
  transfers between devices with their start and end apart: 15 -> 15, of which waited for: 5 -> 5; matrix products, arithmetic and copies ran while one was open for 3% -> 3% of each run, Pallas kernels for 32% -> 27%
where the time goes in v10:
time: 68.2 us; the launch traced here: 68 us
  starting transfers between devices  27.6 us (40%)
  Pallas kernels  21.6 us (32%)
  waiting for transfers between devices  13.4 us (20%)
  other arithmetic  2.15 us (3%)
  local copies, waits for them, and re-layouts  1.74 us (3%)
  between operations  1.48 us (2%)
    pallas_call x5, Pallas kernels, call(): pl.pallas_call(kernel, out_shape=out_shape, in_specs=specs, out_specs=(VM...  21.6 us
    ppermute x1, waiting for transfers between devices, shards(): theirs = lax.ppermute(jnp.concatenate([ret, pas, meta]), 'ctx', Z_SWAP)  6.47 us
    ppermute x1, starting transfers between devices, shards(): theirs = lax.ppermute(jnp.concatenate([ret, pas, meta]), 'ctx', Z_SWAP)  6.1 us
    ppermute x1, starting transfers between devices, shards(): got_pages = lax.ppermute(pages, 'tp', CORE_SWAP)  5.76 us
    ppermute x3, starting transfers between devices, shards(): lax.ppermute(jnp.where(y + s < 4, pas, far), 'ctx', Y_SHIFT[s])  5.68 us
    ppermute x3, waiting for transfers between devices, shards(): lax.ppermute(message, axes, STAGE_2[s])  5.6 us
    ppermute x3, starting transfers between devices, shards(): got = {s: lax.ppermute(message, axes, STAGE_1[s]) for s in (1, 3, 2)}  3.98 us
    ppermute x3, starting transfers between devices, shards(): lax.ppermute(message, axes, STAGE_2[s])  3.8 us
  transfers between devices with their start and end apart: 15, of which 5 were waited for; matrix products, arithmetic and copies ran while one was open for 3% of the time, Pallas kernels for 27%

profile of v10, /device:TPU:39, one launch (start us, length us, event | category | flops | bytes accessed | tf_op | source)
XLA Modules:
  0.0 68.0 jit_solution(12186264068741530005)
XLA Ops:
  0.6 0.8 %fusion.12 = (bf16[128,128]{1,0:T(8,128)(2,1)S(1)}, bf16[128,128]{1,0:T(8,128)(2,1)S(1)}, bf16[128,128]{1,0:T(8,128)(2,1)S(1)}, bf16[128,128]{1,0:T(8,128)(2,1)S(1)}) fusion(bf16[256,128]{1,0:T(8,128)(2,1)} %param.6, bf16[256,128]{1,0:T(8,128)(2,1)} %param.7), kind=kLoop, calls=%fused_computation.48 | loop fusion | bytes 262144 | tf_op jit(solution)/shard_map/slice | solution.py:269
  1.5 0.8 %collective-permute-start = (bf16[256,128]{1,0:T(8,128)(2,1)S(1)}, bf16[256,128]{1,0:T(8,128)(2,1)S(1)}, u32[]{:S(2)}, u32[]{:S(2)}) collective-permute-start(bf16[256,128]{1,0:T(8,128)(2,1)S(1)} %broadcast_select_fusion.5), channel_id=1, source_target_pairs={{0,1},{1,0},{2,3},{3,2},{4,5},{5,4},{6,7},{7,6},{8,9},{9,8},{10,11... | collective-permute-start | bytes 196616 | tf_op jit(solution)/shard_map/ppermute | solution.py:272
  2.3 0.1 collective-permute-start.2
  2.4 0.2 convert_reduce_fusion
  2.7 0.6 copy-done.2
  3.2 0.6 fusion.6
  4.6 0.1 broadcast_in_dim.24
  4.8 6.1 %collective-permute-start.1 = (bf16[528,128]{1,0:T(8,128)(2,1)S(1)}, bf16[528,128]{1,0:T(8,128)(2,1)S(1)}, u32[]{:S(2)}, u32[]{:S(2)}) collective-permute-start(bf16[528,128]{1,0:T(8,128)(2,1)S(1)} %pad_maximum_fusion), channel_id=1, source_target_pairs={{0,32},{8,40},{16,48},{24,56},{32,0},{40,8},{48,16},{56,24},{64,96... | collective-permute-start | bytes 405512 | tf_op jit(solution)/shard_map/ppermute | solution.py:283
  10.9 6.5 %collective-permute-done.1 = bf16[528,128]{1,0:T(8,128)(2,1)S(1)} collective-permute-done((bf16[528,128]{1,0:T(8,128)(2,1)S(1)}, bf16[528,128]{1,0:T(8,128)(2,1)S(1)}, u32[]{:S(2)}, u32[]{:S(2)}) %collective-permute-start.1) | collective-permute-done | bytes 135200 | tf_op jit(solution)/shard_map/ppermute | solution.py:283
  17.5 0.2 collective-permute-start.4
  17.7 0.1 stack.36.sc
  17.8 1.3 %collective-permute-start.3 = (bf16[256,128]{1,0:T(8,128)(2,1)S(1)}, bf16[256,128]{1,0:T(8,128)(2,1)S(1)}, u32[]{:S(2)}, u32[]{:S(2)}) collective-permute-start(bf16[256,128]{1,0:T(8,128)(2,1)S(1)} %get-tuple-element.49), channel_id=1, source_target_pairs={{0,64},{8,72},{16,80},{24,88},{64,128},{72,136},{80,144},{88,152},... | collective-permute-start | bytes 196616 | tf_op jit(solution)/shard_map/ppermute | solution.py:285
  19.1 3.8 %collective-permute-start.5 = (bf16[656,128]{1,0:T(8,128)(2,1)S(1)}, bf16[656,128]{1,0:T(8,128)(2,1)S(1)}, u32[]{:S(2)}, u32[]{:S(2)}) collective-permute-start(bf16[656,128]{1,0:T(8,128)(2,1)S(1)} %constant_dynamic-update-slice_fusion), channel_id=1, source_target_pairs={{0,16},{1,129},{2,18},{3,131},{4,20},{5,133},{6,22},{7,135},{8,24}... | collective-permute-start | bytes 503816 | tf_op jit(solution)/shard_map/ppermute | solution.py:294
  22.9 0.2 collective-permute-done.3
  23.2 3.0 %collective-permute-start.10 = (bf16[256,128]{1,0:T(8,128)(2,1)S(1)}, bf16[256,128]{1,0:T(8,128)(2,1)S(1)}, u32[]{:S(2)}, u32[]{:S(2)}) collective-permute-start(bf16[256,128]{1,0:T(8,128)(2,1)S(1)} %get-tuple-element.51), channel_id=1, source_target_pairs={{0,16},{8,24},{16,0},{24,8},{32,48},{40,56},{48,32},{56,40},{64,80... | collective-permute-start | bytes 196616 | tf_op jit(solution)/shard_map/ppermute | solution.py:297
  26.2 0.4 collective-permute-start.9
  26.6 2.3 %collective-permute-start.11 = (bf16[256,128]{1,0:T(8,128)(2,1)S(1)}, bf16[256,128]{1,0:T(8,128)(2,1)S(1)}, u32[]{:S(2)}, u32[]{:S(2)}) collective-permute-start(bf16[256,128]{1,0:T(8,128)(2,1)S(1)} %get-tuple-element.40), channel_id=1, source_target_pairs={{0,24},{8,0},{16,8},{24,16},{32,56},{40,32},{48,40},{56,48},{64,88... | collective-permute-start | bytes 196616 | tf_op jit(solution)/shard_map/ppermute | solution.py:297
  29.0 0.1 constant_dynamic-update-slice_fusion.5
  29.1 0.9 %collective-permute-start.7 = (bf16[2192,128]{1,0:T(8,128)(2,1)S(1)}, bf16[2192,128]{1,0:T(8,128)(2,1)S(1)}, u32[]{:S(2)}, u32[]{:S(2)}) collective-permute-start(bf16[2192,128]{1,0:T(8,128)(2,1)S(1)} %get-tuple-element.42.here.r0), channel_id=1, source_target_pairs={{0,64},{1,9},{2,66},{3,11},{4,68},{5,13},{6,70},{7,15},{8,72},{9,1... | collective-permute-start | bytes 1683464 | tf_op jit(solution)/shard_map/ppermute | solution.py:304
  29.9 1.9 %collective-permute-start.8 = (bf16[2192,128]{1,0:T(8,128)(2,1)S(1)}, bf16[2192,128]{1,0:T(8,128)(2,1)S(1)}, u32[]{:S(2)}, u32[]{:S(2)}) collective-permute-start(bf16[2192,128]{1,0:T(8,128)(2,1)S(1)} %get-tuple-element.42.here.r0), channel_id=1, source_target_pairs={{0,192},{1,25},{2,194},{3,27},{4,196},{5,29},{6,198},{7,31},{8,200... | collective-permute-start | bytes 1683464 | tf_op jit(solution)/shard_map/ppermute | solution.py:304
  31.8 1.1 %collective-permute-start.12 = (bf16[2192,128]{1,0:T(8,128)(2,1)S(1)}, bf16[2192,128]{1,0:T(8,128)(2,1)S(1)}, u32[]{:S(2)}, u32[]{:S(2)}) collective-permute-start(bf16[2192,128]{1,0:T(8,128)(2,1)S(1)} %get-tuple-element.42.here.r0), channel_id=1, source_target_pairs={{0,128},{1,17},{2,130},{3,19},{4,132},{5,21},{6,134},{7,23},{8,136... | collective-permute-start | bytes 1683464 | tf_op jit(solution)/shard_map/ppermute | solution.py:304
  32.9 6.6 %shard_map.68 = (f32[8,256,128]{2,1,0:T(8,128)S(1)}, f32[8,256,128]{2,1,0:T(8,128)S(1)}, f32[8,256,128]{2,1,0:T(8,128)S(1)}, f32[8,256,128]{2,1,0:T(8,128)S(1)},...) custom-call(s32[8]{0:T(128)S(1)} %stack.36.sc, bf16[256,1024]{1,0:T(8,128)(2,1)S(1)} %copy-done, ...), custom_call_target="tpu_custom_call" | custom-call | flops 32212254720 | bytes 4194304 | tf_op jit(solution)/shard_map/pallas_call | solution.py:246
  39.5 0.3 collective-permute-done.7.r1
  39.8 5.3 %collective-permute-done.8.r3 = bf16[2192,128]{1,0:T(8,128)(2,1)S(1)} collective-permute-done((bf16[2192,128]{1,0:T(8,128)(2,1)S(1)}, bf16[2192,128]{1,0:T(8,128)(2,1)S(1)}, u32[]{:S(2)}, u32[]{:S(2)}) %collective-permute-start.8) | collective-permute-done | bytes 561184 | tf_op jit(solution)/shard_map/ppermute | solution.py:304
  45.1 6.5 %shard_map.69 = (f32[8,256,128]{2,1,0:T(8,128)S(1)}, f32[8,256,128]{2,1,0:T(8,128)S(1)}, f32[8,256,128]{2,1,0:T(8,128)S(1)}) custom-call(s32[8]{0:T(128)S(1)} %stack.36.sc, bf16[256,1024]{1,0:T(8,128)(2,1)S(1)} %copy-done, bf16[256,1024]{1,0:T(8,128)(2,1)S(1)} %collective-permute-done.2.q_other, bf16[2192,128]{1,0:T(8,128)(2,1)S(1)} %collective-permute-done.7.r1, ...), custom_call_target="tpu_custom_call" | custom-call | flops 4294967296 | bytes 4194304 | tf_op jit(solution)/shard_map/pallas_call | solution.py:246
  51.6 1.4 %shard_map.72 = bf16[32,32,256]{2,1,0:T(8,128)(2,1)S(1)} custom-call(s32[8]{0:T(128)S(1)} %stack.36.sc, bf16[2192,128]{1,0:T(8,128)(2,1)S(1)} %get-tuple-element.42.here.r0, bf16[2192,128]{1,0:T(8,128)(2,1)S(1)} %collective-permute-done.7.r1, bf16[2192,128]{1,0:T(8,128)(2,1)S(1)} %collective-permute-done.12.r2, bf16[2192,128]{1,0:T(8,128)(2,1)S(1)} %collective-permute-done.8.r3), custom_call_target="tpu_custom_call" | custom-call | flops 134217728 | bytes 4194304 | tf_op jit(solution)/shard_map/pallas_call | solution.py:246
  53.0 5.8 %collective-permute-start.14 = (bf16[32,32,256]{2,1,0:T(8,128)(2,1)S(1)}, bf16[32,32,256]{2,1,0:T(8,128)(2,1)S(1)}, u32[]{:S(2)}, u32[]{:S(2)}) collective-permute-start(bf16[32,32,256]{2,1,0:T(8,128)(2,1)S(1)} %shard_map.72), channel_id=1, source_target_pairs={{0,1},{1,0},{2,3},{3,2},{4,5},{5,4},{6,7},{7,6},{8,9},{9,8},{10,11... | collective-permute-start | bytes 1572872 | tf_op jit(solution)/shard_map/ppermute | solution.py:318
  58.8 5.5 %shard_map.70 = (bf16[256,1024]{1,0:T(8,128)(2,1)S(1)}, f32[256,128]{1,0:T(8,128)S(1)}, bf16[256,1152]{1,0:T(8,128)(2,1)S(1)}) custom-call(s32[8]{0:T(128)S(1)} %stack.36.sc, bf16[256,1024]{1,0:T(8,128)(2,1)S(1)} %copy-done, bf16[256,1024]{1,0:T(8,128)(2,1)S(1)} %collective-permute-done.2.q_other, bf16[2192,128]{1,0:T(8,128)(2,1)S(1)} %collective-permute-done.12.r2, ...), custom_call_target="tpu_custom_call" | custom-call | flops 2684354560 | bytes 4194304 | tf_op jit(solution)/shard_map/pallas_call | solution.py:246
  64.3 0.1 collective-permute-start.13
  64.4 0.8 %add_select_fusion = bf16[32,32,256]{2,1,0:T(8,128)(2,1)} fusion(bf16[32,32,256]{2,1,0:T(8,128)(2,1)S(1)} %shard_map.72, bf16[32,32,256]{2,1,0:T(8,128)(2,1)S(1)} %collective-permute-done.14, pred[]{:T(512)S(6)} %eq.80), kind=kLoop, calls=%fused_computation | loop fusion | flops 524288 | bytes 1572865 | tf_op jit(solution)/shard_map/jit(_where)/select_n | solution.py:332
  65.3 1.1 %collective-permute-done.13.got = bf16[256,1152]{1,0:T(8,128)(2,1)S(1)} collective-permute-done((bf16[256,1152]{1,0:T(8,128)(2,1)S(1)}, bf16[256,1152]{1,0:T(8,128)(2,1)S(1)}, u32[]{:S(2)}, u32[]{:S(2)}) %collective-permute-start.13) | collective-permute-done | bytes 589856 | tf_op jit(solution)/shard_map/ppermute | solution.py:329
  66.4 1.6 %shard_map.71 = bf16[256,1024]{1,0:T(8,128)(2,1)} custom-call(bf16[256,1024]{1,0:T(8,128)(2,1)S(1)} %get-tuple-element.37.keep, f32[256,128]{1,0:T(8,128)S(1)} %get-tuple-element.38.keep_ml, bf16[256,1152]{1,0:T(8,128)(2,1)S(1)} %collective-permute-done.13.got), custom_call_target="tpu_custom_call" | custom-call | flops 134217728 | bytes 4194304 | tf_op jit(solution)/shard_map/pallas_call | solution.py:246
  (38 shorter events, 0.6 us)
Async XLA Ops:
  1.5 0.9 %copy-start.1 = (s32[16]{0:T(128)S(1)}, s32[16]{0:T(128)}, u32[]{:S(2)}) copy-start(s32[16]{0:T(128)} %param.9) | copy-start | bytes 196
  1.5 3.2 %collective-permute-start = (bf16[256,128]{1,0:T(8,128)(2,1)S(1)}, bf16[256,128]{1,0:T(8,128)(2,1)S(1)}, u32[]{:S(2)}, u32[]{:S(2)}) collective-permute-start(bf16[256,128]{1,0:T(8,128)(2,1)S(1)} %broadcast_select_fusion.5), channel_id=1, source_target_pairs={{0,1},{1,0},{2,3},{3,2},{4,5},{5,4},{6,7},{7,6},{8,9},{9,8},{10,11... | collective-permute-start | bytes 196616 | tf_op jit(solution)/shard_map/ppermute | solution.py:272
  2.3 15.1 %collective-permute-start.2 = (bf16[256,1024]{1,0:T(8,128)(2,1)}, bf16[256,1024]{1,0:T(8,128)(2,1)S(1)}, u32[]{:S(2)}, u32[]{:S(2)}) collective-permute-start(bf16[256,1024]{1,0:T(8,128)(2,1)} %q_own.5), channel_id=1, source_target_pairs={{0,1},{1,0},{2,3},{3,2},{4,5},{5,4},{6,7},{7,6},{8,9},{9,8},{10,11... | collective-permute-start | bytes 1572872 | tf_op jit(solution)/shard_map/ppermute | solution.py:273
  2.6 0.7 copy-start.2
  4.8 12.6 %collective-permute-start.1 = (bf16[528,128]{1,0:T(8,128)(2,1)S(1)}, bf16[528,128]{1,0:T(8,128)(2,1)S(1)}, u32[]{:S(2)}, u32[]{:S(2)}) collective-permute-start(bf16[528,128]{1,0:T(8,128)(2,1)S(1)} %pad_maximum_fusion), channel_id=1, source_target_pairs={{0,32},{8,40},{16,48},{24,56},{32,0},{40,8},{48,16},{56,24},{64,96... | collective-permute-start | bytes 405512 | tf_op jit(solution)/shard_map/ppermute | solution.py:283
  17.5 5.6 %collective-permute-start.4 = (bf16[656,128]{1,0:T(8,128)(2,1)S(1)}, bf16[656,128]{1,0:T(8,128)(2,1)S(1)}, u32[]{:S(2)}, u32[]{:S(2)}) collective-permute-start(bf16[656,128]{1,0:T(8,128)(2,1)S(1)} %constant_dynamic-update-slice_fusion), channel_id=1, source_target_pairs={{0,8},{1,65},{2,10},{3,67},{4,12},{5,69},{6,14},{7,71},{8,16},{9,7... | collective-permute-start | bytes 503816 | tf_op jit(solution)/shard_map/ppermute | solution.py:294
  17.8 5.3 %collective-permute-start.3 = (bf16[256,128]{1,0:T(8,128)(2,1)S(1)}, bf16[256,128]{1,0:T(8,128)(2,1)S(1)}, u32[]{:S(2)}, u32[]{:S(2)}) collective-permute-start(bf16[256,128]{1,0:T(8,128)(2,1)S(1)} %get-tuple-element.49), channel_id=1, source_target_pairs={{0,64},{8,72},{16,80},{24,88},{64,128},{72,136},{80,144},{88,152},... | collective-permute-start | bytes 196616 | tf_op jit(solution)/shard_map/ppermute | solution.py:285
  19.1 9.8 %collective-permute-start.5 = (bf16[656,128]{1,0:T(8,128)(2,1)S(1)}, bf16[656,128]{1,0:T(8,128)(2,1)S(1)}, u32[]{:S(2)}, u32[]{:S(2)}) collective-permute-start(bf16[656,128]{1,0:T(8,128)(2,1)S(1)} %constant_dynamic-update-slice_fusion), channel_id=1, source_target_pairs={{0,16},{1,129},{2,18},{3,131},{4,20},{5,133},{6,22},{7,135},{8,24}... | collective-permute-start | bytes 503816 | tf_op jit(solution)/shard_map/ppermute | solution.py:294
  22.9 6.1 %collective-permute-start.6 = (bf16[656,128]{1,0:T(8,128)(2,1)S(1)}, bf16[656,128]{1,0:T(8,128)(2,1)S(1)}, u32[]{:S(2)}, u32[]{:S(2)}) collective-permute-start(bf16[656,128]{1,0:T(8,128)(2,1)S(1)} %constant_dynamic-update-slice_fusion), channel_id=1, source_target_pairs={{0,24},{1,193},{2,26},{3,195},{4,28},{5,197},{6,30},{7,199},{8,0},... | collective-permute-start | bytes 503816 | tf_op jit(solution)/shard_map/ppermute | solution.py:294
  23.2 9.7 %copy-start = (bf16[256,1024]{1,0:T(8,128)(2,1)S(1)}, bf16[256,1024]{1,0:T(8,128)(2,1)}, u32[]{:S(2)}) copy-start(bf16[256,1024]{1,0:T(8,128)(2,1)} %q_own.5) | copy-start | bytes 1572868
  23.2 8.7 %collective-permute-start.10 = (bf16[256,128]{1,0:T(8,128)(2,1)S(1)}, bf16[256,128]{1,0:T(8,128)(2,1)S(1)}, u32[]{:S(2)}, u32[]{:S(2)}) collective-permute-start(bf16[256,128]{1,0:T(8,128)(2,1)S(1)} %get-tuple-element.51), channel_id=1, source_target_pairs={{0,16},{8,24},{16,0},{24,8},{32,48},{40,56},{48,32},{56,40},{64,80... | collective-permute-start | bytes 196616 | tf_op jit(solution)/shard_map/ppermute | solution.py:297
  26.2 6.7 %collective-permute-start.9 = (bf16[256,128]{1,0:T(8,128)(2,1)S(1)}, bf16[256,128]{1,0:T(8,128)(2,1)S(1)}, u32[]{:S(2)}, u32[]{:S(2)}) collective-permute-start(bf16[256,128]{1,0:T(8,128)(2,1)S(1)} %get-tuple-element.52), channel_id=1, source_target_pairs={{0,8},{8,16},{16,24},{24,0},{32,40},{40,48},{48,56},{56,32},{64,72... | collective-permute-start | bytes 196616 | tf_op jit(solution)/shard_map/ppermute | solution.py:297
  26.6 6.3 %collective-permute-start.11 = (bf16[256,128]{1,0:T(8,128)(2,1)S(1)}, bf16[256,128]{1,0:T(8,128)(2,1)S(1)}, u32[]{:S(2)}, u32[]{:S(2)}) collective-permute-start(bf16[256,128]{1,0:T(8,128)(2,1)S(1)} %get-tuple-element.40), channel_id=1, source_target_pairs={{0,24},{8,0},{16,8},{24,16},{32,56},{40,32},{48,40},{56,48},{64,88... | collective-permute-start | bytes 196616 | tf_op jit(solution)/shard_map/ppermute | solution.py:297
  29.1 10.7 %collective-permute-start.7 = (bf16[2192,128]{1,0:T(8,128)(2,1)S(1)}, bf16[2192,128]{1,0:T(8,128)(2,1)S(1)}, u32[]{:S(2)}, u32[]{:S(2)}) collective-permute-start(bf16[2192,128]{1,0:T(8,128)(2,1)S(1)} %get-tuple-element.42.here.r0), channel_id=1, source_target_pairs={{0,64},{1,9},{2,66},{3,11},{4,68},{5,13},{6,70},{7,15},{8,72},{9,1... | collective-permute-start | bytes 1683464 | tf_op jit(solution)/shard_map/ppermute | solution.py:304
  29.9 15.1 %collective-permute-start.8 = (bf16[2192,128]{1,0:T(8,128)(2,1)S(1)}, bf16[2192,128]{1,0:T(8,128)(2,1)S(1)}, u32[]{:S(2)}, u32[]{:S(2)}) collective-permute-start(bf16[2192,128]{1,0:T(8,128)(2,1)S(1)} %get-tuple-element.42.here.r0), channel_id=1, source_target_pairs={{0,192},{1,25},{2,194},{3,27},{4,196},{5,29},{6,198},{7,31},{8,200... | collective-permute-start | bytes 1683464 | tf_op jit(solution)/shard_map/ppermute | solution.py:304
  31.8 19.8 %collective-permute-start.12 = (bf16[2192,128]{1,0:T(8,128)(2,1)S(1)}, bf16[2192,128]{1,0:T(8,128)(2,1)S(1)}, u32[]{:S(2)}, u32[]{:S(2)}) collective-permute-start(bf16[2192,128]{1,0:T(8,128)(2,1)S(1)} %get-tuple-element.42.here.r0), channel_id=1, source_target_pairs={{0,128},{1,17},{2,130},{3,19},{4,132},{5,21},{6,134},{7,23},{8,136... | collective-permute-start | bytes 1683464 | tf_op jit(solution)/shard_map/ppermute | solution.py:304
  53.0 11.4 %collective-permute-start.14 = (bf16[32,32,256]{2,1,0:T(8,128)(2,1)S(1)}, bf16[32,32,256]{2,1,0:T(8,128)(2,1)S(1)}, u32[]{:S(2)}, u32[]{:S(2)}) collective-permute-start(bf16[32,32,256]{2,1,0:T(8,128)(2,1)S(1)} %shard_map.72), channel_id=1, source_target_pairs={{0,1},{1,0},{2,3},{3,2},{4,5},{5,4},{6,7},{7,6},{8,9},{9,8},{10,11... | collective-permute-start | bytes 1572872 | tf_op jit(solution)/shard_map/ppermute | solution.py:318
  64.3 2.1 %collective-permute-start.13 = (bf16[256,1152]{1,0:T(8,128)(2,1)S(1)}, bf16[256,1152]{1,0:T(8,128)(2,1)S(1)}, u32[]{:S(2)}, u32[]{:S(2)}) collective-permute-start(bf16[256,1152]{1,0:T(8,128)(2,1)S(1)} %get-tuple-element.39), channel_id=1, source_target_pairs={{0,1},{1,0},{2,3},{3,2},{4,5},{5,4},{6,7},{7,6},{8,9},{9,8},{10,11... | collective-permute-start | bytes 1769480 | tf_op jit(solution)/shard_map/ppermute | solution.py:329

commit v11 on v10

--- a/solution.py
+++ b/solution.py
@@ -76,8 +76,8 @@
     v_s[pl.ds(at, rows), 0:HD] = ref[first + gap:first + gap + rows, :]
 
 
-def put_ranges(k_s, v_s, at, ref):
-    for n in range(8):
+def put_ranges(k_s, v_s, at, ref, count=8):
+    for n in range(count):
         put_keys(k_s, v_s, at + n * HALF, ref, n * ROWS, HALF, HALF)
 
 
@@ -159,10 +159,11 @@
         heads(i)
 
 
-def last_kernel(sc, q_own, q_other, r2, sink, mp_in, lp_in, op_in, m_in, l_in, o_in, keep, keep_ml, send,
+def last_kernel(sc, q_own, q_other, r2a, r2b, sink, mp_in, lp_in, op_in, m_in, l_in, o_in, keep, keep_ml, send,
                 kr, vr, ks, vs, mlr_s, mlp_s):
     core, c, is_r = sc[3], sc[4], sc[5]
-    put_ranges(kr, vr, 0, r2)
+    put_ranges(kr, vr, 0, r2a, 4)
+    put_ranges(kr, vr, 4 * HALF, r2b, 4)
     put_range_bias(kr, vr, sc, (2,))
     ks[...] = jnp.zeros((HALF, 2 * HD), BF16)
     vs[...] = jnp.zeros((HALF, 2 * HD), BF16)
@@ -218,19 +219,20 @@
         out_ref[:, cols] = out.astype(BF16)
 
 
-def pages_kernel(sc, r0, r1, r2, r3, out_ref):
+def pages_kernel(sc, r0, r1, r2a, r2b, r3, out_ref):
     c = sc[4]
     row = iota((2 * PAGE, HD), 0)
     lane = iota((2 * PAGE, HD), 1)
     same_row = (lane & (PAGE - 1)) == (row & (PAGE - 1))
     want = (2 * c + (row >> 4)).astype(F32)
-    for outer, ref in enumerate((r0, r1, r2, r3)):
-        codes = ref[8 * ROWS:8 * ROWS + META, :].astype(F32)
+    for outer, (refa, refb, base) in enumerate(((r0, r0, 0), (r1, r1, 0), (r2a, r2b, 4), (r3, r3, 0))):
+        codes = refb[(8 - base) * ROWS:(8 - base) * ROWS + META, :].astype(F32)
         for n in range(8):
+            ref, slot = (refa, n) if n < 4 else (refb, n - base)
             select = jnp.where(same_row & (codes[n:n + 1, :] == want), 1.0, 0.0).astype(BF16)
             block = range_of(sc, n >> 1, outer, n & 1)
             for part in range(2):
-                at = n * ROWS + part * HALF
+                at = slot * ROWS + part * HALF
                 pages = jnp.dot(select, ref[at:at + HALF, :], preferred_element_type=F32)
                 out_ref[block, :, part * HD:(part + 1) * HD] = pages.astype(BF16)
 
@@ -301,20 +303,24 @@
         sink = jnp.where(y == s, got[s][2 * ROWS:2 * ROWS + 2 * SINK], sink)
     message = jnp.concatenate([both] + [got[s][:2 * ROWS] for s in (1, 2, 3)] + [meta, sink])
 
-    r = {0: message} | {s: lax.ppermute(message, axes, STAGE_2[s]) for s in (1, 3, 2)}
+    r = {0: message} | {s: lax.ppermute(message, axes, STAGE_2[s]) for s in (1, 3)}
     state = (jax.ShapeDtypeStruct((GROUP, ROWS, HD), F32),) * 3
     unit = 2 * 2048 * 256 * 512
     *now_p, now_m, now_l, now_o = call(
         near_kernel, state + state, keys(5 * HALF) + keys(8 * HALF), 60 * unit,
         sc, q, q_other, message, pas, p[1], p[2], p[3], far)
-    for s in (1, 2, 3):
-        sink = jnp.where(x == s, r[s][8 * ROWS + META:], sink)
+    late, now_m = lax.optimization_barrier((message, now_m))
+    part = 4 * ROWS
+    two = [lax.ppermute(late[:part], axes, STAGE_2[2]), lax.ppermute(late[part:], axes, STAGE_2[2])]
     now_m, now_l, now_o = call(
         middle_kernel, state, keys(16 * HALF), 8 * unit, sc, q, q_other, r[1], r[3], now_m, now_l, now_o)
+    for s in (1, 2, 3):
+        tail = r[s][8 * ROWS + META:] if s != 2 else two[1][4 * ROWS + META:]
+        sink = jnp.where(x == s, tail, sink)
     sc_l, now_m = lax.optimization_barrier((sc, now_m))
     pages = call(
         pages_kernel, jax.ShapeDtypeStruct((32, 2 * PAGE, 2 * HD), BF16), [], unit // 4,
-        sc_l, *[r[s] for s in range(4)])
+        sc_l, r[0], r[1], *two, r[3])
     got_pages = lax.ppermute(pages, "tp", CORE_SWAP)
     keep, keep_ml, send = call(
         last_kernel,
@@ -324,7 +330,7 @@
             jax.ShapeDtypeStruct((ROWS, (GROUP + 1) * HD), BF16),
         ),
         keys(8 * HALF) + keys(HALF) + [pltpu.VMEM((ROWS, HD), F32)] * 2,
-        5 * unit, sc_l, q, q_other, r[2], sink, *now_p, now_m, now_l, now_o)
+        5 * unit, sc_l, q, q_other, *two, sink, *now_p, now_m, now_l, now_o)
 
     got = lax.ppermute(send, "tp", CORE_SWAP)
     attn_out = call(

time: 68.2 us -> 65.2 us (0.956)
  the two profiles are of different devices: /device:TPU:39 before, /device:TPU:33 now
where the time goes in v11:
time: 65.2 us; the launch traced here: 65 us
  starting transfers between devices  29.8 us (46%)
  Pallas kernels  21.4 us (33%)
  waiting for transfers between devices  8.3 us (13%)
  other arithmetic  2.15 us (3%)
  local copies, waits for them, and re-layouts  1.78 us (3%)
  between operations  1.51 us (2%)
    pallas_call x5, Pallas kernels, call(): pl.pallas_call(kernel, out_shape=out_shape, in_specs=specs, out_specs=(VM...  21.4 us
    ppermute x1, waiting for transfers between devices, shards(): theirs = lax.ppermute(jnp.concatenate([ret, pas, meta]), 'ctx', Z_SWAP)  6.47 us
    ppermute x1, starting transfers between devices, shards(): theirs = lax.ppermute(jnp.concatenate([ret, pas, meta]), 'ctx', Z_SWAP)  6.1 us
    ppermute x3, starting transfers between devices, shards(): lax.ppermute(jnp.where(y + s < 4, pas, far), 'ctx', Y_SHIFT[s])  5.68 us
    ppermute x3, starting transfers between devices, shards(): got = {s: lax.ppermute(message, axes, STAGE_1[s]) for s in (1, 3, 2)}  4.63 us
    ppermute x1, starting transfers between devices, shards(): got_pages = lax.ppermute(pages, 'tp', CORE_SWAP)  3.56 us
    ppermute x1, starting transfers between devices, shards(): from_x = lax.ppermute(theirs[ROWS:2 * ROWS], 'ctx', X_STEP)  3.11 us
    ppermute x2, starting transfers between devices, shards(): lax.ppermute(message, axes, STAGE_2[s])  2.75 us
  transfers between devices with their start and end apart: 16, of which 3 were waited for; matrix products, arithmetic and copies ran while one was open for 4% of the time, Pallas kernels for 29%

profile of v11, /device:TPU:33, one launch (start us, length us, event | category | flops | bytes accessed | tf_op | source)
XLA Modules:
  0.0 65.0 jit_solution(2396333469955222005)
XLA Ops:
  0.6 0.8 %fusion.12 = (bf16[128,128]{1,0:T(8,128)(2,1)S(1)}, bf16[128,128]{1,0:T(8,128)(2,1)S(1)}, bf16[128,128]{1,0:T(8,128)(2,1)S(1)}, bf16[128,128]{1,0:T(8,128)(2,1)S(1)}) fusion(bf16[256,128]{1,0:T(8,128)(2,1)} %param.6, bf16[256,128]{1,0:T(8,128)(2,1)} %param.7), kind=kLoop, calls=%fused_computation.48 | loop fusion | bytes 262144 | tf_op jit(solution)/shard_map/slice | solution.py:271
  1.5 0.8 %collective-permute-start = (bf16[256,128]{1,0:T(8,128)(2,1)S(1)}, bf16[256,128]{1,0:T(8,128)(2,1)S(1)}, u32[]{:S(2)}, u32[]{:S(2)}) collective-permute-start(bf16[256,128]{1,0:T(8,128)(2,1)S(1)} %broadcast_select_fusion.5), channel_id=1, source_target_pairs={{0,1},{1,0},{2,3},{3,2},{4,5},{5,4},{6,7},{7,6},{8,9},{9,8},{10,11... | collective-permute-start | bytes 196616 | tf_op jit(solution)/shard_map/ppermute | solution.py:274
  2.3 0.1 collective-permute-start.2
  2.4 0.2 convert_reduce_fusion
  2.7 0.6 copy-done.2
  3.2 0.6 fusion.6
  4.6 0.1 broadcast_in_dim.24
  4.8 6.1 %collective-permute-start.1 = (bf16[528,128]{1,0:T(8,128)(2,1)S(1)}, bf16[528,128]{1,0:T(8,128)(2,1)S(1)}, u32[]{:S(2)}, u32[]{:S(2)}) collective-permute-start(bf16[528,128]{1,0:T(8,128)(2,1)S(1)} %pad_maximum_fusion), channel_id=1, source_target_pairs={{0,32},{8,40},{16,48},{24,56},{32,0},{40,8},{48,16},{56,24},{64,96... | collective-permute-start | bytes 405512 | tf_op jit(solution)/shard_map/ppermute | solution.py:285
  10.9 6.5 %collective-permute-done.1 = bf16[528,128]{1,0:T(8,128)(2,1)S(1)} collective-permute-done((bf16[528,128]{1,0:T(8,128)(2,1)S(1)}, bf16[528,128]{1,0:T(8,128)(2,1)S(1)}, u32[]{:S(2)}, u32[]{:S(2)}) %collective-permute-start.1) | collective-permute-done | bytes 135200 | tf_op jit(solution)/shard_map/ppermute | solution.py:285
  17.5 1.2 %collective-permute-start.4 = (bf16[656,128]{1,0:T(8,128)(2,1)S(1)}, bf16[656,128]{1,0:T(8,128)(2,1)S(1)}, u32[]{:S(2)}, u32[]{:S(2)}) collective-permute-start(bf16[656,128]{1,0:T(8,128)(2,1)S(1)} %constant_dynamic-update-slice_fusion), channel_id=1, source_target_pairs={{0,8},{1,65},{2,10},{3,67},{4,12},{5,69},{6,14},{7,71},{8,16},{9,7... | collective-permute-start | bytes 503816 | tf_op jit(solution)/shard_map/ppermute | solution.py:296
  18.7 0.1 stack.36.sc
  18.8 3.1 %collective-permute-start.3 = (bf16[256,128]{1,0:T(8,128)(2,1)S(1)}, bf16[256,128]{1,0:T(8,128)(2,1)S(1)}, u32[]{:S(2)}, u32[]{:S(2)}) collective-permute-start(bf16[256,128]{1,0:T(8,128)(2,1)S(1)} %get-tuple-element.53), channel_id=1, source_target_pairs={{0,64},{8,72},{16,80},{24,88},{64,128},{72,136},{80,144},{88,152},... | collective-permute-start | bytes 196616 | tf_op jit(solution)/shard_map/ppermute | solution.py:287
  21.9 1.5 %collective-permute-start.5 = (bf16[656,128]{1,0:T(8,128)(2,1)S(1)}, bf16[656,128]{1,0:T(8,128)(2,1)S(1)}, u32[]{:S(2)}, u32[]{:S(2)}) collective-permute-start(bf16[656,128]{1,0:T(8,128)(2,1)S(1)} %constant_dynamic-update-slice_fusion), channel_id=1, source_target_pairs={{0,16},{1,129},{2,18},{3,131},{4,20},{5,133},{6,22},{7,135},{8,24}... | collective-permute-start | bytes 503816 | tf_op jit(solution)/shard_map/ppermute | solution.py:296
  23.5 1.9 %collective-permute-start.6 = (bf16[656,128]{1,0:T(8,128)(2,1)S(1)}, bf16[656,128]{1,0:T(8,128)(2,1)S(1)}, u32[]{:S(2)}, u32[]{:S(2)}) collective-permute-start(bf16[656,128]{1,0:T(8,128)(2,1)S(1)} %constant_dynamic-update-slice_fusion), channel_id=1, source_target_pairs={{0,24},{1,193},{2,26},{3,195},{4,28},{5,197},{6,30},{7,199},{8,0},... | collective-permute-start | bytes 503816 | tf_op jit(solution)/shard_map/ppermute | solution.py:296
  25.4 3.0 %collective-permute-start.10 = (bf16[256,128]{1,0:T(8,128)(2,1)S(1)}, bf16[256,128]{1,0:T(8,128)(2,1)S(1)}, u32[]{:S(2)}, u32[]{:S(2)}) collective-permute-start(bf16[256,128]{1,0:T(8,128)(2,1)S(1)} %get-tuple-element.55), channel_id=1, source_target_pairs={{0,16},{8,24},{16,0},{24,8},{32,48},{40,56},{48,32},{56,40},{64,80... | collective-permute-start | bytes 196616 | tf_op jit(solution)/shard_map/ppermute | solution.py:299
  28.4 0.4 collective-permute-start.9
  28.8 2.3 %collective-permute-start.11 = (bf16[256,128]{1,0:T(8,128)(2,1)S(1)}, bf16[256,128]{1,0:T(8,128)(2,1)S(1)}, u32[]{:S(2)}, u32[]{:S(2)}) collective-permute-start(bf16[256,128]{1,0:T(8,128)(2,1)S(1)} %get-tuple-element.44), channel_id=1, source_target_pairs={{0,24},{8,0},{16,8},{24,16},{32,56},{40,32},{48,40},{56,48},{64,88... | collective-permute-start | bytes 196616 | tf_op jit(solution)/shard_map/ppermute | solution.py:299
  31.2 0.1 constant_dynamic-update-slice_fusion.5
  31.3 0.1 collective-permute-start.7
  31.4 2.7 %collective-permute-start.8 = (bf16[2192,128]{1,0:T(8,128)(2,1)S(1)}, bf16[2192,128]{1,0:T(8,128)(2,1)S(1)}, u32[]{:S(2)}, u32[]{:S(2)}) collective-permute-start(bf16[2192,128]{1,0:T(8,128)(2,1)S(1)} %get-tuple-element.34.here.r0), channel_id=1, source_target_pairs={{0,192},{1,25},{2,194},{3,27},{4,196},{5,29},{6,198},{7,31},{8,200... | collective-permute-start | bytes 1683464 | tf_op jit(solution)/shard_map/ppermute | solution.py:306
  34.1 6.6 %shard_map.68 = (f32[8,256,128]{2,1,0:T(8,128)S(1)}, f32[8,256,128]{2,1,0:T(8,128)S(1)}, f32[8,256,128]{2,1,0:T(8,128)S(1)}, f32[8,256,128]{2,1,0:T(8,128)S(1)},...) custom-call(s32[8]{0:T(128)S(1)} %stack.36.sc, bf16[256,1024]{1,0:T(8,128)(2,1)S(1)} %copy-done, ...), custom_call_target="tpu_custom_call" | custom-call | flops 32212254720 | bytes 4194304 | tf_op jit(solution)/shard_map/pallas_call | solution.py:248
  40.7 1.0 %collective-permute-start.13 = (bf16[1168,128]{1,0:T(8,128)(2,1)S(1)}, bf16[1168,128]{1,0:T(8,128)(2,1)S(1)}, u32[]{:S(2)}, u32[]{:S(2)}) collective-permute-start(bf16[1168,128]{1,0:T(8,128)(2,1)S(1)} %slice.98), channel_id=1, source_target_pairs={{0,128},{1,17},{2,130},{3,19},{4,132},{5,21},{6,134},{7,23},{8,136... | collective-permute-start | bytes 897032 | tf_op jit(solution)/shard_map/ppermute | solution.py:314
  41.7 2.1 %collective-permute-start.12 = (bf16[1024,128]{1,0:T(8,128)(2,1)S(1)}, bf16[1024,128]{1,0:T(8,128)(2,1)S(1)}, u32[]{:S(2)}, u32[]{:S(2)}) collective-permute-start(bf16[1024,128]{1,0:T(8,128)(2,1)S(1)} %slice.97), channel_id=1, source_target_pairs={{0,128},{1,17},{2,130},{3,19},{4,132},{5,21},{6,134},{7,23},{8,136... | collective-permute-start | bytes 786440 | tf_op jit(solution)/shard_map/ppermute | solution.py:314
  43.8 6.6 %shard_map.69 = (f32[8,256,128]{2,1,0:T(8,128)S(1)}, f32[8,256,128]{2,1,0:T(8,128)S(1)}, f32[8,256,128]{2,1,0:T(8,128)S(1)}) custom-call(s32[8]{0:T(128)S(1)} %stack.36.sc, bf16[256,1024]{1,0:T(8,128)(2,1)S(1)} %copy-done, bf16[256,1024]{1,0:T(8,128)(2,1)S(1)} %collective-permute-done.2.q_other, bf16[2192,128]{1,0:T(8,128)(2,1)S(1)} %collective-permute-done.7.r1, ...), custom_call_target="tpu_custom_call" | custom-call | flops 4294967296 | bytes 4194304 | tf_op jit(solution)/shard_map/pallas_call | solution.py:248
  50.4 0.7 %collective-permute-done.12.r2a = bf16[1024,128]{1,0:T(8,128)(2,1)S(1)} collective-permute-done((bf16[1024,128]{1,0:T(8,128)(2,1)S(1)}, bf16[1024,128]{1,0:T(8,128)(2,1)S(1)}, u32[]{:S(2)}, u32[]{:S(2)}) %collective-permute-start.12) | collective-permute-done | bytes 262176 | tf_op jit(solution)/shard_map/ppermute | solution.py:314
  51.1 1.2 %shard_map.72 = bf16[32,32,256]{2,1,0:T(8,128)(2,1)S(1)} custom-call(s32[8]{0:T(128)S(1)} %stack.36.sc, bf16[2192,128]{1,0:T(8,128)(2,1)S(1)} %get-tuple-element.34.here.r0, bf16[2192,128]{1,0:T(8,128)(2,1)S(1)} %collective-permute-done.7.r1, bf16[1024,128]{1,0:T(8,128)(2,1)S(1)} %collective-permute-done.12.r2a, ...), custom_call_target="tpu_custom_call" | custom-call | flops 134217728 | bytes 4194304 | tf_op jit(solution)/shard_map/pallas_call | solution.py:248
  52.3 3.6 %collective-permute-start.15 = (bf16[32,32,256]{2,1,0:T(8,128)(2,1)S(1)}, bf16[32,32,256]{2,1,0:T(8,128)(2,1)S(1)}, u32[]{:S(2)}, u32[]{:S(2)}) collective-permute-start(bf16[32,32,256]{2,1,0:T(8,128)(2,1)S(1)} %shard_map.72), channel_id=1, source_target_pairs={{0,1},{1,0},{2,3},{3,2},{4,5},{5,4},{6,7},{7,6},{8,9},{9,8},{10,11... | collective-permute-start | bytes 1572872 | tf_op jit(solution)/shard_map/ppermute | solution.py:324
  55.8 5.5 %shard_map.70 = (bf16[256,1024]{1,0:T(8,128)(2,1)S(1)}, f32[256,128]{1,0:T(8,128)S(1)}, bf16[256,1152]{1,0:T(8,128)(2,1)S(1)}) custom-call(s32[8]{0:T(128)S(1)} %stack.36.sc, bf16[256,1024]{1,0:T(8,128)(2,1)S(1)} %copy-done, bf16[256,1024]{1,0:T(8,128)(2,1)S(1)} %collective-permute-done.2.q_other, bf16[1024,128]{1,0:T(8,128)(2,1)S(1)} %collective-permute-done.12.r2a, ...), custom_call_target="tpu_custom_call" | custom-call | flops 2684354560 | bytes 4194304 | tf_op jit(solution)/shard_map/pallas_call | solution.py:248
  61.3 0.1 collective-permute-start.14
  61.4 0.9 %add_select_fusion = bf16[32,32,256]{2,1,0:T(8,128)(2,1)} fusion(bf16[32,32,256]{2,1,0:T(8,128)(2,1)S(1)} %shard_map.72, bf16[32,32,256]{2,1,0:T(8,128)(2,1)S(1)} %collective-permute-done.15, pred[]{:T(512)S(6)} %eq.80), kind=kLoop, calls=%fused_computation | loop fusion | flops 524288 | bytes 1572865 | tf_op jit(solution)/shard_map/jit(_where)/select_n | solution.py:338
  62.3 1.1 %collective-permute-done.14.got = bf16[256,1152]{1,0:T(8,128)(2,1)S(1)} collective-permute-done((bf16[256,1152]{1,0:T(8,128)(2,1)S(1)}, bf16[256,1152]{1,0:T(8,128)(2,1)S(1)}, u32[]{:S(2)}, u32[]{:S(2)}) %collective-permute-start.14) | collective-permute-done | bytes 589856 | tf_op jit(solution)/shard_map/ppermute | solution.py:335
  63.4 1.6 %shard_map.71 = bf16[256,1024]{1,0:T(8,128)(2,1)} custom-call(bf16[256,1024]{1,0:T(8,128)(2,1)S(1)} %get-tuple-element.41.keep, f32[256,128]{1,0:T(8,128)S(1)} %get-tuple-element.42.keep_ml, bf16[256,1152]{1,0:T(8,128)(2,1)S(1)} %collective-permute-done.14.got), custom_call_target="tpu_custom_call" | custom-call | flops 134217728 | bytes 4194304 | tf_op jit(solution)/shard_map/pallas_call | solution.py:248
  (42 shorter events, 0.7 us)
Async XLA Ops:
  1.5 0.9 %copy-start.1 = (s32[16]{0:T(128)S(1)}, s32[16]{0:T(128)}, u32[]{:S(2)}) copy-start(s32[16]{0:T(128)} %param.9) | copy-start | bytes 196
  1.5 3.2 %collective-permute-start = (bf16[256,128]{1,0:T(8,128)(2,1)S(1)}, bf16[256,128]{1,0:T(8,128)(2,1)S(1)}, u32[]{:S(2)}, u32[]{:S(2)}) collective-permute-start(bf16[256,128]{1,0:T(8,128)(2,1)S(1)} %broadcast_select_fusion.5), channel_id=1, source_target_pairs={{0,1},{1,0},{2,3},{3,2},{4,5},{5,4},{6,7},{7,6},{8,9},{9,8},{10,11... | collective-permute-start | bytes 196616 | tf_op jit(solution)/shard_map/ppermute | solution.py:274
  2.3 15.1 %collective-permute-start.2 = (bf16[256,1024]{1,0:T(8,128)(2,1)}, bf16[256,1024]{1,0:T(8,128)(2,1)S(1)}, u32[]{:S(2)}, u32[]{:S(2)}) collective-permute-start(bf16[256,1024]{1,0:T(8,128)(2,1)} %q_own.5), channel_id=1, source_target_pairs={{0,1},{1,0},{2,3},{3,2},{4,5},{5,4},{6,7},{7,6},{8,9},{9,8},{10,11... | collective-permute-start | bytes 1572872 | tf_op jit(solution)/shard_map/ppermute | solution.py:275
  2.6 0.7 %copy-start.2 = (s32[8]{0:T(128)S(1)}, s32[8]{0:T(128)}, u32[]{:S(2)}) copy-start(s32[8]{0:T(128)} %param.8) | copy-start | bytes 100
  4.8 12.6 %collective-permute-start.1 = (bf16[528,128]{1,0:T(8,128)(2,1)S(1)}, bf16[528,128]{1,0:T(8,128)(2,1)S(1)}, u32[]{:S(2)}, u32[]{:S(2)}) collective-permute-start(bf16[528,128]{1,0:T(8,128)(2,1)S(1)} %pad_maximum_fusion), channel_id=1, source_target_pairs={{0,32},{8,40},{16,48},{24,56},{32,0},{40,8},{48,16},{56,24},{64,96... | collective-permute-start | bytes 405512 | tf_op jit(solution)/shard_map/ppermute | solution.py:285
  17.5 7.9 %collective-permute-start.4 = (bf16[656,128]{1,0:T(8,128)(2,1)S(1)}, bf16[656,128]{1,0:T(8,128)(2,1)S(1)}, u32[]{:S(2)}, u32[]{:S(2)}) collective-permute-start(bf16[656,128]{1,0:T(8,128)(2,1)S(1)} %constant_dynamic-update-slice_fusion), channel_id=1, source_target_pairs={{0,8},{1,65},{2,10},{3,67},{4,12},{5,69},{6,14},{7,71},{8,16},{9,7... | collective-permute-start | bytes 503816 | tf_op jit(solution)/shard_map/ppermute | solution.py:296
  18.8 6.5 %collective-permute-start.3 = (bf16[256,128]{1,0:T(8,128)(2,1)S(1)}, bf16[256,128]{1,0:T(8,128)(2,1)S(1)}, u32[]{:S(2)}, u32[]{:S(2)}) collective-permute-start(bf16[256,128]{1,0:T(8,128)(2,1)S(1)} %get-tuple-element.53), channel_id=1, source_target_pairs={{0,64},{8,72},{16,80},{24,88},{64,128},{72,136},{80,144},{88,152},... | collective-permute-start | bytes 196616 | tf_op jit(solution)/shard_map/ppermute | solution.py:287
  21.9 9.2 %collective-permute-start.5 = (bf16[656,128]{1,0:T(8,128)(2,1)S(1)}, bf16[656,128]{1,0:T(8,128)(2,1)S(1)}, u32[]{:S(2)}, u32[]{:S(2)}) collective-permute-start(bf16[656,128]{1,0:T(8,128)(2,1)S(1)} %constant_dynamic-update-slice_fusion), channel_id=1, source_target_pairs={{0,16},{1,129},{2,18},{3,131},{4,20},{5,133},{6,22},{7,135},{8,24}... | collective-permute-start | bytes 503816 | tf_op jit(solution)/shard_map/ppermute | solution.py:296
  23.5 7.7 %collective-permute-start.6 = (bf16[656,128]{1,0:T(8,128)(2,1)S(1)}, bf16[656,128]{1,0:T(8,128)(2,1)S(1)}, u32[]{:S(2)}, u32[]{:S(2)}) collective-permute-start(bf16[656,128]{1,0:T(8,128)(2,1)S(1)} %constant_dynamic-update-slice_fusion), channel_id=1, source_target_pairs={{0,24},{1,193},{2,26},{3,195},{4,28},{5,197},{6,30},{7,199},{8,0},... | collective-permute-start | bytes 503816 | tf_op jit(solution)/shard_map/ppermute | solution.py:296
  25.4 8.7 %copy-start = (bf16[256,1024]{1,0:T(8,128)(2,1)S(1)}, bf16[256,1024]{1,0:T(8,128)(2,1)}, u32[]{:S(2)}) copy-start(bf16[256,1024]{1,0:T(8,128)(2,1)} %q_own.5) | copy-start | bytes 1572868
  25.4 8.7 %collective-permute-start.10 = (bf16[256,128]{1,0:T(8,128)(2,1)S(1)}, bf16[256,128]{1,0:T(8,128)(2,1)S(1)}, u32[]{:S(2)}, u32[]{:S(2)}) collective-permute-start(bf16[256,128]{1,0:T(8,128)(2,1)S(1)} %get-tuple-element.55), channel_id=1, source_target_pairs={{0,16},{8,24},{16,0},{24,8},{32,48},{40,56},{48,32},{56,40},{64,80... | collective-permute-start | bytes 196616 | tf_op jit(solution)/shard_map/ppermute | solution.py:299
  28.4 5.7 %collective-permute-start.9 = (bf16[256,128]{1,0:T(8,128)(2,1)S(1)}, bf16[256,128]{1,0:T(8,128)(2,1)S(1)}, u32[]{:S(2)}, u32[]{:S(2)}) collective-permute-start(bf16[256,128]{1,0:T(8,128)(2,1)S(1)} %get-tuple-element.56), channel_id=1, source_target_pairs={{0,8},{8,16},{16,24},{24,0},{32,40},{40,48},{48,56},{56,32},{64,72... | collective-permute-start | bytes 196616 | tf_op jit(solution)/shard_map/ppermute | solution.py:299
  28.8 5.3 %collective-permute-start.11 = (bf16[256,128]{1,0:T(8,128)(2,1)S(1)}, bf16[256,128]{1,0:T(8,128)(2,1)S(1)}, u32[]{:S(2)}, u32[]{:S(2)}) collective-permute-start(bf16[256,128]{1,0:T(8,128)(2,1)S(1)} %get-tuple-element.44), channel_id=1, source_target_pairs={{0,24},{8,0},{16,8},{24,16},{32,56},{40,32},{48,40},{56,48},{64,88... | collective-permute-start | bytes 196616 | tf_op jit(solution)/shard_map/ppermute | solution.py:299
  31.3 12.5 %collective-permute-start.7 = (bf16[2192,128]{1,0:T(8,128)(2,1)S(1)}, bf16[2192,128]{1,0:T(8,128)(2,1)S(1)}, u32[]{:S(2)}, u32[]{:S(2)}) collective-permute-start(bf16[2192,128]{1,0:T(8,128)(2,1)S(1)} %get-tuple-element.34.here.r0), channel_id=1, source_target_pairs={{0,64},{1,9},{2,66},{3,11},{4,68},{5,13},{6,70},{7,15},{8,72},{9,1... | collective-permute-start | bytes 1683464 | tf_op jit(solution)/shard_map/ppermute | solution.py:306
  31.4 12.4 %collective-permute-start.8 = (bf16[2192,128]{1,0:T(8,128)(2,1)S(1)}, bf16[2192,128]{1,0:T(8,128)(2,1)S(1)}, u32[]{:S(2)}, u32[]{:S(2)}) collective-permute-start(bf16[2192,128]{1,0:T(8,128)(2,1)S(1)} %get-tuple-element.34.here.r0), channel_id=1, source_target_pairs={{0,192},{1,25},{2,194},{3,27},{4,196},{5,29},{6,198},{7,31},{8,200... | collective-permute-start | bytes 1683464 | tf_op jit(solution)/shard_map/ppermute | solution.py:306
  40.7 10.3 %collective-permute-start.13 = (bf16[1168,128]{1,0:T(8,128)(2,1)S(1)}, bf16[1168,128]{1,0:T(8,128)(2,1)S(1)}, u32[]{:S(2)}, u32[]{:S(2)}) collective-permute-start(bf16[1168,128]{1,0:T(8,128)(2,1)S(1)} %slice.98), channel_id=1, source_target_pairs={{0,128},{1,17},{2,130},{3,19},{4,132},{5,21},{6,134},{7,23},{8,136... | collective-permute-start | bytes 897032 | tf_op jit(solution)/shard_map/ppermute | solution.py:314
  41.7 9.3 %collective-permute-start.12 = (bf16[1024,128]{1,0:T(8,128)(2,1)S(1)}, bf16[1024,128]{1,0:T(8,128)(2,1)S(1)}, u32[]{:S(2)}, u32[]{:S(2)}) collective-permute-start(bf16[1024,128]{1,0:T(8,128)(2,1)S(1)} %slice.97), channel_id=1, source_target_pairs={{0,128},{1,17},{2,130},{3,19},{4,132},{5,21},{6,134},{7,23},{8,136... | collective-permute-start | bytes 786440 | tf_op jit(solution)/shard_map/ppermute | solution.py:314
  52.3 9.2 %collective-permute-start.15 = (bf16[32,32,256]{2,1,0:T(8,128)(2,1)S(1)}, bf16[32,32,256]{2,1,0:T(8,128)(2,1)S(1)}, u32[]{:S(2)}, u32[]{:S(2)}) collective-permute-start(bf16[32,32,256]{2,1,0:T(8,128)(2,1)S(1)} %shard_map.72), channel_id=1, source_target_pairs={{0,1},{1,0},{2,3},{3,2},{4,5},{5,4},{6,7},{7,6},{8,9},{9,8},{10,11... | collective-permute-start | bytes 1572872 | tf_op jit(solution)/shard_map/ppermute | solution.py:324
  61.3 2.1 %collective-permute-start.14 = (bf16[256,1152]{1,0:T(8,128)(2,1)S(1)}, bf16[256,1152]{1,0:T(8,128)(2,1)S(1)}, u32[]{:S(2)}, u32[]{:S(2)}) collective-permute-start(bf16[256,1152]{1,0:T(8,128)(2,1)S(1)} %get-tuple-element.43), channel_id=1, source_target_pairs={{0,1},{1,0},{2,3},{3,2},{4,5},{5,4},{6,7},{7,6},{8,9},{9,8},{10,11... | collective-permute-start | bytes 1769480 | tf_op jit(solution)/shard_map/ppermute | solution.py:335

commit v12 on v11

--- a/solution.py
+++ b/solution.py
@@ -16,7 +16,8 @@
 HALF = 128
 META = 16
 CHUNK = 1024
-WIDE = 2
+WIDE = 4
+MIDDLE_WIDE = 2
 NEG = -1e30
 SCALE = math.log2(math.e) / math.sqrt(HD)
 F32 = jnp.float32
@@ -146,16 +147,16 @@
     put_range_bias(kr, vr, sc, (1, 3))
 
     def heads(i):
-        at = [WIDE * i + u for u in range(WIDE)]
+        at = [MIDDLE_WIDE * i + u for u in range(MIDDLE_WIDE)]
         q = [load_head(q_own, q_other, is_r, a) for a in at]
         state = [(m_in[a], l_in[a], o_in[a]) for a in at]
         for n in range(2):
             rows = slice(n * CHUNK, (n + 1) * CHUNK)
-            state = [fold(state[u], q[u], kr[rows, :], vr[rows, :]) for u in range(WIDE)]
-        for u in range(WIDE):
+            state = [fold(state[u], q[u], kr[rows, :], vr[rows, :]) for u in range(MIDDLE_WIDE)]
+        for u in range(MIDDLE_WIDE):
             m_out[at[u]], l_out[at[u]], o_out[at[u]] = state[u]
 
-    for i in range(GROUP // WIDE):
+    for i in range(GROUP // MIDDLE_WIDE):
         heads(i)
 
 

time: 65.2 us -> 64.2 us (0.985)
  Pallas kernels: 21.4 us -> 20.4 us
    pallas_call x5, Pallas kernels: 21.4 us -> 20.4 us  [call(): pl.pallas_call(kernel, out_shape=out_shape, in_specs=specs, out_specs=(VM...]
  transfers between devices with their start and end apart: 16 -> 16, of which waited for: 3 -> 3; matrix products, arithmetic and copies ran while one was open for 4% -> 4% of each run, Pallas kernels for 29% -> 28%
where the time goes in v12:
time: 64.2 us; the launch traced here: 64 us
  starting transfers between devices  29.8 us (46%)
  Pallas kernels  20.4 us (32%)
  waiting for transfers between devices  8.31 us (13%)
  other arithmetic  2.15 us (3%)
  local copies, waits for them, and re-layouts  1.78 us (3%)
  between operations  1.51 us (2%)
    pallas_call x5, Pallas kernels, call(): pl.pallas_call(kernel, out_shape=out_shape, in_specs=specs, out_specs=(VM...  20.4 us
    ppermute x1, waiting for transfers between devices, shards(): theirs = lax.ppermute(jnp.concatenate([ret, pas, meta]), 'ctx', Z_SWAP)  6.47 us
    ppermute x1, starting transfers between devices, shards(): theirs = lax.ppermute(jnp.concatenate([ret, pas, meta]), 'ctx', Z_SWAP)  6.1 us
    ppermute x3, starting transfers between devices, shards(): lax.ppermute(jnp.where(y + s < 4, pas, far), 'ctx', Y_SHIFT[s])  5.68 us
    ppermute x3, starting transfers between devices, shards(): got = {s: lax.ppermute(message, axes, STAGE_1[s]) for s in (1, 3, 2)}  4.63 us
    ppermute x1, starting transfers between devices, shards(): got_pages = lax.ppermute(pages, 'tp', CORE_SWAP)  3.57 us
    ppermute x1, starting transfers between devices, shards(): from_x = lax.ppermute(theirs[ROWS:2 * ROWS], 'ctx', X_STEP)  3.11 us
    ppermute x2, starting transfers between devices, shards(): lax.ppermute(message, axes, STAGE_2[s])  2.75 us
  transfers between devices with their start and end apart: 16, of which 3 were waited for; matrix products, arithmetic and copies ran while one was open for 4% of the time, Pallas kernels for 28%

profile of v12, /device:TPU:33, one launch (start us, length us, event | category | flops | bytes accessed | tf_op | source)
XLA Modules:
  0.0 64.0 jit_solution(17284734668853202671)
XLA Ops:
  0.6 0.8 %fusion.12 = (bf16[128,128]{1,0:T(8,128)(2,1)S(1)}, bf16[128,128]{1,0:T(8,128)(2,1)S(1)}, bf16[128,128]{1,0:T(8,128)(2,1)S(1)}, bf16[128,128]{1,0:T(8,128)(2,1)S(1)}) fusion(bf16[256,128]{1,0:T(8,128)(2,1)} %param.6, bf16[256,128]{1,0:T(8,128)(2,1)} %param.7), kind=kLoop, calls=%fused_computation.48 | loop fusion | bytes 262144 | tf_op jit(solution)/shard_map/slice | solution.py:272
  1.5 0.8 %collective-permute-start = (bf16[256,128]{1,0:T(8,128)(2,1)S(1)}, bf16[256,128]{1,0:T(8,128)(2,1)S(1)}, u32[]{:S(2)}, u32[]{:S(2)}) collective-permute-start(bf16[256,128]{1,0:T(8,128)(2,1)S(1)} %broadcast_select_fusion.5), channel_id=1, source_target_pairs={{0,1},{1,0},{2,3},{3,2},{4,5},{5,4},{6,7},{7,6},{8,9},{9,8},{10,11... | collective-permute-start | bytes 196616 | tf_op jit(solution)/shard_map/ppermute | solution.py:275
  2.3 0.1 collective-permute-start.2
  2.4 0.2 convert_reduce_fusion
  2.7 0.6 copy-done.2
  3.2 0.6 fusion.6
  4.6 0.1 broadcast_in_dim.24
  4.8 6.1 %collective-permute-start.1 = (bf16[528,128]{1,0:T(8,128)(2,1)S(1)}, bf16[528,128]{1,0:T(8,128)(2,1)S(1)}, u32[]{:S(2)}, u32[]{:S(2)}) collective-permute-start(bf16[528,128]{1,0:T(8,128)(2,1)S(1)} %pad_maximum_fusion), channel_id=1, source_target_pairs={{0,32},{8,40},{16,48},{24,56},{32,0},{40,8},{48,16},{56,24},{64,96... | collective-permute-start | bytes 405512 | tf_op jit(solution)/shard_map/ppermute | solution.py:286
  10.9 6.5 %collective-permute-done.1 = bf16[528,128]{1,0:T(8,128)(2,1)S(1)} collective-permute-done((bf16[528,128]{1,0:T(8,128)(2,1)S(1)}, bf16[528,128]{1,0:T(8,128)(2,1)S(1)}, u32[]{:S(2)}, u32[]{:S(2)}) %collective-permute-start.1) | collective-permute-done | bytes 135200 | tf_op jit(solution)/shard_map/ppermute | solution.py:286
  17.5 1.2 %collective-permute-start.4 = (bf16[656,128]{1,0:T(8,128)(2,1)S(1)}, bf16[656,128]{1,0:T(8,128)(2,1)S(1)}, u32[]{:S(2)}, u32[]{:S(2)}) collective-permute-start(bf16[656,128]{1,0:T(8,128)(2,1)S(1)} %constant_dynamic-update-slice_fusion), channel_id=1, source_target_pairs={{0,8},{1,65},{2,10},{3,67},{4,12},{5,69},{6,14},{7,71},{8,16},{9,7... | collective-permute-start | bytes 503816 | tf_op jit(solution)/shard_map/ppermute | solution.py:297
  18.7 0.1 stack.36.sc
  18.8 3.1 %collective-permute-start.3 = (bf16[256,128]{1,0:T(8,128)(2,1)S(1)}, bf16[256,128]{1,0:T(8,128)(2,1)S(1)}, u32[]{:S(2)}, u32[]{:S(2)}) collective-permute-start(bf16[256,128]{1,0:T(8,128)(2,1)S(1)} %get-tuple-element.53), channel_id=1, source_target_pairs={{0,64},{8,72},{16,80},{24,88},{64,128},{72,136},{80,144},{88,152},... | collective-permute-start | bytes 196616 | tf_op jit(solution)/shard_map/ppermute | solution.py:288
  21.9 1.5 %collective-permute-start.5 = (bf16[656,128]{1,0:T(8,128)(2,1)S(1)}, bf16[656,128]{1,0:T(8,128)(2,1)S(1)}, u32[]{:S(2)}, u32[]{:S(2)}) collective-permute-start(bf16[656,128]{1,0:T(8,128)(2,1)S(1)} %constant_dynamic-update-slice_fusion), channel_id=1, source_target_pairs={{0,16},{1,129},{2,18},{3,131},{4,20},{5,133},{6,22},{7,135},{8,24}... | collective-permute-start | bytes 503816 | tf_op jit(solution)/shard_map/ppermute | solution.py:297
  23.5 1.9 %collective-permute-start.6 = (bf16[656,128]{1,0:T(8,128)(2,1)S(1)}, bf16[656,128]{1,0:T(8,128)(2,1)S(1)}, u32[]{:S(2)}, u32[]{:S(2)}) collective-permute-start(bf16[656,128]{1,0:T(8,128)(2,1)S(1)} %constant_dynamic-update-slice_fusion), channel_id=1, source_target_pairs={{0,24},{1,193},{2,26},{3,195},{4,28},{5,197},{6,30},{7,199},{8,0},... | collective-permute-start | bytes 503816 | tf_op jit(solution)/shard_map/ppermute | solution.py:297
  25.4 3.0 %collective-permute-start.10 = (bf16[256,128]{1,0:T(8,128)(2,1)S(1)}, bf16[256,128]{1,0:T(8,128)(2,1)S(1)}, u32[]{:S(2)}, u32[]{:S(2)}) collective-permute-start(bf16[256,128]{1,0:T(8,128)(2,1)S(1)} %get-tuple-element.55), channel_id=1, source_target_pairs={{0,16},{8,24},{16,0},{24,8},{32,48},{40,56},{48,32},{56,40},{64,80... | collective-permute-start | bytes 196616 | tf_op jit(solution)/shard_map/ppermute | solution.py:300
  28.4 0.4 collective-permute-start.9
  28.8 2.3 %collective-permute-start.11 = (bf16[256,128]{1,0:T(8,128)(2,1)S(1)}, bf16[256,128]{1,0:T(8,128)(2,1)S(1)}, u32[]{:S(2)}, u32[]{:S(2)}) collective-permute-start(bf16[256,128]{1,0:T(8,128)(2,1)S(1)} %get-tuple-element.44), channel_id=1, source_target_pairs={{0,24},{8,0},{16,8},{24,16},{32,56},{40,32},{48,40},{56,48},{64,88... | collective-permute-start | bytes 196616 | tf_op jit(solution)/shard_map/ppermute | solution.py:300
  31.2 0.1 constant_dynamic-update-slice_fusion.5
  31.3 0.1 collective-permute-start.7
  31.4 2.7 %collective-permute-start.8 = (bf16[2192,128]{1,0:T(8,128)(2,1)S(1)}, bf16[2192,128]{1,0:T(8,128)(2,1)S(1)}, u32[]{:S(2)}, u32[]{:S(2)}) collective-permute-start(bf16[2192,128]{1,0:T(8,128)(2,1)S(1)} %get-tuple-element.34.here.r0), channel_id=1, source_target_pairs={{0,192},{1,25},{2,194},{3,27},{4,196},{5,29},{6,198},{7,31},{8,200... | collective-permute-start | bytes 1683464 | tf_op jit(solution)/shard_map/ppermute | solution.py:307
  34.1 5.9 %shard_map.68 = (f32[8,256,128]{2,1,0:T(8,128)S(1)}, f32[8,256,128]{2,1,0:T(8,128)S(1)}, f32[8,256,128]{2,1,0:T(8,128)S(1)}, f32[8,256,128]{2,1,0:T(8,128)S(1)},...) custom-call(s32[8]{0:T(128)S(1)} %stack.36.sc, bf16[256,1024]{1,0:T(8,128)(2,1)S(1)} %copy-done, ...), custom_call_target="tpu_custom_call" | custom-call | flops 32212254720 | bytes 4194304 | tf_op jit(solution)/shard_map/pallas_call | solution.py:249
  40.0 1.0 %collective-permute-start.13 = (bf16[1168,128]{1,0:T(8,128)(2,1)S(1)}, bf16[1168,128]{1,0:T(8,128)(2,1)S(1)}, u32[]{:S(2)}, u32[]{:S(2)}) collective-permute-start(bf16[1168,128]{1,0:T(8,128)(2,1)S(1)} %slice.98), channel_id=1, source_target_pairs={{0,128},{1,17},{2,130},{3,19},{4,132},{5,21},{6,134},{7,23},{8,136... | collective-permute-start | bytes 897032 | tf_op jit(solution)/shard_map/ppermute | solution.py:315
  41.0 2.1 %collective-permute-start.12 = (bf16[1024,128]{1,0:T(8,128)(2,1)S(1)}, bf16[1024,128]{1,0:T(8,128)(2,1)S(1)}, u32[]{:S(2)}, u32[]{:S(2)}) collective-permute-start(bf16[1024,128]{1,0:T(8,128)(2,1)S(1)} %slice.97), channel_id=1, source_target_pairs={{0,128},{1,17},{2,130},{3,19},{4,132},{5,21},{6,134},{7,23},{8,136... | collective-permute-start | bytes 786440 | tf_op jit(solution)/shard_map/ppermute | solution.py:315
  43.1 6.6 %shard_map.69 = (f32[8,256,128]{2,1,0:T(8,128)S(1)}, f32[8,256,128]{2,1,0:T(8,128)S(1)}, f32[8,256,128]{2,1,0:T(8,128)S(1)}) custom-call(s32[8]{0:T(128)S(1)} %stack.36.sc, bf16[256,1024]{1,0:T(8,128)(2,1)S(1)} %copy-done, bf16[256,1024]{1,0:T(8,128)(2,1)S(1)} %collective-permute-done.2.q_other, bf16[2192,128]{1,0:T(8,128)(2,1)S(1)} %collective-permute-done.7.r1, ...), custom_call_target="tpu_custom_call" | custom-call | flops 4294967296 | bytes 4194304 | tf_op jit(solution)/shard_map/pallas_call | solution.py:249
  49.7 0.7 %collective-permute-done.12.r2a = bf16[1024,128]{1,0:T(8,128)(2,1)S(1)} collective-permute-done((bf16[1024,128]{1,0:T(8,128)(2,1)S(1)}, bf16[1024,128]{1,0:T(8,128)(2,1)S(1)}, u32[]{:S(2)}, u32[]{:S(2)}) %collective-permute-start.12) | collective-permute-done | bytes 262176 | tf_op jit(solution)/shard_map/ppermute | solution.py:315
  50.4 1.2 %shard_map.72 = bf16[32,32,256]{2,1,0:T(8,128)(2,1)S(1)} custom-call(s32[8]{0:T(128)S(1)} %stack.36.sc, bf16[2192,128]{1,0:T(8,128)(2,1)S(1)} %get-tuple-element.34.here.r0, bf16[2192,128]{1,0:T(8,128)(2,1)S(1)} %collective-permute-done.7.r1, bf16[1024,128]{1,0:T(8,128)(2,1)S(1)} %collective-permute-done.12.r2a, ...), custom_call_target="tpu_custom_call" | custom-call | flops 134217728 | bytes 4194304 | tf_op jit(solution)/shard_map/pallas_call | solution.py:249
  51.6 3.6 %collective-permute-start.15 = (bf16[32,32,256]{2,1,0:T(8,128)(2,1)S(1)}, bf16[32,32,256]{2,1,0:T(8,128)(2,1)S(1)}, u32[]{:S(2)}, u32[]{:S(2)}) collective-permute-start(bf16[32,32,256]{2,1,0:T(8,128)(2,1)S(1)} %shard_map.72), channel_id=1, source_target_pairs={{0,1},{1,0},{2,3},{3,2},{4,5},{5,4},{6,7},{7,6},{8,9},{9,8},{10,11... | collective-permute-start | bytes 1572872 | tf_op jit(solution)/shard_map/ppermute | solution.py:325
  55.1 5.2 %shard_map.70 = (bf16[256,1024]{1,0:T(8,128)(2,1)S(1)}, f32[256,128]{1,0:T(8,128)S(1)}, bf16[256,1152]{1,0:T(8,128)(2,1)S(1)}) custom-call(s32[8]{0:T(128)S(1)} %stack.36.sc, bf16[256,1024]{1,0:T(8,128)(2,1)S(1)} %copy-done, bf16[256,1024]{1,0:T(8,128)(2,1)S(1)} %collective-permute-done.2.q_other, bf16[1024,128]{1,0:T(8,128)(2,1)S(1)} %collective-permute-done.12.r2a, ...), custom_call_target="tpu_custom_call" | custom-call | flops 2684354560 | bytes 4194304 | tf_op jit(solution)/shard_map/pallas_call | solution.py:249
  60.3 0.1 collective-permute-start.14
  60.4 0.9 %add_select_fusion = bf16[32,32,256]{2,1,0:T(8,128)(2,1)} fusion(bf16[32,32,256]{2,1,0:T(8,128)(2,1)S(1)} %shard_map.72, bf16[32,32,256]{2,1,0:T(8,128)(2,1)S(1)} %collective-permute-done.15, pred[]{:T(512)S(6)} %eq.80), kind=kLoop, calls=%fused_computation | loop fusion | flops 524288 | bytes 1572865 | tf_op jit(solution)/shard_map/jit(_where)/select_n | solution.py:339
  61.3 1.1 %collective-permute-done.14.got = bf16[256,1152]{1,0:T(8,128)(2,1)S(1)} collective-permute-done((bf16[256,1152]{1,0:T(8,128)(2,1)S(1)}, bf16[256,1152]{1,0:T(8,128)(2,1)S(1)}, u32[]{:S(2)}, u32[]{:S(2)}) %collective-permute-start.14) | collective-permute-done | bytes 589856 | tf_op jit(solution)/shard_map/ppermute | solution.py:336
  62.4 1.6 %shard_map.71 = bf16[256,1024]{1,0:T(8,128)(2,1)} custom-call(bf16[256,1024]{1,0:T(8,128)(2,1)S(1)} %get-tuple-element.41.keep, f32[256,128]{1,0:T(8,128)S(1)} %get-tuple-element.42.keep_ml, bf16[256,1152]{1,0:T(8,128)(2,1)S(1)} %collective-permute-done.14.got), custom_call_target="tpu_custom_call" | custom-call | flops 134217728 | bytes 4194304 | tf_op jit(solution)/shard_map/pallas_call | solution.py:249
  (42 shorter events, 0.7 us)
Async XLA Ops:
  1.5 0.9 %copy-start.1 = (s32[16]{0:T(128)S(1)}, s32[16]{0:T(128)}, u32[]{:S(2)}) copy-start(s32[16]{0:T(128)} %param.9) | copy-start | bytes 196
  1.5 3.2 %collective-permute-start = (bf16[256,128]{1,0:T(8,128)(2,1)S(1)}, bf16[256,128]{1,0:T(8,128)(2,1)S(1)}, u32[]{:S(2)}, u32[]{:S(2)}) collective-permute-start(bf16[256,128]{1,0:T(8,128)(2,1)S(1)} %broadcast_select_fusion.5), channel_id=1, source_target_pairs={{0,1},{1,0},{2,3},{3,2},{4,5},{5,4},{6,7},{7,6},{8,9},{9,8},{10,11... | collective-permute-start | bytes 196616 | tf_op jit(solution)/shard_map/ppermute | solution.py:275
  2.3 15.1 %collective-permute-start.2 = (bf16[256,1024]{1,0:T(8,128)(2,1)}, bf16[256,1024]{1,0:T(8,128)(2,1)S(1)}, u32[]{:S(2)}, u32[]{:S(2)}) collective-permute-start(bf16[256,1024]{1,0:T(8,128)(2,1)} %q_own.5), channel_id=1, source_target_pairs={{0,1},{1,0},{2,3},{3,2},{4,5},{5,4},{6,7},{7,6},{8,9},{9,8},{10,11... | collective-permute-start | bytes 1572872 | tf_op jit(solution)/shard_map/ppermute | solution.py:276
  2.6 0.7 %copy-start.2 = (s32[8]{0:T(128)S(1)}, s32[8]{0:T(128)}, u32[]{:S(2)}) copy-start(s32[8]{0:T(128)} %param.8) | copy-start | bytes 100
  4.8 12.6 %collective-permute-start.1 = (bf16[528,128]{1,0:T(8,128)(2,1)S(1)}, bf16[528,128]{1,0:T(8,128)(2,1)S(1)}, u32[]{:S(2)}, u32[]{:S(2)}) collective-permute-start(bf16[528,128]{1,0:T(8,128)(2,1)S(1)} %pad_maximum_fusion), channel_id=1, source_target_pairs={{0,32},{8,40},{16,48},{24,56},{32,0},{40,8},{48,16},{56,24},{64,96... | collective-permute-start | bytes 405512 | tf_op jit(solution)/shard_map/ppermute | solution.py:286
  17.5 7.9 %collective-permute-start.4 = (bf16[656,128]{1,0:T(8,128)(2,1)S(1)}, bf16[656,128]{1,0:T(8,128)(2,1)S(1)}, u32[]{:S(2)}, u32[]{:S(2)}) collective-permute-start(bf16[656,128]{1,0:T(8,128)(2,1)S(1)} %constant_dynamic-update-slice_fusion), channel_id=1, source_target_pairs={{0,8},{1,65},{2,10},{3,67},{4,12},{5,69},{6,14},{7,71},{8,16},{9,7... | collective-permute-start | bytes 503816 | tf_op jit(solution)/shard_map/ppermute | solution.py:297
  18.8 6.5 %collective-permute-start.3 = (bf16[256,128]{1,0:T(8,128)(2,1)S(1)}, bf16[256,128]{1,0:T(8,128)(2,1)S(1)}, u32[]{:S(2)}, u32[]{:S(2)}) collective-permute-start(bf16[256,128]{1,0:T(8,128)(2,1)S(1)} %get-tuple-element.53), channel_id=1, source_target_pairs={{0,64},{8,72},{16,80},{24,88},{64,128},{72,136},{80,144},{88,152},... | collective-permute-start | bytes 196616 | tf_op jit(solution)/shard_map/ppermute | solution.py:288
  21.9 9.2 %collective-permute-start.5 = (bf16[656,128]{1,0:T(8,128)(2,1)S(1)}, bf16[656,128]{1,0:T(8,128)(2,1)S(1)}, u32[]{:S(2)}, u32[]{:S(2)}) collective-permute-start(bf16[656,128]{1,0:T(8,128)(2,1)S(1)} %constant_dynamic-update-slice_fusion), channel_id=1, source_target_pairs={{0,16},{1,129},{2,18},{3,131},{4,20},{5,133},{6,22},{7,135},{8,24}... | collective-permute-start | bytes 503816 | tf_op jit(solution)/shard_map/ppermute | solution.py:297
  23.5 7.7 %collective-permute-start.6 = (bf16[656,128]{1,0:T(8,128)(2,1)S(1)}, bf16[656,128]{1,0:T(8,128)(2,1)S(1)}, u32[]{:S(2)}, u32[]{:S(2)}) collective-permute-start(bf16[656,128]{1,0:T(8,128)(2,1)S(1)} %constant_dynamic-update-slice_fusion), channel_id=1, source_target_pairs={{0,24},{1,193},{2,26},{3,195},{4,28},{5,197},{6,30},{7,199},{8,0},... | collective-permute-start | bytes 503816 | tf_op jit(solution)/shard_map/ppermute | solution.py:297
  25.4 8.7 %copy-start = (bf16[256,1024]{1,0:T(8,128)(2,1)S(1)}, bf16[256,1024]{1,0:T(8,128)(2,1)}, u32[]{:S(2)}) copy-start(bf16[256,1024]{1,0:T(8,128)(2,1)} %q_own.5) | copy-start | bytes 1572868
  25.4 8.7 %collective-permute-start.10 = (bf16[256,128]{1,0:T(8,128)(2,1)S(1)}, bf16[256,128]{1,0:T(8,128)(2,1)S(1)}, u32[]{:S(2)}, u32[]{:S(2)}) collective-permute-start(bf16[256,128]{1,0:T(8,128)(2,1)S(1)} %get-tuple-element.55), channel_id=1, source_target_pairs={{0,16},{8,24},{16,0},{24,8},{32,48},{40,56},{48,32},{56,40},{64,80... | collective-permute-start | bytes 196616 | tf_op jit(solution)/shard_map/ppermute | solution.py:300
  28.4 5.7 %collective-permute-start.9 = (bf16[256,128]{1,0:T(8,128)(2,1)S(1)}, bf16[256,128]{1,0:T(8,128)(2,1)S(1)}, u32[]{:S(2)}, u32[]{:S(2)}) collective-permute-start(bf16[256,128]{1,0:T(8,128)(2,1)S(1)} %get-tuple-element.56), channel_id=1, source_target_pairs={{0,8},{8,16},{16,24},{24,0},{32,40},{40,48},{48,56},{56,32},{64,72... | collective-permute-start | bytes 196616 | tf_op jit(solution)/shard_map/ppermute | solution.py:300
  28.8 5.3 %collective-permute-start.11 = (bf16[256,128]{1,0:T(8,128)(2,1)S(1)}, bf16[256,128]{1,0:T(8,128)(2,1)S(1)}, u32[]{:S(2)}, u32[]{:S(2)}) collective-permute-start(bf16[256,128]{1,0:T(8,128)(2,1)S(1)} %get-tuple-element.44), channel_id=1, source_target_pairs={{0,24},{8,0},{16,8},{24,16},{32,56},{40,32},{48,40},{56,48},{64,88... | collective-permute-start | bytes 196616 | tf_op jit(solution)/shard_map/ppermute | solution.py:300
  31.3 11.8 %collective-permute-start.7 = (bf16[2192,128]{1,0:T(8,128)(2,1)S(1)}, bf16[2192,128]{1,0:T(8,128)(2,1)S(1)}, u32[]{:S(2)}, u32[]{:S(2)}) collective-permute-start(bf16[2192,128]{1,0:T(8,128)(2,1)S(1)} %get-tuple-element.34.here.r0), channel_id=1, source_target_pairs={{0,64},{1,9},{2,66},{3,11},{4,68},{5,13},{6,70},{7,15},{8,72},{9,1... | collective-permute-start | bytes 1683464 | tf_op jit(solution)/shard_map/ppermute | solution.py:307
  31.4 11.7 %collective-permute-start.8 = (bf16[2192,128]{1,0:T(8,128)(2,1)S(1)}, bf16[2192,128]{1,0:T(8,128)(2,1)S(1)}, u32[]{:S(2)}, u32[]{:S(2)}) collective-permute-start(bf16[2192,128]{1,0:T(8,128)(2,1)S(1)} %get-tuple-element.34.here.r0), channel_id=1, source_target_pairs={{0,192},{1,25},{2,194},{3,27},{4,196},{5,29},{6,198},{7,31},{8,200... | collective-permute-start | bytes 1683464 | tf_op jit(solution)/shard_map/ppermute | solution.py:307
  40.0 10.3 %collective-permute-start.13 = (bf16[1168,128]{1,0:T(8,128)(2,1)S(1)}, bf16[1168,128]{1,0:T(8,128)(2,1)S(1)}, u32[]{:S(2)}, u32[]{:S(2)}) collective-permute-start(bf16[1168,128]{1,0:T(8,128)(2,1)S(1)} %slice.98), channel_id=1, source_target_pairs={{0,128},{1,17},{2,130},{3,19},{4,132},{5,21},{6,134},{7,23},{8,136... | collective-permute-start | bytes 897032 | tf_op jit(solution)/shard_map/ppermute | solution.py:315
  41.0 9.3 %collective-permute-start.12 = (bf16[1024,128]{1,0:T(8,128)(2,1)S(1)}, bf16[1024,128]{1,0:T(8,128)(2,1)S(1)}, u32[]{:S(2)}, u32[]{:S(2)}) collective-permute-start(bf16[1024,128]{1,0:T(8,128)(2,1)S(1)} %slice.97), channel_id=1, source_target_pairs={{0,128},{1,17},{2,130},{3,19},{4,132},{5,21},{6,134},{7,23},{8,136... | collective-permute-start | bytes 786440 | tf_op jit(solution)/shard_map/ppermute | solution.py:315
  51.6 8.9 %collective-permute-start.15 = (bf16[32,32,256]{2,1,0:T(8,128)(2,1)S(1)}, bf16[32,32,256]{2,1,0:T(8,128)(2,1)S(1)}, u32[]{:S(2)}, u32[]{:S(2)}) collective-permute-start(bf16[32,32,256]{2,1,0:T(8,128)(2,1)S(1)} %shard_map.72), channel_id=1, source_target_pairs={{0,1},{1,0},{2,3},{3,2},{4,5},{5,4},{6,7},{7,6},{8,9},{9,8},{10,11... | collective-permute-start | bytes 1572872 | tf_op jit(solution)/shard_map/ppermute | solution.py:325
  60.3 2.1 %collective-permute-start.14 = (bf16[256,1152]{1,0:T(8,128)(2,1)S(1)}, bf16[256,1152]{1,0:T(8,128)(2,1)S(1)}, u32[]{:S(2)}, u32[]{:S(2)}) collective-permute-start(bf16[256,1152]{1,0:T(8,128)(2,1)S(1)} %get-tuple-element.43), channel_id=1, source_target_pairs={{0,1},{1,0},{2,3},{3,2},{4,5},{5,4},{6,7},{7,6},{8,9},{9,8},{10,11... | collective-permute-start | bytes 1769480 | tf_op jit(solution)/shard_map/ppermute | solution.py:336
